TPU v7x, 32 devices: a whole 2x2x4 slice. The times are simulated.
32 devices in a mesh: row: 4 (over y, x), col: 8 (over z, core).
Axes of the slice: x: 2, y: 2, z: 4, core: 2. Of those that a mesh axis runs over, the one named last changes fastest.
Arguments:
- film_embeds: float32 [4096, 1024], P(('row', 'col')), may hold values from -120 to 120
- text_embeds: float32 [4096, 1024], P(('col', 'row')), may hold values from -150 to 150
- matched_text_index: int32 [4096], replicated, may hold values from 0 to 4095, as said below
- sharpness_factor: float32 [1], replicated, may hold values from 20 to 60
- affinity_offset: float32 [1], replicated, may hold values from -12 to -6
Outputs:
- clip_loss: float32 [4096], P(('row', 'col'))
- grad_videos: float32 [4096, 1024], P(('row', 'col'))
- grad_captions: float32 [4096, 1024], P(('col', 'row'))
Inputs may be any that keep to these rules, and one draw needn't show every extreme that they name: `matched_text_index`: each caption is the positive of exactly one clip.
All inputs are finite; a program needn't handle non-finite values.
Results may differ from a plain program's by a relative error of at most 0.0037.
Values may be sent and summed in bfloat16 or wider, within the bound.
No kernel may reach another device: no remote copies, remote signals or barrier semaphores. Data moves between devices by JAX's collectives and lax.ppermute only.
A program may use at most 128 MiB of HBM per device.

v0:
```python
import math

import jax
import jax.numpy as jnp
from jax import lax
from jax.sharding import PartitionSpec as P


def normalize(embed):
    inverse = lax.rsqrt(jnp.sum(embed * embed, axis=1, keepdims=True) + 1e-06)
    return (embed * inverse, inverse)


def backward_norm(hat, inverse, grad_hat):
    return inverse * (grad_hat - hat * jnp.sum(hat * grad_hat, axis=1, keepdims=True))


def shards(film_embeds, text_embeds, matched_text_index, sharpness_factor, affinity_offset):
    vhat, vnorm = normalize(film_embeds)
    chat, cnorm = normalize(text_embeds)
    width = film_embeds.shape[1]
    vrows = lax.all_gather(vhat.astype(jnp.bfloat16), "col", axis=0, tiled=True)
    crows = lax.all_gather(chat.astype(jnp.bfloat16), "row", axis=0, tiled=True)
    film_entries_local = vrows.shape[0]
    caption_row_count = crows.shape[0]
    similarity_multiplier = sharpness_factor[0]
    shift = affinity_offset[0]
    labels = lax.dynamic_slice_in_dim(
        matched_text_index, lax.axis_index("row") * film_entries_local, film_entries_local, 0
    )
    matching_text_indices = lax.axis_index("col") * caption_row_count + jnp.arange(
        caption_row_count, dtype=jnp.int32
    )
    step_rows = math.gcd(film_entries_local, 512)
    vblocks = vrows.reshape(film_entries_local // step_rows, step_rows, width)
    lblocks = labels.reshape(film_entries_local // step_rows, step_rows)

    def tile(pair):
        vblock, lblock = pair
        logits = (
            jnp.dot(vblock, crows.T, preferred_element_type=jnp.float32) * similarity_multiplier
            + shift
        )
        match = lblock[:, None] == matching_text_indices[None, :]
        sign = jnp.where(match, 1.0, -1.0).astype(jnp.float32)
        losses = jnp.sum(jax.nn.softplus(-sign * logits), axis=1)
        coef = (jax.nn.sigmoid(logits) - match.astype(jnp.float32)).astype(jnp.bfloat16)
        return (coef, losses)

    own_rows = film_embeds.shape[0]
    count = own_rows * lax.axis_size("col")
    sub = math.gcd(count, 512)
    vpart = vrows.reshape(count // sub, sub, width)
    lpart = labels.reshape(count // sub, sub)

    def one(pair):
        coef, losses = tile(pair)
        return (
            similarity_multiplier * jnp.dot(coef, crows, preferred_element_type=jnp.float32),
            losses,
        )

    grads, losses = lax.map(one, (vpart, lpart))
    dvhat = lax.psum_scatter(
        (grads.reshape(count, width), losses.reshape(count))[0],
        "col",
        scatter_dimension=0,
        tiled=True,
    )
    clip_loss = lax.psum_scatter(
        lax.map(lambda pair: tile(pair)[1], (vblocks, lblocks)).reshape(film_entries_local),
        "col",
        scatter_dimension=0,
        tiled=True,
    )

    def add(total, pair):
        vblock, lblock = pair
        logits = (
            jnp.dot(vblock, crows.T, preferred_element_type=jnp.float32) * similarity_multiplier
            + shift
        )
        match = lblock[:, None] == matching_text_indices[None, :]
        coef = (jax.nn.sigmoid(logits) - match.astype(jnp.float32)).astype(jnp.bfloat16)
        return (
            total
            + lax.dot_general(
                coef, vblock, (((0,), (0,)), ((), ())), preferred_element_type=jnp.float32
            ),
            None,
        )

    total, discarded_value = lax.scan(
        add,
        jnp.zeros((text_embeds.shape[0] * lax.axis_size("row"), width), jnp.float32),
        (vblocks, lblocks),
    )
    dchat = lax.psum_scatter(similarity_multiplier * total, "row", scatter_dimension=0, tiled=True)
    return (clip_loss, backward_norm(vhat, vnorm, dvhat), backward_norm(chat, cnorm, dchat))


def solution(mesh):
    return jax.shard_map(
        shards,
        mesh=mesh,
        in_specs=(P(("row", "col"), None), P(("col", "row"), None), P(), P(), P()),
        out_specs=(P(("row", "col")), P(("row", "col"), None), P(("col", "row"), None)),
        check_vma=False,
    )
```

profile of v0, /device:TPU:0, one launch (start us, length us, event | category | flops | bytes accessed | tf_op | source)
XLA Modules:
  0.0 179.5 jit_solution(6964149458271569008)
XLA Ops:
  7.2 0.0 all-gather.5.cloned.1.call-start
  7.2 1.2 multiply_reduce_fusion.2
  8.4 1.8 %multiply_convert_fusion = bf16[128,1024]{1,0:T(8,128)(2,1)} fusion(f32[128,1024]{1,0:T(8,128)} %param.12, f32[128]{0:T(128)S(1)} %add_rsqrt_fusion), kind=kLoop, calls=%fused_computation.65 | loop fusion | flops 262144 | bytes 786944 | tf_op jit(solution)/shard_map/convert_element_type | solution.py:23
  10.3 0.0 all-gather.5.cloned.1.call-update
  10.3 0.0 all-gather.3.cloned.1.call-start
  10.4 1.2 multiply_reduce_fusion.3
  11.5 0.8 multiply_convert_fusion.1
  12.4 0.0 reduce-scatter.5.cloned.1.call-start
  12.4 0.7 dynamic_slice.23
  13.8 26.0 %all-gather.5.cloned.1.call-done = bf16[512,1024]{1,0:T(8,128)(2,1)} async-done(((bf16[128,1024]{1,0:T(8,128)(2,1)}), bf16[512,1024]{1,0:T(8,128)(2,1)}) %all-gather.5.cloned.1.call-update) | async-done | bytes 1048592 | tf_op jit(solution)/shard_map/all_gather | solution.py:23
  39.8 31.3 %all-gather.3.cloned.1.call-done = bf16[1024,1024]{1,0:T(8,128)(2,1)} async-done(((bf16[128,1024]{1,0:T(8,128)(2,1)}), bf16[1024,1024]{1,0:T(8,128)(2,1)}) %all-gather.3.cloned.1.call-update) | async-done | bytes 2097168 | tf_op jit(solution)/shard_map/all_gather | solution.py:22
  71.1 9.9 %while.35 = (s32[]{:T(128)}, f32[512,1024]{1,0:T(8,128)S(1)}, bf16[2,512,1024]{2,1,0:T(8,128)(2,1)}, bf16[512,1024]{1,0:T(8,128)(2,1)}, f32[]{:T(128)}, /*index=...) while((s32[]{:T(128)}, f32[512,1024]{1,0:T(8,128)S(1)}, ...), condition=%wide.region_11.12_spmd.clone, body=%wide.region_10.11_spmd.clone.sunk | while | flops 1077150208 | bytes 7351942 | solution.py:93
  71.1 4.9 %select_add_fusion.2 = f32[512,1024]{1,0:T(8,128)S(1)} fusion(f32[512,1024]{1,0:T(8,128)S(1)} %get-tuple-element.463, bf16[512,1024]{1,0:T(8,128)(2,1)} %get-tuple-element.475, bf16[2,512,1024]{2,1,0:T(8,128)(2,1)} %get-tuple-element.474, s32[]{:T(128)S(6)} %copy.25, pred[]{:T(512)S(6)} %compare.3, s32[512]{0:T(512)S(1)} %iota_add_fusion.8, ...), kind=kOutput, calls=%fused_computation.35.clone.1 | convolution fusion | flops 1077149696 | bytes 7345672 | tf_op jit(solution)/shard_map/while/body/eval_jaxpr/dot_general | solution.py:87
  76.1 4.9 %select_add_fusion.2 = f32[512,1024]{1,0:T(8,128)S(1)} fusion(f32[512,1024]{1,0:T(8,128)S(1)} %get-tuple-element.463, bf16[512,1024]{1,0:T(8,128)(2,1)} %get-tuple-element.475, bf16[2,512,1024]{2,1,0:T(8,128)(2,1)} %get-tuple-element.474, s32[]{:T(128)S(6)} %copy.25, pred[]{:T(512)S(6)} %compare.3, s32[512]{0:T(512)S(1)} %iota_add_fusion.8, ...), kind=kOutput, calls=%fused_computation.35.clone.1 | convolution fusion | flops 1077149696 | bytes 7345672 | tf_op jit(solution)/shard_map/while/body/eval_jaxpr/dot_general | solution.py:87
  81.0 1.5 broadcast_multiply_fusion
  82.5 0.0 reduce-scatter.3.cloned.1.call-start
  82.6 1.5 copy-done.2
  84.1 11.7 %while.34 = (s32[]{:T(128)}, f32[2,512,1024]{2,1,0:T(8,128)}, f32[]{:T(128)}, bf16[2,512,1024]{2,1,0:T(8,128)(2,1)S(1)}, bf16[512,1024]{1,0:T(8,128)(2,1)}, /*in...) while((s32[]{:T(128)}, f32[2,512,1024]{2,1,0:T(8,128)}, f32[]{:T(128)}, ...), condition=%wide.region_7.8_spmd.clone, body=%wide.region_6.7_spmd.clone.sunk | while | flops 1076625920 | bytes 5255789 | solution.py:63
  84.1 5.9 %bitcast_dynamic-update-slice_fusion.2 = f32[2,512,1024]{2,1,0:T(8,128)} fusion(f32[2,512,1024]{2,1,0:T(8,128)} %get-tuple-element.435, s32[]{:T(128)S(6)} %copy.19, bf16[512,1024]{1,0:T(8,128)(2,1)} %get-tuple-element.447, bf16[2,512,1024]{2,1,0:T(8,128)(2,1)S(1)} %get-tuple-element.446, f32[]{:T(128)} %get-tuple-element.445, ...), kind=kOutput, calls=%fused_computation.13.clone.1 | convolution fusion | flops 1076625408 | bytes 5249536 | tf_op jit(solution)/shard_map/while/body/eval_jaxpr/dot_general | solution.py:59
  90.0 5.8 %bitcast_dynamic-update-slice_fusion.2 = f32[2,512,1024]{2,1,0:T(8,128)} fusion(f32[2,512,1024]{2,1,0:T(8,128)} %get-tuple-element.435, s32[]{:T(128)S(6)} %copy.19, bf16[512,1024]{1,0:T(8,128)(2,1)} %get-tuple-element.447, bf16[2,512,1024]{2,1,0:T(8,128)(2,1)S(1)} %get-tuple-element.446, f32[]{:T(128)} %get-tuple-element.445, ...), kind=kOutput, calls=%fused_computation.13.clone.1 | convolution fusion | flops 1076625408 | bytes 5249536 | tf_op jit(solution)/shard_map/while/body/eval_jaxpr/dot_general | solution.py:59
  95.9 0.6 copy-done.3
  96.5 0.6 dynamic-slice
  97.8 8.1 %while.33 = (s32[]{:T(128)}, f32[2,512]{1,0:T(2,128)S(1)}, s32[2,512]{1,0:T(2,128)S(1)}, bf16[2,512,1024]{2,1,0:T(8,128)(2,1)S(1)}, bf16[512,1024]{1,0:T(8,128)(...) while((s32[]{:T(128)}, f32[2,512]{1,0:T(2,128)S(1)}, ...), condition=%wide.region_4.5_spmd.clone, body=%wide.region_2.4_spmd.clone.sunk | while | flops 540278784 | bytes 2113669 | solution.py:71
  97.8 4.0 %fusion.73 = f32[512]{0:T(512)S(1)} fusion(bf16[512,1024]{1,0:T(8,128)(2,1)} %get-tuple-element.419, bf16[2,512,1024]{2,1,0:T(8,128)(2,1)S(1)} %get-tuple-element.418, s32[]{:T(128)S(6)} %copy.13, f32[]{:T(128)} %get-tuple-element.421, f32[]{:T(128)} %get-tuple-element.420, s32[512]{0:T(512)S(1)} %bitcast.64, s32[512]{0:T(512)S(1)} %iota_add_fusion.6), kind=kOutput, calls=%fused_computation.7.clone.1 | convolution fusion | flops 540278272 | bytes 2103308 | tf_op jit(solution)/shard_map/while/body/eval_jaxpr/dot_general | solution.py:41
  101.8 3.9 %fusion.73 = f32[512]{0:T(512)S(1)} fusion(bf16[512,1024]{1,0:T(8,128)(2,1)} %get-tuple-element.419, bf16[2,512,1024]{2,1,0:T(8,128)(2,1)S(1)} %get-tuple-element.418, s32[]{:T(128)S(6)} %copy.13, f32[]{:T(128)} %get-tuple-element.421, f32[]{:T(128)} %get-tuple-element.420, s32[512]{0:T(512)S(1)} %bitcast.64, s32[512]{0:T(512)S(1)} %iota_add_fusion.6), kind=kOutput, calls=%fused_computation.7.clone.1 | convolution fusion | flops 540278272 | bytes 2103308 | tf_op jit(solution)/shard_map/while/body/eval_jaxpr/dot_general | solution.py:41
  105.8 15.4 %all-reduce = f32[1024]{0:T(1024)S(1)} all-reduce(f32[1024]{0:T(1024)S(1)} %bitcast.65), channel_id=2, replica_groups=mesh['row'=4,'col'=8] {'col'}, use_global_device_ids=true, to_apply=%region_5.6.clone | all-reduce | flops 1024 | bytes 8192
  121.3 0.6 dynamic-slice.1
  121.9 1.2 multiply_reduce_fusion
  123.1 2.0 %subtract_multiply_fusion = f32[128,1024]{1,0:T(8,128)} fusion(f32[128,1024]{1,0:T(8,128)} %reduce-scatter.5.cloned.1.call-done, f32[128,1024]{1,0:T(8,128)S(1)} %copy-done, f32[128]{0:T(128)S(1)} %multiply_reduce_fusion, f32[128]{0:T(128)S(1)} %add_rsqrt_fusion), kind=kLoop, calls=%fused_computation.59 | loop fusion | flops 524288 | bytes 1573888 | tf_op jit(solution)/shard_map/mul | solution.py:15
  125.1 44.6 %reduce-scatter.3.cloned.1.call-done = f32[128,1024]{1,0:T(8,128)} async-done(((f32[1024,1024]{1,0:T(8,128)}), f32[128,1024]{1,0:T(8,128)}) %reduce-scatter.3.cloned.1.call-update) | async-done | bytes 524304 | tf_op jit(solution)/shard_map/reduce_scatter | solution.py:64
  169.7 1.2 multiply_reduce_fusion.1
  170.9 2.0 %subtract_multiply_fusion.1 = f32[128,1024]{1,0:T(8,128)} fusion(f32[128,1024]{1,0:T(8,128)} %reduce-scatter.3.cloned.1.call-done, f32[128,1024]{1,0:T(8,128)S(1)} %copy-done.1, f32[128]{0:T(128)S(1)} %multiply_reduce_fusion.1, f32[128]{0:T(128)S(1)} %add_rsqrt_fusion.1), kind=kLoop, calls=%fused_computation.61 | loop fusion | flops 524288 | bytes 1573888 | tf_op jit(solution)/shard_map/mul | solution.py:15
  (31 shorter events, 0.3 us)
Async XLA Ops:
  7.2 4.4 %copy-start.1 = (f32[128,1024]{1,0:T(8,128)S(1)}, f32[128,1024]{1,0:T(8,128)}, u32[]{:S(2)}) copy-start(f32[128,1024]{1,0:T(8,128)} %param.11) | copy-start | bytes 1572868
  7.2 32.6 %all-gather.5.cloned.1.call-start = ((), (), s32[]{:S(2)}) async-start(), calls=%async_computation.3 | async-start | bytes 1310720 | tf_op jit(solution)/shard_map/all_gather | solution.py:23
  10.3 60.8 %all-gather.3.cloned.1.call-start = ((), (), s32[]{:S(2)}) async-start(), calls=%async_computation.2 | async-start | bytes 2359296 | tf_op jit(solution)/shard_map/all_gather | solution.py:22
  12.4 109.5 %reduce-scatter.5.cloned.1.call-start = ((), (), s32[]{:S(2)}) async-start(), calls=%async_computation.5 | async-start | bytes 2621440 | tf_op jit(solution)/shard_map/reduce_scatter | solution.py:98
  82.5 1.6 copy-start.2
  82.5 87.1 %reduce-scatter.3.cloned.1.call-start = ((), (), s32[]{:S(2)}) async-start(), calls=%async_computation.4 | async-start | bytes 4718592 | tf_op jit(solution)/shard_map/reduce_scatter | solution.py:64
  95.8 0.7 copy-start.3
  97.7 24.1 %copy-start = (f32[128,1024]{1,0:T(8,128)S(1)}, f32[128,1024]{1,0:T(8,128)}, u32[]{:S(2)}) copy-start(f32[128,1024]{1,0:T(8,128)} %param.12) | copy-start | bytes 1572868
Sparse Core Ops, SparseCore 0:
  10.4 29.3 all-gather.4
  42.0 29.0 all-gather.2
  82.7 34.6 reduce-scatter.4
  119.6 49.9 reduce-scatter.2
where the time goes:
time: 180 us; the launch traced here: 179 us
  waiting for transfers between devices  102 us (57%)
  matrix products  29.5 us (16%)
  blocking collectives  15.4 us (9%)
  between operations  15.2 us (8%)
  other arithmetic  13 us (7%)
  local copies, waits for them, and re-layouts  4.15 us (2%)
    reduce_scatter x1, waiting for transfers between devices, shards(): lax.psum_scatter((grads.reshape(count, width), losses.reshape(count))[0],...  44.6 us
    all_gather x1, waiting for transfers between devices, shards(): vrows = lax.all_gather(vhat.astype(jnp.bfloat16), 'col', axis=0, tiled=True)  31.3 us
    all_gather x1, waiting for transfers between devices, shards(): crows = lax.all_gather(chat.astype(jnp.bfloat16), 'row', axis=0, tiled=True)  26 us
    unnamed x1, blocking collectives  15.4 us
    dot_general x2, matrix products, one(): jnp.dot(coef, crows, preferred_element_type=jnp.float32)  11.7 us
    dot_general x2, matrix products, add(): lax.dot_general(coef, vblock, (((0,), (0,)), ((), ())), preferred_element...  9.85 us
    dot_general x2, matrix products, tile(): jnp.dot(vblock, crows.T, preferred_element_type=jnp.float32)  7.89 us
    mul x2, other arithmetic, backward_norm(): inverse * (grad_hat - hat * jnp.sum(hat * grad_hat, axis=1, keepdims=True))  3.99 us
  transfers between devices with their start and end apart: 4, of which 3 were waited for; matrix products, arithmetic and copies ran while one was open for 15% of the time, Pallas kernels for 0%

commit v1 on v0

v1 whole, which is shorter than its diff:
```python
import jax
import jax.numpy as jnp
from jax import lax
from jax.experimental import pallas as pl
from jax.experimental.pallas import tpu as pltpu
from jax.sharding import PartitionSpec as P

F32, BF16 = jnp.float32, jnp.bfloat16
LANES = 128
VMEM_LIMIT = 56 * 1024 * 1024


def params():
    return pltpu.CompilerParams(vmem_limit_bytes=VMEM_LIMIT)


def in_vmem(count):
    return [pl.BlockSpec(memory_space=pltpu.VMEM)] * count


def unit_rows(rows):
    inverse = lax.rsqrt(jnp.sum(rows * rows, axis=1, keepdims=True) + 1e-06)
    return rows * inverse, inverse


def normalize_kernel(film_ref, text_ref, v_ref, c_ref):
    c_ref[...] = unit_rows(text_ref[...])[0].astype(BF16)
    v_ref[...] = unit_rows(film_ref[...])[0].astype(BF16)


def log1p_unit(e):
    series = e * (1.0 - e * (0.5 - e * (1.0 / 3.0 - e * 0.25)))
    return jnp.where(e < 0.01, series, jnp.log(1.0 + e))


def pair_kernel(clip_blocks, caption_blocks, own_blocks, scalars, bases, labels, *refs):
    v_refs = refs[:clip_blocks]
    c_refs = refs[clip_blocks : clip_blocks + caption_blocks]
    rest = refs[clip_blocks + caption_blocks :]
    dv_refs = rest[:clip_blocks]
    dc_refs = rest[clip_blocks : clip_blocks + own_blocks]
    away, loss_ref, v_all, c_all, coef = rest[clip_blocks + own_blocks :]
    rows, width = v_refs[0].shape
    clips = clip_blocks * rows
    captions = caption_blocks * rows
    for i, ref in enumerate(v_refs):
        v_all[pl.ds(i * rows, rows), :] = ref[...]
    for i, ref in enumerate(c_refs):
        c_all[pl.ds(i * rows, rows), :] = ref[...]
    scale, shift = scalars[0], scalars[1]
    loss_ref[...] = jnp.zeros_like(loss_ref)

    @pl.loop(0, caption_blocks // 2)
    def _(pair):
        start = pl.multiple_of(pair * 2 * rows, 2 * rows)
        dots = lax.dot_general(
            c_all[pl.ds(start, 2 * rows), :],
            v_all[...],
            (((1,), (1,)), ((), ())),
            preferred_element_type=F32,
        )
        for half in range(2):
            logits = dots[half * rows : (half + 1) * rows] * scale + shift
            ids = lax.broadcasted_iota(jnp.int32, (rows, clips), 0) + bases[pair * 2 + half]
            match = ids == labels[...]
            e = jnp.exp(-jnp.abs(logits))
            over = 1.0 / (1.0 + e)
            sigmoid = jnp.where(logits >= 0.0, over, e * over)
            signed = jnp.where(match, -logits, logits)
            losses = jnp.maximum(signed, 0.0) + log1p_unit(e)
            loss_ref[...] += jnp.sum(losses, axis=0, keepdims=True)
            coef[pl.ds(start + half * rows, rows), :] = (
                sigmoid - jnp.where(match, 1.0, 0.0)
            ).astype(BF16)

    chunk = 256

    for i in range(width // chunk):
        columns = pl.ds(i * chunk, chunk)
        part = lax.dot_general(
            coef[...], c_all[:, columns], (((0,), (0,)), ((), ())), preferred_element_type=F32
        )
        for b, ref in enumerate(dv_refs):
            ref[:, columns] = part[b * rows : (b + 1) * rows].astype(ref.dtype)
        part = jnp.dot(coef[...], v_all[:, columns], preferred_element_type=F32)
        for b, ref in enumerate(dc_refs):
            ref[:, columns] = part[b * rows : (b + 1) * rows].astype(ref.dtype)
        away[:, columns] = part[own_blocks * rows :].astype(away.dtype)


def finish_kernel(scalars, film, text, dv, dv_x, dv_z, dc, dc_y, dc_z, loss, loss_x, loss_z, out, gv, gc):
    scale = scalars[0]

    def back(rows, total):
        hat, inverse = unit_rows(rows)
        total = total * scale
        return inverse * (total - hat * jnp.sum(hat * total, axis=1, keepdims=True))

    gv[...] = back(film[...], dv[...] + dv_x[...].astype(F32) + dv_z[...].astype(F32))
    gc[...] = back(text[...], dc[...] + dc_y[...].astype(F32) + dc_z[...].astype(F32))
    out[...] = loss[...] + loss_x[...] + loss_z[...]


def shards(film, text, matched, sharpness, offset):
    rows, width = film.shape
    R, C = lax.axis_size("row"), lax.axis_size("col")
    r, c = lax.axis_index("row"), lax.axis_index("col")
    Y, Z = R // 2, C // 4

    def swap(value, axis, bits):
        size = lax.axis_size(axis)
        return lax.ppermute(value, axis, [(i, i ^ bits) for i in range(size)])

    v16, c16 = pl.pallas_call(
        normalize_kernel,
        out_shape=[jax.ShapeDtypeStruct((rows, width), BF16)] * 2,
        in_specs=in_vmem(2),
        out_specs=in_vmem(2),
        compiler_params=params(),
    )(film, text)

    v_z = swap(v16, "col", 2)
    c_hi = [c16] + [swap(c16, "col", 4 * s) for s in range(1, Z)]
    v_x = swap(v16, "row", 1)
    c_own = [[b] + [swap(b, "row", 2 * t) for t in range(1, Y)] for b in c_hi]
    v_d = swap(v_z, "row", 1)
    c_own = [b for group in c_own for b in group]
    c_other = [swap(b, "col", 1) for b in c_own]
    v_blocks = [v16, v_z, v_x, v_d]
    c_blocks = c_own + c_other
    own = len(c_own)

    clip_ids = [r * C + c, r * C + (c ^ 2), (r ^ 1) * C + c, (r ^ 1) * C + (c ^ 2)]
    labels = jnp.concatenate(
        [lax.dynamic_slice_in_dim(matched, b * rows, rows, 0) for b in clip_ids]
    ).reshape(1, 4 * rows)
    bases = jnp.stack(
        [
            (((c ^ (4 * s)) ^ k) * R + (r ^ (2 * t))) * rows
            for k in range(2)
            for s in range(Z)
            for t in range(Y)
        ]
    ).astype(jnp.int32)
    scalars = jnp.concatenate([sharpness, offset])

    block = lambda dtype, n=1: jax.ShapeDtypeStruct((n * rows, width), dtype)
    outs = pl.pallas_call(
        lambda *refs: pair_kernel(4, 2 * own, own, *refs),
        out_shape=[block(F32)] + [block(BF16)] * 3 + [block(F32)] * own
        + [block(BF16, own), jax.ShapeDtypeStruct((1, 4 * rows), F32)],
        in_specs=[pl.BlockSpec(memory_space=pltpu.SMEM)] * 2 + in_vmem(1 + 4 + 2 * own),
        out_specs=in_vmem(4 + own + 2),
        scratch_shapes=[
            pltpu.VMEM((4 * rows, width), BF16),
            pltpu.VMEM((2 * own * rows, width), BF16),
            pltpu.VMEM((2 * own * rows, 4 * rows), BF16),
        ],
        compiler_params=params(),
    )(scalars, bases, labels, *v_blocks, *c_blocks)
    dv, dv_blocks, dc, away, loss = outs[0], outs[:4], list(outs[4 : 4 + own]), outs[-2], outs[-1]
    loss = [loss[:, i * rows : (i + 1) * rows] for i in range(4)]

    back = swap(away, "col", 1)
    dv_near = swap(dv_blocks[2], "row", 1)
    dv_far = swap(dv_blocks[3], "row", 1)
    loss_near = swap(loss[2], "row", 1)
    loss_far = swap(loss[3], "row", 1)
    dv_z = swap((dv_blocks[1].astype(F32) + dv_far.astype(F32)).astype(BF16), "col", 2)
    loss_z = swap(loss[1] + loss_far, "col", 2)

    dc = [b + back[i * rows : (i + 1) * rows].astype(F32) for i, b in enumerate(dc)]
    grid = [dc[s * Y : (s + 1) * Y] for s in range(Z)]
    total, far = [], []
    for s in range(Z):
        arrived = [swap(grid[s][t].astype(BF16), "row", 2 * t).astype(F32) for t in range(1, Y)]
        total.append((grid[s][0], arrived))
    near = sum(total[0][1])
    for s in range(1, Z):
        here = total[s][0] + sum(total[s][1])
        far.append(swap(here.astype(BF16), "col", 4 * s).astype(F32))
    far = sum(far)

    out, gv, gc = pl.pallas_call(
        finish_kernel,
        out_shape=[jax.ShapeDtypeStruct((1, rows), F32), block(F32), block(F32)],
        in_specs=[pl.BlockSpec(memory_space=pltpu.SMEM)] + in_vmem(11),
        out_specs=in_vmem(3),
        compiler_params=params(),
    )(scalars, film, text, dv, dv_near, dv_z, grid[0][0], near, far, loss[0], loss_near, loss_z)
    return out.reshape(rows), gv, gc


def solution(mesh):
    return jax.shard_map(
        shards,
        mesh=mesh,
        in_specs=(P(("row", "col"), None), P(("col", "row"), None), P(), P(), P()),
        out_specs=(P(("row", "col")), P(("row", "col"), None), P(("col", "row"), None)),
        check_vma=False,
    )
```

time: 180 us -> 78.8 us (0.44)
  waiting for transfers between devices: 102 us -> 30.4 us
  matrix products: 29.5 us -> 0 us
  starting transfers between devices: 0.16 us -> 20.4 us
  Pallas kernels: 0 us -> 15.7 us
  blocking collectives: 15.4 us -> 0 us
  between operations: 15.2 us -> 2.09 us
  other arithmetic: 13 us -> 6.92 us
    all_gather x2 -> x0, waiting for transfers between devices: 57.3 us -> none  [the longest x1 31.3 us: shards(): vrows = lax.all_gather(vhat.astype(jnp.bfloat16), 'col', axis=0, tiled=True)]
    reduce_scatter x2 -> x0, waiting for transfers between devices: 44.6 us -> none  [the longest x1 44.6 us: shards(): lax.psum_scatter((grads.reshape(count, width), losses.reshape(count))[0],...]
    ppermute x0 -> x20, waiting for transfers between devices: none -> 30.4 us  [swap(): return lax.ppermute(value, axis, [(i, i ^ bits) for i in range(size)])]
    dot_general x6 -> x0, matrix products: 29.5 us -> none  [the longest x2 11.7 us: one(): jnp.dot(coef, crows, preferred_element_type=jnp.float32)]
    ppermute x0 -> x20, starting transfers between devices: none -> 20.4 us  [swap(): return lax.ppermute(value, axis, [(i, i ^ bits) for i in range(size)])]
    pallas_call x0 -> x3, Pallas kernels: none -> 15.7 us  [the longest x1 10.2 us: shards(): pl.pallas_call(lambda *refs: pair_kernel(4, 2 * own, own, *refs), out_sha...]
    unnamed x1 -> x0, blocking collectives: 15.4 us -> none
    mul x3 -> x0, other arithmetic: 5.49 us -> none  [the longest x2 3.99 us: backward_norm(): inverse * (grad_hat - hat * jnp.sum(hat * grad_hat, axis=1, keepdims=True))]
  transfers between devices with their start and end apart: 4 -> 20, of which waited for: 3 -> 9; matrix products, arithmetic and copies ran while one was open for 15% -> 9% of each run, Pallas kernels for 0% -> 0%
where the time goes in v1:
time: 78.8 us; the launch traced here: 78.6 us
  waiting for transfers between devices  30.4 us (39%)
  starting transfers between devices  20.4 us (26%)
  Pallas kernels  15.7 us (20%)
  other arithmetic  6.92 us (9%)
  local copies, waits for them, and re-layouts  3.15 us (4%)
  between operations  2.09 us (3%)
    ppermute x20, waiting for transfers between devices, swap(): return lax.ppermute(value, axis, [(i, i ^ bits) for i in range(size)])  30.4 us
    ppermute x20, starting transfers between devices, swap(): return lax.ppermute(value, axis, [(i, i ^ bits) for i in range(size)])  20.4 us
    pallas_call x1, Pallas kernels, shards(): pl.pallas_call(lambda *refs: pair_kernel(4, 2 * own, own, *refs), out_sha...  10.2 us
    pallas_call x1, Pallas kernels, shards(): pl.pallas_call(finish_kernel, out_shape=[jax.ShapeDtypeStruct((1, rows),...  3.35 us
    convert_element_type x2, other arithmetic, shards(): far.append(swap(here.astype(BF16), 'col', 4 * s).astype(F32))  2.99 us
    pallas_call x1, Pallas kernels, shards(): pl.pallas_call(normalize_kernel, out_shape=[jax.ShapeDtypeStruct((rows, w...  2.14 us
    unnamed x36, local copies, waits for them, and re-layouts  1.74 us
  transfers between devices with their start and end apart: 20, of which 9 were waited for; matrix products, arithmetic and copies ran while one was open for 9% of the time, Pallas kernels for 0%

profile of v1, /device:TPU:0, one launch (start us, length us, event | category | flops | bytes accessed | tf_op | source)
XLA Modules:
  0.0 78.6 jit_solution(9257571357537273521)
XLA Ops:
  0.6 2.1 %shard_map.76 = (bf16[128,1024]{1,0:T(8,128)(2,1)}, bf16[128,1024]{1,0:T(8,128)(2,1)}) custom-call(f32[128,1024]{1,0:T(8,128)} %film.1, f32[128,1024]{1,0:T(8,128)} %text.1), custom_call_target="tpu_custom_call" | custom-call | tf_op jit(solution)/shard_map/pallas_call | solution.py:114
  2.8 4.0 %collective-permute-start.4 = (bf16[128,1024]{1,0:T(8,128)(2,1)}, bf16[128,1024]{1,0:T(8,128)(2,1)S(1)}, u32[]{:S(2)}, u32[]{:S(2)}) collective-permute-start(bf16[128,1024]{1,0:T(8,128)(2,1)} %get-tuple-element.19.refs_7_), channel_id=1, source_target_pairs={{0,4},{1,5},{2,6},{3,7},{4,0},{5,1},{6,2},{7,3},{8,12},{9,13},{10,... | collective-permute-start | bytes 786440 | tf_op jit(solution)/shard_map/ppermute | solution.py:112
  6.8 1.5 %collective-permute-start.1 = (bf16[128,1024]{1,0:T(8,128)(2,1)}, bf16[128,1024]{1,0:T(8,128)(2,1)S(1)}, u32[]{:S(2)}, u32[]{:S(2)}) collective-permute-start(bf16[128,1024]{1,0:T(8,128)(2,1)} %get-tuple-element.18.refs_3_), channel_id=1, source_target_pairs={{0,8},{8,0},{16,24},{24,16},{1,9},{9,1},{17,25},{25,17},{2,10},{10... | collective-permute-start | bytes 786440 | tf_op jit(solution)/shard_map/ppermute | solution.py:112
  8.3 1.6 %collective-permute-start = (bf16[128,1024]{1,0:T(8,128)(2,1)}, bf16[128,1024]{1,0:T(8,128)(2,1)S(1)}, u32[]{:S(2)}, u32[]{:S(2)}) collective-permute-start(bf16[128,1024]{1,0:T(8,128)(2,1)} %get-tuple-element.18.refs_3_), channel_id=1, source_target_pairs={{0,2},{1,3},{2,0},{3,1},{4,6},{5,7},{6,4},{7,5},{8,10},{9,11},{10,... | collective-permute-start | bytes 786440 | tf_op jit(solution)/shard_map/ppermute | solution.py:112
  9.9 1.5 %collective-permute-start.3 = (bf16[128,1024]{1,0:T(8,128)(2,1)}, bf16[128,1024]{1,0:T(8,128)(2,1)S(1)}, u32[]{:S(2)}, u32[]{:S(2)}) collective-permute-start(bf16[128,1024]{1,0:T(8,128)(2,1)} %get-tuple-element.19.refs_7_), channel_id=1, source_target_pairs={{0,16},{8,24},{16,0},{24,8},{1,17},{9,25},{17,1},{25,9},{2,18},{10... | collective-permute-start | bytes 786440 | tf_op jit(solution)/shard_map/ppermute | solution.py:112
  11.4 7.7 %collective-permute-done.4.refs_9_ = bf16[128,1024]{1,0:T(8,128)(2,1)S(1)} collective-permute-done((bf16[128,1024]{1,0:T(8,128)(2,1)}, bf16[128,1024]{1,0:T(8,128)(2,1)S(1)}, u32[]{:S(2)}, u32[]{:S(2)}) %collective-permute-start.4) | collective-permute-done | bytes 262176 | tf_op jit(solution)/shard_map/ppermute | solution.py:112
  19.0 1.6 %collective-permute-start.5 = (bf16[128,1024]{1,0:T(8,128)(2,1)S(1)}, bf16[128,1024]{1,0:T(8,128)(2,1)S(1)}, u32[]{:S(2)}, u32[]{:S(2)}) collective-permute-start(bf16[128,1024]{1,0:T(8,128)(2,1)S(1)} %collective-permute-done.4.refs_9_), channel_id=1, source_target_pairs={{0,16},{8,24},{16,0},{24,8},{1,17},{9,25},{17,1},{25,9},{2,18},{10... | collective-permute-start | bytes 786440 | tf_op jit(solution)/shard_map/ppermute | solution.py:112
  21.9 0.6 collective-permute-start.8
  22.5 1.5 %collective-permute-start.2 = (bf16[128,1024]{1,0:T(8,128)(2,1)S(1)}, bf16[128,1024]{1,0:T(8,128)(2,1)S(1)}, u32[]{:S(2)}, u32[]{:S(2)}) collective-permute-start(bf16[128,1024]{1,0:T(8,128)(2,1)S(1)} %collective-permute-done.refs_4_), channel_id=1, source_target_pairs={{0,8},{8,0},{16,24},{24,16},{1,9},{9,1},{17,25},{25,17},{2,10},{10... | collective-permute-start | bytes 786440 | tf_op jit(solution)/shard_map/ppermute | solution.py:112
  24.0 2.5 %collective-permute-done.5.refs_10_ = bf16[128,1024]{1,0:T(8,128)(2,1)S(1)} collective-permute-done((bf16[128,1024]{1,0:T(8,128)(2,1)S(1)}, bf16[128,1024]{1,0:T(8,128)(2,1)S(1)}, u32[]{:S(2)}, u32[]{:S(2)}) %collective-permute-start.5) | collective-permute-done | bytes 262176 | tf_op jit(solution)/shard_map/ppermute | solution.py:112
  26.5 0.6 pad_maximum_fusion.refs_0_.scalars
  27.7 0.8 %fusion = (s32[128]{0:T(128)S(1)}, s32[128]{0:T(128)S(1)}, s32[128]{0:T(128)S(1)}, s32[128]{0:T(128)S(1)}) fusion(s32[4096]{0:T(1024)} %param.7, s32[]{:T(128)S(6)} %select_n.12, s32[]{:T(128)S(6)} %select_n.13, s32[]{:T(128)S(6)} %select_n.15, s32[]{:T(128)S(6)} %select_n.14), kind=kLoop, calls=%fused_computation.8 | loop fusion | bytes 4112 | tf_op jit(solution)/shard_map/dynamic_slice | solution.py:135
  28.5 0.6 pad_add_fusion
  29.1 1.7 %collective-permute-done.2.refs_6_ = bf16[128,1024]{1,0:T(8,128)(2,1)S(1)} collective-permute-done((bf16[128,1024]{1,0:T(8,128)(2,1)S(1)}, bf16[128,1024]{1,0:T(8,128)(2,1)S(1)}, u32[]{:S(2)}, u32[]{:S(2)}) %collective-permute-start.2) | collective-permute-done | bytes 262176 | tf_op jit(solution)/shard_map/ppermute | solution.py:112
  30.9 0.6 copy-done.9
  31.8 10.2 %shard_map.77 = (f32[128,1024]{1,0:T(8,128)}, bf16[128,1024]{1,0:T(8,128)(2,1)}, bf16[128,1024]{1,0:T(8,128)(2,1)}, bf16[128,1024]{1,0:T(8,128)(2,1)}, f32[128,1...) custom-call(f32[2]{0:T(128)} %pad_maximum_fusion.refs_0_.scalars, ...), custom_call_target="tpu_custom_call" | custom-call | tf_op jit(solution)/shard_map/pallas_call | solution.py:148
  42.1 2.9 %collective-permute-done.13 = bf16[512,1024]{1,0:T(8,128)(2,1)S(1)} collective-permute-done((bf16[512,1024]{1,0:T(8,128)(2,1)}, bf16[512,1024]{1,0:T(8,128)(2,1)S(1)}, u32[]{:S(2)}, u32[]{:S(2)}) %collective-permute-start.13) | collective-permute-done | bytes 1048608 | tf_op jit(solution)/shard_map/ppermute | solution.py:112
  45.0 1.2 %add_convert_fusion.1 = bf16[128,1024]{1,0:T(8,128)(2,1)S(1)} fusion(f32[128,1024]{1,0:T(8,128)} %get-tuple-element.28, bf16[512,1024]{1,0:T(8,128)(2,1)S(1)} %collective-permute-done.13), kind=kLoop, calls=%fused_computation.1 | loop fusion | flops 393216 | bytes 1048576 | tf_op jit(solution)/shard_map/convert_element_type | solution.py:176
  46.7 1.5 %collective-permute-start.10 = (bf16[128,1024]{1,0:T(8,128)(2,1)}, bf16[128,1024]{1,0:T(8,128)(2,1)S(1)}, u32[]{:S(2)}, u32[]{:S(2)}) collective-permute-start(bf16[128,1024]{1,0:T(8,128)(2,1)} %get-tuple-element.21), channel_id=1, source_target_pairs={{0,8},{8,0},{16,24},{24,16},{1,9},{9,1},{17,25},{25,17},{2,10},{10... | collective-permute-start | bytes 786440 | tf_op jit(solution)/shard_map/ppermute | solution.py:112
  48.7 5.9 %collective-permute-done.15 = bf16[128,1024]{1,0:T(8,128)(2,1)S(1)} collective-permute-done((bf16[128,1024]{1,0:T(8,128)(2,1)S(1)}, bf16[128,1024]{1,0:T(8,128)(2,1)S(1)}, u32[]{:S(2)}, u32[]{:S(2)}) %collective-permute-start.15) | collective-permute-done | bytes 262176 | tf_op jit(solution)/shard_map/ppermute | solution.py:112
  54.6 2.1 %add_convert_fusion = (bf16[128,1024]{1,0:T(8,128)(2,1)S(1)}, bf16[128,1024]{1,0:T(8,128)(2,1)S(1)}, f32[128,1024]{1,0:T(8,128)}) fusion(bf16[128,1024]{1,0:T(8,128)(2,1)S(1)} %collective-permute-done.15, f32[128,1024]{1,0:T(8,128)} %get-tuple-element.27, bf16[512,1024]{1,0:T(8,128)(2,1)S(1)} %collective-permute-done.13, f32[128,1024]{1,0:T(8,128)S(1)} %copy-done.1, ...), kind=kLoop, calls=%fused_computation | loop fusion | flops 1310720 | bytes 3670016 | tf_op jit(solution)/shard_map/convert_element_type | solution.py:181
  57.2 3.4 %collective-permute-done.11 = bf16[128,1024]{1,0:T(8,128)(2,1)S(1)} collective-permute-done((bf16[128,1024]{1,0:T(8,128)(2,1)}, bf16[128,1024]{1,0:T(8,128)(2,1)S(1)}, u32[]{:S(2)}, u32[]{:S(2)}) %collective-permute-start.11) | collective-permute-done | bytes 262176 | tf_op jit(solution)/shard_map/ppermute | solution.py:112
  60.7 1.4 %collective-permute-start.12 = (bf16[128,1024]{1,0:T(8,128)(2,1)S(1)}, bf16[128,1024]{1,0:T(8,128)(2,1)S(1)}, u32[]{:S(2)}, u32[]{:S(2)}) collective-permute-start(bf16[128,1024]{1,0:T(8,128)(2,1)S(1)} %add_convert_fusion.3), channel_id=1, source_target_pairs={{0,2},{1,3},{2,0},{3,1},{4,6},{5,7},{6,4},{7,5},{8,10},{9,11},{10,... | collective-permute-start | bytes 786440 | tf_op jit(solution)/shard_map/ppermute | solution.py:112
  62.1 1.4 %collective-permute-start.18 = (f32[1,128]{1,0:T(1,128)S(1)}, f32[1,128]{1,0:T(1,128)S(1)}, u32[]{:S(2)}, u32[]{:S(2)}) collective-permute-start(f32[1,128]{1,0:T(1,128)S(1)} %slice.31), channel_id=1, source_target_pairs={{0,8},{8,0},{16,24},{24,16},{1,9},{9,1},{17,25},{25,17},{2,10},{10... | collective-permute-start | bytes 1544 | tf_op jit(solution)/shard_map/ppermute | solution.py:112
  63.5 2.1 %collective-permute-done.18 = f32[1,128]{1,0:T(1,128)S(1)} collective-permute-done((f32[1,128]{1,0:T(1,128)S(1)}, f32[1,128]{1,0:T(1,128)S(1)}, u32[]{:S(2)}, u32[]{:S(2)}) %collective-permute-start.18) | collective-permute-done | bytes 544 | tf_op jit(solution)/shard_map/ppermute | solution.py:112
  65.6 0.6 slice_add_fusion
  66.2 0.7 collective-permute-start.19
  66.9 4.0 %collective-permute-done.16 = bf16[128,1024]{1,0:T(8,128)(2,1)S(1)} collective-permute-done((bf16[128,1024]{1,0:T(8,128)(2,1)S(1)}, bf16[128,1024]{1,0:T(8,128)(2,1)S(1)}, u32[]{:S(2)}, u32[]{:S(2)}) %collective-permute-start.16) | collective-permute-done | bytes 262176 | tf_op jit(solution)/shard_map/ppermute | solution.py:112
  70.9 1.5 %collective-permute-start.17 = (f32[1,128]{1,0:T(1,128)S(1)}, f32[1,128]{1,0:T(1,128)S(1)}, u32[]{:S(2)}, u32[]{:S(2)}) collective-permute-start(f32[1,128]{1,0:T(1,128)S(1)} %get-tuple-element.41), channel_id=1, source_target_pairs={{0,8},{8,0},{16,24},{24,16},{1,9},{9,1},{17,25},{25,17},{2,10},{10... | collective-permute-start | bytes 1544 | tf_op jit(solution)/shard_map/ppermute | solution.py:112
  72.4 0.8 %convert_element_type.51.dc_z = f32[128,1024]{1,0:T(8,128)} convert(bf16[128,1024]{1,0:T(8,128)(2,1)S(1)} %collective-permute-done.16) | non-fusion elementwise | flops 131072 | bytes 786432 | tf_op jit(solution)/shard_map/convert_element_type | solution.py:181
  73.2 0.9 %convert_element_type.45.dc_y = f32[128,1024]{1,0:T(8,128)} convert(bf16[128,1024]{1,0:T(8,128)(2,1)S(1)} %collective-permute-done.14) | non-fusion elementwise | flops 131072 | bytes 786432 | tf_op jit(solution)/shard_map/convert_element_type | solution.py:176
  75.2 3.4 %shard_map.78 = (f32[1,128]{1,0:T(1,128)}, f32[128,1024]{1,0:T(8,128)}, f32[128,1024]{1,0:T(8,128)}) custom-call(f32[2]{0:T(128)} %pad_maximum_fusion.refs_0_.scalars, f32[128,1024]{1,0:T(8,128)} %film.1, f32[128,1024]{1,0:T(8,128)} %text.1, f32[128,1024]{1,0:T(8,128)} %get-tuple-element.20.dv, bf16[128,1024]{1,0:T(8,128)(2,1)} %copy-done.12, ...), custom_call_target="tpu_custom_call" | custom-call | tf_op jit(solution)/shard_map/pallas_call | solution.py:184
  (58 shorter events, 3.7 us)
Async XLA Ops:
  2.8 16.3 %collective-permute-start.4 = (bf16[128,1024]{1,0:T(8,128)(2,1)}, bf16[128,1024]{1,0:T(8,128)(2,1)S(1)}, u32[]{:S(2)}, u32[]{:S(2)}) collective-permute-start(bf16[128,1024]{1,0:T(8,128)(2,1)} %get-tuple-element.19.refs_7_), channel_id=1, source_target_pairs={{0,4},{1,5},{2,6},{3,7},{4,0},{5,1},{6,2},{7,3},{8,12},{9,13},{10,... | collective-permute-start | bytes 786440 | tf_op jit(solution)/shard_map/ppermute | solution.py:112
  6.8 15.1 %collective-permute-start.1 = (bf16[128,1024]{1,0:T(8,128)(2,1)}, bf16[128,1024]{1,0:T(8,128)(2,1)S(1)}, u32[]{:S(2)}, u32[]{:S(2)}) collective-permute-start(bf16[128,1024]{1,0:T(8,128)(2,1)} %get-tuple-element.18.refs_3_), channel_id=1, source_target_pairs={{0,8},{8,0},{16,24},{24,16},{1,9},{9,1},{17,25},{25,17},{2,10},{10... | collective-permute-start | bytes 786440 | tf_op jit(solution)/shard_map/ppermute | solution.py:112
  8.3 14.2 %collective-permute-start = (bf16[128,1024]{1,0:T(8,128)(2,1)}, bf16[128,1024]{1,0:T(8,128)(2,1)S(1)}, u32[]{:S(2)}, u32[]{:S(2)}) collective-permute-start(bf16[128,1024]{1,0:T(8,128)(2,1)} %get-tuple-element.18.refs_3_), channel_id=1, source_target_pairs={{0,2},{1,3},{2,0},{3,1},{4,6},{5,7},{6,4},{7,5},{8,10},{9,11},{10,... | collective-permute-start | bytes 786440 | tf_op jit(solution)/shard_map/ppermute | solution.py:112
  9.9 14.1 %collective-permute-start.3 = (bf16[128,1024]{1,0:T(8,128)(2,1)}, bf16[128,1024]{1,0:T(8,128)(2,1)S(1)}, u32[]{:S(2)}, u32[]{:S(2)}) collective-permute-start(bf16[128,1024]{1,0:T(8,128)(2,1)} %get-tuple-element.19.refs_7_), channel_id=1, source_target_pairs={{0,16},{8,24},{16,0},{24,8},{1,17},{9,25},{17,1},{25,9},{2,18},{10... | collective-permute-start | bytes 786440 | tf_op jit(solution)/shard_map/ppermute | solution.py:112
  19.0 11.8 %copy-start.2 = (bf16[128,1024]{1,0:T(8,128)(2,1)}, bf16[128,1024]{1,0:T(8,128)(2,1)S(1)}, u32[]{:S(2)}) copy-start(bf16[128,1024]{1,0:T(8,128)(2,1)S(1)} %collective-permute-done.4.refs_9_) | copy-start | bytes 786436
  19.0 7.4 %collective-permute-start.5 = (bf16[128,1024]{1,0:T(8,128)(2,1)S(1)}, bf16[128,1024]{1,0:T(8,128)(2,1)S(1)}, u32[]{:S(2)}, u32[]{:S(2)}) collective-permute-start(bf16[128,1024]{1,0:T(8,128)(2,1)S(1)} %collective-permute-done.4.refs_9_), channel_id=1, source_target_pairs={{0,16},{8,24},{16,0},{24,8},{1,17},{9,25},{17,1},{25,9},{2,18},{10... | collective-permute-start | bytes 786440 | tf_op jit(solution)/shard_map/ppermute | solution.py:112
  20.6 8.5 %collective-permute-start.6 = (bf16[128,1024]{1,0:T(8,128)(2,1)}, bf16[128,1024]{1,0:T(8,128)(2,1)S(1)}, u32[]{:S(2)}, u32[]{:S(2)}) collective-permute-start(bf16[128,1024]{1,0:T(8,128)(2,1)} %get-tuple-element.19.refs_7_), channel_id=1, source_target_pairs={{0,1},{1,0},{2,3},{3,2},{4,5},{5,4},{6,7},{7,6},{8,9},{9,8},{10,11... | collective-permute-start | bytes 786440 | tf_op jit(solution)/shard_map/ppermute | solution.py:112
  21.9 8.9 %copy-start.3 = (bf16[128,1024]{1,0:T(8,128)(2,1)}, bf16[128,1024]{1,0:T(8,128)(2,1)S(1)}, u32[]{:S(2)}) copy-start(bf16[128,1024]{1,0:T(8,128)(2,1)S(1)} %collective-permute-done.1.refs_5_) | copy-start | bytes 786436
  21.9 8.9 %collective-permute-start.8 = (bf16[128,1024]{1,0:T(8,128)(2,1)S(1)}, bf16[128,1024]{1,0:T(8,128)(2,1)S(1)}, u32[]{:S(2)}, u32[]{:S(2)}) collective-permute-start(bf16[128,1024]{1,0:T(8,128)(2,1)S(1)} %collective-permute-done.4.refs_9_), channel_id=1, source_target_pairs={{0,1},{1,0},{2,3},{3,2},{4,5},{5,4},{6,7},{7,6},{8,9},{9,8},{10,11... | collective-permute-start | bytes 786440 | tf_op jit(solution)/shard_map/ppermute | solution.py:112
  22.5 8.4 %copy-start.4 = (bf16[128,1024]{1,0:T(8,128)(2,1)}, bf16[128,1024]{1,0:T(8,128)(2,1)S(1)}, u32[]{:S(2)}) copy-start(bf16[128,1024]{1,0:T(8,128)(2,1)S(1)} %collective-permute-done.refs_4_) | copy-start | bytes 786436
  22.5 8.3 %collective-permute-start.2 = (bf16[128,1024]{1,0:T(8,128)(2,1)S(1)}, bf16[128,1024]{1,0:T(8,128)(2,1)S(1)}, u32[]{:S(2)}, u32[]{:S(2)}) collective-permute-start(bf16[128,1024]{1,0:T(8,128)(2,1)S(1)} %collective-permute-done.refs_4_), channel_id=1, source_target_pairs={{0,8},{8,0},{16,24},{24,16},{1,9},{9,1},{17,25},{25,17},{2,10},{10... | collective-permute-start | bytes 786440 | tf_op jit(solution)/shard_map/ppermute | solution.py:112
  24.0 6.9 %copy-start.5 = (bf16[128,1024]{1,0:T(8,128)(2,1)}, bf16[128,1024]{1,0:T(8,128)(2,1)S(1)}, u32[]{:S(2)}) copy-start(bf16[128,1024]{1,0:T(8,128)(2,1)S(1)} %collective-permute-done.3.refs_8_) | copy-start | bytes 786436
  24.0 6.8 %collective-permute-start.7 = (bf16[128,1024]{1,0:T(8,128)(2,1)S(1)}, bf16[128,1024]{1,0:T(8,128)(2,1)S(1)}, u32[]{:S(2)}, u32[]{:S(2)}) collective-permute-start(bf16[128,1024]{1,0:T(8,128)(2,1)S(1)} %collective-permute-done.3.refs_8_), channel_id=1, source_target_pairs={{0,1},{1,0},{2,3},{3,2},{4,5},{5,4},{6,7},{7,6},{8,9},{9,8},{10,11... | collective-permute-start | bytes 786440 | tf_op jit(solution)/shard_map/ppermute | solution.py:112
  26.5 4.4 %copy-start.6 = (bf16[128,1024]{1,0:T(8,128)(2,1)}, bf16[128,1024]{1,0:T(8,128)(2,1)S(1)}, u32[]{:S(2)}) copy-start(bf16[128,1024]{1,0:T(8,128)(2,1)S(1)} %collective-permute-done.5.refs_10_) | copy-start | bytes 786436
  26.5 4.4 %collective-permute-start.9 = (bf16[128,1024]{1,0:T(8,128)(2,1)S(1)}, bf16[128,1024]{1,0:T(8,128)(2,1)S(1)}, u32[]{:S(2)}, u32[]{:S(2)}) collective-permute-start(bf16[128,1024]{1,0:T(8,128)(2,1)S(1)} %collective-permute-done.5.refs_10_), channel_id=1, source_target_pairs={{0,1},{1,0},{2,3},{3,2},{4,5},{5,4},{6,7},{7,6},{8,9},{9,8},{10,11... | collective-permute-start | bytes 786440 | tf_op jit(solution)/shard_map/ppermute | solution.py:112
  29.1 1.8 %copy-start.7 = (bf16[128,1024]{1,0:T(8,128)(2,1)}, bf16[128,1024]{1,0:T(8,128)(2,1)S(1)}, u32[]{:S(2)}) copy-start(bf16[128,1024]{1,0:T(8,128)(2,1)S(1)} %collective-permute-done.6.refs_11_) | copy-start | bytes 786436
  30.8 0.9 %copy-start.10 = (bf16[128,1024]{1,0:T(8,128)(2,1)}, bf16[128,1024]{1,0:T(8,128)(2,1)S(1)}, u32[]{:S(2)}) copy-start(bf16[128,1024]{1,0:T(8,128)(2,1)S(1)} %collective-permute-done.7.refs_12_) | copy-start | bytes 786436
  30.9 1.0 %copy-start.11 = (bf16[128,1024]{1,0:T(8,128)(2,1)}, bf16[128,1024]{1,0:T(8,128)(2,1)S(1)}, u32[]{:S(2)}) copy-start(bf16[128,1024]{1,0:T(8,128)(2,1)S(1)} %collective-permute-done.9.refs_14_) | copy-start | bytes 786436
  42.0 2.9 %collective-permute-start.13 = (bf16[512,1024]{1,0:T(8,128)(2,1)}, bf16[512,1024]{1,0:T(8,128)(2,1)S(1)}, u32[]{:S(2)}, u32[]{:S(2)}) collective-permute-start(bf16[512,1024]{1,0:T(8,128)(2,1)} %get-tuple-element.25), channel_id=1, source_target_pairs={{0,1},{1,0},{2,3},{3,2},{4,5},{5,4},{6,7},{7,6},{8,9},{9,8},{10,11... | collective-permute-start | bytes 3145736 | tf_op jit(solution)/shard_map/ppermute | solution.py:112
  45.0 9.6 %copy-start = (f32[128,1024]{1,0:T(8,128)S(1)}, f32[128,1024]{1,0:T(8,128)}, u32[]{:S(2)}) copy-start(f32[128,1024]{1,0:T(8,128)} %get-tuple-element.24) | copy-start | bytes 1572868
  45.0 9.6 %copy-start.1 = (f32[128,1024]{1,0:T(8,128)S(1)}, f32[128,1024]{1,0:T(8,128)}, u32[]{:S(2)}) copy-start(f32[128,1024]{1,0:T(8,128)} %get-tuple-element.26) | copy-start | bytes 1572868
  46.2 8.4 %collective-permute-start.15 = (bf16[128,1024]{1,0:T(8,128)(2,1)S(1)}, bf16[128,1024]{1,0:T(8,128)(2,1)S(1)}, u32[]{:S(2)}, u32[]{:S(2)}) collective-permute-start(bf16[128,1024]{1,0:T(8,128)(2,1)S(1)} %add_convert_fusion.1), channel_id=1, source_target_pairs={{0,16},{8,24},{16,0},{24,8},{1,17},{9,25},{17,1},{25,9},{2,18},{10... | collective-permute-start | bytes 786440 | tf_op jit(solution)/shard_map/ppermute | solution.py:112
  46.7 27.7 %collective-permute-start.10 = (bf16[128,1024]{1,0:T(8,128)(2,1)}, bf16[128,1024]{1,0:T(8,128)(2,1)S(1)}, u32[]{:S(2)}, u32[]{:S(2)}) collective-permute-start(bf16[128,1024]{1,0:T(8,128)(2,1)} %get-tuple-element.21), channel_id=1, source_target_pairs={{0,8},{8,0},{16,24},{24,16},{1,9},{9,1},{17,25},{25,17},{2,10},{10... | collective-permute-start | bytes 786440 | tf_op jit(solution)/shard_map/ppermute | solution.py:112
  48.2 12.4 %collective-permute-start.11 = (bf16[128,1024]{1,0:T(8,128)(2,1)}, bf16[128,1024]{1,0:T(8,128)(2,1)S(1)}, u32[]{:S(2)}, u32[]{:S(2)}) collective-permute-start(bf16[128,1024]{1,0:T(8,128)(2,1)} %get-tuple-element.23), channel_id=1, source_target_pairs={{0,8},{8,0},{16,24},{24,16},{1,9},{9,1},{17,25},{25,17},{2,10},{10... | collective-permute-start | bytes 786440 | tf_op jit(solution)/shard_map/ppermute | solution.py:112
  54.6 6.0 %copy-start.13 = (bf16[128,1024]{1,0:T(8,128)(2,1)S(1)}, bf16[128,1024]{1,0:T(8,128)(2,1)}, u32[]{:S(2)}) copy-start(bf16[128,1024]{1,0:T(8,128)(2,1)} %get-tuple-element.22) | copy-start | bytes 786436
  56.7 14.1 %collective-permute-start.16 = (bf16[128,1024]{1,0:T(8,128)(2,1)S(1)}, bf16[128,1024]{1,0:T(8,128)(2,1)S(1)}, u32[]{:S(2)}, u32[]{:S(2)}) collective-permute-start(bf16[128,1024]{1,0:T(8,128)(2,1)S(1)} %get-tuple-element.33), channel_id=1, source_target_pairs={{0,4},{1,5},{2,6},{3,7},{4,0},{5,1},{6,2},{7,3},{8,12},{9,13},{10,... | collective-permute-start | bytes 786440 | tf_op jit(solution)/shard_map/ppermute | solution.py:112
  56.7 16.5 %collective-permute-start.14 = (bf16[128,1024]{1,0:T(8,128)(2,1)S(1)}, bf16[128,1024]{1,0:T(8,128)(2,1)S(1)}, u32[]{:S(2)}, u32[]{:S(2)}) collective-permute-start(bf16[128,1024]{1,0:T(8,128)(2,1)S(1)} %get-tuple-element.34), channel_id=1, source_target_pairs={{0,16},{8,24},{16,0},{24,8},{1,17},{9,25},{17,1},{25,9},{2,18},{10... | collective-permute-start | bytes 786440 | tf_op jit(solution)/shard_map/ppermute | solution.py:112
  60.6 1.5 %copy-start.15 = (f32[1,512]{1,0:T(1,128)S(1)}, f32[1,512]{1,0:T(1,128)}, u32[]{:S(2)}) copy-start(f32[1,512]{1,0:T(1,128)} %get-tuple-element.29) | copy-start | bytes 6148
  60.7 13.8 %collective-permute-start.12 = (bf16[128,1024]{1,0:T(8,128)(2,1)S(1)}, bf16[128,1024]{1,0:T(8,128)(2,1)S(1)}, u32[]{:S(2)}, u32[]{:S(2)}) collective-permute-start(bf16[128,1024]{1,0:T(8,128)(2,1)S(1)} %add_convert_fusion.3), channel_id=1, source_target_pairs={{0,2},{1,3},{2,0},{3,1},{4,6},{5,7},{6,4},{7,5},{8,10},{9,11},{10,... | collective-permute-start | bytes 786440 | tf_op jit(solution)/shard_map/ppermute | solution.py:112
  62.1 3.5 %collective-permute-start.18 = (f32[1,128]{1,0:T(1,128)S(1)}, f32[1,128]{1,0:T(1,128)S(1)}, u32[]{:S(2)}, u32[]{:S(2)}) collective-permute-start(f32[1,128]{1,0:T(1,128)S(1)} %slice.31), channel_id=1, source_target_pairs={{0,8},{8,0},{16,24},{24,16},{1,9},{9,1},{17,25},{25,17},{2,10},{10... | collective-permute-start | bytes 1544 | tf_op jit(solution)/shard_map/ppermute | solution.py:112
  66.2 7.9 %collective-permute-start.19 = (f32[1,128]{1,0:T(1,128)S(1)}, f32[1,128]{1,0:T(1,128)S(1)}, u32[]{:S(2)}, u32[]{:S(2)}) collective-permute-start(f32[1,128]{1,0:T(1,128)S(1)} %get-tuple-element.40), channel_id=1, source_target_pairs={{0,2},{1,3},{2,0},{3,1},{4,6},{5,7},{6,4},{7,5},{8,10},{9,11},{10,... | collective-permute-start | bytes 1544 | tf_op jit(solution)/shard_map/ppermute | solution.py:112
  70.9 3.5 %collective-permute-start.17 = (f32[1,128]{1,0:T(1,128)S(1)}, f32[1,128]{1,0:T(1,128)S(1)}, u32[]{:S(2)}, u32[]{:S(2)}) collective-permute-start(f32[1,128]{1,0:T(1,128)S(1)} %get-tuple-element.41), channel_id=1, source_target_pairs={{0,8},{8,0},{16,24},{24,16},{1,9},{9,1},{17,25},{25,17},{2,10},{10... | collective-permute-start | bytes 1544 | tf_op jit(solution)/shard_map/ppermute | solution.py:112
  (6 other events, 4.1 us)

commit v2 on v0

v2 whole, which is shorter than its diff:
```python
import jax
import jax.numpy as jnp
from jax import lax
from jax.experimental import pallas as pl
from jax.experimental.pallas import tpu as pltpu
from jax.sharding import PartitionSpec as P

F32, BF16 = jnp.float32, jnp.bfloat16
MIB = 1024 * 1024
SPECS = {
    "s": pl.BlockSpec(memory_space=pltpu.SMEM),
    "v": pl.BlockSpec(memory_space=pltpu.VMEM),
    "h": pl.BlockSpec(memory_space=pl.ANY),
}


def vm(shape, dtype=BF16):
    return pltpu.VMEM(shape, dtype)


def call(name, kernel, out_shape, specs, *args, limit=4, flops=0, scratch=(), aliases={}):
    space = {"v": pltpu.VMEM, "h": pltpu.HBM}
    args = [
        pltpu.with_memory_space_constraint(a, space[s]) if s in space else a
        for a, s in zip(args, specs)
    ]
    return pl.pallas_call(
        kernel,
        name=name,
        out_shape=out_shape,
        in_specs=[SPECS[s] for s in specs],
        out_specs=[SPECS["v"]] * len(out_shape),
        scratch_shapes=list(scratch),
        input_output_aliases=aliases,
        compiler_params=pltpu.CompilerParams(vmem_limit_bytes=limit * MIB),
        cost_estimate=pl.CostEstimate(flops=flops, bytes_accessed=0, transcendentals=0),
    )(*args)


def unit_rows(rows):
    inverse = lax.rsqrt(jnp.sum(rows * rows, axis=1, keepdims=True) + 1e-06)
    return rows * inverse, inverse


def dot_nt(a, b):
    return lax.dot_general(a, b, (((1,), (1,)), ((), ())), preferred_element_type=F32)


def dot_tn(a, b):
    return lax.dot_general(a, b, (((0,), (0,)), ((), ())), preferred_element_type=F32)


def dot_nn(a, b):
    return jnp.dot(a, b, preferred_element_type=F32)


def log1p_sum(e):
    rows = e.shape[0]
    u = e
    for _ in range(3):
        rows //= 2
        a, b = u[:rows], u[rows:]
        u = a + b + a * b
    series = u * (1.0 - u * (0.5 - u * (1.0 / 3.0 - u * 0.25)))
    logs = jnp.where(u < 0.01, series, jnp.log(1.0 + u))
    return jnp.sum(logs, axis=0, keepdims=True)


def pairs(dots, scale, shift, base, labels, counted):
    logits = dots * scale + shift
    match = lax.broadcasted_iota(jnp.int32, logits.shape, 0) == labels - base
    e = jnp.exp(-jnp.abs(logits))
    whole = 1.0 + e
    over = pl.reciprocal(whole, approx=True)
    over = over * (2.0 - whole * over)
    sigmoid = jnp.where(logits >= 0.0, over, e * over)
    coef = (sigmoid - jnp.where(match, 1.0, 0.0)).astype(BF16)
    if not counted:
        return coef, None
    e, logits, match = e[:, :counted], logits[:, :counted], match[:, :counted]
    linear = jnp.maximum(jnp.where(match, -logits, logits), 0.0)
    return coef, jnp.sum(linear, axis=0, keepdims=True) + log1p_sum(e)


def shards(film, text, matched, sharpness, offset):
    rows, width = film.shape
    R, C = lax.axis_size("row"), lax.axis_size("col")
    Y, Z = R // 2, C // 4
    CHUNK = 256
    mat = (rows, width)
    limit = 6 + 2 * (Y * Z * 2 * rows) // 1024

    def swap(value, axis, bits):
        size = lax.axis_size(axis)
        return lax.ppermute(value, axis, [(i, i ^ bits) for i in range(size)])

    def cap_base(s, t, k):
        r, c = lax.axis_index("row"), lax.axis_index("col")
        return ((c ^ (4 * s + k)) * R + (r ^ (2 * t))) * rows

    def clip_index(x, z, k):
        r, c = lax.axis_index("row"), lax.axis_index("col")
        return (r ^ x) * C + (c ^ (2 * z + k))

    near = [(0, t) for t in range(Y)]
    up = [(s, 0) for s in range(1, Z)]
    diag = [(s, t) for s in range(1, Z) for t in range(1, Y)]
    caps_a = [(*p, 0) for p in near + up]
    caps_b = [(*p, 1) for p in near]
    caps_c = [(*p, 1) for p in up + diag]
    caps_d = [(*p, 0) for p in diag]
    clip_order = [(0, 0, 0), (1, 0, 0), (0, 1, 0), (0, 0, 1), (1, 0, 1), (0, 1, 1), (1, 1, 1), (1, 1, 0)]
    na, nb, nc, nd = (len(g) * rows for g in (caps_a, caps_b, caps_c, caps_d))
    n1, n3, n5 = rows, 3 * rows, 5 * rows

    PARTS = 4

    def normalize_kernel(film, text, matched, v16, c16, vhat, chat, vinv, cinv, labels, fbuf, tbuf, sems):
        step = rows // PARTS
        copies = []
        for j, (src, buf) in enumerate(((text, tbuf), (film, fbuf))):
            for i in range(PARTS):
                part = pl.ds(i * step, step)
                copies.append(pltpu.make_async_copy(src.at[part], buf.at[part], sems.at[j * PARTS + i]))
        for copy in copies:
            copy.start()
        labels[...] = jnp.concatenate(
            [matched[pl.ds(clip_index(*p), 1), :] for p in clip_order], axis=1
        )
        for copy in copies[:PARTS]:
            copy.wait()
        hat, inverse = unit_rows(tbuf[...])
        chat[...], cinv[...], c16[...] = hat, inverse, hat.astype(BF16)
        for copy in copies[PARTS:]:
            copy.wait()
        hat, inverse = unit_rows(fbuf[...])
        vhat[...], vinv[...], v16[...] = hat, inverse, hat.astype(BF16)

    v16, c16, vhat, chat, vinv, cinv, labels = pl.pallas_call(
        normalize_kernel,
        name="normalize",
        out_shape=[vm(mat), vm(mat), vm(mat, F32), vm(mat, F32), vm((rows, 1), F32), vm((rows, 1), F32),
                   vm((1, 8 * rows), jnp.int32)],
        in_specs=[SPECS["h"], SPECS["h"], SPECS["v"]],
        out_specs=[SPECS["v"]] * 7,
        scratch_shapes=[pltpu.VMEM(mat, F32)] * 2
        + [pltpu.SemaphoreType.DMA((2 * PARTS,))],
        compiler_params=pltpu.CompilerParams(vmem_limit_bytes=8 * MIB),
    )(*[
        pltpu.with_memory_space_constraint(a, pltpu.HBM)
        for a in (film, text, matched.reshape(-1, rows))
    ])

    def hand_on_kernel(block, *refs):
        pass

    def hand_on(name, block, *after, flops=0):
        return call(
            name, hand_on_kernel, [vm(block.shape, block.dtype)], "v" * (1 + len(after)),
            block, *after, aliases={0: 0}, flops=flops,
        )[0]

    LONG = 10**10

    def consts_kernel(scale, shift, out):
        out[0:1, :] = jnp.full((1, 128), scale[0], F32)
        out[1:2, :] = jnp.full((1, 128), shift[0], F32)

    (consts,) = call("consts", consts_kernel, [vm((2, 128), F32)], "ss", sharpness, offset)

    def copies_kernel(v16, c16, v_out, c_out, both):
        v_out[...] = v16[...]
        c_out[...] = c16[...]
        both[:rows, :] = c16[...]
        both[rows:, :] = v16[...]

    c_z = [hand_on("captions_z", swap(c16, "col", 4 * s), consts, flops=LONG) for s in range(1, Z)]
    v_z = hand_on("clips_z", swap(v16, "col", 2), flops=LONG)
    v16b, c16b, both = call("copies", copies_kernel, [vm(mat), vm(mat), vm((2 * rows, width))], "vv", v16, c16)
    c_y = [swap(c16b, "row", 2 * t) for t in range(1, Y)]
    v_x = swap(v16b, "row", 1)
    both_k = swap(both, "col", 1)
    c_d = [swap(b, "row", 2 * t) for b in c_z for t in range(1, Y)]
    v_d = swap(v_z, "row", 1)
    cy_k = [swap(b, "col", 1) for b in c_y]
    vx_k = swap(v_x, "col", 1)
    cz_k = [swap(b, "col", 1) for b in c_z]
    vz_k = swap(v_z, "col", 1)

    def stack(target, blocks):
        for i, b in enumerate(blocks):
            target[pl.ds(i * rows, rows), :] = b[...]

    def strip(consts, caps, captions, clips, labels, counted, put):
        total = jnp.zeros((1, counted), F32) if counted else None
        scale, shift = consts[0:1, 0:1], consts[1:2, 0:1]
        dots = dot_nt(captions, clips)
        for i, p in enumerate(caps):
            block = dots[i * rows : (i + 1) * rows]
            coef, add = pairs(block, scale, shift, cap_base(*p), labels, counted)
            put(i, coef)
            if counted:
                total += add
        return total

    def put_in(target, first=0, cols=None):
        def put(i, coef):
            where = pl.ds(first + i * rows, rows)
            target[where, :] = coef if cols is None else coef[:, :cols]
        return put

    def early_kernel(consts, labels, both, both_k, *refs):
        n = Y - 1 + Z - 1
        c_yz, v_xz, refs = refs[:n], refs[n : n + 2], refs[n + 2 :]
        cy_k, vx_k, refs = refs[: Y - 1], refs[Y - 1], refs[Y:]
        CA, VA, P1, Q1, loss = refs
        stack(CA, [both.at[:rows], *c_yz, both_k.at[:rows], *cy_k])
        stack(VA, [both.at[rows:], *v_xz, both_k.at[rows:], vx_k])
        total = strip(consts, caps_a, CA[:na, :], VA[...], labels[:, :n5], n3, put_in(P1))
        total += strip(consts, caps_b, CA[na:, :], VA[:n3, :], labels[:, :n3], n3, put_in(Q1))
        loss[...] = total

    CA, VA, P1, Q1, loss1 = call(
        "early_pairs", early_kernel,
        [vm((na + nb, width)), vm((n5, width)), vm((na, n5)), vm((nb, n3)), vm((1, n3), F32)],
        "vv" + "v" * (2 + len(c_y) + len(c_z) + 2 + len(c_y) + 1),
        consts, labels, both, both_k, *c_y, *c_z, v_x, v_z, *cy_k, vx_k,
        flops=2 * 21 * rows * rows * width, limit=limit,
    )

    v_d = hand_on("clips_d", v_d, loss1)
    c_d = [hand_on("captions_d", b, loss1) for b in c_d]
    vd_k = swap(v_d, "col", 1)
    cd_k = [swap(b, "col", 1) for b in c_d]

    def far_captions_kernel(consts, labels, VA, loss1, *refs):
        n = len(caps_d)
        caps, clips, refs = refs[:n], refs[n : n + 3], refs[n + 3 :]
        VB, b, loss, dcs, (CD, b2) = refs[0], refs[1], refs[2], refs[3:-2], refs[-2:]
        stack(CD, caps)
        stack(VB, clips)
        loss[...] = loss1[...] + strip(
            consts, caps_d, CD[...], VA[...], labels[:, :n5], n3, put_in(b)
        )
        strip(consts, caps_d, CD[...], VB[...], labels[:, n5:], 0, put_in(b2))
        for i in range(width // CHUNK):
            cols = pl.ds(i * CHUNK, CHUNK)
            part = dot_nn(b[...], VA[:, cols]) + dot_nn(b2[...], VB[:, cols])
            for j, ref in enumerate(dcs):
                ref[:, cols] = part[j * rows : (j + 1) * rows].astype(BF16)

    VB, b, loss2, *dc_d = call(
        "far_captions", far_captions_kernel,
        [vm((3 * n1, width)), vm((nd, n5)), vm((1, n3), F32)] + [vm(mat)] * len(caps_d),
        "vv" + "v" * (2 + len(caps_d) + 3),
        consts, labels, VA, loss1, *c_d, vz_k, vd_k, v_d,
        flops=2 * 16 * rows * rows * width, limit=limit,
        scratch=[pltpu.VMEM((nd, width), BF16), pltpu.VMEM((nd, 3 * n1), BF16)],
    )

    def far_clips_kernel(consts, labels, loss2, CA, vd, *refs):
        n = len(caps_c) + len(caps_d)
        caps, (CB, a, loss, dv) = refs[:n], refs[n:]
        stack(CB, caps)
        late = labels[:, 7 * n1 :]
        total = strip(consts, caps_a + caps_b, CA[...], vd[...], late, n1, put_in(a))
        total += strip(consts, caps_c + caps_d, CB[...], vd[...], late, n1, put_in(a, na + nb))
        loss[...] = total
        for i in range(width // CHUNK):
            cols = pl.ds(i * CHUNK, CHUNK)
            dv[:, cols] = (
                dot_tn(a[: na + nb, :], CA[:, cols]) + dot_tn(a[na + nb :, :], CB[:, cols])
            ).astype(BF16)

    CB, a, loss_d, dv_d = call(
        "far_clips", far_clips_kernel,
        [vm((nc + nd, width)), vm((na + nb + nc + nd, n1)), vm((1, n1), F32), vm(mat)],
        "vvv" + "v" * (2 + len(caps_c) + len(caps_d)),
        consts, labels, loss2, CA, v_d, *cz_k, *cd_k, *c_d,
        flops=2 * 16 * rows * rows * width, limit=limit,
    )

    def near(name, clip, first, count, dtype, *after):
        clips = slice(clip * rows, (clip + 1) * rows)
        caps = slice(first * rows, (first + count) * rows)

        def near_kernel(consts, labels, CA, VA, P1, Q1, CB, VB, a, b, loss2, *refs):
            loss, dv, *dcs, c, d = refs[len(after) :]
            loss[...] = loss2[:, clips] + strip(
                consts, caps_c, CB[:nc, :], VA[clips, :], labels[:, clips], n1, put_in(c)
            )
            strip(
                consts, caps_a[first : first + count], CA[caps, :], VB[: 2 * n1, :],
                labels[:, n5 : 7 * n1], 0, put_in(d),
            )
            for i in range(width // CHUNK):
                cols = pl.ds(i * CHUNK, CHUNK)
                part = (
                    dot_tn(P1[:, clips], CA[:na, cols])
                    + dot_tn(Q1[:, clips], CA[na:, cols])
                    + dot_tn(c[...], CB[:nc, cols])
                    + dot_tn(b[:, clips], CB[nc:, cols])
                )
                dv[:, cols] = part.astype(dv.dtype)
                part = (
                    dot_nn(P1[caps, :], VA[:, cols])
                    + dot_nn(d[...], VB[: 2 * n1, cols])
                    + dot_nn(a[caps, :], VB[2 * n1 :, cols])
                )
                for j, ref in enumerate(dcs):
                    ref[:, cols] = part[j * rows : (j + 1) * rows].astype(ref.dtype)

        return call(
            name, near_kernel,
            [vm((1, n1), F32)] + [vm(mat, dtype)] * (1 + count),
            "v" * (11 + len(after)),
            consts, labels, CA, VA, P1, Q1, CB, VB, a, b, loss2, *after,
            flops=2 * 20 * rows * rows * width, limit=limit,
            scratch=[pltpu.VMEM((nc, n1), BF16), pltpu.VMEM((count * rows, 2 * n1), BF16)],
        )

    far_c = [[swap(dc_d[s * (Y - 1) + t - 1], "row", 2 * t) for t in range(1, Y)] for s in range(Z - 1)]
    far_v = swap(dv_d, "row", 1)
    loss_z, dvz, *dcz = near("near_z", 2, Y, Z - 1, F32)

    def add_kernel(*refs):
        total = refs[0][...].astype(F32)
        for ref in refs[1:-1]:
            total += ref[...].astype(F32)
        refs[-1][...] = total.astype(BF16)

    def add(name, *terms):
        return call(name, add_kernel, [vm(mat)], "v" * len(terms), *terms)[0]

    sum_c = [add("add_captions", dcz[s], *far_c[s]) for s in range(Z - 1)]
    sum_v = add("add_clips", dvz, far_v)
    got_h = [
        hand_on("captions_back", swap(sum_c[s], "col", 4 * (s + 1)), flops=LONG) for s in range(Z - 1)
    ]
    got_z = hand_on("clips_back", swap(sum_v, "col", 2), flops=LONG)

    loss_x, dvx, *dcy = near("near_xy", 1, 1, Y - 1, BF16, sum_v, *sum_c)
    got_x = swap(dvx, "row", 1)
    got_y = [swap(dcy[t - 1], "row", 2 * t) for t in range(1, Y)]
    loss_0, dv0, dc0 = near("near_own", 0, 0, 1, F32, loss_x)

    def pack_kernel(x, d, out):
        out[0:1, :] = x[...]
        out[1:2, :] = d[...]

    (loss_x,) = call("pack_loss", pack_kernel, [vm((2, n1), F32)], "vv", loss_x, loss_d)

    def loss_kernel(loss_z, arrived, out):
        out[...] = loss_z[...] + arrived[1:2, :]

    far_loss = swap(loss_x, "row", 1)
    (sum_loss,) = call("add_loss", loss_kernel, [vm((1, n1), F32)], "vv", loss_z, far_loss)
    got_loss = swap(sum_loss, "col", 2)

    def finish(name, losses, *args):
        def finish_kernel(consts, hat_ref, inverse_ref, *refs):
            adds, (grad, *loss, buf, sem) = refs[: -3 - bool(losses)], refs[-3 - bool(losses) :]
            total = adds[losses][...]
            for ref in adds[losses + 1 :]:
                total += ref[...].astype(F32)
            total = total * consts[0:1, 0:1]
            hat = hat_ref[...]
            along = jnp.sum(hat * total, axis=1, keepdims=True)
            buf[...] = inverse_ref[...] * (total - hat * along)
            copy = pltpu.make_async_copy(buf, grad, sem)
            copy.start()
            if losses:
                loss_0, far_loss, got_loss = adds[:losses]
                loss[0][...] = loss_0[...] + far_loss[0:1, :] + got_loss[...]
            copy.wait()

        shapes = [jax.ShapeDtypeStruct(mat, F32)] + [jax.ShapeDtypeStruct((1, rows), F32)] * bool(losses)
        return pl.pallas_call(
            finish_kernel,
            name=name,
            out_shape=shapes,
            in_specs=[SPECS["v"]] * len(args),
            out_specs=[SPECS["h"]] + [SPECS["v"]] * bool(losses),
            scratch_shapes=[pltpu.VMEM(mat, F32), pltpu.SemaphoreType.DMA],
            compiler_params=pltpu.CompilerParams(vmem_limit_bytes=4 * MIB),
        )(*[pltpu.with_memory_space_constraint(x, pltpu.VMEM) for x in args])

    gv, clip_loss = finish(
        "finish_clips", 3, consts, vhat, vinv, loss_0, far_loss, got_loss, dv0, got_x, got_z
    )
    (gc,) = finish("finish_captions", 0, consts, chat, cinv, dc0, *got_y, *got_h)
    return clip_loss.reshape(rows), gv, gc


def solution(mesh):
    return jax.shard_map(
        shards,
        mesh=mesh,
        in_specs=(P(("row", "col"), None), P(("col", "row"), None), P(), P(), P()),
        out_specs=(P(("row", "col")), P(("row", "col"), None), P(("col", "row"), None)),
        check_vma=False,
    )
```

time: 180 us -> 57.9 us (0.32)
  waiting for transfers between devices: 102 us -> 20.4 us
  matrix products: 29.5 us -> 0 us
  starting transfers between devices: 0.16 us -> 20.5 us
  blocking collectives: 15.4 us -> 0 us
  Pallas kernels: 0 us -> 14.7 us
  between operations: 15.2 us -> 2.06 us
  other arithmetic: 13 us -> 0 us
  local copies, waits for them, and re-layouts: 4.15 us -> 0 us
    all_gather x2 -> x0, waiting for transfers between devices: 57.3 us -> none  [the longest x1 31.3 us: shards(): vrows = lax.all_gather(vhat.astype(jnp.bfloat16), 'col', axis=0, tiled=True)]
    reduce_scatter x2 -> x0, waiting for transfers between devices: 44.6 us -> none  [the longest x1 44.6 us: shards(): lax.psum_scatter((grads.reshape(count, width), losses.reshape(count))[0],...]
    dot_general x6 -> x0, matrix products: 29.5 us -> none  [the longest x2 11.7 us: one(): jnp.dot(coef, crows, preferred_element_type=jnp.float32)]
    ppermute x0 -> x21, starting transfers between devices: none -> 20.5 us  [swap(): return lax.ppermute(value, axis, [(i, i ^ bits) for i in range(size)])]
    ppermute x0 -> x21, waiting for transfers between devices: none -> 20.4 us  [swap(): return lax.ppermute(value, axis, [(i, i ^ bits) for i in range(size)])]
    unnamed x1 -> x0, blocking collectives: 15.4 us -> none
    pallas_call x0 -> x21, Pallas kernels: none -> 14.7 us  [the longest x18 9.84 us: call(): pl.pallas_call(kernel, name=name, out_shape=out_shape, in_specs=[SPECS[s]...]
    mul x3 -> x0, other arithmetic: 5.49 us -> none  [the longest x2 3.99 us: backward_norm(): inverse * (grad_hat - hat * jnp.sum(hat * grad_hat, axis=1, keepdims=True))]
  transfers between devices with their start and end apart: 4 -> 21, of which waited for: 3 -> 8; matrix products, arithmetic and copies ran while one was open for 15% -> 0% of each run, Pallas kernels for 0% -> 19%
where the time goes in v2:
time: 57.9 us; the launch traced here: 57.6 us
  starting transfers between devices  20.5 us (35%)
  waiting for transfers between devices  20.4 us (35%)
  Pallas kernels  14.7 us (25%)
  between operations  2.06 us (4%)
    ppermute x21, starting transfers between devices, swap(): return lax.ppermute(value, axis, [(i, i ^ bits) for i in range(size)])  20.5 us
    ppermute x21, waiting for transfers between devices, swap(): return lax.ppermute(value, axis, [(i, i ^ bits) for i in range(size)])  20.4 us
    pallas_call x18, Pallas kernels, call(): pl.pallas_call(kernel, name=name, out_shape=out_shape, in_specs=[SPECS[s]...  9.84 us
    pallas_call x2, Pallas kernels, finish(): pl.pallas_call(finish_kernel, name=name, out_shape=shapes, in_specs=[SPEC...  2.65 us
    pallas_call x1, Pallas kernels, shards(): pl.pallas_call(normalize_kernel, name='normalize', out_shape=[vm(mat), vm...  2.22 us
  transfers between devices with their start and end apart: 21, of which 8 were waited for; matrix products, arithmetic and copies ran while one was open for 0% of the time, Pallas kernels for 19%

profile of v2, /device:TPU:0, one launch (start us, length us, event | category | flops | bytes accessed | tf_op | source)
XLA Modules:
  0.0 57.6 jit_solution(17850589872437281255)
XLA Ops:
  0.6 2.2 %normalize.1 = (bf16[128,1024]{1,0:T(8,128)(2,1)S(1)}, bf16[128,1024]{1,0:T(8,128)(2,1)S(1)}, f32[128,1024]{1,0:T(8,128)S(1)}, f32[128,1024]{1,0:T(8,128)S(1)}, ...) custom-call(f32[128,1024]{1,0:T(8,128)} %film.1, f32[128,1024]{1,0:T(8,128)} %text.1, ...), custom_call_target="tpu_custom_call" | custom-call | tf_op jit(solution)/shard_map/normalize/pallas_call | solution.py:139
  2.9 3.1 %collective-permute-start.4 = (bf16[128,1024]{1,0:T(8,128)(2,1)S(1)}, bf16[128,1024]{1,0:T(8,128)(2,1)S(1)}, u32[]{:S(2)}, u32[]{:S(2)}) collective-permute-start(bf16[128,1024]{1,0:T(8,128)(2,1)S(1)} %get-tuple-element.40.v16), channel_id=1, source_target_pairs={{0,2},{1,3},{2,0},{3,1},{4,6},{5,7},{6,4},{7,5},{8,10},{9,11},{10,... | collective-permute-start | bytes 786440 | tf_op jit(solution)/shard_map/ppermute | solution.py:95
  5.9 2.6 %collective-permute-start.2 = (bf16[128,1024]{1,0:T(8,128)(2,1)S(1)}, bf16[128,1024]{1,0:T(8,128)(2,1)S(1)}, u32[]{:S(2)}, u32[]{:S(2)}) collective-permute-start(bf16[128,1024]{1,0:T(8,128)(2,1)S(1)} %get-tuple-element.41.c16), channel_id=1, source_target_pairs={{0,4},{1,5},{2,6},{3,7},{4,0},{5,1},{6,2},{7,3},{8,12},{9,13},{10,... | collective-permute-start | bytes 786440 | tf_op jit(solution)/shard_map/ppermute | solution.py:95
  8.6 1.6 %collective-permute-start.1 = (bf16[128,1024]{1,0:T(8,128)(2,1)S(1)}, bf16[128,1024]{1,0:T(8,128)(2,1)S(1)}, u32[]{:S(2)}, u32[]{:S(2)}) collective-permute-start(bf16[128,1024]{1,0:T(8,128)(2,1)S(1)} %get-tuple-element.43), channel_id=1, source_target_pairs={{0,16},{8,24},{16,0},{24,8},{1,17},{9,25},{17,1},{25,9},{2,18},{10... | collective-permute-start | bytes 786440 | tf_op jit(solution)/shard_map/ppermute | solution.py:95
  10.2 1.5 %collective-permute-start.3 = (bf16[128,1024]{1,0:T(8,128)(2,1)S(1)}, bf16[128,1024]{1,0:T(8,128)(2,1)S(1)}, u32[]{:S(2)}, u32[]{:S(2)}) collective-permute-start(bf16[128,1024]{1,0:T(8,128)(2,1)S(1)} %get-tuple-element.44), channel_id=1, source_target_pairs={{0,8},{8,0},{16,24},{24,16},{1,9},{9,1},{17,25},{25,17},{2,10},{10... | collective-permute-start | bytes 786440 | tf_op jit(solution)/shard_map/ppermute | solution.py:95
  13.0 4.8 %collective-permute-done.4.block = bf16[128,1024]{1,0:T(8,128)(2,1)S(1)} collective-permute-done((bf16[128,1024]{1,0:T(8,128)(2,1)S(1)}, bf16[128,1024]{1,0:T(8,128)(2,1)S(1)}, u32[]{:S(2)}, u32[]{:S(2)}) %collective-permute-start.4) | collective-permute-done | bytes 262176 | tf_op jit(solution)/shard_map/ppermute | solution.py:95
  17.8 1.7 %collective-permute-start.9 = (bf16[128,1024]{1,0:T(8,128)(2,1)S(1)}, bf16[128,1024]{1,0:T(8,128)(2,1)S(1)}, u32[]{:S(2)}, u32[]{:S(2)}) collective-permute-start(bf16[128,1024]{1,0:T(8,128)(2,1)S(1)} %clips_z.1.refs_3_), channel_id=1, source_target_pairs={{0,8},{8,0},{16,24},{24,16},{1,9},{9,1},{17,25},{25,17},{2,10},{10... | collective-permute-start | bytes 786440 | tf_op jit(solution)/shard_map/ppermute | solution.py:95
  19.4 0.5 collective-permute-start.6
  19.9 0.3 collective-permute-done.2.block
  20.3 1.5 %collective-permute-start.7 = (bf16[128,1024]{1,0:T(8,128)(2,1)S(1)}, bf16[128,1024]{1,0:T(8,128)(2,1)S(1)}, u32[]{:S(2)}, u32[]{:S(2)}) collective-permute-start(bf16[128,1024]{1,0:T(8,128)(2,1)S(1)} %captions_z.1.refs_1_), channel_id=1, source_target_pairs={{0,16},{8,24},{16,0},{24,8},{1,17},{9,25},{17,1},{25,9},{2,18},{10... | collective-permute-start | bytes 786440 | tf_op jit(solution)/shard_map/ppermute | solution.py:95
  21.8 2.0 %early_pairs.1 = (bf16[640,1024]{1,0:T(8,128)(2,1)S(1)}, bf16[640,1024]{1,0:T(8,128)(2,1)S(1)}, bf16[384,640]{1,0:T(8,128)(2,1)S(1)}, bf16[256,384]{1,0:T(8,128)(2,1)S(1)}, f32[1,384]{1,0:T(1,128)S(1)}) custom-call(f32[2,128]{1,0:T(2,128)S(1)} %consts.1.refs_0_, s32[1,1024]{1,0:T(1,128)S(1)} %get-tuple-element.39.labels, ...), custom_call_target="tpu_custom_call" | custom-call | flops 704643072 | tf_op jit(solution)/shard_map/early_pairs/pallas_call | solution.py:27
  23.8 1.4 %collective-permute-done.9.block = bf16[128,1024]{1,0:T(8,128)(2,1)S(1)} collective-permute-done((bf16[128,1024]{1,0:T(8,128)(2,1)S(1)}, bf16[128,1024]{1,0:T(8,128)(2,1)S(1)}, u32[]{:S(2)}, u32[]{:S(2)}) %collective-permute-start.9) | collective-permute-done | bytes 262176 | tf_op jit(solution)/shard_map/ppermute | solution.py:95
  25.2 0.5 collective-permute-start.11
  25.8 2.5 %collective-permute-done.7.block = bf16[128,1024]{1,0:T(8,128)(2,1)S(1)} collective-permute-done((bf16[128,1024]{1,0:T(8,128)(2,1)S(1)}, bf16[128,1024]{1,0:T(8,128)(2,1)S(1)}, u32[]{:S(2)}, u32[]{:S(2)}) %collective-permute-start.7) | collective-permute-done | bytes 262176 | tf_op jit(solution)/shard_map/ppermute | solution.py:95
  28.2 1.6 %far_captions.1 = (bf16[384,1024]{1,0:T(8,128)(2,1)S(1)}, bf16[128,640]{1,0:T(8,128)(2,1)S(1)}, f32[1,384]{1,0:T(1,128)S(1)}, bf16[128,1024]{1,0:T(8,128)(2,1)S(1)}) custom-call(f32[2,128]{1,0:T(2,128)S(1)} %consts.1.refs_0_, s32[1,1024]{1,0:T(1,128)S(1)} %get-tuple-element.39.labels, bf16[640,1024]{1,0:T(8,128)(2,1)S(1)} %get-tuple-element.46.VA, ...), custom_call_target="tpu_custom_call" | custom-call | flops 536870912 | tf_op jit(solution)/shard_map/far_captions/pallas_call | solution.py:27
  29.8 1.6 %collective-permute-start.14 = (bf16[128,1024]{1,0:T(8,128)(2,1)S(1)}, bf16[128,1024]{1,0:T(8,128)(2,1)S(1)}, u32[]{:S(2)}, u32[]{:S(2)}) collective-permute-start(bf16[128,1024]{1,0:T(8,128)(2,1)S(1)} %get-tuple-element.58), channel_id=1, source_target_pairs={{0,16},{8,24},{16,0},{24,8},{1,17},{9,25},{17,1},{25,9},{2,18},{10... | collective-permute-start | bytes 786440 | tf_op jit(solution)/shard_map/ppermute | solution.py:95
  31.4 1.8 %far_clips.1 = (bf16[384,1024]{1,0:T(8,128)(2,1)S(1)}, bf16[1024,128]{1,0:T(8,128)(2,1)S(1)}, f32[1,128]{1,0:T(1,128)S(1)}, bf16[128,1024]{1,0:T(8,128)(2,1)S(1)}) custom-call(f32[2,128]{1,0:T(2,128)S(1)} %consts.1.refs_0_, s32[1,1024]{1,0:T(1,128)S(1)} %get-tuple-element.39.labels, f32[1,384]{1,0:T(1,128)S(1)} %get-tuple-element.50.loss2, ...), custom_call_target="tpu_custom_call" | custom-call | flops 536870912 | tf_op jit(solution)/shard_map/far_clips/pallas_call | solution.py:27
  33.2 0.6 %collective-permute-start.13 = (bf16[128,1024]{1,0:T(8,128)(2,1)S(1)}, bf16[128,1024]{1,0:T(8,128)(2,1)S(1)}, u32[]{:S(2)}, u32[]{:S(2)}) collective-permute-start(bf16[128,1024]{1,0:T(8,128)(2,1)S(1)} %get-tuple-element.56), channel_id=1, source_target_pairs={{0,8},{8,0},{16,24},{24,16},{1,9},{9,1},{17,25},{25,17},{2,10},{10... | collective-permute-start | bytes 786440 | tf_op jit(solution)/shard_map/ppermute | solution.py:95
  33.8 1.4 %near_z.1 = (f32[1,128]{1,0:T(1,128)S(1)}, f32[128,1024]{1,0:T(8,128)S(1)}, f32[128,1024]{1,0:T(8,128)S(1)}) custom-call(f32[2,128]{1,0:T(2,128)S(1)} %consts.1.refs_0_, s32[1,1024]{1,0:T(1,128)S(1)} %get-tuple-element.39.labels, bf16[640,1024]{1,0:T(8,128)(2,1)S(1)} %get-tuple-element.45.CA, bf16[640,1024]{1,0:T(8,128)(2,1)S(1)} %get-tuple-element.46.VA, ...), custom_call_target="tpu_custom_call" | custom-call | flops 671088640 | tf_op jit(solution)/shard_map/near_z/pallas_call | solution.py:27
  35.2 3.3 %collective-permute-done.14.refs_1_ = bf16[128,1024]{1,0:T(8,128)(2,1)S(1)} collective-permute-done((bf16[128,1024]{1,0:T(8,128)(2,1)S(1)}, bf16[128,1024]{1,0:T(8,128)(2,1)S(1)}, u32[]{:S(2)}, u32[]{:S(2)}) %collective-permute-start.14) | collective-permute-done | bytes 262176 | tf_op jit(solution)/shard_map/ppermute | solution.py:95
  38.6 0.6 %collective-permute-start.20 = (bf16[128,1024]{1,0:T(8,128)(2,1)S(1)}, bf16[128,1024]{1,0:T(8,128)(2,1)S(1)}, u32[]{:S(2)}, u32[]{:S(2)}) collective-permute-start(bf16[128,1024]{1,0:T(8,128)(2,1)S(1)} %add_captions.1.refs_1_), channel_id=1, source_target_pairs={{0,4},{1,5},{2,6},{3,7},{4,0},{5,1},{6,2},{7,3},{8,12},{9,13},{10,... | collective-permute-start | bytes 786440 | tf_op jit(solution)/shard_map/ppermute | solution.py:95
  39.3 2.4 %collective-permute-done.13.refs_1_ = bf16[128,1024]{1,0:T(8,128)(2,1)S(1)} collective-permute-done((bf16[128,1024]{1,0:T(8,128)(2,1)S(1)}, bf16[128,1024]{1,0:T(8,128)(2,1)S(1)}, u32[]{:S(2)}, u32[]{:S(2)}) %collective-permute-start.13) | collective-permute-done | bytes 262176 | tf_op jit(solution)/shard_map/ppermute | solution.py:95
  41.9 1.5 %near_xy.1 = (f32[1,128]{1,0:T(1,128)S(1)}, bf16[128,1024]{1,0:T(8,128)(2,1)S(1)}, bf16[128,1024]{1,0:T(8,128)(2,1)S(1)}) custom-call(f32[2,128]{1,0:T(2,128)S(1)} %consts.1.refs_0_, s32[1,1024]{1,0:T(1,128)S(1)} %get-tuple-element.39.labels, bf16[640,1024]{1,0:T(8,128)(2,1)S(1)} %get-tuple-element.45.CA, bf16[640,1024]{1,0:T(8,128)(2,1)S(1)} %get-tuple-element.46.VA, ...), custom_call_target="tpu_custom_call" | custom-call | flops 671088640 | tf_op jit(solution)/shard_map/near_xy/pallas_call | solution.py:27
  43.3 1.1 %collective-permute-start.15 = (f32[2,128]{1,0:T(2,128)S(1)}, f32[2,128]{1,0:T(2,128)S(1)}, u32[]{:S(2)}, u32[]{:S(2)}) collective-permute-start(f32[2,128]{1,0:T(2,128)S(1)} %pack_loss.1), channel_id=1, source_target_pairs={{0,8},{8,0},{16,24},{24,16},{1,9},{9,1},{17,25},{25,17},{2,10},{10... | collective-permute-start | bytes 3080 | tf_op jit(solution)/shard_map/ppermute | solution.py:95
  44.5 1.4 %near_own.1 = (f32[1,128]{1,0:T(1,128)S(1)}, f32[128,1024]{1,0:T(8,128)S(1)}, f32[128,1024]{1,0:T(8,128)S(1)}) custom-call(f32[2,128]{1,0:T(2,128)S(1)} %consts.1.refs_0_, s32[1,1024]{1,0:T(1,128)S(1)} %get-tuple-element.39.labels, bf16[640,1024]{1,0:T(8,128)(2,1)S(1)} %get-tuple-element.45.CA, bf16[640,1024]{1,0:T(8,128)(2,1)S(1)} %get-tuple-element.46.VA, ...), custom_call_target="tpu_custom_call" | custom-call | flops 671088640 | tf_op jit(solution)/shard_map/near_own/pallas_call | solution.py:27
  45.9 1.0 %collective-permute-start.17 = (bf16[128,1024]{1,0:T(8,128)(2,1)S(1)}, bf16[128,1024]{1,0:T(8,128)(2,1)S(1)}, u32[]{:S(2)}, u32[]{:S(2)}) collective-permute-start(bf16[128,1024]{1,0:T(8,128)(2,1)S(1)} %get-tuple-element.64), channel_id=1, source_target_pairs={{0,8},{8,0},{16,24},{24,16},{1,9},{9,1},{17,25},{25,17},{2,10},{10... | collective-permute-start | bytes 786440 | tf_op jit(solution)/shard_map/ppermute | solution.py:95
  46.9 1.5 %collective-permute-start.19 = (bf16[128,1024]{1,0:T(8,128)(2,1)S(1)}, bf16[128,1024]{1,0:T(8,128)(2,1)S(1)}, u32[]{:S(2)}, u32[]{:S(2)}) collective-permute-start(bf16[128,1024]{1,0:T(8,128)(2,1)S(1)} %get-tuple-element.70), channel_id=1, source_target_pairs={{0,16},{8,24},{16,0},{24,8},{1,17},{9,25},{17,1},{25,9},{2,18},{10... | collective-permute-start | bytes 786440 | tf_op jit(solution)/shard_map/ppermute | solution.py:95
  48.5 1.0 %collective-permute-start.16 = (f32[1,128]{1,0:T(1,128)S(1)}, f32[1,128]{1,0:T(1,128)S(1)}, u32[]{:S(2)}, u32[]{:S(2)}) collective-permute-start(f32[1,128]{1,0:T(1,128)S(1)} %add_loss.1), channel_id=1, source_target_pairs={{0,2},{1,3},{2,0},{3,1},{4,6},{5,7},{6,4},{7,5},{8,10},{9,11},{10,... | collective-permute-start | bytes 1544 | tf_op jit(solution)/shard_map/ppermute | solution.py:95
  49.4 3.7 %collective-permute-done.20.block = bf16[128,1024]{1,0:T(8,128)(2,1)S(1)} collective-permute-done((bf16[128,1024]{1,0:T(8,128)(2,1)S(1)}, bf16[128,1024]{1,0:T(8,128)(2,1)S(1)}, u32[]{:S(2)}, u32[]{:S(2)}) %collective-permute-start.20) | collective-permute-done | bytes 262176 | tf_op jit(solution)/shard_map/ppermute | solution.py:95
  53.1 1.9 %collective-permute-done.18.block = bf16[128,1024]{1,0:T(8,128)(2,1)S(1)} collective-permute-done((bf16[128,1024]{1,0:T(8,128)(2,1)S(1)}, bf16[128,1024]{1,0:T(8,128)(2,1)S(1)}, u32[]{:S(2)}, u32[]{:S(2)}) %collective-permute-start.18) | collective-permute-done | bytes 262176 | tf_op jit(solution)/shard_map/ppermute | solution.py:95
  55.0 1.1 %finish_captions.1 = f32[128,1024]{1,0:T(8,128)} custom-call(f32[2,128]{1,0:T(2,128)S(1)} %consts.1.refs_0_, f32[128,1024]{1,0:T(8,128)S(1)} %get-tuple-element.67.hat_ref, f32[128,1]{1,0:T(8,128)S(1)} %get-tuple-element.68.inverse_ref, f32[128,1024]{1,0:T(8,128)S(1)} %get-tuple-element.69.refs_0_, bf16[128,1024]{1,0:T(8,128)(2,1)S(1)} %collective-permute-done.19.refs_1_, ...), custom_call_target="tpu_custom_call" | custom-call | tf_op jit(solution)/shard_map/finish_captions/pallas_call | solution.py:378
  56.1 1.6 %finish_clips.1 = (f32[128,1024]{1,0:T(8,128)}, f32[1,128]{1,0:T(1,128)}) custom-call(f32[2,128]{1,0:T(2,128)S(1)} %consts.1.refs_0_, f32[128,1024]{1,0:T(8,128)S(1)} %get-tuple-element.37.hat_ref, f32[128,1]{1,0:T(8,128)S(1)} %get-tuple-element.38.inverse_ref, f32[1,128]{1,0:T(1,128)S(1)} %get-tuple-element.60.refs_0_, ...), custom_call_target="tpu_custom_call" | custom-call | tf_op jit(solution)/shard_map/finish_clips/pallas_call | solution.py:378
  (31 shorter events, 0.4 us)
Async XLA Ops:
  2.9 14.9 %collective-permute-start.4 = (bf16[128,1024]{1,0:T(8,128)(2,1)S(1)}, bf16[128,1024]{1,0:T(8,128)(2,1)S(1)}, u32[]{:S(2)}, u32[]{:S(2)}) collective-permute-start(bf16[128,1024]{1,0:T(8,128)(2,1)S(1)} %get-tuple-element.40.v16), channel_id=1, source_target_pairs={{0,2},{1,3},{2,0},{3,1},{4,6},{5,7},{6,4},{7,5},{8,10},{9,11},{10,... | collective-permute-start | bytes 786440 | tf_op jit(solution)/shard_map/ppermute | solution.py:95
  5.9 14.3 %collective-permute-start.2 = (bf16[128,1024]{1,0:T(8,128)(2,1)S(1)}, bf16[128,1024]{1,0:T(8,128)(2,1)S(1)}, u32[]{:S(2)}, u32[]{:S(2)}) collective-permute-start(bf16[128,1024]{1,0:T(8,128)(2,1)S(1)} %get-tuple-element.41.c16), channel_id=1, source_target_pairs={{0,4},{1,5},{2,6},{3,7},{4,0},{5,1},{6,2},{7,3},{8,12},{9,13},{10,... | collective-permute-start | bytes 786440 | tf_op jit(solution)/shard_map/ppermute | solution.py:95
  8.6 10.8 %collective-permute-start.1 = (bf16[128,1024]{1,0:T(8,128)(2,1)S(1)}, bf16[128,1024]{1,0:T(8,128)(2,1)S(1)}, u32[]{:S(2)}, u32[]{:S(2)}) collective-permute-start(bf16[128,1024]{1,0:T(8,128)(2,1)S(1)} %get-tuple-element.43), channel_id=1, source_target_pairs={{0,16},{8,24},{16,0},{24,8},{1,17},{9,25},{17,1},{25,9},{2,18},{10... | collective-permute-start | bytes 786440 | tf_op jit(solution)/shard_map/ppermute | solution.py:95
  10.2 9.2 %collective-permute-start.3 = (bf16[128,1024]{1,0:T(8,128)(2,1)S(1)}, bf16[128,1024]{1,0:T(8,128)(2,1)S(1)}, u32[]{:S(2)}, u32[]{:S(2)}) collective-permute-start(bf16[128,1024]{1,0:T(8,128)(2,1)S(1)} %get-tuple-element.44), channel_id=1, source_target_pairs={{0,8},{8,0},{16,24},{24,16},{1,9},{9,1},{17,25},{25,17},{2,10},{10... | collective-permute-start | bytes 786440 | tf_op jit(solution)/shard_map/ppermute | solution.py:95
  11.7 10.1 %collective-permute-start = (bf16[256,1024]{1,0:T(8,128)(2,1)S(1)}, bf16[256,1024]{1,0:T(8,128)(2,1)S(1)}, u32[]{:S(2)}, u32[]{:S(2)}) collective-permute-start(bf16[256,1024]{1,0:T(8,128)(2,1)S(1)} %get-tuple-element.42.both), channel_id=1, source_target_pairs={{0,1},{1,0},{2,3},{3,2},{4,5},{5,4},{6,7},{7,6},{8,9},{9,8},{10,11... | collective-permute-start | bytes 1572872 | tf_op jit(solution)/shard_map/ppermute | solution.py:95
  17.8 7.5 %collective-permute-start.9 = (bf16[128,1024]{1,0:T(8,128)(2,1)S(1)}, bf16[128,1024]{1,0:T(8,128)(2,1)S(1)}, u32[]{:S(2)}, u32[]{:S(2)}) collective-permute-start(bf16[128,1024]{1,0:T(8,128)(2,1)S(1)} %clips_z.1.refs_3_), channel_id=1, source_target_pairs={{0,8},{8,0},{16,24},{24,16},{1,9},{9,1},{17,25},{25,17},{2,10},{10... | collective-permute-start | bytes 786440 | tf_op jit(solution)/shard_map/ppermute | solution.py:95
  19.4 2.4 %collective-permute-start.5 = (bf16[128,1024]{1,0:T(8,128)(2,1)S(1)}, bf16[128,1024]{1,0:T(8,128)(2,1)S(1)}, u32[]{:S(2)}, u32[]{:S(2)}) collective-permute-start(bf16[128,1024]{1,0:T(8,128)(2,1)S(1)} %collective-permute-done.1.refs_0_), channel_id=1, source_target_pairs={{0,1},{1,0},{2,3},{3,2},{4,5},{5,4},{6,7},{7,6},{8,9},{9,8},{10,11... | collective-permute-start | bytes 786440 | tf_op jit(solution)/shard_map/ppermute | solution.py:95
  19.4 2.4 %collective-permute-start.6 = (bf16[128,1024]{1,0:T(8,128)(2,1)S(1)}, bf16[128,1024]{1,0:T(8,128)(2,1)S(1)}, u32[]{:S(2)}, u32[]{:S(2)}) collective-permute-start(bf16[128,1024]{1,0:T(8,128)(2,1)S(1)} %collective-permute-done.3.refs_2_), channel_id=1, source_target_pairs={{0,1},{1,0},{2,3},{3,2},{4,5},{5,4},{6,7},{7,6},{8,9},{9,8},{10,11... | collective-permute-start | bytes 786440 | tf_op jit(solution)/shard_map/ppermute | solution.py:95
  20.3 7.9 %collective-permute-start.7 = (bf16[128,1024]{1,0:T(8,128)(2,1)S(1)}, bf16[128,1024]{1,0:T(8,128)(2,1)S(1)}, u32[]{:S(2)}, u32[]{:S(2)}) collective-permute-start(bf16[128,1024]{1,0:T(8,128)(2,1)S(1)} %captions_z.1.refs_1_), channel_id=1, source_target_pairs={{0,16},{8,24},{16,0},{24,8},{1,17},{9,25},{17,1},{25,9},{2,18},{10... | collective-permute-start | bytes 786440 | tf_op jit(solution)/shard_map/ppermute | solution.py:95
  21.8 6.4 %collective-permute-start.8 = (bf16[128,1024]{1,0:T(8,128)(2,1)S(1)}, bf16[128,1024]{1,0:T(8,128)(2,1)S(1)}, u32[]{:S(2)}, u32[]{:S(2)}) collective-permute-start(bf16[128,1024]{1,0:T(8,128)(2,1)S(1)} %clips_z.1.refs_3_), channel_id=1, source_target_pairs={{0,1},{1,0},{2,3},{3,2},{4,5},{5,4},{6,7},{7,6},{8,9},{9,8},{10,11... | collective-permute-start | bytes 786440 | tf_op jit(solution)/shard_map/ppermute | solution.py:95
  25.2 3.0 %collective-permute-start.10 = (bf16[128,1024]{1,0:T(8,128)(2,1)S(1)}, bf16[128,1024]{1,0:T(8,128)(2,1)S(1)}, u32[]{:S(2)}, u32[]{:S(2)}) collective-permute-start(bf16[128,1024]{1,0:T(8,128)(2,1)S(1)} %clips_d.1.refs_3_.vd), channel_id=1, source_target_pairs={{0,1},{1,0},{2,3},{3,2},{4,5},{5,4},{6,7},{7,6},{8,9},{9,8},{10,11... | collective-permute-start | bytes 786440 | tf_op jit(solution)/shard_map/ppermute | solution.py:95
  25.2 6.1 %collective-permute-start.11 = (bf16[128,1024]{1,0:T(8,128)(2,1)S(1)}, bf16[128,1024]{1,0:T(8,128)(2,1)S(1)}, u32[]{:S(2)}, u32[]{:S(2)}) collective-permute-start(bf16[128,1024]{1,0:T(8,128)(2,1)S(1)} %captions_z.1.refs_1_), channel_id=1, source_target_pairs={{0,1},{1,0},{2,3},{3,2},{4,5},{5,4},{6,7},{7,6},{8,9},{9,8},{10,11... | collective-permute-start | bytes 786440 | tf_op jit(solution)/shard_map/ppermute | solution.py:95
  28.2 3.2 %collective-permute-start.12 = (bf16[128,1024]{1,0:T(8,128)(2,1)S(1)}, bf16[128,1024]{1,0:T(8,128)(2,1)S(1)}, u32[]{:S(2)}, u32[]{:S(2)}) collective-permute-start(bf16[128,1024]{1,0:T(8,128)(2,1)S(1)} %captions_d.1.refs_0_.refs_2_), channel_id=1, source_target_pairs={{0,1},{1,0},{2,3},{3,2},{4,5},{5,4},{6,7},{7,6},{8,9},{9,8},{10,11... | collective-permute-start | bytes 786440 | tf_op jit(solution)/shard_map/ppermute | solution.py:95
  29.8 8.8 %collective-permute-start.14 = (bf16[128,1024]{1,0:T(8,128)(2,1)S(1)}, bf16[128,1024]{1,0:T(8,128)(2,1)S(1)}, u32[]{:S(2)}, u32[]{:S(2)}) collective-permute-start(bf16[128,1024]{1,0:T(8,128)(2,1)S(1)} %get-tuple-element.58), channel_id=1, source_target_pairs={{0,16},{8,24},{16,0},{24,8},{1,17},{9,25},{17,1},{25,9},{2,18},{10... | collective-permute-start | bytes 786440 | tf_op jit(solution)/shard_map/ppermute | solution.py:95
  33.2 8.5 %collective-permute-start.13 = (bf16[128,1024]{1,0:T(8,128)(2,1)S(1)}, bf16[128,1024]{1,0:T(8,128)(2,1)S(1)}, u32[]{:S(2)}, u32[]{:S(2)}) collective-permute-start(bf16[128,1024]{1,0:T(8,128)(2,1)S(1)} %get-tuple-element.56), channel_id=1, source_target_pairs={{0,8},{8,0},{16,24},{24,16},{1,9},{9,1},{17,25},{25,17},{2,10},{10... | collective-permute-start | bytes 786440 | tf_op jit(solution)/shard_map/ppermute | solution.py:95
  38.6 14.5 %collective-permute-start.20 = (bf16[128,1024]{1,0:T(8,128)(2,1)S(1)}, bf16[128,1024]{1,0:T(8,128)(2,1)S(1)}, u32[]{:S(2)}, u32[]{:S(2)}) collective-permute-start(bf16[128,1024]{1,0:T(8,128)(2,1)S(1)} %add_captions.1.refs_1_), channel_id=1, source_target_pairs={{0,4},{1,5},{2,6},{3,7},{4,0},{5,1},{6,2},{7,3},{8,12},{9,13},{10,... | collective-permute-start | bytes 786440 | tf_op jit(solution)/shard_map/ppermute | solution.py:95
  41.7 13.2 %collective-permute-start.18 = (bf16[128,1024]{1,0:T(8,128)(2,1)S(1)}, bf16[128,1024]{1,0:T(8,128)(2,1)S(1)}, u32[]{:S(2)}, u32[]{:S(2)}) collective-permute-start(bf16[128,1024]{1,0:T(8,128)(2,1)S(1)} %add_clips.1.refs_0_), channel_id=1, source_target_pairs={{0,2},{1,3},{2,0},{3,1},{4,6},{5,7},{6,4},{7,5},{8,10},{9,11},{10,... | collective-permute-start | bytes 786440 | tf_op jit(solution)/shard_map/ppermute | solution.py:95
  43.3 5.1 %collective-permute-start.15 = (f32[2,128]{1,0:T(2,128)S(1)}, f32[2,128]{1,0:T(2,128)S(1)}, u32[]{:S(2)}, u32[]{:S(2)}) collective-permute-start(f32[2,128]{1,0:T(2,128)S(1)} %pack_loss.1), channel_id=1, source_target_pairs={{0,8},{8,0},{16,24},{24,16},{1,9},{9,1},{17,25},{25,17},{2,10},{10... | collective-permute-start | bytes 3080 | tf_op jit(solution)/shard_map/ppermute | solution.py:95
  45.9 10.2 %collective-permute-start.17 = (bf16[128,1024]{1,0:T(8,128)(2,1)S(1)}, bf16[128,1024]{1,0:T(8,128)(2,1)S(1)}, u32[]{:S(2)}, u32[]{:S(2)}) collective-permute-start(bf16[128,1024]{1,0:T(8,128)(2,1)S(1)} %get-tuple-element.64), channel_id=1, source_target_pairs={{0,8},{8,0},{16,24},{24,16},{1,9},{9,1},{17,25},{25,17},{2,10},{10... | collective-permute-start | bytes 786440 | tf_op jit(solution)/shard_map/ppermute | solution.py:95
  46.9 8.0 %collective-permute-start.19 = (bf16[128,1024]{1,0:T(8,128)(2,1)S(1)}, bf16[128,1024]{1,0:T(8,128)(2,1)S(1)}, u32[]{:S(2)}, u32[]{:S(2)}) collective-permute-start(bf16[128,1024]{1,0:T(8,128)(2,1)S(1)} %get-tuple-element.70), channel_id=1, source_target_pairs={{0,16},{8,24},{16,0},{24,8},{1,17},{9,25},{17,1},{25,9},{2,18},{10... | collective-permute-start | bytes 786440 | tf_op jit(solution)/shard_map/ppermute | solution.py:95
  48.5 7.6 %collective-permute-start.16 = (f32[1,128]{1,0:T(1,128)S(1)}, f32[1,128]{1,0:T(1,128)S(1)}, u32[]{:S(2)}, u32[]{:S(2)}) collective-permute-start(f32[1,128]{1,0:T(1,128)S(1)} %add_loss.1), channel_id=1, source_target_pairs={{0,2},{1,3},{2,0},{3,1},{4,6},{5,7},{6,4},{7,5},{8,10},{9,11},{10,... | collective-permute-start | bytes 1544 | tf_op jit(solution)/shard_map/ppermute | solution.py:95

commit v3 on v0

v3 whole, which is shorter than its diff:
```python
import jax
import jax.numpy as jnp
from jax import lax
from jax.experimental import pallas as pl
from jax.experimental.pallas import tpu as pltpu
from jax.sharding import PartitionSpec as P

F32, BF16 = jnp.float32, jnp.bfloat16
MIB = 1024 * 1024
CHUNK = 256
PARTS = 4
LONG = 10**10
SPECS = {
    "s": pl.BlockSpec(memory_space=pltpu.SMEM),
    "v": pl.BlockSpec(memory_space=pltpu.VMEM),
    "h": pl.BlockSpec(memory_space=pl.ANY),
}


def vm(shape, dtype=BF16):
    return pltpu.VMEM(shape, dtype)


def call(name, kernel, out_shape, args, spec="v", out_spec="v", limit=4, flops=0, scratch=(), aliases={}):
    space = {"v": pltpu.VMEM, "h": pltpu.HBM}
    if spec in space:
        args = [pltpu.with_memory_space_constraint(a, space[spec]) for a in args]
    return pl.pallas_call(
        kernel,
        name=name,
        out_shape=out_shape,
        in_specs=[SPECS[spec]] * len(args),
        out_specs=[SPECS[out_spec]] * len(out_shape),
        scratch_shapes=list(scratch),
        input_output_aliases=aliases,
        compiler_params=pltpu.CompilerParams(vmem_limit_bytes=limit * MIB),
        cost_estimate=pl.CostEstimate(flops=flops, bytes_accessed=0, transcendentals=0),
    )(*args)


def hand_on(name, block, *after, flops=0):
    return call(
        name, lambda *refs: None, [vm(block.shape, block.dtype)], [block, *after],
        aliases={0: 0}, flops=flops,
    )[0]


def unit_rows(rows):
    inverse = lax.rsqrt(jnp.sum(rows * rows, axis=1, keepdims=True) + 1e-06)
    return rows * inverse, inverse


def dot_nt(a, b):
    return lax.dot_general(a, b, (((1,), (1,)), ((), ())), preferred_element_type=F32)


def dot_tn(a, b):
    return lax.dot_general(a, b, (((0,), (0,)), ((), ())), preferred_element_type=F32)


def dot_nn(a, b):
    return jnp.dot(a, b, preferred_element_type=F32)


def log1p_sum(e):
    rows = e.shape[0]
    u = e
    for _ in range(3):
        rows //= 2
        a, b = u[:rows], u[rows:]
        u = a + b + a * b
    series = u * (1.0 - u * (0.5 - u * (1.0 / 3.0 - u * 0.25)))
    logs = jnp.where(u < 0.01, series, jnp.log(1.0 + u))
    return jnp.sum(logs, axis=0, keepdims=True)


def pairs(dots, scale, shift, base, labels, counted):
    logits = dots * scale + shift
    match = lax.broadcasted_iota(jnp.int32, logits.shape, 0) == labels - base
    e = jnp.exp(-jnp.abs(logits))
    whole = 1.0 + e
    over = pl.reciprocal(whole, approx=True)
    over = over * (2.0 - whole * over)
    sigmoid = jnp.where(logits >= 0.0, over, e * over)
    coef = (sigmoid - jnp.where(match, 1.0, 0.0)).astype(BF16)
    if not counted:
        return coef, None
    e, logits, match = e[:, :counted], logits[:, :counted], match[:, :counted]
    linear = jnp.maximum(jnp.where(match, -logits, logits), 0.0)
    return coef, jnp.sum(linear, axis=0, keepdims=True) + log1p_sum(e)


def stack(target, blocks):
    at = 0
    for b in blocks:
        target[pl.ds(at, b.shape[0]), :] = b[...]
        at += b.shape[0]


def shards(film, text, matched, sharpness, offset):
    rows, width = film.shape
    half = rows // 2
    R, C = lax.axis_size("row"), lax.axis_size("col")
    Y, Z = R // 2, C // 4
    mat, hmat = (rows, width), (half, width)
    limit = 6 + 2 * (Y * Z * 2 * rows) // 1024

    def swap(value, axis, bits):
        size = lax.axis_size(axis)
        return lax.ppermute(value, axis, [(i, i ^ bits) for i in range(size)])

    def first_caption(s, t, k):
        r, c = lax.axis_index("row"), lax.axis_index("col")
        return ((c ^ (4 * s + k)) * R + (r ^ (2 * t))) * rows

    def clip_index(x, z, k):
        r, c = lax.axis_index("row"), lax.axis_index("col")
        return (r ^ x) * C + (c ^ (2 * z + k))

    near = [(0, t) for t in range(Y)]
    up = [(s, 0) for s in range(1, Z)]
    diag = [(s, t) for s in range(1, Z) for t in range(1, Y)]
    clip_order = [(x, z, k) for k in range(2) for z in range(2) for x in range(2)]
    nn, nh = len(near) * rows, (len(up) + len(diag)) * half
    n1, n3, n4 = rows, 3 * rows, 4 * rows

    def near_pieces(k):
        return [(*p, k, 0, rows) for p in near]

    def half_pieces(k, h):
        return [(*p, k, h * half, half) for p in up + diag]

    def strip(consts, pieces, captions, clips, labels, counted, put):
        scale, shift = consts[0:1, 0:1], consts[1:2, 0:1]
        dots = dot_nt(captions, clips)
        at, total = 0, 0.0
        for s, t, k, first, size in pieces:
            base = first_caption(s, t, k) + first
            coef, add = pairs(dots[at : at + size], scale, shift, base, labels, counted)
            put(at, coef)
            total = total + add if counted else None
            at += size
        return total

    def put_in(target, first=0):
        def put(at, coef):
            target[pl.ds(first + at, coef.shape[0]), :] = coef
        return put

    def normalize_kernel(film, text, matched, v16, c16, ca, vhat, chat, vinv, cinv, labels, fbuf, tbuf, mbuf, sems):
        step = rows // PARTS
        get_matched = pltpu.make_async_copy(matched, mbuf, sems.at[2 * PARTS])
        copies = []
        for j, (src, buf) in enumerate(((film, fbuf), (text, tbuf))):
            for i in range(PARTS):
                part = pl.ds(i * step, step)
                copies.append(pltpu.make_async_copy(src.at[part], buf.at[part], sems.at[j * PARTS + i]))
        for copy in copies:
            copy.start()
        get_matched.start()
        for copy in copies[:PARTS]:
            copy.wait()
        hat, inverse = unit_rows(fbuf[...])
        vhat[...], vinv[...], v16[...] = hat, inverse, hat.astype(BF16)
        for copy in copies[PARTS:]:
            copy.wait()
        hat, inverse = unit_rows(tbuf[...])
        chat[...], cinv[...], c16[...] = hat, inverse, hat.astype(BF16)
        ca[...] = hat[:half].astype(BF16)
        get_matched.wait()
        labels[...] = jnp.concatenate(
            [mbuf[pl.ds(clip_index(*p), 1), :] for p in clip_order], axis=1
        )

    matched = matched.reshape(-1, rows)
    v16, c16, ca, vhat, chat, vinv, cinv, labels = call(
        "normalize", normalize_kernel,
        [vm(mat), vm(mat), vm(hmat), vm(mat, F32), vm(mat, F32), vm((rows, 1), F32), vm((rows, 1), F32),
         vm((1, 8 * rows), jnp.int32)],
        [film, text, matched], spec="h", limit=8,
        scratch=[pltpu.VMEM(mat, F32)] * 2
        + [pltpu.VMEM(matched.shape, jnp.int32), pltpu.SemaphoreType.DMA((2 * PARTS + 1,))],
    )

    def consts_kernel(scale, shift, out):
        out[0:1, :] = jnp.full((1, 128), scale[0], F32)
        out[1:2, :] = jnp.full((1, 128), shift[0], F32)

    (consts,) = call("consts", consts_kernel, [vm((2, 128), F32)], [sharpness, offset], spec="s")

    def copies_kernel(v16, c16, v_out, c_out, cb, both):
        v_out[...] = v16[...]
        c_out[...] = c16[...]
        cb[...] = c16[half:, :]
        both[:rows, :] = c16[...]
        both[rows:, :] = v16[...]

    v_z = hand_on("clips_z", swap(v16, "col", 2), flops=LONG)
    c_za = [hand_on("captions_za", swap(ca, "col", 4 * s), flops=LONG) for s in range(1, Z)]
    v16b, c16b, cb, both = call(
        "copies", copies_kernel, [vm(mat), vm(mat), vm(hmat), vm((2 * rows, width))], [v16, c16]
    )
    c_y = [swap(c16b, "row", 2 * t) for t in range(1, Y)]
    v_x = swap(v16b, "row", 1)
    c_za = [hand_on("captions_zy", b, consts, *c_y) for b in c_za]
    v_z = hand_on("clips_zx", v_z, v_x)
    c_zb = [swap(cb, "col", 4 * s) for s in range(1, Z)]
    both_k = swap(both, "col", 1)
    v_d = swap(v_z, "row", 1)
    c_da = [hand_on("captions_da", swap(b, "row", 2 * t), flops=LONG) for b in c_za for t in range(1, Y)]
    c_db = [swap(b, "row", 2 * t) for b in c_zb for t in range(1, Y)]
    cy_k = [swap(b, "col", 1) for b in c_y]
    vx_k = swap(v_x, "col", 1)
    vz_k = swap(v_z, "col", 1)
    vd_k = swap(v_d, "col", 1)
    c_h = [c_za + c_da]
    ch_k = [[swap(b, "col", 1) for b in c_h[0]]]

    def stack_kernel(both, both_k, vx, vz, vd, vxk, vzk, vdk, VV):
        stack(VV, [both.at[rows:], vx, vz, vd, both_k.at[rows:], vxk, vzk, vdk])

    (VV,) = call("clips", stack_kernel, [vm((8 * n1, width))], [both, both_k, v_x, v_z, v_d, vx_k, vz_k, vd_k])

    def half_sums(h):
        def half_kernel(consts, labels, VV, *refs):
            n = len(c_h[h])
            caps, (loss, p, *sums, H, coef) = refs[:n], refs[n:]
            stack(H, caps)
            loss[...] = strip(consts, half_pieces(0, h), H[...], VV[...], labels[...], n4, put_in(coef))
            p[...] = coef[:, :n4]
            for i in range(width // CHUNK):
                cols = pl.ds(i * CHUNK, CHUNK)
                part = dot_nn(coef[...], VV[:, cols])
                for j, ref in enumerate(sums):
                    ref[:, cols] = part[j * half : (j + 1) * half].astype(ref.dtype)

        loss, p, *sums = call(
            "half_" + "ab"[h], half_kernel,
            [vm((1, n4), F32), vm((nh, n4))] + [vm(hmat, F32)] * len(up) + [vm(hmat)] * len(diag),
            [consts, labels, VV, *c_h[h]],
            flops=2 * 16 * rows * rows * width, limit=limit,
            scratch=[pltpu.VMEM((nh, width), BF16), pltpu.VMEM((nh, 8 * n1), BF16)],
        )
        return loss, p, sums[: len(up)], sums[len(up) :]

    loss_a, p_a, dcz_a, dcd_a = half_sums(0)

    def diagonal_kernel(consts, labels, both, both_k, vd, *refs):
        n = len(near) - 1
        m = len(c_h[0])
        cy, cyk, c_a, c_ak = refs[:n], refs[n : 2 * n], refs[2 * n : 2 * n + m], refs[2 * n + m : 2 * n + 2 * m]
        S1, g, loss = refs[2 * n + 2 * m :]
        stack(S1, [both.at[:rows], *cy, *c_a, both_k.at[:rows], *cyk, *c_ak])
        m = nn + nh
        late = labels[:, n3:n4]
        strip(consts, near_pieces(0) + half_pieces(0, 0), S1[:m, :], vd[...], late, 0, put_in(g))
        loss[...] = strip(
            consts, near_pieces(1) + half_pieces(1, 0), S1[m:, :], vd[...], late, n1, put_in(g, m)
        )

    S1, g1, loss_d1 = call(
        "diagonal_clips", diagonal_kernel,
        [vm((2 * (nn + nh), width)), vm((2 * (nn + nh), n1)), vm((1, n1), F32)],
        [consts, labels, both, both_k, v_d, *c_y, *cy_k, *c_h[0], *ch_k[0]],
        flops=2 * 6 * rows * rows * width, limit=limit,
    )

    c_h.append([hand_on("captions_b", b, loss_a, flops=LONG // 3) for b in c_zb + c_db])
    ch_k.append([swap(b, "col", 1) for b in c_h[1]])
    loss_b, p_b, dcz_b, dcd_b = half_sums(1)

    def far_clips_kernel(consts, labels, vd, S1, g1, p_b, *refs):
        m = len(c_h[1])
        caps, (S2, loss, dv, g2) = refs[: 2 * m], refs[2 * m :]
        stack(S2, caps)
        g2[:nh, :] = p_b[:, n3:]
        loss[...] = strip(
            consts, half_pieces(1, 1), S2[nh:, :], vd[...], labels[:, n3:n4], n1, put_in(g2, nh)
        )
        for i in range(width // CHUNK):
            cols = pl.ds(i * CHUNK, CHUNK)
            dv[:, cols] = (dot_tn(g1[...], S1[:, cols]) + dot_tn(g2[...], S2[:, cols])).astype(BF16)

    S2, loss_d2, dv_d = call(
        "far_clips", far_clips_kernel,
        [vm((2 * nh, width)), vm((1, n1), F32), vm(mat)],
        [consts, labels, v_d, S1, g1, p_b, *c_h[1], *ch_k[1]],
        flops=2 * 9 * rows * rows * width, limit=limit,
        scratch=[pltpu.VMEM((2 * nh, n1), BF16)],
    )

    far_v = swap(dv_d, "row", 1)

    def add_kernel(*refs):
        total = refs[0][...].astype(F32)
        for ref in refs[1:-1]:
            total += ref[...].astype(F32)
        refs[-1][...] = total.astype(BF16)

    def add(name, *terms):
        return call(name, add_kernel, [vm(terms[0].shape)], terms)[0]

    def captions_back(h, dcz, dcd):
        far = [
            [
                hand_on("far_" + "ab"[h], swap(dcd[s * (Y - 1) + t - 1], "row", 2 * t), dv_d, flops=LONG)
                for t in range(1, Y)
            ]
            for s in range(Z - 1)
        ]
        sums = [add("add_" + "ab"[h], dcz[s], *far[s]) for s in range(Z - 1)]
        return sums, [swap(sums[s], "col", 4 * (s + 1)) for s in range(Z - 1)]

    sums_a, got_a = captions_back(0, dcz_a, dcd_a)
    sums_b, got_b = captions_back(1, dcz_b, dcd_b)

    def near_captions_kernel(consts, labels, VV, S1, dv_d, *refs):
        loss, p, *sums, coef = refs[Z - 1 :]
        loss[...] = strip(consts, near_pieces(0), S1[:nn, :], VV[...], labels[...], n4, put_in(coef))
        p[...] = coef[:, :n3]
        for i in range(width // CHUNK):
            cols = pl.ds(i * CHUNK, CHUNK)
            part = dot_nn(coef[...], VV[:, cols])
            for j, ref in enumerate(sums):
                ref[:, cols] = part[j * rows : (j + 1) * rows].astype(ref.dtype)

    loss_n, p_n, dc0, *dcy = call(
        "near_captions", near_captions_kernel,
        [vm((1, n4), F32), vm((nn, n3)), vm(mat, F32)] + [vm(mat)] * (Y - 1),
        [consts, labels, VV, S1, dv_d, *sums_a],
        flops=2 * 32 * rows * rows * width, limit=limit,
        scratch=[pltpu.VMEM((nn, 8 * n1), BF16)],
    )

    def z_clips_kernel(consts, labels, VV, S1, S2, p_n, p_a, p_b, *refs):
        loss, G1, G2, dv = refs[Z - 1 :]
        m = nn + nh
        G1[:nn, :] = p_n[...]
        G1[nn:m, :] = p_a[:, :n3]
        G2[:nh, :] = p_b[:, :n3]
        own = VV[:n3, :]
        loss[...] = strip(
            consts, near_pieces(1) + half_pieces(1, 0), S1[m:, :], own, labels[:, :n3], n3, put_in(G1, m)
        ) + strip(consts, half_pieces(1, 1), S2[nh:, :], own, labels[:, :n3], n3, put_in(G2, nh))
        for i in range(width // CHUNK):
            cols = pl.ds(i * CHUNK, CHUNK)
            dv[:, cols] = dot_tn(G1[:, 2 * n1 :], S1[:, cols]) + dot_tn(G2[:, 2 * n1 :], S2[:, cols])

    loss_k, G1, G2, dvz = call(
        "z_clips", z_clips_kernel,
        [vm((1, n3), F32), vm((2 * (nn + nh), n3)), vm((2 * nh, n3)), vm(mat, F32)],
        [consts, labels, VV, S1, S2, p_n, p_a, p_b, *sums_b],
        flops=2 * 20 * rows * rows * width, limit=limit,
    )

    sum_v = add("add_clips", dvz, far_v)
    got_z = hand_on("clips_back", swap(sum_v, "col", 2), flops=LONG)
    got_h = [[hand_on("captions_back", b, sum_v, flops=LONG) for b in got] for got in (got_a, got_b)]
    got_y = [swap(dcy[t - 1], "row", 2 * t) for t in range(1, Y)]

    def losses_kernel(l_a, l_b, l_n, l_k, l_d1, l_d2, loss_0, loss_x, loss_z):
        total = l_a[...] + l_b[...] + l_n[...]
        own = total[:, :n3] + l_k[...]
        loss_0[...] = own[:, :n1]
        loss_x[0:1, :] = own[:, n1 : 2 * n1]
        loss_x[1:2, :] = total[:, n3:] + l_d1[...] + l_d2[...]
        loss_z[...] = own[:, 2 * n1 :]

    def add_loss_kernel(loss_z, arrived, out):
        out[...] = loss_z[...] + arrived[1:2, :]

    loss_0, loss_x, loss_z = call(
        "losses", losses_kernel, [vm((1, n1), F32), vm((2, n1), F32), vm((1, n1), F32)],
        [loss_a, loss_b, loss_n, loss_k, loss_d1, loss_d2],
    )
    far_loss = swap(loss_x, "row", 1)
    (sum_loss,) = call("add_loss", add_loss_kernel, [vm((1, n1), F32)], [loss_z, far_loss])
    got_loss = swap(sum_loss, "col", 2)

    def near_clips_kernel(S1, S2, G1, G2, sum_v, sum_loss, dv0, dvx):
        for i in range(width // CHUNK):
            cols = pl.ds(i * CHUNK, CHUNK)
            part = dot_tn(G1[:, : 2 * n1], S1[:, cols]) + dot_tn(G2[:, : 2 * n1], S2[:, cols])
            dv0[:, cols] = part[:n1]
            dvx[:, cols] = part[n1:].astype(BF16)

    dv0, dvx = call(
        "near_clips", near_clips_kernel, [vm(mat, F32), vm(mat)],
        [S1, S2, G1, G2, sum_v, sum_loss],
        flops=2 * 16 * rows * rows * width, limit=limit,
    )
    got_x = swap(dvx, "row", 1)

    def finish(name, losses, consts, hat, inverse, own, whole, halves):
        tail = 2 + 2 * bool(losses)

        def finish_kernel(consts, hat_ref, inverse_ref, *refs):
            adds, (grad, *loss, buf, sems) = refs[: -1 - tail], refs[-1 - tail :]
            copies = []
            if losses:
                out, lbuf = loss
                loss_0, far_loss, got_loss = adds[:3]
                lbuf[...] = loss_0[...] + far_loss[0:1, :] + got_loss[...]
                copies.append(pltpu.make_async_copy(lbuf, out, sems.at[2]))
                copies[-1].start()
            adds = adds[len(losses) :]
            for i in range(2):
                part = pl.ds(i * half, half)
                total = adds[0][part, :]
                for ref in adds[1 : 1 + len(whole)]:
                    total += ref[part, :].astype(F32)
                for ref in adds[1 + len(whole) :][i * len(halves[0]) : (i + 1) * len(halves[0])]:
                    total += ref[...].astype(F32)
                total = total * consts[0:1, 0:1]
                hat = hat_ref[part, :]
                along = jnp.sum(hat * total, axis=1, keepdims=True)
                buf[part, :] = inverse_ref[part, :] * (total - hat * along)
                copies.append(pltpu.make_async_copy(buf.at[part], grad.at[part], sems.at[i]))
                copies[-1].start()
            for copy in copies:
                copy.wait()

        return call(
            name, finish_kernel,
            [jax.ShapeDtypeStruct(mat, F32)] + [jax.ShapeDtypeStruct((1, rows), F32)] * bool(losses),
            [consts, hat, inverse, *losses, own, *whole, *halves[0], *halves[1]], out_spec="h",
            scratch=[pltpu.VMEM((1, rows), F32)] * bool(losses)
            + [pltpu.VMEM(mat, F32), pltpu.SemaphoreType.DMA((3,))],
        )

    (gc,) = finish("finish_captions", [], consts, chat, cinv, dc0, got_y, got_h)
    gv, clip_loss = finish(
        "finish_clips", [loss_0, far_loss, got_loss], consts, vhat, vinv, dv0, [got_x, got_z], ([], [])
    )
    return clip_loss.reshape(rows), gv, gc


def solution(mesh):
    return jax.shard_map(
        shards,
        mesh=mesh,
        in_specs=(P(("row", "col"), None), P(("col", "row"), None), P(), P(), P()),
        out_specs=(P(("row", "col")), P(("row", "col"), None), P(("col", "row"), None)),
        check_vma=False,
    )
```

time: 180 us -> 57.5 us (0.32)
  waiting for transfers between devices: 102 us -> 15.5 us
  matrix products: 29.5 us -> 0 us
  starting transfers between devices: 0.16 us -> 26.6 us
  blocking collectives: 15.4 us -> 0 us
  between operations: 15.2 us -> 2.09 us
  Pallas kernels: 0 us -> 13.1 us
  other arithmetic: 13 us -> 0 us
  local copies, waits for them, and re-layouts: 4.15 us -> 0 us
    all_gather x2 -> x0, waiting for transfers between devices: 57.3 us -> none  [the longest x1 31.3 us: shards(): vrows = lax.all_gather(vhat.astype(jnp.bfloat16), 'col', axis=0, tiled=True)]
    reduce_scatter x2 -> x0, waiting for transfers between devices: 44.6 us -> none  [the longest x1 44.6 us: shards(): lax.psum_scatter((grads.reshape(count, width), losses.reshape(count))[0],...]
    dot_general x6 -> x0, matrix products: 29.5 us -> none  [the longest x2 11.7 us: one(): jnp.dot(coef, crows, preferred_element_type=jnp.float32)]
    ppermute x0 -> x27, starting transfers between devices: none -> 26.6 us  [swap(): return lax.ppermute(value, axis, [(i, i ^ bits) for i in range(size)])]
    ppermute x0 -> x27, waiting for transfers between devices: none -> 15.5 us  [swap(): return lax.ppermute(value, axis, [(i, i ^ bits) for i in range(size)])]
    unnamed x1 -> x0, blocking collectives: 15.4 us -> none
    pallas_call x0 -> x30, Pallas kernels: none -> 13.1 us  [call(): pl.pallas_call(kernel, name=name, out_shape=out_shape, in_specs=[SPECS[sp...]
    mul x3 -> x0, other arithmetic: 5.49 us -> none  [the longest x2 3.99 us: backward_norm(): inverse * (grad_hat - hat * jnp.sum(hat * grad_hat, axis=1, keepdims=True))]
  transfers between devices with their start and end apart: 4 -> 27, of which waited for: 3 -> 11; matrix products, arithmetic and copies ran while one was open for 15% -> 0% of each run, Pallas kernels for 0% -> 18%
where the time goes in v3:
time: 57.5 us; the launch traced here: 57.3 us
  starting transfers between devices  26.6 us (46%)
  waiting for transfers between devices  15.5 us (27%)
  Pallas kernels  13.1 us (23%)
  between operations  2.09 us (4%)
    ppermute x27, starting transfers between devices, swap(): return lax.ppermute(value, axis, [(i, i ^ bits) for i in range(size)])  26.6 us
    ppermute x27, waiting for transfers between devices, swap(): return lax.ppermute(value, axis, [(i, i ^ bits) for i in range(size)])  15.5 us
    pallas_call x30, Pallas kernels, call(): pl.pallas_call(kernel, name=name, out_shape=out_shape, in_specs=[SPECS[sp...  13.1 us
  transfers between devices with their start and end apart: 27, of which 11 were waited for; matrix products, arithmetic and copies ran while one was open for 0% of the time, Pallas kernels for 18%

profile of v3, /device:TPU:0, one launch (start us, length us, event | category | flops | bytes accessed | tf_op | source)
XLA Modules:
  0.0 57.3 jit_solution(9537930077219506776)
XLA Ops:
  0.6 1.5 %normalize.1 = (bf16[128,1024]{1,0:T(8,128)(2,1)S(1)}, bf16[128,1024]{1,0:T(8,128)(2,1)S(1)}, bf16[64,1024]{1,0:T(8,128)(2,1)S(1)}, f32[128,1024]{1,0:T(8,128)S(...) custom-call(f32[128,1024]{1,0:T(8,128)} %film.1, ...), custom_call_target="tpu_custom_call" | custom-call | tf_op jit(solution)/shard_map/normalize/pallas_call | solution.py:28
  2.2 3.1 %collective-permute-start.2 = (bf16[128,1024]{1,0:T(8,128)(2,1)S(1)}, bf16[128,1024]{1,0:T(8,128)(2,1)S(1)}, u32[]{:S(2)}, u32[]{:S(2)}) collective-permute-start(bf16[128,1024]{1,0:T(8,128)(2,1)S(1)} %get-tuple-element.47.v16), channel_id=1, source_target_pairs={{0,2},{1,3},{2,0},{3,1},{4,6},{5,7},{6,4},{7,5},{8,10},{9,11},{10,... | collective-permute-start | bytes 786440 | tf_op jit(solution)/shard_map/ppermute | solution.py:110
  5.3 1.6 %collective-permute-start.8 = (bf16[128,1024]{1,0:T(8,128)(2,1)S(1)}, bf16[128,1024]{1,0:T(8,128)(2,1)S(1)}, u32[]{:S(2)}, u32[]{:S(2)}) collective-permute-start(bf16[128,1024]{1,0:T(8,128)(2,1)S(1)} %get-tuple-element.52), channel_id=1, source_target_pairs={{0,16},{8,24},{16,0},{24,8},{1,17},{9,25},{17,1},{25,9},{2,18},{10... | collective-permute-start | bytes 786440 | tf_op jit(solution)/shard_map/ppermute | solution.py:110
  6.9 2.6 %collective-permute-start.7 = (bf16[64,1024]{1,0:T(8,128)(2,1)S(1)}, bf16[64,1024]{1,0:T(8,128)(2,1)S(1)}, u32[]{:S(2)}, u32[]{:S(2)}) collective-permute-start(bf16[64,1024]{1,0:T(8,128)(2,1)S(1)} %get-tuple-element.51), channel_id=1, source_target_pairs={{0,4},{1,5},{2,6},{3,7},{4,0},{5,1},{6,2},{7,3},{8,12},{9,13},{10,... | collective-permute-start | bytes 393224 | tf_op jit(solution)/shard_map/ppermute | solution.py:110
  9.5 1.5 %collective-permute-start.1 = (bf16[128,1024]{1,0:T(8,128)(2,1)S(1)}, bf16[128,1024]{1,0:T(8,128)(2,1)S(1)}, u32[]{:S(2)}, u32[]{:S(2)}) collective-permute-start(bf16[128,1024]{1,0:T(8,128)(2,1)S(1)} %get-tuple-element.50), channel_id=1, source_target_pairs={{0,8},{8,0},{16,24},{24,16},{1,9},{9,1},{17,25},{25,17},{2,10},{10... | collective-permute-start | bytes 786440 | tf_op jit(solution)/shard_map/ppermute | solution.py:110
  12.7 2.7 %collective-permute-done.2.refs_0_ = bf16[128,1024]{1,0:T(8,128)(2,1)S(1)} collective-permute-done((bf16[128,1024]{1,0:T(8,128)(2,1)S(1)}, bf16[128,1024]{1,0:T(8,128)(2,1)S(1)}, u32[]{:S(2)}, u32[]{:S(2)}) %collective-permute-start.2) | collective-permute-done | bytes 262176 | tf_op jit(solution)/shard_map/ppermute | solution.py:110
  15.3 1.4 %collective-permute-done.1.refs_1_.vx = bf16[128,1024]{1,0:T(8,128)(2,1)S(1)} collective-permute-done((bf16[128,1024]{1,0:T(8,128)(2,1)S(1)}, bf16[128,1024]{1,0:T(8,128)(2,1)S(1)}, u32[]{:S(2)}, u32[]{:S(2)}) %collective-permute-start.1) | collective-permute-done | bytes 262176 | tf_op jit(solution)/shard_map/ppermute | solution.py:110
  16.7 1.5 %collective-permute-start.3 = (bf16[128,1024]{1,0:T(8,128)(2,1)S(1)}, bf16[128,1024]{1,0:T(8,128)(2,1)S(1)}, u32[]{:S(2)}, u32[]{:S(2)}) collective-permute-start(bf16[128,1024]{1,0:T(8,128)(2,1)S(1)} %clips_zx.1.vz), channel_id=1, source_target_pairs={{0,8},{8,0},{16,24},{24,16},{1,9},{9,1},{17,25},{25,17},{2,10},{10... | collective-permute-start | bytes 786440 | tf_op jit(solution)/shard_map/ppermute | solution.py:110
  18.2 1.5 %collective-permute-start.9 = (bf16[64,1024]{1,0:T(8,128)(2,1)S(1)}, bf16[64,1024]{1,0:T(8,128)(2,1)S(1)}, u32[]{:S(2)}, u32[]{:S(2)}) collective-permute-start(bf16[64,1024]{1,0:T(8,128)(2,1)S(1)} %captions_zy.1.refs_0_.refs_2_), channel_id=1, source_target_pairs={{0,16},{8,24},{16,0},{24,8},{1,17},{9,25},{17,1},{25,9},{2,18},{10... | collective-permute-start | bytes 393224 | tf_op jit(solution)/shard_map/ppermute | solution.py:110
  19.7 1.6 %collective-permute-done.10.refs_0_ = bf16[64,1024]{1,0:T(8,128)(2,1)S(1)} collective-permute-done((bf16[64,1024]{1,0:T(8,128)(2,1)S(1)}, bf16[64,1024]{1,0:T(8,128)(2,1)S(1)}, u32[]{:S(2)}, u32[]{:S(2)}) %collective-permute-start.10) | collective-permute-done | bytes 131104 | tf_op jit(solution)/shard_map/ppermute | solution.py:110
  21.3 0.8 %collective-permute-start.11 = (bf16[64,1024]{1,0:T(8,128)(2,1)S(1)}, bf16[64,1024]{1,0:T(8,128)(2,1)S(1)}, u32[]{:S(2)}, u32[]{:S(2)}) collective-permute-start(bf16[64,1024]{1,0:T(8,128)(2,1)S(1)} %collective-permute-done.10.refs_0_), channel_id=1, source_target_pairs={{0,16},{8,24},{16,0},{24,8},{1,17},{9,25},{17,1},{25,9},{2,18},{10... | collective-permute-start | bytes 393224 | tf_op jit(solution)/shard_map/ppermute | solution.py:110
  22.2 1.3 %collective-permute-done.9.refs_0_ = bf16[64,1024]{1,0:T(8,128)(2,1)S(1)} collective-permute-done((bf16[64,1024]{1,0:T(8,128)(2,1)S(1)}, bf16[64,1024]{1,0:T(8,128)(2,1)S(1)}, u32[]{:S(2)}, u32[]{:S(2)}) %collective-permute-start.9) | collective-permute-done | bytes 131104 | tf_op jit(solution)/shard_map/ppermute | solution.py:110
  25.5 1.4 %half_a.1 = (f32[1,512]{1,0:T(1,128)S(1)}, bf16[128,512]{1,0:T(8,128)(2,1)S(1)}, f32[64,1024]{1,0:T(8,128)S(1)}, bf16[64,1024]{1,0:T(8,128)(2,1)S(1)}) custom-call(f32[2,128]{1,0:T(2,128)S(1)} %consts.1.refs_1_, s32[1,1024]{1,0:T(1,128)S(1)} %get-tuple-element.46.labels, bf16[1024,1024]{1,0:T(8,128)(2,1)S(1)} %clips.1.VV, ...), custom_call_target="tpu_custom_call" | custom-call | flops 536870912 | tf_op jit(solution)/shard_map/half_a/pallas_call | solution.py:28
  27.6 1.4 %half_b.1 = (f32[1,512]{1,0:T(1,128)S(1)}, bf16[128,512]{1,0:T(8,128)(2,1)S(1)}, f32[64,1024]{1,0:T(8,128)S(1)}, bf16[64,1024]{1,0:T(8,128)(2,1)S(1)}) custom-call(f32[2,128]{1,0:T(2,128)S(1)} %consts.1.refs_1_, s32[1,1024]{1,0:T(1,128)S(1)} %get-tuple-element.46.labels, bf16[1024,1024]{1,0:T(8,128)(2,1)S(1)} %clips.1.VV, ...), custom_call_target="tpu_custom_call" | custom-call | flops 536870912 | tf_op jit(solution)/shard_map/half_b/pallas_call | solution.py:28
  29.0 2.5 %collective-permute-start.18 = (bf16[64,1024]{1,0:T(8,128)(2,1)S(1)}, bf16[64,1024]{1,0:T(8,128)(2,1)S(1)}, u32[]{:S(2)}, u32[]{:S(2)}) collective-permute-start(bf16[64,1024]{1,0:T(8,128)(2,1)S(1)} %get-tuple-element.67), channel_id=1, source_target_pairs={{0,16},{8,24},{16,0},{24,8},{1,17},{9,25},{17,1},{25,9},{2,18},{10... | collective-permute-start | bytes 393224 | tf_op jit(solution)/shard_map/ppermute | solution.py:110
  31.6 0.8 %diagonal_clips.1 = (bf16[768,1024]{1,0:T(8,128)(2,1)S(1)}, bf16[768,128]{1,0:T(8,128)(2,1)S(1)}, f32[1,128]{1,0:T(1,128)S(1)}) custom-call(f32[2,128]{1,0:T(2,128)S(1)} %consts.1.refs_1_, s32[1,1024]{1,0:T(1,128)S(1)} %get-tuple-element.46.labels, bf16[256,1024]{1,0:T(8,128)(2,1)S(1)} %get-tuple-element.49.both, ...), custom_call_target="tpu_custom_call" | custom-call | flops 201326592 | tf_op jit(solution)/shard_map/diagonal_clips/pallas_call | solution.py:28
  32.5 0.8 %far_clips.1 = (bf16[256,1024]{1,0:T(8,128)(2,1)S(1)}, f32[1,128]{1,0:T(1,128)S(1)}, bf16[128,1024]{1,0:T(8,128)(2,1)S(1)}) custom-call(f32[2,128]{1,0:T(2,128)S(1)} %consts.1.refs_1_, s32[1,1024]{1,0:T(1,128)S(1)} %get-tuple-element.46.labels, bf16[128,1024]{1,0:T(8,128)(2,1)S(1)} %collective-permute-done.3.vd, bf16[768,1024]{1,0:T(8,128)(2,1)S(1)} %get-tuple-element.56.S1, ...), custom_call_target="tpu_custom_call" | custom-call | flops 301989888 | tf_op jit(solution)/shard_map/far_clips/pallas_call | solution.py:28
  33.8 2.0 %collective-permute-done.18.refs_0_ = bf16[64,1024]{1,0:T(8,128)(2,1)S(1)} collective-permute-done((bf16[64,1024]{1,0:T(8,128)(2,1)S(1)}, bf16[64,1024]{1,0:T(8,128)(2,1)S(1)}, u32[]{:S(2)}, u32[]{:S(2)}) %collective-permute-start.18) | collective-permute-done | bytes 131104 | tf_op jit(solution)/shard_map/ppermute | solution.py:110
  35.8 0.8 %collective-permute-start.26 = (bf16[64,1024]{1,0:T(8,128)(2,1)S(1)}, bf16[64,1024]{1,0:T(8,128)(2,1)S(1)}, u32[]{:S(2)}, u32[]{:S(2)}) collective-permute-start(bf16[64,1024]{1,0:T(8,128)(2,1)S(1)} %add_b.1.refs_0_), channel_id=1, source_target_pairs={{0,4},{1,5},{2,6},{3,7},{4,0},{5,1},{6,2},{7,3},{8,12},{9,13},{10,... | collective-permute-start | bytes 393224 | tf_op jit(solution)/shard_map/ppermute | solution.py:110
  36.6 1.5 %collective-permute-done.17.refs_0_ = bf16[64,1024]{1,0:T(8,128)(2,1)S(1)} collective-permute-done((bf16[64,1024]{1,0:T(8,128)(2,1)S(1)}, bf16[64,1024]{1,0:T(8,128)(2,1)S(1)}, u32[]{:S(2)}, u32[]{:S(2)}) %collective-permute-start.17) | collective-permute-done | bytes 131104 | tf_op jit(solution)/shard_map/ppermute | solution.py:110
  38.2 2.1 %near_captions.1 = (f32[1,512]{1,0:T(1,128)S(1)}, bf16[256,384]{1,0:T(8,128)(2,1)S(1)}, f32[128,1024]{1,0:T(8,128)S(1)}, bf16[128,1024]{1,0:T(8,128)(2,1)S(1)}) custom-call(f32[2,128]{1,0:T(2,128)S(1)} %consts.1.refs_1_, s32[1,1024]{1,0:T(1,128)S(1)} %get-tuple-element.46.labels, bf16[1024,1024]{1,0:T(8,128)(2,1)S(1)} %clips.1.VV, ...), custom_call_target="tpu_custom_call" | custom-call | flops 1073741824 | tf_op jit(solution)/shard_map/near_captions/pallas_call | solution.py:28
  40.3 1.8 %z_clips.1 = (f32[1,384]{1,0:T(1,128)S(1)}, bf16[768,384]{1,0:T(8,128)(2,1)S(1)}, bf16[256,384]{1,0:T(8,128)(2,1)S(1)}, f32[128,1024]{1,0:T(8,128)S(1)}) custom-call(f32[2,128]{1,0:T(2,128)S(1)} %consts.1.refs_1_, s32[1,1024]{1,0:T(1,128)S(1)} %get-tuple-element.46.labels, bf16[1024,1024]{1,0:T(8,128)(2,1)S(1)} %clips.1.VV, ...), custom_call_target="tpu_custom_call" | custom-call | flops 671088640 | tf_op jit(solution)/shard_map/z_clips/pallas_call | solution.py:28
  42.1 0.6 collective-permute-start.19
  42.7 1.1 %collective-permute-start.25 = (bf16[64,1024]{1,0:T(8,128)(2,1)S(1)}, bf16[64,1024]{1,0:T(8,128)(2,1)S(1)}, u32[]{:S(2)}, u32[]{:S(2)}) collective-permute-start(bf16[64,1024]{1,0:T(8,128)(2,1)S(1)} %add_a.1.refs_0_), channel_id=1, source_target_pairs={{0,4},{1,5},{2,6},{3,7},{4,0},{5,1},{6,2},{7,3},{8,12},{9,13},{10,... | collective-permute-start | bytes 393224 | tf_op jit(solution)/shard_map/ppermute | solution.py:110
  43.8 1.7 %collective-permute-start.24 = (bf16[128,1024]{1,0:T(8,128)(2,1)S(1)}, bf16[128,1024]{1,0:T(8,128)(2,1)S(1)}, u32[]{:S(2)}, u32[]{:S(2)}) collective-permute-start(bf16[128,1024]{1,0:T(8,128)(2,1)S(1)} %get-tuple-element.84), channel_id=1, source_target_pairs={{0,16},{8,24},{16,0},{24,8},{1,17},{9,25},{17,1},{25,9},{2,18},{10... | collective-permute-start | bytes 786440 | tf_op jit(solution)/shard_map/ppermute | solution.py:110
  45.8 2.9 %collective-permute-start.20 = (f32[1,128]{1,0:T(1,128)S(1)}, f32[1,128]{1,0:T(1,128)S(1)}, u32[]{:S(2)}, u32[]{:S(2)}) collective-permute-start(f32[1,128]{1,0:T(1,128)S(1)} %add_loss.1.sum_loss), channel_id=1, source_target_pairs={{0,2},{1,3},{2,0},{3,1},{4,6},{5,7},{6,4},{7,5},{8,10},{9,11},{10,... | collective-permute-start | bytes 1544 | tf_op jit(solution)/shard_map/ppermute | solution.py:110
  48.8 0.8 %near_clips.1 = (f32[128,1024]{1,0:T(8,128)S(1)}, bf16[128,1024]{1,0:T(8,128)(2,1)S(1)}) custom-call(bf16[768,1024]{1,0:T(8,128)(2,1)S(1)} %get-tuple-element.56.S1, bf16[256,1024]{1,0:T(8,128)(2,1)S(1)} %get-tuple-element.63.S2, bf16[768,384]{1,0:T(8,128)(2,1)S(1)} %get-tuple-element.74.G1, bf16[256,384]{1,0:T(8,128)(2,1)S(1)} %get-tuple-element.75.G2, ...), custom_call_target="tpu_custom_call" | custom-call | flops 536870912 | tf_op jit(solution)/shard_map/near_clips/pallas_call | solution.py:28
  49.6 1.5 %collective-permute-start.22 = (bf16[128,1024]{1,0:T(8,128)(2,1)S(1)}, bf16[128,1024]{1,0:T(8,128)(2,1)S(1)}, u32[]{:S(2)}, u32[]{:S(2)}) collective-permute-start(bf16[128,1024]{1,0:T(8,128)(2,1)S(1)} %get-tuple-element.78), channel_id=1, source_target_pairs={{0,8},{8,0},{16,24},{24,16},{1,9},{9,1},{17,25},{25,17},{2,10},{10... | collective-permute-start | bytes 786440 | tf_op jit(solution)/shard_map/ppermute | solution.py:110
  51.1 1.1 %finish_captions.1 = f32[128,1024]{1,0:T(8,128)} custom-call(f32[2,128]{1,0:T(2,128)S(1)} %consts.1.refs_1_, f32[128,1024]{1,0:T(8,128)S(1)} %get-tuple-element.81.hat_ref, f32[128,1]{1,0:T(8,128)S(1)} %get-tuple-element.82.inverse_ref, f32[128,1024]{1,0:T(8,128)S(1)} %get-tuple-element.83.refs_0_, bf16[128,1024]{1,0:T(8,128)(2,1)S(1)} %collective-permute-done.24.refs_1_, ...), custom_call_target="tpu_custom_call" | custom-call | tf_op jit(solution)/shard_map/finish_captions/pallas_call | solution.py:28
  52.2 3.4 %collective-permute-done.23.refs_0_ = bf16[128,1024]{1,0:T(8,128)(2,1)S(1)} collective-permute-done((bf16[128,1024]{1,0:T(8,128)(2,1)S(1)}, bf16[128,1024]{1,0:T(8,128)(2,1)S(1)}, u32[]{:S(2)}, u32[]{:S(2)}) %collective-permute-start.23) | collective-permute-done | bytes 262176 | tf_op jit(solution)/shard_map/ppermute | solution.py:110
  55.6 0.7 %collective-permute-done.22.refs_4_ = bf16[128,1024]{1,0:T(8,128)(2,1)S(1)} collective-permute-done((bf16[128,1024]{1,0:T(8,128)(2,1)S(1)}, bf16[128,1024]{1,0:T(8,128)(2,1)S(1)}, u32[]{:S(2)}, u32[]{:S(2)}) %collective-permute-start.22) | collective-permute-done | bytes 262176 | tf_op jit(solution)/shard_map/ppermute | solution.py:110
  56.2 1.1 %finish_clips.1 = (f32[128,1024]{1,0:T(8,128)}, f32[1,128]{1,0:T(1,128)}) custom-call(f32[2,128]{1,0:T(2,128)S(1)} %consts.1.refs_1_, f32[128,1024]{1,0:T(8,128)S(1)} %get-tuple-element.44.hat_ref, f32[128,1]{1,0:T(8,128)S(1)} %get-tuple-element.45.inverse_ref, f32[1,128]{1,0:T(1,128)S(1)} %get-tuple-element.71.refs_0_, ...), custom_call_target="tpu_custom_call" | custom-call | tf_op jit(solution)/shard_map/finish_clips/pallas_call | solution.py:28
  (52 shorter events, 4.1 us)
Async XLA Ops:
  2.2 13.1 %collective-permute-start.2 = (bf16[128,1024]{1,0:T(8,128)(2,1)S(1)}, bf16[128,1024]{1,0:T(8,128)(2,1)S(1)}, u32[]{:S(2)}, u32[]{:S(2)}) collective-permute-start(bf16[128,1024]{1,0:T(8,128)(2,1)S(1)} %get-tuple-element.47.v16), channel_id=1, source_target_pairs={{0,2},{1,3},{2,0},{3,1},{4,6},{5,7},{6,4},{7,5},{8,10},{9,11},{10,... | collective-permute-start | bytes 786440 | tf_op jit(solution)/shard_map/ppermute | solution.py:110
  5.3 12.9 %collective-permute-start.8 = (bf16[128,1024]{1,0:T(8,128)(2,1)S(1)}, bf16[128,1024]{1,0:T(8,128)(2,1)S(1)}, u32[]{:S(2)}, u32[]{:S(2)}) collective-permute-start(bf16[128,1024]{1,0:T(8,128)(2,1)S(1)} %get-tuple-element.52), channel_id=1, source_target_pairs={{0,16},{8,24},{16,0},{24,8},{1,17},{9,25},{17,1},{25,9},{2,18},{10... | collective-permute-start | bytes 786440 | tf_op jit(solution)/shard_map/ppermute | solution.py:110
  6.9 11.3 %collective-permute-start.7 = (bf16[64,1024]{1,0:T(8,128)(2,1)S(1)}, bf16[64,1024]{1,0:T(8,128)(2,1)S(1)}, u32[]{:S(2)}, u32[]{:S(2)}) collective-permute-start(bf16[64,1024]{1,0:T(8,128)(2,1)S(1)} %get-tuple-element.51), channel_id=1, source_target_pairs={{0,4},{1,5},{2,6},{3,7},{4,0},{5,1},{6,2},{7,3},{8,12},{9,13},{10,... | collective-permute-start | bytes 393224 | tf_op jit(solution)/shard_map/ppermute | solution.py:110
  9.5 7.2 %collective-permute-start.1 = (bf16[128,1024]{1,0:T(8,128)(2,1)S(1)}, bf16[128,1024]{1,0:T(8,128)(2,1)S(1)}, u32[]{:S(2)}, u32[]{:S(2)}) collective-permute-start(bf16[128,1024]{1,0:T(8,128)(2,1)S(1)} %get-tuple-element.50), channel_id=1, source_target_pairs={{0,8},{8,0},{16,24},{24,16},{1,9},{9,1},{17,25},{25,17},{2,10},{10... | collective-permute-start | bytes 786440 | tf_op jit(solution)/shard_map/ppermute | solution.py:110
  11.0 10.3 %collective-permute-start.10 = (bf16[64,1024]{1,0:T(8,128)(2,1)S(1)}, bf16[64,1024]{1,0:T(8,128)(2,1)S(1)}, u32[]{:S(2)}, u32[]{:S(2)}) collective-permute-start(bf16[64,1024]{1,0:T(8,128)(2,1)S(1)} %get-tuple-element.54), channel_id=1, source_target_pairs={{0,4},{1,5},{2,6},{3,7},{4,0},{5,1},{6,2},{7,3},{8,12},{9,13},{10,... | collective-permute-start | bytes 393224 | tf_op jit(solution)/shard_map/ppermute | solution.py:110
  16.7 6.7 %collective-permute-start.3 = (bf16[128,1024]{1,0:T(8,128)(2,1)S(1)}, bf16[128,1024]{1,0:T(8,128)(2,1)S(1)}, u32[]{:S(2)}, u32[]{:S(2)}) collective-permute-start(bf16[128,1024]{1,0:T(8,128)(2,1)S(1)} %clips_zx.1.vz), channel_id=1, source_target_pairs={{0,8},{8,0},{16,24},{24,16},{1,9},{9,1},{17,25},{25,17},{2,10},{10... | collective-permute-start | bytes 786440 | tf_op jit(solution)/shard_map/ppermute | solution.py:110
  18.2 5.2 %collective-permute-start.9 = (bf16[64,1024]{1,0:T(8,128)(2,1)S(1)}, bf16[64,1024]{1,0:T(8,128)(2,1)S(1)}, u32[]{:S(2)}, u32[]{:S(2)}) collective-permute-start(bf16[64,1024]{1,0:T(8,128)(2,1)S(1)} %captions_zy.1.refs_0_.refs_2_), channel_id=1, source_target_pairs={{0,16},{8,24},{16,0},{24,8},{1,17},{9,25},{17,1},{25,9},{2,18},{10... | collective-permute-start | bytes 393224 | tf_op jit(solution)/shard_map/ppermute | solution.py:110
  19.7 4.3 %collective-permute-start = (bf16[256,1024]{1,0:T(8,128)(2,1)S(1)}, bf16[256,1024]{1,0:T(8,128)(2,1)S(1)}, u32[]{:S(2)}, u32[]{:S(2)}) collective-permute-start(bf16[256,1024]{1,0:T(8,128)(2,1)S(1)} %get-tuple-element.49.both), channel_id=1, source_target_pairs={{0,1},{1,0},{2,3},{3,2},{4,5},{5,4},{6,7},{7,6},{8,9},{9,8},{10,11... | collective-permute-start | bytes 1572872 | tf_op jit(solution)/shard_map/ppermute | solution.py:110
  21.3 5.6 %collective-permute-start.11 = (bf16[64,1024]{1,0:T(8,128)(2,1)S(1)}, bf16[64,1024]{1,0:T(8,128)(2,1)S(1)}, u32[]{:S(2)}, u32[]{:S(2)}) collective-permute-start(bf16[64,1024]{1,0:T(8,128)(2,1)S(1)} %collective-permute-done.10.refs_0_), channel_id=1, source_target_pairs={{0,16},{8,24},{16,0},{24,8},{1,17},{9,25},{17,1},{25,9},{2,18},{10... | collective-permute-start | bytes 393224 | tf_op jit(solution)/shard_map/ppermute | solution.py:110
  22.1 1.9 %collective-permute-start.5 = (bf16[128,1024]{1,0:T(8,128)(2,1)S(1)}, bf16[128,1024]{1,0:T(8,128)(2,1)S(1)}, u32[]{:S(2)}, u32[]{:S(2)}) collective-permute-start(bf16[128,1024]{1,0:T(8,128)(2,1)S(1)} %clips_zx.1.vz), channel_id=1, source_target_pairs={{0,1},{1,0},{2,3},{3,2},{4,5},{5,4},{6,7},{7,6},{8,9},{9,8},{10,11... | collective-permute-start | bytes 786440 | tf_op jit(solution)/shard_map/ppermute | solution.py:110
  23.5 1.5 %collective-permute-start.4 = (bf16[128,1024]{1,0:T(8,128)(2,1)S(1)}, bf16[128,1024]{1,0:T(8,128)(2,1)S(1)}, u32[]{:S(2)}, u32[]{:S(2)}) collective-permute-start(bf16[128,1024]{1,0:T(8,128)(2,1)S(1)} %collective-permute-done.1.refs_1_.vx), channel_id=1, source_target_pairs={{0,1},{1,0},{2,3},{3,2},{4,5},{5,4},{6,7},{7,6},{8,9},{9,8},{10,11... | collective-permute-start | bytes 786440 | tf_op jit(solution)/shard_map/ppermute | solution.py:110
  23.5 1.9 %collective-permute-start.6 = (bf16[128,1024]{1,0:T(8,128)(2,1)S(1)}, bf16[128,1024]{1,0:T(8,128)(2,1)S(1)}, u32[]{:S(2)}, u32[]{:S(2)}) collective-permute-start(bf16[128,1024]{1,0:T(8,128)(2,1)S(1)} %collective-permute-done.3.vd), channel_id=1, source_target_pairs={{0,1},{1,0},{2,3},{3,2},{4,5},{5,4},{6,7},{7,6},{8,9},{9,8},{10,11... | collective-permute-start | bytes 786440 | tf_op jit(solution)/shard_map/ppermute | solution.py:110
  24.0 5.0 %collective-permute-start.13 = (bf16[64,1024]{1,0:T(8,128)(2,1)S(1)}, bf16[64,1024]{1,0:T(8,128)(2,1)S(1)}, u32[]{:S(2)}, u32[]{:S(2)}) collective-permute-start(bf16[64,1024]{1,0:T(8,128)(2,1)S(1)} %captions_zy.1.refs_0_.refs_2_), channel_id=1, source_target_pairs={{0,1},{1,0},{2,3},{3,2},{4,5},{5,4},{6,7},{7,6},{8,9},{9,8},{10,11... | collective-permute-start | bytes 393224 | tf_op jit(solution)/shard_map/ppermute | solution.py:110
  24.1 7.5 %collective-permute-start.12 = (bf16[128,1024]{1,0:T(8,128)(2,1)S(1)}, bf16[128,1024]{1,0:T(8,128)(2,1)S(1)}, u32[]{:S(2)}, u32[]{:S(2)}) collective-permute-start(bf16[128,1024]{1,0:T(8,128)(2,1)S(1)} %collective-permute-done.8.refs_2_.refs_0_), channel_id=1, source_target_pairs={{0,1},{1,0},{2,3},{3,2},{4,5},{5,4},{6,7},{7,6},{8,9},{9,8},{10,11... | collective-permute-start | bytes 786440 | tf_op jit(solution)/shard_map/ppermute | solution.py:110
  25.0 6.6 %collective-permute-start.14 = (bf16[64,1024]{1,0:T(8,128)(2,1)S(1)}, bf16[64,1024]{1,0:T(8,128)(2,1)S(1)}, u32[]{:S(2)}, u32[]{:S(2)}) collective-permute-start(bf16[64,1024]{1,0:T(8,128)(2,1)S(1)} %captions_da.1.refs_1_.refs_3_), channel_id=1, source_target_pairs={{0,1},{1,0},{2,3},{3,2},{4,5},{5,4},{6,7},{7,6},{8,9},{9,8},{10,11... | collective-permute-start | bytes 393224 | tf_op jit(solution)/shard_map/ppermute | solution.py:110
  27.0 5.5 %collective-permute-start.16 = (bf16[64,1024]{1,0:T(8,128)(2,1)S(1)}, bf16[64,1024]{1,0:T(8,128)(2,1)S(1)}, u32[]{:S(2)}, u32[]{:S(2)}) collective-permute-start(bf16[64,1024]{1,0:T(8,128)(2,1)S(1)} %captions_b.3.refs_1_), channel_id=1, source_target_pairs={{0,1},{1,0},{2,3},{3,2},{4,5},{5,4},{6,7},{7,6},{8,9},{9,8},{10,11... | collective-permute-start | bytes 393224 | tf_op jit(solution)/shard_map/ppermute | solution.py:110
  27.2 5.3 %collective-permute-start.15 = (bf16[64,1024]{1,0:T(8,128)(2,1)S(1)}, bf16[64,1024]{1,0:T(8,128)(2,1)S(1)}, u32[]{:S(2)}, u32[]{:S(2)}) collective-permute-start(bf16[64,1024]{1,0:T(8,128)(2,1)S(1)} %captions_b.2.refs_0_), channel_id=1, source_target_pairs={{0,1},{1,0},{2,3},{3,2},{4,5},{5,4},{6,7},{7,6},{8,9},{9,8},{10,11... | collective-permute-start | bytes 393224 | tf_op jit(solution)/shard_map/ppermute | solution.py:110
  29.0 6.8 %collective-permute-start.18 = (bf16[64,1024]{1,0:T(8,128)(2,1)S(1)}, bf16[64,1024]{1,0:T(8,128)(2,1)S(1)}, u32[]{:S(2)}, u32[]{:S(2)}) collective-permute-start(bf16[64,1024]{1,0:T(8,128)(2,1)S(1)} %get-tuple-element.67), channel_id=1, source_target_pairs={{0,16},{8,24},{16,0},{24,8},{1,17},{9,25},{17,1},{25,9},{2,18},{10... | collective-permute-start | bytes 393224 | tf_op jit(solution)/shard_map/ppermute | solution.py:110
  32.4 5.8 %collective-permute-start.17 = (bf16[64,1024]{1,0:T(8,128)(2,1)S(1)}, bf16[64,1024]{1,0:T(8,128)(2,1)S(1)}, u32[]{:S(2)}, u32[]{:S(2)}) collective-permute-start(bf16[64,1024]{1,0:T(8,128)(2,1)S(1)} %get-tuple-element.61), channel_id=1, source_target_pairs={{0,16},{8,24},{16,0},{24,8},{1,17},{9,25},{17,1},{25,9},{2,18},{10... | collective-permute-start | bytes 393224 | tf_op jit(solution)/shard_map/ppermute | solution.py:110
  33.3 15.4 %collective-permute-start.21 = (bf16[128,1024]{1,0:T(8,128)(2,1)S(1)}, bf16[128,1024]{1,0:T(8,128)(2,1)S(1)}, u32[]{:S(2)}, u32[]{:S(2)}) collective-permute-start(bf16[128,1024]{1,0:T(8,128)(2,1)S(1)} %get-tuple-element.59.refs_1_.dv_d), channel_id=1, source_target_pairs={{0,8},{8,0},{16,24},{24,16},{1,9},{9,1},{17,25},{25,17},{2,10},{10... | collective-permute-start | bytes 786440 | tf_op jit(solution)/shard_map/ppermute | solution.py:110
  35.8 13.8 %collective-permute-start.26 = (bf16[64,1024]{1,0:T(8,128)(2,1)S(1)}, bf16[64,1024]{1,0:T(8,128)(2,1)S(1)}, u32[]{:S(2)}, u32[]{:S(2)}) collective-permute-start(bf16[64,1024]{1,0:T(8,128)(2,1)S(1)} %add_b.1.refs_0_), channel_id=1, source_target_pairs={{0,4},{1,5},{2,6},{3,7},{4,0},{5,1},{6,2},{7,3},{8,12},{9,13},{10,... | collective-permute-start | bytes 393224 | tf_op jit(solution)/shard_map/ppermute | solution.py:110
  42.1 3.6 %collective-permute-start.19 = (f32[2,128]{1,0:T(2,128)S(1)}, f32[2,128]{1,0:T(2,128)S(1)}, u32[]{:S(2)}, u32[]{:S(2)}) collective-permute-start(f32[2,128]{1,0:T(2,128)S(1)} %get-tuple-element.72), channel_id=1, source_target_pairs={{0,8},{8,0},{16,24},{24,16},{1,9},{9,1},{17,25},{25,17},{2,10},{10... | collective-permute-start | bytes 3080 | tf_op jit(solution)/shard_map/ppermute | solution.py:110
  42.7 8.4 %collective-permute-start.25 = (bf16[64,1024]{1,0:T(8,128)(2,1)S(1)}, bf16[64,1024]{1,0:T(8,128)(2,1)S(1)}, u32[]{:S(2)}, u32[]{:S(2)}) collective-permute-start(bf16[64,1024]{1,0:T(8,128)(2,1)S(1)} %add_a.1.refs_0_), channel_id=1, source_target_pairs={{0,4},{1,5},{2,6},{3,7},{4,0},{5,1},{6,2},{7,3},{8,12},{9,13},{10,... | collective-permute-start | bytes 393224 | tf_op jit(solution)/shard_map/ppermute | solution.py:110
  43.8 7.2 %collective-permute-start.24 = (bf16[128,1024]{1,0:T(8,128)(2,1)S(1)}, bf16[128,1024]{1,0:T(8,128)(2,1)S(1)}, u32[]{:S(2)}, u32[]{:S(2)}) collective-permute-start(bf16[128,1024]{1,0:T(8,128)(2,1)S(1)} %get-tuple-element.84), channel_id=1, source_target_pairs={{0,16},{8,24},{16,0},{24,8},{1,17},{9,25},{17,1},{25,9},{2,18},{10... | collective-permute-start | bytes 786440 | tf_op jit(solution)/shard_map/ppermute | solution.py:110
  45.8 9.8 %collective-permute-start.20 = (f32[1,128]{1,0:T(1,128)S(1)}, f32[1,128]{1,0:T(1,128)S(1)}, u32[]{:S(2)}, u32[]{:S(2)}) collective-permute-start(f32[1,128]{1,0:T(1,128)S(1)} %add_loss.1.sum_loss), channel_id=1, source_target_pairs={{0,2},{1,3},{2,0},{3,1},{4,6},{5,7},{6,4},{7,5},{8,10},{9,11},{10,... | collective-permute-start | bytes 1544 | tf_op jit(solution)/shard_map/ppermute | solution.py:110
  48.8 6.8 %collective-permute-start.23 = (bf16[128,1024]{1,0:T(8,128)(2,1)S(1)}, bf16[128,1024]{1,0:T(8,128)(2,1)S(1)}, u32[]{:S(2)}, u32[]{:S(2)}) collective-permute-start(bf16[128,1024]{1,0:T(8,128)(2,1)S(1)} %add_clips.1.sum_v.refs_1_), channel_id=1, source_target_pairs={{0,2},{1,3},{2,0},{3,1},{4,6},{5,7},{6,4},{7,5},{8,10},{9,11},{10,... | collective-permute-start | bytes 786440 | tf_op jit(solution)/shard_map/ppermute | solution.py:110
  49.6 6.6 %collective-permute-start.22 = (bf16[128,1024]{1,0:T(8,128)(2,1)S(1)}, bf16[128,1024]{1,0:T(8,128)(2,1)S(1)}, u32[]{:S(2)}, u32[]{:S(2)}) collective-permute-start(bf16[128,1024]{1,0:T(8,128)(2,1)S(1)} %get-tuple-element.78), channel_id=1, source_target_pairs={{0,8},{8,0},{16,24},{24,16},{1,9},{9,1},{17,25},{25,17},{2,10},{10... | collective-permute-start | bytes 786440 | tf_op jit(solution)/shard_map/ppermute | solution.py:110

commit v4 on v3

--- a/solution.py
+++ b/solution.py
@@ -147,7 +147,7 @@
             target[pl.ds(first + at, coef.shape[0]), :] = coef
         return put
 
-    def normalize_kernel(film, text, matched, v16, c16, ca, vhat, chat, vinv, cinv, labels, fbuf, tbuf, mbuf, sems):
+    def normalize_kernel(film, text, matched, v16, c16, va, vb, ca, cb, vhat, chat, vinv, cinv, labels, fbuf, tbuf, mbuf, sems):
         step = rows // PARTS
         get_matched = pltpu.make_async_copy(matched, mbuf, sems.at[2 * PARTS])
         copies = []
@@ -162,20 +162,23 @@
             copy.wait()
         hat, inverse = unit_rows(fbuf[...])
         vhat[...], vinv[...], v16[...] = hat, inverse, hat.astype(BF16)
+        va[...] = hat[:half].astype(BF16)
+        vb[...] = hat[half:].astype(BF16)
         for copy in copies[PARTS:]:
             copy.wait()
         hat, inverse = unit_rows(tbuf[...])
         chat[...], cinv[...], c16[...] = hat, inverse, hat.astype(BF16)
         ca[...] = hat[:half].astype(BF16)
+        cb[...] = hat[half:].astype(BF16)
         get_matched.wait()
         labels[...] = jnp.concatenate(
             [mbuf[pl.ds(clip_index(*p), 1), :] for p in clip_order], axis=1
         )
 
     matched = matched.reshape(-1, rows)
-    v16, c16, ca, vhat, chat, vinv, cinv, labels = call(
+    v16, c16, va, vb, ca, cb, vhat, chat, vinv, cinv, labels = call(
         "normalize", normalize_kernel,
-        [vm(mat), vm(mat), vm(hmat), vm(mat, F32), vm(mat, F32), vm((rows, 1), F32), vm((rows, 1), F32),
+        [vm(mat), vm(mat)] + [vm(hmat)] * 4 + [vm(mat, F32), vm(mat, F32), vm((rows, 1), F32), vm((rows, 1), F32),
          vm((1, 8 * rows), jnp.int32)],
         [film, text, matched], spec="h", limit=8,
         scratch=[pltpu.VMEM(mat, F32)] * 2
@@ -188,44 +191,36 @@
 
     (consts,) = call("consts", consts_kernel, [vm((2, 128), F32)], [sharpness, offset], spec="s")
 
-    def copies_kernel(v16, c16, v_out, c_out, cb, both):
-        v_out[...] = v16[...]
-        c_out[...] = c16[...]
-        cb[...] = c16[half:, :]
-        both[:rows, :] = c16[...]
-        both[rows:, :] = v16[...]
-
-    v_z = hand_on("clips_z", swap(v16, "col", 2), flops=LONG)
-    c_za = [hand_on("captions_za", swap(ca, "col", 4 * s), flops=LONG) for s in range(1, Z)]
-    v16b, c16b, cb, both = call(
-        "copies", copies_kernel, [vm(mat), vm(mat), vm(hmat), vm((2 * rows, width))], [v16, c16]
-    )
-    c_y = [swap(c16b, "row", 2 * t) for t in range(1, Y)]
-    v_x = swap(v16b, "row", 1)
-    c_za = [hand_on("captions_zy", b, consts, *c_y) for b in c_za]
-    v_z = hand_on("clips_zx", v_z, v_x)
-    c_zb = [swap(cb, "col", 4 * s) for s in range(1, Z)]
-    both_k = swap(both, "col", 1)
-    v_d = swap(v_z, "row", 1)
+    def join(name, *blocks):
+        def join_kernel(*refs):
+            stack(refs[-1], refs[:-1])
+
+        return call(name, join_kernel, [vm((sum(b.shape[0] for b in blocks), width))], blocks)[0]
+
+    v_z = [hand_on("clips_z", swap(b, "col", 2), flops=LONG) for b in (va, vb)]
+    c_za = [hand_on("captions_za", swap(ca, "col", 4 * s), consts, flops=LONG) for s in range(1, Z)]
+    cb = hand_on("captions_hb", cb, v_z[0])
+    c_zb = [hand_on("captions_zb", swap(cb, "col", 4 * s), flops=LONG) for s in range(1, Z)]
+    c_y = [swap(c16, "row", 2 * t) for t in range(1, Y)]
+    v_x = swap(v16, "row", 1)
+    v_d = [swap(b, "row", 1) for b in v_z]
     c_da = [hand_on("captions_da", swap(b, "row", 2 * t), flops=LONG) for b in c_za for t in range(1, Y)]
     c_db = [swap(b, "row", 2 * t) for b in c_zb for t in range(1, Y)]
-    cy_k = [swap(b, "col", 1) for b in c_y]
-    vx_k = swap(v_x, "col", 1)
-    vz_k = swap(v_z, "col", 1)
+    N = join("near_blocks", c16, *c_y, v16, v_x, *v_z)
+    N_k = swap(N, "col", 1)
+    v_d = join("diagonal_block", *v_d)
     vd_k = swap(v_d, "col", 1)
-    c_h = [c_za + c_da]
-    ch_k = [[swap(b, "col", 1) for b in c_h[0]]]
-
-    def stack_kernel(both, both_k, vx, vz, vd, vxk, vzk, vdk, VV):
-        stack(VV, [both.at[rows:], vx, vz, vd, both_k.at[rows:], vxk, vzk, vdk])
-
-    (VV,) = call("clips", stack_kernel, [vm((8 * n1, width))], [both, both_k, v_x, v_z, v_d, vx_k, vz_k, vd_k])
+    H = [join("half_a_blocks", *c_za, *c_da)]
+    H_k = [swap(H[0], "col", 1)]
+
+    def clips_kernel(N, N_k, vd, vdk, VV):
+        stack(VV, [N.at[nn:], vd, N_k.at[nn:], vdk])
+
+    (VV,) = call("clips", clips_kernel, [vm((8 * n1, width))], [N, N_k, v_d, vd_k])
 
     def half_sums(h):
-        def half_kernel(consts, labels, VV, *refs):
-            n = len(c_h[h])
-            caps, (loss, p, *sums, H, coef) = refs[:n], refs[n:]
-            stack(H, caps)
+        def half_kernel(consts, labels, VV, H, loss, p, *refs):
+            sums, coef = refs[:-1], refs[-1]
             loss[...] = strip(consts, half_pieces(0, h), H[...], VV[...], labels[...], n4, put_in(coef))
             p[...] = coef[:, :n4]
             for i in range(width // CHUNK):
@@ -237,20 +232,16 @@
         loss, p, *sums = call(
             "half_" + "ab"[h], half_kernel,
             [vm((1, n4), F32), vm((nh, n4))] + [vm(hmat, F32)] * len(up) + [vm(hmat)] * len(diag),
-            [consts, labels, VV, *c_h[h]],
+            [consts, labels, VV, H[h]],
             flops=2 * 16 * rows * rows * width, limit=limit,
-            scratch=[pltpu.VMEM((nh, width), BF16), pltpu.VMEM((nh, 8 * n1), BF16)],
+            scratch=[pltpu.VMEM((nh, 8 * n1), BF16)],
         )
         return loss, p, sums[: len(up)], sums[len(up) :]
 
     loss_a, p_a, dcz_a, dcd_a = half_sums(0)
 
-    def diagonal_kernel(consts, labels, both, both_k, vd, *refs):
-        n = len(near) - 1
-        m = len(c_h[0])
-        cy, cyk, c_a, c_ak = refs[:n], refs[n : 2 * n], refs[2 * n : 2 * n + m], refs[2 * n + m : 2 * n + 2 * m]
-        S1, g, loss = refs[2 * n + 2 * m :]
-        stack(S1, [both.at[:rows], *cy, *c_a, both_k.at[:rows], *cyk, *c_ak])
+    def diagonal_kernel(consts, labels, N, N_k, vd, H, H_k, after, S1, g, loss):
+        stack(S1, [N.at[:nn], H, N_k.at[:nn], H_k])
         m = nn + nh
         late = labels[:, n3:n4]
         strip(consts, near_pieces(0) + half_pieces(0, 0), S1[:m, :], vd[...], late, 0, put_in(g))
@@ -261,18 +252,17 @@
     S1, g1, loss_d1 = call(
         "diagonal_clips", diagonal_kernel,
         [vm((2 * (nn + nh), width)), vm((2 * (nn + nh), n1)), vm((1, n1), F32)],
-        [consts, labels, both, both_k, v_d, *c_y, *cy_k, *c_h[0], *ch_k[0]],
+        [consts, labels, N, N_k, v_d, H[0], H_k[0], loss_a],
         flops=2 * 6 * rows * rows * width, limit=limit,
     )
 
-    c_h.append([hand_on("captions_b", b, loss_a, flops=LONG // 3) for b in c_zb + c_db])
-    ch_k.append([swap(b, "col", 1) for b in c_h[1]])
+    c_db = [hand_on("captions_db", b, loss_d1, flops=LONG) for b in c_db]
+    H.append(join("half_b_blocks", *c_zb, *c_db))
+    H_k.append(swap(H[1], "col", 1))
     loss_b, p_b, dcz_b, dcd_b = half_sums(1)
 
-    def far_clips_kernel(consts, labels, vd, S1, g1, p_b, *refs):
-        m = len(c_h[1])
-        caps, (S2, loss, dv, g2) = refs[: 2 * m], refs[2 * m :]
-        stack(S2, caps)
+    def far_clips_kernel(consts, labels, vd, S1, g1, p_b, H, H_k, S2, loss, dv, g2):
+        stack(S2, [H, H_k])
         g2[:nh, :] = p_b[:, n3:]
         loss[...] = strip(
             consts, half_pieces(1, 1), S2[nh:, :], vd[...], labels[:, n3:n4], n1, put_in(g2, nh)
@@ -284,7 +274,7 @@
     S2, loss_d2, dv_d = call(
         "far_clips", far_clips_kernel,
         [vm((2 * nh, width)), vm((1, n1), F32), vm(mat)],
-        [consts, labels, v_d, S1, g1, p_b, *c_h[1], *ch_k[1]],
+        [consts, labels, v_d, S1, g1, p_b, H[1], H_k[1]],
         flops=2 * 9 * rows * rows * width, limit=limit,
         scratch=[pltpu.VMEM((2 * nh, n1), BF16)],
     )
@@ -300,22 +290,23 @@
     def add(name, *terms):
         return call(name, add_kernel, [vm(terms[0].shape)], terms)[0]
 
-    def captions_back(h, dcz, dcd):
+    def captions_back(h, dcz, dcd, after):
         far = [
             [
-                hand_on("far_" + "ab"[h], swap(dcd[s * (Y - 1) + t - 1], "row", 2 * t), dv_d, flops=LONG)
+                hand_on("far_" + "ab"[h], swap(dcd[s * (Y - 1) + t - 1], "row", 2 * t), after, flops=LONG)
                 for t in range(1, Y)
             ]
             for s in range(Z - 1)
         ]
+        far = [[hand_on("far_" + "ab"[h], b, dv_d) for b in group] for group in far]
         sums = [add("add_" + "ab"[h], dcz[s], *far[s]) for s in range(Z - 1)]
         return sums, [swap(sums[s], "col", 4 * (s + 1)) for s in range(Z - 1)]
 
-    sums_a, got_a = captions_back(0, dcz_a, dcd_a)
-    sums_b, got_b = captions_back(1, dcz_b, dcd_b)
+    sums_a, got_a = captions_back(0, dcz_a, dcd_a, loss_b)
+    sums_b, got_b = captions_back(1, dcz_b, dcd_b, sums_a[0])
 
     def near_captions_kernel(consts, labels, VV, S1, dv_d, *refs):
-        loss, p, *sums, coef = refs[Z - 1 :]
+        loss, p, *sums, coef = refs[2 * (Z - 1) :]
         loss[...] = strip(consts, near_pieces(0), S1[:nn, :], VV[...], labels[...], n4, put_in(coef))
         p[...] = coef[:, :n3]
         for i in range(width // CHUNK):
@@ -327,13 +318,13 @@
     loss_n, p_n, dc0, *dcy = call(
         "near_captions", near_captions_kernel,
         [vm((1, n4), F32), vm((nn, n3)), vm(mat, F32)] + [vm(mat)] * (Y - 1),
-        [consts, labels, VV, S1, dv_d, *sums_a],
+        [consts, labels, VV, S1, dv_d, *sums_a, *sums_b],
         flops=2 * 32 * rows * rows * width, limit=limit,
         scratch=[pltpu.VMEM((nn, 8 * n1), BF16)],
     )
 
     def z_clips_kernel(consts, labels, VV, S1, S2, p_n, p_a, p_b, *refs):
-        loss, G1, G2, dv = refs[Z - 1 :]
+        loss, G1, G2, dv = refs
         m = nn + nh
         G1[:nn, :] = p_n[...]
         G1[nn:m, :] = p_a[:, :n3]
@@ -349,16 +340,16 @@
     loss_k, G1, G2, dvz = call(
         "z_clips", z_clips_kernel,
         [vm((1, n3), F32), vm((2 * (nn + nh), n3)), vm((2 * nh, n3)), vm(mat, F32)],
-        [consts, labels, VV, S1, S2, p_n, p_a, p_b, *sums_b],
+        [consts, labels, VV, S1, S2, p_n, p_a, p_b],
         flops=2 * 20 * rows * rows * width, limit=limit,
     )
 
     sum_v = add("add_clips", dvz, far_v)
-    got_z = hand_on("clips_back", swap(sum_v, "col", 2), flops=LONG)
-    got_h = [[hand_on("captions_back", b, sum_v, flops=LONG) for b in got] for got in (got_a, got_b)]
-    got_y = [swap(dcy[t - 1], "row", 2 * t) for t in range(1, Y)]
-
-    def losses_kernel(l_a, l_b, l_n, l_k, l_d1, l_d2, loss_0, loss_x, loss_z):
+    got_z = hand_on("clips_back", swap(sum_v, "col", 2), flops=3 * LONG)
+    got_h = [[hand_on("captions_back", b, sum_v, flops=3 * LONG) for b in got] for got in (got_a, got_b)]
+    got_y = [hand_on("captions_y", swap(dcy[t - 1], "row", 2 * t), sum_v, flops=LONG) for t in range(1, Y)]
+
+    def losses_kernel(l_a, l_b, l_n, l_k, l_d1, l_d2, got, sum_v, loss_0, loss_x, loss_z):
         total = l_a[...] + l_b[...] + l_n[...]
         own = total[:, :n3] + l_k[...]
         loss_0[...] = own[:, :n1]
@@ -371,13 +362,13 @@
 
     loss_0, loss_x, loss_z = call(
         "losses", losses_kernel, [vm((1, n1), F32), vm((2, n1), F32), vm((1, n1), F32)],
-        [loss_a, loss_b, loss_n, loss_k, loss_d1, loss_d2],
+        [loss_a, loss_b, loss_n, loss_k, loss_d1, loss_d2, got_a[0], sum_v],
     )
     far_loss = swap(loss_x, "row", 1)
     (sum_loss,) = call("add_loss", add_loss_kernel, [vm((1, n1), F32)], [loss_z, far_loss])
     got_loss = swap(sum_loss, "col", 2)
 
-    def near_clips_kernel(S1, S2, G1, G2, sum_v, sum_loss, dv0, dvx):
+    def near_clips_kernel(S1, S2, G1, G2, dv0, dvx):
         for i in range(width // CHUNK):
             cols = pl.ds(i * CHUNK, CHUNK)
             part = dot_tn(G1[:, : 2 * n1], S1[:, cols]) + dot_tn(G2[:, : 2 * n1], S2[:, cols])
@@ -386,16 +377,16 @@
 
     dv0, dvx = call(
         "near_clips", near_clips_kernel, [vm(mat, F32), vm(mat)],
-        [S1, S2, G1, G2, sum_v, sum_loss],
+        [S1, S2, G1, G2],
         flops=2 * 16 * rows * rows * width, limit=limit,
     )
-    got_x = swap(dvx, "row", 1)
-
-    def finish(name, losses, consts, hat, inverse, own, whole, halves):
+    got_x = hand_on("clips_x", swap(dvx, "row", 1), sum_v, flops=LONG)
+
+    def finish(name, losses, consts, hat, inverse, own, whole, halves, *after):
         tail = 2 + 2 * bool(losses)
 
         def finish_kernel(consts, hat_ref, inverse_ref, *refs):
-            adds, (grad, *loss, buf, sems) = refs[: -1 - tail], refs[-1 - tail :]
+            adds, (grad, *loss, buf, sems) = refs[: -1 - tail - len(after)], refs[-1 - tail :]
             copies = []
             if losses:
                 out, lbuf = loss
@@ -423,12 +414,12 @@
         return call(
             name, finish_kernel,
             [jax.ShapeDtypeStruct(mat, F32)] + [jax.ShapeDtypeStruct((1, rows), F32)] * bool(losses),
-            [consts, hat, inverse, *losses, own, *whole, *halves[0], *halves[1]], out_spec="h",
+            [consts, hat, inverse, *losses, own, *whole, *halves[0], *halves[1], *after], out_spec="h",
             scratch=[pltpu.VMEM((1, rows), F32)] * bool(losses)
             + [pltpu.VMEM(mat, F32), pltpu.SemaphoreType.DMA((3,))],
         )
 
-    (gc,) = finish("finish_captions", [], consts, chat, cinv, dc0, got_y, got_h)
+    (gc,) = finish("finish_captions", [], consts, chat, cinv, dc0, got_y, got_h, sum_loss)
     gv, clip_loss = finish(
         "finish_clips", [loss_0, far_loss, got_loss], consts, vhat, vinv, dv0, [got_x, got_z], ([], [])
     )

time: 57.5 us -> 56.5 us (0.983)
  waiting for transfers between devices: 15.5 us -> 11.9 us
  starting transfers between devices: 26.6 us -> 29.1 us
    ppermute x27 -> x24, waiting for transfers between devices: 15.5 us -> 11.9 us  [swap(): return lax.ppermute(value, axis, [(i, i ^ bits) for i in range(size)])]
    ppermute x27 -> x24, starting transfers between devices: 26.6 us -> 29.1 us  [swap(): return lax.ppermute(value, axis, [(i, i ^ bits) for i in range(size)])]
    pallas_call x30 -> x37, Pallas kernels: 13.1 us -> 13.2 us  [call(): pl.pallas_call(kernel, name=name, out_shape=out_shape, in_specs=[SPECS[sp...]
  transfers between devices with their start and end apart: 27 -> 24, of which waited for: 11 -> 10; matrix products, arithmetic and copies ran while one was open for 0% -> 0% of each run, Pallas kernels for 18% -> 19%
where the time goes in v4:
time: 56.5 us; the launch traced here: 56.4 us
  starting transfers between devices  29.1 us (52%)
  Pallas kernels  13.2 us (23%)
  waiting for transfers between devices  11.9 us (21%)
  between operations  2.15 us (4%)
    ppermute x24, starting transfers between devices, swap(): return lax.ppermute(value, axis, [(i, i ^ bits) for i in range(size)])  29.1 us
    pallas_call x37, Pallas kernels, call(): pl.pallas_call(kernel, name=name, out_shape=out_shape, in_specs=[SPECS[sp...  13.2 us
    ppermute x24, waiting for transfers between devices, swap(): return lax.ppermute(value, axis, [(i, i ^ bits) for i in range(size)])  11.9 us
  transfers between devices with their start and end apart: 24, of which 10 were waited for; matrix products, arithmetic and copies ran while one was open for 0% of the time, Pallas kernels for 19%

profile of v4, /device:TPU:0, one launch (start us, length us, event | category | flops | bytes accessed | tf_op | source)
XLA Modules:
  0.0 56.4 jit_solution(9329649065133304197)
XLA Ops:
  0.6 1.5 %normalize.1 = (bf16[128,1024]{1,0:T(8,128)(2,1)S(1)}, bf16[128,1024]{1,0:T(8,128)(2,1)S(1)}, bf16[64,1024]{1,0:T(8,128)(2,1)S(1)}, bf16[64,1024]{1,0:T(8,128)(2...) custom-call(f32[128,1024]{1,0:T(8,128)} %film.1, ...), custom_call_target="tpu_custom_call" | custom-call | tf_op jit(solution)/shard_map/normalize/pallas_call | solution.py:28
  2.2 3.1 %collective-permute-start.2 = (bf16[64,1024]{1,0:T(8,128)(2,1)S(1)}, bf16[64,1024]{1,0:T(8,128)(2,1)S(1)}, u32[]{:S(2)}, u32[]{:S(2)}) collective-permute-start(bf16[64,1024]{1,0:T(8,128)(2,1)S(1)} %get-tuple-element.48), channel_id=1, source_target_pairs={{0,2},{1,3},{2,0},{3,1},{4,6},{5,7},{6,4},{7,5},{8,10},{9,11},{10,... | collective-permute-start | bytes 393224 | tf_op jit(solution)/shard_map/ppermute | solution.py:110
  5.3 3.0 %collective-permute-start.8 = (bf16[64,1024]{1,0:T(8,128)(2,1)S(1)}, bf16[64,1024]{1,0:T(8,128)(2,1)S(1)}, u32[]{:S(2)}, u32[]{:S(2)}) collective-permute-start(bf16[64,1024]{1,0:T(8,128)(2,1)S(1)} %get-tuple-element.50), channel_id=1, source_target_pairs={{0,4},{1,5},{2,6},{3,7},{4,0},{5,1},{6,2},{7,3},{8,12},{9,13},{10,... | collective-permute-start | bytes 393224 | tf_op jit(solution)/shard_map/ppermute | solution.py:110
  8.3 1.5 %collective-permute-start = (bf16[128,1024]{1,0:T(8,128)(2,1)S(1)}, bf16[128,1024]{1,0:T(8,128)(2,1)S(1)}, u32[]{:S(2)}, u32[]{:S(2)}) collective-permute-start(bf16[128,1024]{1,0:T(8,128)(2,1)S(1)} %get-tuple-element.46.refs_0_), channel_id=1, source_target_pairs={{0,16},{8,24},{16,0},{24,8},{1,17},{9,25},{17,1},{25,9},{2,18},{10... | collective-permute-start | bytes 786440 | tf_op jit(solution)/shard_map/ppermute | solution.py:110
  9.8 1.5 %collective-permute-start.1 = (bf16[128,1024]{1,0:T(8,128)(2,1)S(1)}, bf16[128,1024]{1,0:T(8,128)(2,1)S(1)}, u32[]{:S(2)}, u32[]{:S(2)}) collective-permute-start(bf16[128,1024]{1,0:T(8,128)(2,1)S(1)} %get-tuple-element.47.refs_2_), channel_id=1, source_target_pairs={{0,8},{8,0},{16,24},{24,16},{1,9},{9,1},{17,25},{25,17},{2,10},{10... | collective-permute-start | bytes 786440 | tf_op jit(solution)/shard_map/ppermute | solution.py:110
  12.7 1.7 %collective-permute-start.5 = (bf16[64,1024]{1,0:T(8,128)(2,1)S(1)}, bf16[64,1024]{1,0:T(8,128)(2,1)S(1)}, u32[]{:S(2)}, u32[]{:S(2)}) collective-permute-start(bf16[64,1024]{1,0:T(8,128)(2,1)S(1)} %clips_z.2.refs_4_.refs_1_), channel_id=1, source_target_pairs={{0,8},{8,0},{16,24},{24,16},{1,9},{9,1},{17,25},{25,17},{2,10},{10... | collective-permute-start | bytes 393224 | tf_op jit(solution)/shard_map/ppermute | solution.py:110
  14.4 2.7 %collective-permute-start.10 = (bf16[64,1024]{1,0:T(8,128)(2,1)S(1)}, bf16[64,1024]{1,0:T(8,128)(2,1)S(1)}, u32[]{:S(2)}, u32[]{:S(2)}) collective-permute-start(bf16[64,1024]{1,0:T(8,128)(2,1)S(1)} %captions_hb.1), channel_id=1, source_target_pairs={{0,4},{1,5},{2,6},{3,7},{4,0},{5,1},{6,2},{7,3},{8,12},{9,13},{10,... | collective-permute-start | bytes 393224 | tf_op jit(solution)/shard_map/ppermute | solution.py:110
  17.1 1.5 %collective-permute-start.9 = (bf16[64,1024]{1,0:T(8,128)(2,1)S(1)}, bf16[64,1024]{1,0:T(8,128)(2,1)S(1)}, u32[]{:S(2)}, u32[]{:S(2)}) collective-permute-start(bf16[64,1024]{1,0:T(8,128)(2,1)S(1)} %captions_za.1.refs_0_), channel_id=1, source_target_pairs={{0,16},{8,24},{16,0},{24,8},{1,17},{9,25},{17,1},{25,9},{2,18},{10... | collective-permute-start | bytes 393224 | tf_op jit(solution)/shard_map/ppermute | solution.py:110
  18.6 1.5 %collective-permute-start.6 = (bf16[64,1024]{1,0:T(8,128)(2,1)S(1)}, bf16[64,1024]{1,0:T(8,128)(2,1)S(1)}, u32[]{:S(2)}, u32[]{:S(2)}) collective-permute-start(bf16[64,1024]{1,0:T(8,128)(2,1)S(1)} %clips_z.3.refs_5_), channel_id=1, source_target_pairs={{0,8},{8,0},{16,24},{24,16},{1,9},{9,1},{17,25},{25,17},{2,10},{10... | collective-permute-start | bytes 393224 | tf_op jit(solution)/shard_map/ppermute | solution.py:110
  20.3 1.8 %collective-permute-done.9.refs_0_ = bf16[64,1024]{1,0:T(8,128)(2,1)S(1)} collective-permute-done((bf16[64,1024]{1,0:T(8,128)(2,1)S(1)}, bf16[64,1024]{1,0:T(8,128)(2,1)S(1)}, u32[]{:S(2)}, u32[]{:S(2)}) %collective-permute-start.9) | collective-permute-done | bytes 131104 | tf_op jit(solution)/shard_map/ppermute | solution.py:110
  22.2 1.4 %collective-permute-done.6.refs_1_ = bf16[64,1024]{1,0:T(8,128)(2,1)S(1)} collective-permute-done((bf16[64,1024]{1,0:T(8,128)(2,1)S(1)}, bf16[64,1024]{1,0:T(8,128)(2,1)S(1)}, u32[]{:S(2)}, u32[]{:S(2)}) %collective-permute-start.6) | collective-permute-done | bytes 131104 | tf_op jit(solution)/shard_map/ppermute | solution.py:110
  23.7 0.9 %collective-permute-start.11 = (bf16[64,1024]{1,0:T(8,128)(2,1)S(1)}, bf16[64,1024]{1,0:T(8,128)(2,1)S(1)}, u32[]{:S(2)}, u32[]{:S(2)}) collective-permute-start(bf16[64,1024]{1,0:T(8,128)(2,1)S(1)} %captions_zb.1.refs_0_), channel_id=1, source_target_pairs={{0,16},{8,24},{16,0},{24,8},{1,17},{9,25},{17,1},{25,9},{2,18},{10... | collective-permute-start | bytes 393224 | tf_op jit(solution)/shard_map/ppermute | solution.py:110
  25.4 1.4 %half_a.1 = (f32[1,512]{1,0:T(1,128)S(1)}, bf16[128,512]{1,0:T(8,128)(2,1)S(1)}, f32[64,1024]{1,0:T(8,128)S(1)}, bf16[64,1024]{1,0:T(8,128)(2,1)S(1)}) custom-call(f32[2,128]{1,0:T(2,128)S(1)} %consts.1.refs_1_, s32[1,1024]{1,0:T(1,128)S(1)} %get-tuple-element.45.labels, bf16[1024,1024]{1,0:T(8,128)(2,1)S(1)} %clips.1.VV, bf16[128,1024]{1,0:T(8,128)(2,1)S(1)} %half_a_blocks.1.H), custom_call_target="tpu_custom_call" | custom-call | flops 536870912 | tf_op jit(solution)/shard_map/half_a/pallas_call | solution.py:28
  27.5 0.8 %diagonal_clips.1 = (bf16[768,1024]{1,0:T(8,128)(2,1)S(1)}, bf16[768,128]{1,0:T(8,128)(2,1)S(1)}, f32[1,128]{1,0:T(1,128)S(1)}) custom-call(f32[2,128]{1,0:T(2,128)S(1)} %consts.1.refs_1_, s32[1,1024]{1,0:T(1,128)S(1)} %get-tuple-element.45.labels, bf16[640,1024]{1,0:T(8,128)(2,1)S(1)} %near_blocks.1.N, bf16[640,1024]{1,0:T(8,128)(2,1)S(1)} %collective-permute-done.4.N_k, ...), custom_call_target="tpu_custom_call" | custom-call | flops 201326592 | tf_op jit(solution)/shard_map/diagonal_clips/pallas_call | solution.py:28
  28.3 1.3 %collective-permute-done.11.refs_0_ = bf16[64,1024]{1,0:T(8,128)(2,1)S(1)} collective-permute-done((bf16[64,1024]{1,0:T(8,128)(2,1)S(1)}, bf16[64,1024]{1,0:T(8,128)(2,1)S(1)}, u32[]{:S(2)}, u32[]{:S(2)}) %collective-permute-start.11) | collective-permute-done | bytes 131104 | tf_op jit(solution)/shard_map/ppermute | solution.py:110
  29.7 1.5 %half_b.1 = (f32[1,512]{1,0:T(1,128)S(1)}, bf16[128,512]{1,0:T(8,128)(2,1)S(1)}, f32[64,1024]{1,0:T(8,128)S(1)}, bf16[64,1024]{1,0:T(8,128)(2,1)S(1)}) custom-call(f32[2,128]{1,0:T(2,128)S(1)} %consts.1.refs_1_, s32[1,1024]{1,0:T(1,128)S(1)} %get-tuple-element.45.labels, bf16[1024,1024]{1,0:T(8,128)(2,1)S(1)} %clips.1.VV, bf16[128,1024]{1,0:T(8,128)(2,1)S(1)} %half_b_blocks.1.H), custom_call_target="tpu_custom_call" | custom-call | flops 536870912 | tf_op jit(solution)/shard_map/half_b/pallas_call | solution.py:28
  31.7 0.7 %collective-permute-done.14.refs_0_ = bf16[64,1024]{1,0:T(8,128)(2,1)S(1)} collective-permute-done((bf16[64,1024]{1,0:T(8,128)(2,1)S(1)}, bf16[64,1024]{1,0:T(8,128)(2,1)S(1)}, u32[]{:S(2)}, u32[]{:S(2)}) %collective-permute-start.14) | collective-permute-done | bytes 131104 | tf_op jit(solution)/shard_map/ppermute | solution.py:110
  32.4 0.8 %far_clips.1 = (bf16[256,1024]{1,0:T(8,128)(2,1)S(1)}, f32[1,128]{1,0:T(1,128)S(1)}, bf16[128,1024]{1,0:T(8,128)(2,1)S(1)}) custom-call(f32[2,128]{1,0:T(2,128)S(1)} %consts.1.refs_1_, s32[1,1024]{1,0:T(1,128)S(1)} %get-tuple-element.45.labels, bf16[128,1024]{1,0:T(8,128)(2,1)S(1)} %diagonal_block.1.vd, bf16[768,1024]{1,0:T(8,128)(2,1)S(1)} %get-tuple-element.55.S1, ...), custom_call_target="tpu_custom_call" | custom-call | flops 301989888 | tf_op jit(solution)/shard_map/far_clips/pallas_call | solution.py:28
  33.2 1.6 %collective-permute-start.17 = (bf16[128,1024]{1,0:T(8,128)(2,1)S(1)}, bf16[128,1024]{1,0:T(8,128)(2,1)S(1)}, u32[]{:S(2)}, u32[]{:S(2)}) collective-permute-start(bf16[128,1024]{1,0:T(8,128)(2,1)S(1)} %get-tuple-element.58.refs_1_.dv_d), channel_id=1, source_target_pairs={{0,8},{8,0},{16,24},{24,16},{1,9},{9,1},{17,25},{25,17},{2,10},{10... | collective-permute-start | bytes 786440 | tf_op jit(solution)/shard_map/ppermute | solution.py:110
  34.9 2.2 %collective-permute-done.15.refs_0_ = bf16[64,1024]{1,0:T(8,128)(2,1)S(1)} collective-permute-done((bf16[64,1024]{1,0:T(8,128)(2,1)S(1)}, bf16[64,1024]{1,0:T(8,128)(2,1)S(1)}, u32[]{:S(2)}, u32[]{:S(2)}) %collective-permute-start.15) | collective-permute-done | bytes 131104 | tf_op jit(solution)/shard_map/ppermute | solution.py:110
  37.2 0.7 %collective-permute-start.23 = (bf16[64,1024]{1,0:T(8,128)(2,1)S(1)}, bf16[64,1024]{1,0:T(8,128)(2,1)S(1)}, u32[]{:S(2)}, u32[]{:S(2)}) collective-permute-start(bf16[64,1024]{1,0:T(8,128)(2,1)S(1)} %add_b.1.refs_1_), channel_id=1, source_target_pairs={{0,4},{1,5},{2,6},{3,7},{4,0},{5,1},{6,2},{7,3},{8,12},{9,13},{10,... | collective-permute-start | bytes 393224 | tf_op jit(solution)/shard_map/ppermute | solution.py:110
  37.9 2.1 %near_captions.1 = (f32[1,512]{1,0:T(1,128)S(1)}, bf16[256,384]{1,0:T(8,128)(2,1)S(1)}, f32[128,1024]{1,0:T(8,128)S(1)}, bf16[128,1024]{1,0:T(8,128)(2,1)S(1)}) custom-call(f32[2,128]{1,0:T(2,128)S(1)} %consts.1.refs_1_, s32[1,1024]{1,0:T(1,128)S(1)} %get-tuple-element.45.labels, bf16[1024,1024]{1,0:T(8,128)(2,1)S(1)} %clips.1.VV, ...), custom_call_target="tpu_custom_call" | custom-call | flops 1073741824 | tf_op jit(solution)/shard_map/near_captions/pallas_call | solution.py:28
  40.0 1.8 %z_clips.1 = (f32[1,384]{1,0:T(1,128)S(1)}, bf16[768,384]{1,0:T(8,128)(2,1)S(1)}, bf16[256,384]{1,0:T(8,128)(2,1)S(1)}, f32[128,1024]{1,0:T(8,128)S(1)}) custom-call(f32[2,128]{1,0:T(2,128)S(1)} %consts.1.refs_1_, s32[1,1024]{1,0:T(1,128)S(1)} %get-tuple-element.45.labels, bf16[1024,1024]{1,0:T(8,128)(2,1)S(1)} %clips.1.VV, ...), custom_call_target="tpu_custom_call" | custom-call | flops 671088640 | tf_op jit(solution)/shard_map/z_clips/pallas_call | solution.py:28
  41.8 0.8 %near_clips.1 = (f32[128,1024]{1,0:T(8,128)S(1)}, bf16[128,1024]{1,0:T(8,128)(2,1)S(1)}) custom-call(bf16[768,1024]{1,0:T(8,128)(2,1)S(1)} %get-tuple-element.55.S1, bf16[256,1024]{1,0:T(8,128)(2,1)S(1)} %get-tuple-element.64.S2, bf16[768,384]{1,0:T(8,128)(2,1)S(1)} %get-tuple-element.73.G1, bf16[256,384]{1,0:T(8,128)(2,1)S(1)} %get-tuple-element.74.G2), custom_call_target="tpu_custom_call" | custom-call | flops 536870912 | tf_op jit(solution)/shard_map/near_clips/pallas_call | solution.py:28
  42.5 1.0 %collective-permute-start.20 = (bf16[128,1024]{1,0:T(8,128)(2,1)S(1)}, bf16[128,1024]{1,0:T(8,128)(2,1)S(1)}, u32[]{:S(2)}, u32[]{:S(2)}) collective-permute-start(bf16[128,1024]{1,0:T(8,128)(2,1)S(1)} %get-tuple-element.76), channel_id=1, source_target_pairs={{0,8},{8,0},{16,24},{24,16},{1,9},{9,1},{17,25},{25,17},{2,10},{10... | collective-permute-start | bytes 786440 | tf_op jit(solution)/shard_map/ppermute | solution.py:110
  44.1 3.0 %collective-permute-start.21 = (bf16[128,1024]{1,0:T(8,128)(2,1)S(1)}, bf16[128,1024]{1,0:T(8,128)(2,1)S(1)}, u32[]{:S(2)}, u32[]{:S(2)}) collective-permute-start(bf16[128,1024]{1,0:T(8,128)(2,1)S(1)} %add_clips.1.sum_v.refs_1_), channel_id=1, source_target_pairs={{0,2},{1,3},{2,0},{3,1},{4,6},{5,7},{6,4},{7,5},{8,10},{9,11},{10,... | collective-permute-start | bytes 786440 | tf_op jit(solution)/shard_map/ppermute | solution.py:110
  47.7 1.2 %collective-permute-done.23.refs_0_ = bf16[64,1024]{1,0:T(8,128)(2,1)S(1)} collective-permute-done((bf16[64,1024]{1,0:T(8,128)(2,1)S(1)}, bf16[64,1024]{1,0:T(8,128)(2,1)S(1)}, u32[]{:S(2)}, u32[]{:S(2)}) %collective-permute-start.23) | collective-permute-done | bytes 131104 | tf_op jit(solution)/shard_map/ppermute | solution.py:110
  48.9 1.0 %collective-permute-done.20.refs_0_ = bf16[128,1024]{1,0:T(8,128)(2,1)S(1)} collective-permute-done((bf16[128,1024]{1,0:T(8,128)(2,1)S(1)}, bf16[128,1024]{1,0:T(8,128)(2,1)S(1)}, u32[]{:S(2)}, u32[]{:S(2)}) %collective-permute-start.20) | collective-permute-done | bytes 262176 | tf_op jit(solution)/shard_map/ppermute | solution.py:110
  49.9 1.2 %collective-permute-done.22.refs_0_ = bf16[128,1024]{1,0:T(8,128)(2,1)S(1)} collective-permute-done((bf16[128,1024]{1,0:T(8,128)(2,1)S(1)}, bf16[128,1024]{1,0:T(8,128)(2,1)S(1)}, u32[]{:S(2)}, u32[]{:S(2)}) %collective-permute-start.22) | collective-permute-done | bytes 262176 | tf_op jit(solution)/shard_map/ppermute | solution.py:110
  51.1 2.7 %collective-permute-start.19 = (f32[1,128]{1,0:T(1,128)S(1)}, f32[1,128]{1,0:T(1,128)S(1)}, u32[]{:S(2)}, u32[]{:S(2)}) collective-permute-start(f32[1,128]{1,0:T(1,128)S(1)} %add_loss.1.refs_4_), channel_id=1, source_target_pairs={{0,2},{1,3},{2,0},{3,1},{4,6},{5,7},{6,4},{7,5},{8,10},{9,11},{10,... | collective-permute-start | bytes 1544 | tf_op jit(solution)/shard_map/ppermute | solution.py:110
  53.8 1.1 %finish_captions.1 = f32[128,1024]{1,0:T(8,128)} custom-call(f32[2,128]{1,0:T(2,128)S(1)} %consts.1.refs_1_, f32[128,1024]{1,0:T(8,128)S(1)} %get-tuple-element.79.hat_ref, f32[128,1]{1,0:T(8,128)S(1)} %get-tuple-element.80.inverse_ref, f32[128,1024]{1,0:T(8,128)S(1)} %get-tuple-element.81.refs_0_, bf16[128,1024]{1,0:T(8,128)(2,1)S(1)} %captions_y.1.refs_1_, ...), custom_call_target="tpu_custom_call" | custom-call | tf_op jit(solution)/shard_map/finish_captions/pallas_call | solution.py:28
  55.3 1.1 %finish_clips.1 = (f32[128,1024]{1,0:T(8,128)}, f32[1,128]{1,0:T(1,128)}) custom-call(f32[2,128]{1,0:T(2,128)S(1)} %consts.1.refs_1_, f32[128,1024]{1,0:T(8,128)S(1)} %get-tuple-element.43.hat_ref, f32[128,1]{1,0:T(8,128)S(1)} %get-tuple-element.44.inverse_ref, f32[1,128]{1,0:T(1,128)S(1)} %get-tuple-element.70.refs_0_, ...), custom_call_target="tpu_custom_call" | custom-call | tf_op jit(solution)/shard_map/finish_clips/pallas_call | solution.py:28
  (53 shorter events, 4.3 us)
Async XLA Ops:
  2.2 10.5 %collective-permute-start.2 = (bf16[64,1024]{1,0:T(8,128)(2,1)S(1)}, bf16[64,1024]{1,0:T(8,128)(2,1)S(1)}, u32[]{:S(2)}, u32[]{:S(2)}) collective-permute-start(bf16[64,1024]{1,0:T(8,128)(2,1)S(1)} %get-tuple-element.48), channel_id=1, source_target_pairs={{0,2},{1,3},{2,0},{3,1},{4,6},{5,7},{6,4},{7,5},{8,10},{9,11},{10,... | collective-permute-start | bytes 393224 | tf_op jit(solution)/shard_map/ppermute | solution.py:110
  5.3 11.8 %collective-permute-start.3 = (bf16[64,1024]{1,0:T(8,128)(2,1)S(1)}, bf16[64,1024]{1,0:T(8,128)(2,1)S(1)}, u32[]{:S(2)}, u32[]{:S(2)}) collective-permute-start(bf16[64,1024]{1,0:T(8,128)(2,1)S(1)} %get-tuple-element.49), channel_id=1, source_target_pairs={{0,2},{1,3},{2,0},{3,1},{4,6},{5,7},{6,4},{7,5},{8,10},{9,11},{10,... | collective-permute-start | bytes 393224 | tf_op jit(solution)/shard_map/ppermute | solution.py:110
  5.3 9.0 %collective-permute-start.8 = (bf16[64,1024]{1,0:T(8,128)(2,1)S(1)}, bf16[64,1024]{1,0:T(8,128)(2,1)S(1)}, u32[]{:S(2)}, u32[]{:S(2)}) collective-permute-start(bf16[64,1024]{1,0:T(8,128)(2,1)S(1)} %get-tuple-element.50), channel_id=1, source_target_pairs={{0,4},{1,5},{2,6},{3,7},{4,0},{5,1},{6,2},{7,3},{8,12},{9,13},{10,... | collective-permute-start | bytes 393224 | tf_op jit(solution)/shard_map/ppermute | solution.py:110
  8.3 10.3 %collective-permute-start = (bf16[128,1024]{1,0:T(8,128)(2,1)S(1)}, bf16[128,1024]{1,0:T(8,128)(2,1)S(1)}, u32[]{:S(2)}, u32[]{:S(2)}) collective-permute-start(bf16[128,1024]{1,0:T(8,128)(2,1)S(1)} %get-tuple-element.46.refs_0_), channel_id=1, source_target_pairs={{0,16},{8,24},{16,0},{24,8},{1,17},{9,25},{17,1},{25,9},{2,18},{10... | collective-permute-start | bytes 786440 | tf_op jit(solution)/shard_map/ppermute | solution.py:110
  9.8 10.3 %collective-permute-start.1 = (bf16[128,1024]{1,0:T(8,128)(2,1)S(1)}, bf16[128,1024]{1,0:T(8,128)(2,1)S(1)}, u32[]{:S(2)}, u32[]{:S(2)}) collective-permute-start(bf16[128,1024]{1,0:T(8,128)(2,1)S(1)} %get-tuple-element.47.refs_2_), channel_id=1, source_target_pairs={{0,8},{8,0},{16,24},{24,16},{1,9},{9,1},{17,25},{25,17},{2,10},{10... | collective-permute-start | bytes 786440 | tf_op jit(solution)/shard_map/ppermute | solution.py:110
  12.7 9.5 %collective-permute-start.5 = (bf16[64,1024]{1,0:T(8,128)(2,1)S(1)}, bf16[64,1024]{1,0:T(8,128)(2,1)S(1)}, u32[]{:S(2)}, u32[]{:S(2)}) collective-permute-start(bf16[64,1024]{1,0:T(8,128)(2,1)S(1)} %clips_z.2.refs_4_.refs_1_), channel_id=1, source_target_pairs={{0,8},{8,0},{16,24},{24,16},{1,9},{9,1},{17,25},{25,17},{2,10},{10... | collective-permute-start | bytes 393224 | tf_op jit(solution)/shard_map/ppermute | solution.py:110
  14.4 9.3 %collective-permute-start.10 = (bf16[64,1024]{1,0:T(8,128)(2,1)S(1)}, bf16[64,1024]{1,0:T(8,128)(2,1)S(1)}, u32[]{:S(2)}, u32[]{:S(2)}) collective-permute-start(bf16[64,1024]{1,0:T(8,128)(2,1)S(1)} %captions_hb.1), channel_id=1, source_target_pairs={{0,4},{1,5},{2,6},{3,7},{4,0},{5,1},{6,2},{7,3},{8,12},{9,13},{10,... | collective-permute-start | bytes 393224 | tf_op jit(solution)/shard_map/ppermute | solution.py:110
  17.1 5.0 %collective-permute-start.9 = (bf16[64,1024]{1,0:T(8,128)(2,1)S(1)}, bf16[64,1024]{1,0:T(8,128)(2,1)S(1)}, u32[]{:S(2)}, u32[]{:S(2)}) collective-permute-start(bf16[64,1024]{1,0:T(8,128)(2,1)S(1)} %captions_za.1.refs_0_), channel_id=1, source_target_pairs={{0,16},{8,24},{16,0},{24,8},{1,17},{9,25},{17,1},{25,9},{2,18},{10... | collective-permute-start | bytes 393224 | tf_op jit(solution)/shard_map/ppermute | solution.py:110
  18.6 5.0 %collective-permute-start.6 = (bf16[64,1024]{1,0:T(8,128)(2,1)S(1)}, bf16[64,1024]{1,0:T(8,128)(2,1)S(1)}, u32[]{:S(2)}, u32[]{:S(2)}) collective-permute-start(bf16[64,1024]{1,0:T(8,128)(2,1)S(1)} %clips_z.3.refs_5_), channel_id=1, source_target_pairs={{0,8},{8,0},{16,24},{24,16},{1,9},{9,1},{17,25},{25,17},{2,10},{10... | collective-permute-start | bytes 393224 | tf_op jit(solution)/shard_map/ppermute | solution.py:110
  20.2 5.0 %collective-permute-start.4 = (bf16[640,1024]{1,0:T(8,128)(2,1)S(1)}, bf16[640,1024]{1,0:T(8,128)(2,1)S(1)}, u32[]{:S(2)}, u32[]{:S(2)}) collective-permute-start(bf16[640,1024]{1,0:T(8,128)(2,1)S(1)} %near_blocks.1.N), channel_id=1, source_target_pairs={{0,1},{1,0},{2,3},{3,2},{4,5},{5,4},{6,7},{7,6},{8,9},{9,8},{10,11... | collective-permute-start | bytes 3932168 | tf_op jit(solution)/shard_map/ppermute | solution.py:110
  22.1 5.4 %collective-permute-start.12 = (bf16[128,1024]{1,0:T(8,128)(2,1)S(1)}, bf16[128,1024]{1,0:T(8,128)(2,1)S(1)}, u32[]{:S(2)}, u32[]{:S(2)}) collective-permute-start(bf16[128,1024]{1,0:T(8,128)(2,1)S(1)} %half_a_blocks.1.H), channel_id=1, source_target_pairs={{0,1},{1,0},{2,3},{3,2},{4,5},{5,4},{6,7},{7,6},{8,9},{9,8},{10,11... | collective-permute-start | bytes 786440 | tf_op jit(solution)/shard_map/ppermute | solution.py:110
  23.6 1.6 %collective-permute-start.7 = (bf16[128,1024]{1,0:T(8,128)(2,1)S(1)}, bf16[128,1024]{1,0:T(8,128)(2,1)S(1)}, u32[]{:S(2)}, u32[]{:S(2)}) collective-permute-start(bf16[128,1024]{1,0:T(8,128)(2,1)S(1)} %diagonal_block.1.vd), channel_id=1, source_target_pairs={{0,1},{1,0},{2,3},{3,2},{4,5},{5,4},{6,7},{7,6},{8,9},{9,8},{10,11... | collective-permute-start | bytes 786440 | tf_op jit(solution)/shard_map/ppermute | solution.py:110
  23.7 5.9 %collective-permute-start.11 = (bf16[64,1024]{1,0:T(8,128)(2,1)S(1)}, bf16[64,1024]{1,0:T(8,128)(2,1)S(1)}, u32[]{:S(2)}, u32[]{:S(2)}) collective-permute-start(bf16[64,1024]{1,0:T(8,128)(2,1)S(1)} %captions_zb.1.refs_0_), channel_id=1, source_target_pairs={{0,16},{8,24},{16,0},{24,8},{1,17},{9,25},{17,1},{25,9},{2,18},{10... | collective-permute-start | bytes 393224 | tf_op jit(solution)/shard_map/ppermute | solution.py:110
  26.8 5.6 %collective-permute-start.14 = (bf16[64,1024]{1,0:T(8,128)(2,1)S(1)}, bf16[64,1024]{1,0:T(8,128)(2,1)S(1)}, u32[]{:S(2)}, u32[]{:S(2)}) collective-permute-start(bf16[64,1024]{1,0:T(8,128)(2,1)S(1)} %get-tuple-element.60), channel_id=1, source_target_pairs={{0,16},{8,24},{16,0},{24,8},{1,17},{9,25},{17,1},{25,9},{2,18},{10... | collective-permute-start | bytes 393224 | tf_op jit(solution)/shard_map/ppermute | solution.py:110
  29.6 2.8 %collective-permute-start.13 = (bf16[128,1024]{1,0:T(8,128)(2,1)S(1)}, bf16[128,1024]{1,0:T(8,128)(2,1)S(1)}, u32[]{:S(2)}, u32[]{:S(2)}) collective-permute-start(bf16[128,1024]{1,0:T(8,128)(2,1)S(1)} %half_b_blocks.1.H), channel_id=1, source_target_pairs={{0,1},{1,0},{2,3},{3,2},{4,5},{5,4},{6,7},{7,6},{8,9},{9,8},{10,11... | collective-permute-start | bytes 786440 | tf_op jit(solution)/shard_map/ppermute | solution.py:110
  31.2 6.0 %collective-permute-start.15 = (bf16[64,1024]{1,0:T(8,128)(2,1)S(1)}, bf16[64,1024]{1,0:T(8,128)(2,1)S(1)}, u32[]{:S(2)}, u32[]{:S(2)}) collective-permute-start(bf16[64,1024]{1,0:T(8,128)(2,1)S(1)} %get-tuple-element.62), channel_id=1, source_target_pairs={{0,16},{8,24},{16,0},{24,8},{1,17},{9,25},{17,1},{25,9},{2,18},{10... | collective-permute-start | bytes 393224 | tf_op jit(solution)/shard_map/ppermute | solution.py:110
  33.2 10.8 %collective-permute-start.17 = (bf16[128,1024]{1,0:T(8,128)(2,1)S(1)}, bf16[128,1024]{1,0:T(8,128)(2,1)S(1)}, u32[]{:S(2)}, u32[]{:S(2)}) collective-permute-start(bf16[128,1024]{1,0:T(8,128)(2,1)S(1)} %get-tuple-element.58.refs_1_.dv_d), channel_id=1, source_target_pairs={{0,8},{8,0},{16,24},{24,16},{1,9},{9,1},{17,25},{25,17},{2,10},{10... | collective-permute-start | bytes 786440 | tf_op jit(solution)/shard_map/ppermute | solution.py:110
  34.8 12.2 %collective-permute-start.16 = (bf16[64,1024]{1,0:T(8,128)(2,1)S(1)}, bf16[64,1024]{1,0:T(8,128)(2,1)S(1)}, u32[]{:S(2)}, u32[]{:S(2)}) collective-permute-start(bf16[64,1024]{1,0:T(8,128)(2,1)S(1)} %add_a.1.refs_1_.refs_0_), channel_id=1, source_target_pairs={{0,4},{1,5},{2,6},{3,7},{4,0},{5,1},{6,2},{7,3},{8,12},{9,13},{10,... | collective-permute-start | bytes 393224 | tf_op jit(solution)/shard_map/ppermute | solution.py:110
  37.2 11.7 %collective-permute-start.23 = (bf16[64,1024]{1,0:T(8,128)(2,1)S(1)}, bf16[64,1024]{1,0:T(8,128)(2,1)S(1)}, u32[]{:S(2)}, u32[]{:S(2)}) collective-permute-start(bf16[64,1024]{1,0:T(8,128)(2,1)S(1)} %add_b.1.refs_1_), channel_id=1, source_target_pairs={{0,4},{1,5},{2,6},{3,7},{4,0},{5,1},{6,2},{7,3},{8,12},{9,13},{10,... | collective-permute-start | bytes 393224 | tf_op jit(solution)/shard_map/ppermute | solution.py:110
  42.5 7.4 %collective-permute-start.20 = (bf16[128,1024]{1,0:T(8,128)(2,1)S(1)}, bf16[128,1024]{1,0:T(8,128)(2,1)S(1)}, u32[]{:S(2)}, u32[]{:S(2)}) collective-permute-start(bf16[128,1024]{1,0:T(8,128)(2,1)S(1)} %get-tuple-element.76), channel_id=1, source_target_pairs={{0,8},{8,0},{16,24},{24,16},{1,9},{9,1},{17,25},{25,17},{2,10},{10... | collective-permute-start | bytes 786440 | tf_op jit(solution)/shard_map/ppermute | solution.py:110
  43.5 7.6 %collective-permute-start.22 = (bf16[128,1024]{1,0:T(8,128)(2,1)S(1)}, bf16[128,1024]{1,0:T(8,128)(2,1)S(1)}, u32[]{:S(2)}, u32[]{:S(2)}) collective-permute-start(bf16[128,1024]{1,0:T(8,128)(2,1)S(1)} %get-tuple-element.82), channel_id=1, source_target_pairs={{0,16},{8,24},{16,0},{24,8},{1,17},{9,25},{17,1},{25,9},{2,18},{10... | collective-permute-start | bytes 786440 | tf_op jit(solution)/shard_map/ppermute | solution.py:110
  44.1 10.8 %collective-permute-start.21 = (bf16[128,1024]{1,0:T(8,128)(2,1)S(1)}, bf16[128,1024]{1,0:T(8,128)(2,1)S(1)}, u32[]{:S(2)}, u32[]{:S(2)}) collective-permute-start(bf16[128,1024]{1,0:T(8,128)(2,1)S(1)} %add_clips.1.sum_v.refs_1_), channel_id=1, source_target_pairs={{0,2},{1,3},{2,0},{3,1},{4,6},{5,7},{6,4},{7,5},{8,10},{9,11},{10,... | collective-permute-start | bytes 786440 | tf_op jit(solution)/shard_map/ppermute | solution.py:110
  47.0 4.1 %collective-permute-start.18 = (f32[2,128]{1,0:T(2,128)S(1)}, f32[2,128]{1,0:T(2,128)S(1)}, u32[]{:S(2)}, u32[]{:S(2)}) collective-permute-start(f32[2,128]{1,0:T(2,128)S(1)} %get-tuple-element.71), channel_id=1, source_target_pairs={{0,8},{8,0},{16,24},{24,16},{1,9},{9,1},{17,25},{25,17},{2,10},{10... | collective-permute-start | bytes 3080 | tf_op jit(solution)/shard_map/ppermute | solution.py:110
  51.1 4.2 %collective-permute-start.19 = (f32[1,128]{1,0:T(1,128)S(1)}, f32[1,128]{1,0:T(1,128)S(1)}, u32[]{:S(2)}, u32[]{:S(2)}) collective-permute-start(f32[1,128]{1,0:T(1,128)S(1)} %add_loss.1.refs_4_), channel_id=1, source_target_pairs={{0,2},{1,3},{2,0},{3,1},{4,6},{5,7},{6,4},{7,5},{8,10},{9,11},{10,... | collective-permute-start | bytes 1544 | tf_op jit(solution)/shard_map/ppermute | solution.py:110

commit v5 on v4

v5 whole, which is shorter than its diff:
```python
import jax
import jax.numpy as jnp
from jax import lax
from jax.experimental import pallas as pl
from jax.experimental.pallas import tpu as pltpu
from jax.sharding import PartitionSpec as P

F32, BF16 = jnp.float32, jnp.bfloat16
MIB = 1024 * 1024
CHUNK = 256
PARTS = 4
LONG = 10**10
SPECS = {
    "s": pl.BlockSpec(memory_space=pltpu.SMEM),
    "v": pl.BlockSpec(memory_space=pltpu.VMEM),
    "h": pl.BlockSpec(memory_space=pl.ANY),
}


def vm(shape, dtype=BF16):
    return pltpu.VMEM(shape, dtype)


def call(name, kernel, out_shape, args, spec="v", out_spec="v", limit=4, flops=0, scratch=(), aliases={}):
    space = {"v": pltpu.VMEM, "h": pltpu.HBM}
    if spec in space:
        args = [pltpu.with_memory_space_constraint(a, space[spec]) for a in args]
    return pl.pallas_call(
        kernel,
        name=name,
        out_shape=out_shape,
        in_specs=[SPECS[spec]] * len(args),
        out_specs=[SPECS[out_spec]] * len(out_shape),
        scratch_shapes=list(scratch),
        input_output_aliases=aliases,
        compiler_params=pltpu.CompilerParams(vmem_limit_bytes=limit * MIB),
        cost_estimate=pl.CostEstimate(flops=flops, bytes_accessed=0, transcendentals=0),
    )(*args)


def hand_on(name, block, *after, flops=0):
    return call(
        name, lambda *refs: None, [vm(block.shape, block.dtype)], [block, *after],
        aliases={0: 0}, flops=flops,
    )[0]


def unit_rows(rows):
    inverse = lax.rsqrt(jnp.sum(rows * rows, axis=1, keepdims=True) + 1e-06)
    return rows * inverse, inverse


def dot_nt(a, b):
    return lax.dot_general(a, b, (((1,), (1,)), ((), ())), preferred_element_type=F32)


def dot_tn(a, b):
    return lax.dot_general(a, b, (((0,), (0,)), ((), ())), preferred_element_type=F32)


def dot_nn(a, b):
    return jnp.dot(a, b, preferred_element_type=F32)


def log1p_sum(e):
    rows = e.shape[0]
    u = e
    for _ in range(3):
        rows //= 2
        a, b = u[:rows], u[rows:]
        u = a + b + a * b
    series = u * (1.0 - u * (0.5 - u * (1.0 / 3.0 - u * 0.25)))
    logs = jnp.where(u < 0.01, series, jnp.log(1.0 + u))
    return jnp.sum(logs, axis=0, keepdims=True)


def pairs(dots, scale, shift, base, labels, counted):
    logits = dots * scale + shift
    match = lax.broadcasted_iota(jnp.int32, logits.shape, 0) == labels - base
    e = jnp.exp(-jnp.abs(logits))
    whole = 1.0 + e
    over = pl.reciprocal(whole, approx=True)
    over = over * (2.0 - whole * over)
    sigmoid = jnp.where(logits >= 0.0, over, e * over)
    coef = (sigmoid - jnp.where(match, 1.0, 0.0)).astype(BF16)
    if not counted:
        return coef, None
    e, logits, match = e[:, :counted], logits[:, :counted], match[:, :counted]
    linear = jnp.maximum(jnp.where(match, -logits, logits), 0.0)
    return coef, jnp.sum(linear, axis=0, keepdims=True) + log1p_sum(e)


def stack(target, blocks):
    at = 0
    for b in blocks:
        target[pl.ds(at, b.shape[0]), :] = b[...]
        at += b.shape[0]


def shards(film, text, matched, sharpness, offset):
    rows, width = film.shape
    half = rows // 2
    R, C = lax.axis_size("row"), lax.axis_size("col")
    Y, Z = R // 2, C // 4
    mat, hmat = (rows, width), (half, width)
    limit = 6 + 2 * (Y * Z * 2 * rows) // 1024

    def swap(value, axis, bits):
        size = lax.axis_size(axis)
        return lax.ppermute(value, axis, [(i, i ^ bits) for i in range(size)])

    def first_caption(s, t, k):
        r, c = lax.axis_index("row"), lax.axis_index("col")
        return ((c ^ (4 * s + k)) * R + (r ^ (2 * t))) * rows

    def clip_index(x, z, k):
        r, c = lax.axis_index("row"), lax.axis_index("col")
        return (r ^ x) * C + (c ^ (2 * z + k))

    near = [(0, t) for t in range(Y)]
    up = [(s, 0) for s in range(1, Z)]
    diag = [(s, t) for s in range(1, Z) for t in range(1, Y)]
    clip_order = [(x, z, k) for k in range(2) for z in range(2) for x in range(2)]
    nn, na, nd = len(near) * rows, len(near + up) * rows, len(diag) * rows
    n1, n3, n4, n7 = rows, 3 * rows, 4 * rows, 7 * rows

    def strip(consts, blocks, k, captions, clips, labels, counted, put):
        scale, shift = consts[0:1, 0:1], consts[1:2, 0:1]
        dots = dot_nt(captions, clips)
        total = 0.0
        for i, (s, t) in enumerate(blocks):
            block = dots[i * rows : (i + 1) * rows]
            coef, add = pairs(block, scale, shift, first_caption(s, t, k), labels, counted)
            put(i * rows, coef)
            total = total + add if counted else None
        return total

    def put_in(target, first=0, left=0):
        def put(at, coef):
            target[pl.ds(first + at, coef.shape[0]), pl.ds(left, coef.shape[1])] = coef
        return put

    def normalize_kernel(film, text, matched, v16, c16, va, vb, vhat, chat, vinv, cinv, labels, fbuf, tbuf, mbuf, sems):
        step = rows // PARTS
        get_matched = pltpu.make_async_copy(matched, mbuf, sems.at[2 * PARTS])
        copies = []
        for j, (src, buf) in enumerate(((film, fbuf), (text, tbuf))):
            for i in range(PARTS):
                part = pl.ds(i * step, step)
                copies.append(pltpu.make_async_copy(src.at[part], buf.at[part], sems.at[j * PARTS + i]))
        for copy in copies:
            copy.start()
        get_matched.start()
        for copy in copies[:PARTS]:
            copy.wait()
        hat, inverse = unit_rows(fbuf[...])
        vhat[...], vinv[...], v16[...] = hat, inverse, hat.astype(BF16)
        va[...] = hat[:half].astype(BF16)
        vb[...] = hat[half:].astype(BF16)
        for copy in copies[PARTS:]:
            copy.wait()
        hat, inverse = unit_rows(tbuf[...])
        chat[...], cinv[...], c16[...] = hat, inverse, hat.astype(BF16)
        get_matched.wait()
        labels[...] = jnp.concatenate(
            [mbuf[pl.ds(clip_index(*p), 1), :] for p in clip_order], axis=1
        )

    matched = matched.reshape(-1, rows)
    v16, c16, va, vb, vhat, chat, vinv, cinv, labels = call(
        "normalize", normalize_kernel,
        [vm(mat), vm(mat)] + [vm(hmat)] * 2 + [vm(mat, F32), vm(mat, F32), vm((rows, 1), F32), vm((rows, 1), F32),
         vm((1, 8 * rows), jnp.int32)],
        [film, text, matched], spec="h", limit=8,
        scratch=[pltpu.VMEM(mat, F32)] * 2
        + [pltpu.VMEM(matched.shape, jnp.int32), pltpu.SemaphoreType.DMA((2 * PARTS + 1,))],
    )

    def consts_kernel(scale, shift, out):
        out[0:1, :] = jnp.full((1, 128), scale[0], F32)
        out[1:2, :] = jnp.full((1, 128), shift[0], F32)

    (consts,) = call("consts", consts_kernel, [vm((2, 128), F32)], [sharpness, offset], spec="s")

    def join(name, *blocks):
        def join_kernel(*refs):
            stack(refs[-1], refs[:-1])

        return call(name, join_kernel, [vm((sum(b.shape[0] for b in blocks), width))], blocks)[0]

    v_z = [hand_on("clips_z", swap(b, "col", 2), flops=LONG) for b in (va, vb)]
    c_z = [hand_on("captions_z", swap(c16, "col", 4 * s), consts, flops=1 * LONG) for s in range(1, Z)]
    c_y = [swap(c16, "row", 2 * t) for t in range(1, Y)]
    v_x = swap(v16, "row", 1)
    v_d = [hand_on("clips_d", swap(b, "row", 1), flops=2 * LONG // 4) for b in v_z]
    c_d = [swap(b, "row", 2 * t) for b in c_z for t in range(1, Y)]
    N = join("near_blocks", c16, *c_y, v16, v_x, *v_z)
    N_k = hand_on("near_other", swap(N, "col", 1), flops=4 * LONG // 4)
    cz_k = [swap(b, "col", 1) for b in c_z]
    v_d = join("diagonal_clips", *v_d)
    vd_k = swap(v_d, "col", 1)

    def early_kernel(consts, labels, N, N_k, *refs):
        n = len(up)
        cz, czk, (S1, p, q, loss) = refs[:n], refs[n : 2 * n], refs[2 * n :]
        stack(S1, [N.at[:nn], *cz, N_k.at[:nn], *czk])
        own = N[nn:, :]
        loss[...] = strip(
            consts, near + up, 0, S1[:na, :], own, labels[:, :n3], n3, put_in(p)
        ) + strip(consts, near + up, 1, S1[na:, :], own, labels[:, :n3], n3, put_in(q))
        strip(
            consts, near + up, 0, S1[:na, :], N_k[nn:, :], labels[:, n4:n7], 0, put_in(p, left=n3)
        )

    S1, p, q, loss_a = call(
        "early_pairs", early_kernel,
        [vm((2 * na, width)), vm((na, 2 * n3)), vm((na, n3)), vm((1, n3), F32)],
        [consts, labels, N, N_k, *c_z, *cz_k],
        flops=2 * 27 * rows * rows * width, limit=limit,
    )

    def middle_kernel(consts, labels, N, N_k, vd, vdk, S1, p, q, VV, G1, loss, dc0, *refs):
        dcy, dcz, coef = refs[: Y - 1], refs[Y - 1 : -1], refs[-1]
        stack(VV, [N.at[nn:], vd, N_k.at[nn:], vdk])
        coef[:, :n3] = p[:, :n3]
        coef[:, n4:n7] = p[:, n3:]
        G1[na:, :n3] = q[...]
        late = labels[:, n3:n4]
        loss[...] = strip(
            consts, near + up, 0, S1[:na, :], vd[...], late, n1, put_in(coef, left=n3)
        ) + strip(consts, near + up, 1, S1[na:, :], vd[...], late, n1, put_in(G1, na, n3))
        strip(consts, near + up, 0, S1[:na, :], vdk[...], labels[:, n7:], 0, put_in(coef, left=n7))
        G1[:na, :] = coef[:, :n4]
        for i in range(width // CHUNK):
            cols = pl.ds(i * CHUNK, CHUNK)
            part = dot_nn(coef[...], VV[:, cols])
            for j, ref in enumerate((dc0, *dcy)):
                ref[:, cols] = part[j * rows : (j + 1) * rows].astype(ref.dtype)
            for j, ref in enumerate(dcz):
                ref[:, cols] = part[nn + j * half : nn + (j + 1) * half]

    VV, G1, loss_m, dc0, *dcs = call(
        "middle_sums", middle_kernel,
        [vm((8 * n1, width)), vm((2 * na, n4)), vm((1, n1), F32), vm(mat, F32)]
        + [vm(mat)] * (Y - 1) + [vm(hmat, F32)] * (2 * (Z - 1)),
        [consts, labels, N, N_k, v_d, vd_k, S1, p, q],
        flops=2 * 33 * rows * rows * width, limit=limit,
        scratch=[pltpu.VMEM((na, 8 * n1), BF16)],
    )
    dcy, dcz = dcs[: Y - 1], dcs[Y - 1 :]
    c_d = [hand_on("captions_d", b, dc0, flops=3 * LONG) for b in c_d]
    D_k = [swap(b, "col", 1) for b in c_d]

    def far_captions_kernel(consts, labels, VV, *refs):
        n = len(diag)
        caps, (loss, p, *sums, D, coef) = refs[:n], refs[n:]
        stack(D, caps)
        loss[...] = strip(consts, diag, 0, D[...], VV[...], labels[...], n4, put_in(coef))
        p[...] = coef[:, :n4]
        for i in range(width // CHUNK):
            cols = pl.ds(i * CHUNK, CHUNK)
            part = dot_nn(coef[...], VV[:, cols])
            for j, ref in enumerate(sums):
                ref[:, cols] = part[j * half : (j + 1) * half].astype(BF16)

    loss_c, p_d, *dcd = call(
        "far_captions", far_captions_kernel,
        [vm((1, n4), F32), vm((nd, n4))] + [vm(hmat)] * (2 * len(diag)),
        [consts, labels, VV, *c_d],
        flops=2 * 16 * rows * rows * width, limit=limit,
        scratch=[pltpu.VMEM((nd, width), BF16), pltpu.VMEM((nd, 8 * n1), BF16)],
    )

    def far_clips_kernel(consts, labels, VV, S1, G1, p_d, *refs):
        n = len(diag)
        caps, (S2, G2, loss, dv) = refs[: 2 * n], refs[2 * n :]
        stack(S2, caps)
        G2[:nd, :] = p_d[...]
        loss[...] = strip(consts, diag, 1, S2[nd:, :], VV[:n4, :], labels[:, :n4], n4, put_in(G2, nd))
        for i in range(width // CHUNK):
            cols = pl.ds(i * CHUNK, CHUNK)
            dv[:, cols] = (dot_tn(G1[:, n3:], S1[:, cols]) + dot_tn(G2[:, n3:], S2[:, cols])).astype(BF16)

    S2, G2, loss_d, dv_d = call(
        "far_clips", far_clips_kernel,
        [vm((2 * nd, width)), vm((2 * nd, n4)), vm((1, n4), F32), vm(mat)],
        [consts, labels, VV, S1, G1, p_d, *c_d, *D_k],
        flops=2 * 12 * rows * rows * width, limit=limit,
    )
    far_v = swap(dv_d, "row", 1)

    def near_clips_kernel(S1, S2, G1, G2, dv0, dvx, dvz):
        for i in range(width // CHUNK):
            cols = pl.ds(i * CHUNK, CHUNK)
            part = dot_tn(G1[:, :n3], S1[:, cols]) + dot_tn(G2[:, :n3], S2[:, cols])
            for j, ref in enumerate((dv0, dvx, dvz)):
                ref[:, cols] = part[j * rows : (j + 1) * rows].astype(ref.dtype)

    dv0, dvx, dvz = call(
        "near_clips", near_clips_kernel, [vm(mat, F32), vm(mat), vm(mat, F32)], [S1, S2, G1, G2],
        flops=2 * 24 * rows * rows * width, limit=limit,
    )

    def add_kernel(*refs):
        total = refs[0][...].astype(F32)
        for ref in refs[1:-1]:
            total += ref[...].astype(F32)
        refs[-1][...] = total.astype(BF16)

    def add(name, *terms):
        return call(name, add_kernel, [vm(terms[0].shape)], terms)[0]

    def captions_back(h, *after):
        sums = []
        for s in range(Z - 1):
            far = [
                hand_on("far_" + "ab"[h], swap(dcd[2 * (s * (Y - 1) + t - 1) + h], "row", 2 * t), *after, flops=LONG)
                for t in range(1, Y)
            ]
            sums.append(add("add_" + "ab"[h], dcz[2 * s + h], *far))
        return sums, [swap(sums[s], "col", 4 * (s + 1)) for s in range(Z - 1)]

    sums_a, got_a = captions_back(0, dv_d)
    sums_b, got_b = captions_back(1, sums_a[0])
    sum_v = add("add_clips", dvz, far_v)
    got_z = hand_on("clips_back", swap(sum_v, "col", 2), flops=3 * LONG)
    got_h = [[hand_on("captions_back", b, sum_v, flops=3 * LONG) for b in got] for got in (got_a, got_b)]
    got_y = [hand_on("captions_y", swap(dcy[t - 1], "row", 2 * t), sum_v, flops=LONG) for t in range(1, Y)]
    got_x = hand_on("clips_x", swap(dvx, "row", 1), sum_v, flops=LONG)

    def losses_kernel(l_a, l_m, l_c, l_d, *refs):
        loss_0, loss_x, loss_z = refs[-3:]
        total = l_c[...] + l_d[...]
        own = total[:, :n3] + l_a[...]
        loss_0[...] = own[:, :n1]
        loss_x[0:1, :] = own[:, n1 : 2 * n1]
        loss_x[1:2, :] = total[:, n3:] + l_m[...]
        loss_z[...] = own[:, 2 * n1 :]

    def add_loss_kernel(loss_z, arrived, out):
        out[...] = loss_z[...] + arrived[1:2, :]

    loss_0, loss_x, loss_z = call(
        "losses", losses_kernel, [vm((1, n1), F32), vm((2, n1), F32), vm((1, n1), F32)],
        [loss_a, loss_m, loss_c, loss_d, got_a[0], sum_v],
    )
    far_loss = swap(loss_x, "row", 1)
    (sum_loss,) = call("add_loss", add_loss_kernel, [vm((1, n1), F32)], [loss_z, far_loss])
    got_loss = swap(sum_loss, "col", 2)

    def finish(name, losses, consts, hat, inverse, own, whole, halves, *after):
        tail = 2 + 2 * bool(losses)

        def finish_kernel(consts, hat_ref, inverse_ref, *refs):
            adds, (grad, *loss, buf, sems) = refs[: -1 - tail - len(after)], refs[-1 - tail :]
            copies = []
            if losses:
                out, lbuf = loss
                loss_0, far_loss, got_loss = adds[:3]
                lbuf[...] = loss_0[...] + far_loss[0:1, :] + got_loss[...]
                copies.append(pltpu.make_async_copy(lbuf, out, sems.at[2]))
                copies[-1].start()
            adds = adds[len(losses) :]
            for i in range(2):
                part = pl.ds(i * half, half)
                total = adds[0][part, :]
                for ref in adds[1 : 1 + len(whole)]:
                    total += ref[part, :].astype(F32)
                for ref in adds[1 + len(whole) :][i * len(halves[0]) : (i + 1) * len(halves[0])]:
                    total += ref[...].astype(F32)
                total = total * consts[0:1, 0:1]
                hat = hat_ref[part, :]
                along = jnp.sum(hat * total, axis=1, keepdims=True)
                buf[part, :] = inverse_ref[part, :] * (total - hat * along)
                copies.append(pltpu.make_async_copy(buf.at[part], grad.at[part], sems.at[i]))
                copies[-1].start()
            for copy in copies:
                copy.wait()

        return call(
            name, finish_kernel,
            [jax.ShapeDtypeStruct(mat, F32)] + [jax.ShapeDtypeStruct((1, rows), F32)] * bool(losses),
            [consts, hat, inverse, *losses, own, *whole, *halves[0], *halves[1], *after], out_spec="h",
            scratch=[pltpu.VMEM((1, rows), F32)] * bool(losses)
            + [pltpu.VMEM(mat, F32), pltpu.SemaphoreType.DMA((3,))],
        )

    (gc,) = finish("finish_captions", [], consts, chat, cinv, dc0, got_y, got_h, sum_loss)
    gv, clip_loss = finish(
        "finish_clips", [loss_0, far_loss, got_loss], consts, vhat, vinv, dv0, [got_x, got_z], ([], [])
    )
    return clip_loss.reshape(rows), gv, gc


def solution(mesh):
    return jax.shard_map(
        shards,
        mesh=mesh,
        in_specs=(P(("row", "col"), None), P(("col", "row"), None), P(), P(), P()),
        out_specs=(P(("row", "col")), P(("row", "col"), None), P(("col", "row"), None)),
        check_vma=False,
    )
```

time: 56.5 us -> 59.9 us (1.060)
  waiting for transfers between devices: 11.9 us -> 19.7 us
  starting transfers between devices: 29.1 us -> 25.8 us
  Pallas kernels: 13.2 us -> 12.1 us
    ppermute x24 -> x22, waiting for transfers between devices: 11.9 us -> 19.7 us  [swap(): return lax.ppermute(value, axis, [(i, i ^ bits) for i in range(size)])]
    ppermute x24 -> x22, starting transfers between devices: 29.1 us -> 25.8 us  [swap(): return lax.ppermute(value, axis, [(i, i ^ bits) for i in range(size)])]
    pallas_call x37 -> x30, Pallas kernels: 13.2 us -> 12.1 us  [call(): pl.pallas_call(kernel, name=name, out_shape=out_shape, in_specs=[SPECS[sp...]
  transfers between devices with their start and end apart: 24 -> 22, of which waited for: 10 -> 11; matrix products, arithmetic and copies ran while one was open for 0% -> 0% of each run, Pallas kernels for 19% -> 16%
where the time goes in v5:
time: 59.9 us; the launch traced here: 59.8 us
  starting transfers between devices  25.8 us (43%)
  waiting for transfers between devices  19.7 us (33%)
  Pallas kernels  12.1 us (20%)
  between operations  2.1 us (4%)
    ppermute x22, starting transfers between devices, swap(): return lax.ppermute(value, axis, [(i, i ^ bits) for i in range(size)])  25.8 us
    ppermute x22, waiting for transfers between devices, swap(): return lax.ppermute(value, axis, [(i, i ^ bits) for i in range(size)])  19.7 us
    pallas_call x30, Pallas kernels, call(): pl.pallas_call(kernel, name=name, out_shape=out_shape, in_specs=[SPECS[sp...  12.1 us
  transfers between devices with their start and end apart: 22, of which 11 were waited for; matrix products, arithmetic and copies ran while one was open for 0% of the time, Pallas kernels for 16%

profile of v5, /device:TPU:0, one launch (start us, length us, event | category | flops | bytes accessed | tf_op | source)
XLA Modules:
  0.0 59.8 jit_solution(6806465726693816269)
XLA Ops:
  0.6 1.5 %normalize.1 = (bf16[128,1024]{1,0:T(8,128)(2,1)S(1)}, bf16[128,1024]{1,0:T(8,128)(2,1)S(1)}, bf16[64,1024]{1,0:T(8,128)(2,1)S(1)}, bf16[64,1024]{1,0:T(8,128)(2...) custom-call(f32[128,1024]{1,0:T(8,128)} %film.1, ...), custom_call_target="tpu_custom_call" | custom-call | tf_op jit(solution)/shard_map/normalize/pallas_call | solution.py:28
  2.2 3.1 %collective-permute-start.2 = (bf16[64,1024]{1,0:T(8,128)(2,1)S(1)}, bf16[64,1024]{1,0:T(8,128)(2,1)S(1)}, u32[]{:S(2)}, u32[]{:S(2)}) collective-permute-start(bf16[64,1024]{1,0:T(8,128)(2,1)S(1)} %get-tuple-element.44), channel_id=1, source_target_pairs={{0,2},{1,3},{2,0},{3,1},{4,6},{5,7},{6,4},{7,5},{8,10},{9,11},{10,... | collective-permute-start | bytes 393224 | tf_op jit(solution)/shard_map/ppermute | solution.py:110
  5.3 2.6 %collective-permute-start.5 = (bf16[128,1024]{1,0:T(8,128)(2,1)S(1)}, bf16[128,1024]{1,0:T(8,128)(2,1)S(1)}, u32[]{:S(2)}, u32[]{:S(2)}) collective-permute-start(bf16[128,1024]{1,0:T(8,128)(2,1)S(1)} %get-tuple-element.42.refs_0_), channel_id=1, source_target_pairs={{0,4},{1,5},{2,6},{3,7},{4,0},{5,1},{6,2},{7,3},{8,12},{9,13},{10,... | collective-permute-start | bytes 786440 | tf_op jit(solution)/shard_map/ppermute | solution.py:110
  7.8 1.5 %collective-permute-start = (bf16[128,1024]{1,0:T(8,128)(2,1)S(1)}, bf16[128,1024]{1,0:T(8,128)(2,1)S(1)}, u32[]{:S(2)}, u32[]{:S(2)}) collective-permute-start(bf16[128,1024]{1,0:T(8,128)(2,1)S(1)} %get-tuple-element.42.refs_0_), channel_id=1, source_target_pairs={{0,16},{8,24},{16,0},{24,8},{1,17},{9,25},{17,1},{25,9},{2,18},{10... | collective-permute-start | bytes 786440 | tf_op jit(solution)/shard_map/ppermute | solution.py:110
  9.8 1.5 %collective-permute-start.1 = (bf16[128,1024]{1,0:T(8,128)(2,1)S(1)}, bf16[128,1024]{1,0:T(8,128)(2,1)S(1)}, u32[]{:S(2)}, u32[]{:S(2)}) collective-permute-start(bf16[128,1024]{1,0:T(8,128)(2,1)S(1)} %get-tuple-element.43.refs_2_), channel_id=1, source_target_pairs={{0,8},{8,0},{16,24},{24,16},{1,9},{9,1},{17,25},{25,17},{2,10},{10... | collective-permute-start | bytes 786440 | tf_op jit(solution)/shard_map/ppermute | solution.py:110
  13.2 3.2 %collective-permute-done.3.refs_0_ = bf16[64,1024]{1,0:T(8,128)(2,1)S(1)} collective-permute-done((bf16[64,1024]{1,0:T(8,128)(2,1)S(1)}, bf16[64,1024]{1,0:T(8,128)(2,1)S(1)}, u32[]{:S(2)}, u32[]{:S(2)}) %collective-permute-start.3) | collective-permute-done | bytes 131104 | tf_op jit(solution)/shard_map/ppermute | solution.py:110
  16.5 1.5 %collective-permute-start.8 = (bf16[64,1024]{1,0:T(8,128)(2,1)S(1)}, bf16[64,1024]{1,0:T(8,128)(2,1)S(1)}, u32[]{:S(2)}, u32[]{:S(2)}) collective-permute-start(bf16[64,1024]{1,0:T(8,128)(2,1)S(1)} %clips_z.3.refs_5_), channel_id=1, source_target_pairs={{0,8},{8,0},{16,24},{24,16},{1,9},{9,1},{17,25},{25,17},{2,10},{10... | collective-permute-start | bytes 393224 | tf_op jit(solution)/shard_map/ppermute | solution.py:110
  18.3 1.3 %collective-permute-done.5.refs_0_ = bf16[128,1024]{1,0:T(8,128)(2,1)S(1)} collective-permute-done((bf16[128,1024]{1,0:T(8,128)(2,1)S(1)}, bf16[128,1024]{1,0:T(8,128)(2,1)S(1)}, u32[]{:S(2)}, u32[]{:S(2)}) %collective-permute-start.5) | collective-permute-done | bytes 262176 | tf_op jit(solution)/shard_map/ppermute | solution.py:110
  19.6 1.5 %collective-permute-start.10 = (bf16[128,1024]{1,0:T(8,128)(2,1)S(1)}, bf16[128,1024]{1,0:T(8,128)(2,1)S(1)}, u32[]{:S(2)}, u32[]{:S(2)}) collective-permute-start(bf16[128,1024]{1,0:T(8,128)(2,1)S(1)} %captions_z.1.refs_0_), channel_id=1, source_target_pairs={{0,16},{8,24},{16,0},{24,8},{1,17},{9,25},{17,1},{25,9},{2,18},{10... | collective-permute-start | bytes 786440 | tf_op jit(solution)/shard_map/ppermute | solution.py:110
  21.1 1.2 %collective-permute-done.8.refs_0_ = bf16[64,1024]{1,0:T(8,128)(2,1)S(1)} collective-permute-done((bf16[64,1024]{1,0:T(8,128)(2,1)S(1)}, bf16[64,1024]{1,0:T(8,128)(2,1)S(1)}, u32[]{:S(2)}, u32[]{:S(2)}) %collective-permute-start.8) | collective-permute-done | bytes 131104 | tf_op jit(solution)/shard_map/ppermute | solution.py:110
  22.6 2.5 %early_pairs.1 = (bf16[768,1024]{1,0:T(8,128)(2,1)S(1)}, bf16[384,768]{1,0:T(8,128)(2,1)S(1)}, bf16[384,384]{1,0:T(8,128)(2,1)S(1)}, f32[1,384]{1,0:T(1,128)S(1)}) custom-call(f32[2,128]{1,0:T(2,128)S(1)} %consts.1.refs_1_, s32[1,1024]{1,0:T(1,128)S(1)} %get-tuple-element.41.labels, bf16[640,1024]{1,0:T(8,128)(2,1)S(1)} %near_blocks.1.N, ...), custom_call_target="tpu_custom_call" | custom-call | flops 905969664 | tf_op jit(solution)/shard_map/early_pairs/pallas_call | solution.py:28
  25.2 2.0 %middle_sums.1 = (bf16[1024,1024]{1,0:T(8,128)(2,1)S(1)}, bf16[768,512]{1,0:T(8,128)(2,1)S(1)}, f32[1,128]{1,0:T(1,128)S(1)}, f32[128,1024]{1,0:T(8,128)S(1)}, b...) custom-call(f32[2,128]{1,0:T(2,128)S(1)} %consts.1.refs_1_, ...), custom_call_target="tpu_custom_call" | custom-call | flops 1107296256 | tf_op jit(solution)/shard_map/middle_sums/pallas_call | solution.py:28
  27.6 1.4 %far_captions.1 = (f32[1,512]{1,0:T(1,128)S(1)}, bf16[128,512]{1,0:T(8,128)(2,1)S(1)}, bf16[64,1024]{1,0:T(8,128)(2,1)S(1)}, bf16[64,1024]{1,0:T(8,128)(2,1)S(1)}) custom-call(f32[2,128]{1,0:T(2,128)S(1)} %consts.1.refs_1_, s32[1,1024]{1,0:T(1,128)S(1)} %get-tuple-element.41.labels, bf16[1024,1024]{1,0:T(8,128)(2,1)S(1)} %get-tuple-element.51.VV, ...), custom_call_target="tpu_custom_call" | custom-call | flops 536870912 | tf_op jit(solution)/shard_map/far_captions/pallas_call | solution.py:28
  29.0 0.9 %collective-permute-start.12 = (bf16[64,1024]{1,0:T(8,128)(2,1)S(1)}, bf16[64,1024]{1,0:T(8,128)(2,1)S(1)}, u32[]{:S(2)}, u32[]{:S(2)}) collective-permute-start(bf16[64,1024]{1,0:T(8,128)(2,1)S(1)} %get-tuple-element.58), channel_id=1, source_target_pairs={{0,16},{8,24},{16,0},{24,8},{1,17},{9,25},{17,1},{25,9},{2,18},{10... | collective-permute-start | bytes 393224 | tf_op jit(solution)/shard_map/ppermute | solution.py:110
  29.9 1.2 %collective-permute-start.19 = (bf16[128,1024]{1,0:T(8,128)(2,1)S(1)}, bf16[128,1024]{1,0:T(8,128)(2,1)S(1)}, u32[]{:S(2)}, u32[]{:S(2)}) collective-permute-start(bf16[128,1024]{1,0:T(8,128)(2,1)S(1)} %get-tuple-element.72), channel_id=1, source_target_pairs={{0,16},{8,24},{16,0},{24,8},{1,17},{9,25},{17,1},{25,9},{2,18},{10... | collective-permute-start | bytes 786440 | tf_op jit(solution)/shard_map/ppermute | solution.py:110
  31.1 0.8 %collective-permute-start.20 = (bf16[64,1024]{1,0:T(8,128)(2,1)S(1)}, bf16[64,1024]{1,0:T(8,128)(2,1)S(1)}, u32[]{:S(2)}, u32[]{:S(2)}) collective-permute-start(bf16[64,1024]{1,0:T(8,128)(2,1)S(1)} %get-tuple-element.74), channel_id=1, source_target_pairs={{0,16},{8,24},{16,0},{24,8},{1,17},{9,25},{17,1},{25,9},{2,18},{10... | collective-permute-start | bytes 393224 | tf_op jit(solution)/shard_map/ppermute | solution.py:110
  31.9 1.2 %far_clips.1 = (bf16[256,1024]{1,0:T(8,128)(2,1)S(1)}, bf16[256,512]{1,0:T(8,128)(2,1)S(1)}, f32[1,512]{1,0:T(1,128)S(1)}, bf16[128,1024]{1,0:T(8,128)(2,1)S(1)}) custom-call(f32[2,128]{1,0:T(2,128)S(1)} %consts.1.refs_1_, s32[1,1024]{1,0:T(1,128)S(1)} %get-tuple-element.41.labels, bf16[1024,1024]{1,0:T(8,128)(2,1)S(1)} %get-tuple-element.51.VV, ...), custom_call_target="tpu_custom_call" | custom-call | flops 402653184 | tf_op jit(solution)/shard_map/far_clips/pallas_call | solution.py:28
  33.1 1.4 %collective-permute-start.14 = (bf16[128,1024]{1,0:T(8,128)(2,1)S(1)}, bf16[128,1024]{1,0:T(8,128)(2,1)S(1)}, u32[]{:S(2)}, u32[]{:S(2)}) collective-permute-start(bf16[128,1024]{1,0:T(8,128)(2,1)S(1)} %get-tuple-element.59.refs_1_), channel_id=1, source_target_pairs={{0,8},{8,0},{16,24},{24,16},{1,9},{9,1},{17,25},{25,17},{2,10},{10... | collective-permute-start | bytes 786440 | tf_op jit(solution)/shard_map/ppermute | solution.py:110
  34.5 0.9 %collective-permute-done.12.refs_0_ = bf16[64,1024]{1,0:T(8,128)(2,1)S(1)} collective-permute-done((bf16[64,1024]{1,0:T(8,128)(2,1)S(1)}, bf16[64,1024]{1,0:T(8,128)(2,1)S(1)}, u32[]{:S(2)}, u32[]{:S(2)}) %collective-permute-start.12) | collective-permute-done | bytes 131104 | tf_op jit(solution)/shard_map/ppermute | solution.py:110
  35.5 2.8 %collective-permute-start.13 = (bf16[64,1024]{1,0:T(8,128)(2,1)S(1)}, bf16[64,1024]{1,0:T(8,128)(2,1)S(1)}, u32[]{:S(2)}, u32[]{:S(2)}) collective-permute-start(bf16[64,1024]{1,0:T(8,128)(2,1)S(1)} %add_a.1.refs_1_), channel_id=1, source_target_pairs={{0,4},{1,5},{2,6},{3,7},{4,0},{5,1},{6,2},{7,3},{8,12},{9,13},{10,... | collective-permute-start | bytes 393224 | tf_op jit(solution)/shard_map/ppermute | solution.py:110
  38.3 4.8 %collective-permute-done.20.refs_0_ = bf16[64,1024]{1,0:T(8,128)(2,1)S(1)} collective-permute-done((bf16[64,1024]{1,0:T(8,128)(2,1)S(1)}, bf16[64,1024]{1,0:T(8,128)(2,1)S(1)}, u32[]{:S(2)}, u32[]{:S(2)}) %collective-permute-start.20) | collective-permute-done | bytes 131104 | tf_op jit(solution)/shard_map/ppermute | solution.py:110
  43.2 3.2 %collective-permute-start.21 = (bf16[64,1024]{1,0:T(8,128)(2,1)S(1)}, bf16[64,1024]{1,0:T(8,128)(2,1)S(1)}, u32[]{:S(2)}, u32[]{:S(2)}) collective-permute-start(bf16[64,1024]{1,0:T(8,128)(2,1)S(1)} %add_b.1), channel_id=1, source_target_pairs={{0,4},{1,5},{2,6},{3,7},{4,0},{5,1},{6,2},{7,3},{8,12},{9,13},{10,... | collective-permute-start | bytes 393224 | tf_op jit(solution)/shard_map/ppermute | solution.py:110
  46.3 1.0 %near_clips.1 = (f32[128,1024]{1,0:T(8,128)S(1)}, bf16[128,1024]{1,0:T(8,128)(2,1)S(1)}, f32[128,1024]{1,0:T(8,128)S(1)}) custom-call(bf16[768,1024]{1,0:T(8,128)(2,1)S(1)} %get-tuple-element.47.S1, bf16[256,1024]{1,0:T(8,128)(2,1)S(1)} %get-tuple-element.60.S2, bf16[768,512]{1,0:T(8,128)(2,1)S(1)} %get-tuple-element.54.G1, ...), custom_call_target="tpu_custom_call" | custom-call | flops 805306368 | tf_op jit(solution)/shard_map/near_clips/pallas_call | solution.py:28
  47.4 0.9 %collective-permute-start.17 = (bf16[128,1024]{1,0:T(8,128)(2,1)S(1)}, bf16[128,1024]{1,0:T(8,128)(2,1)S(1)}, u32[]{:S(2)}, u32[]{:S(2)}) collective-permute-start(bf16[128,1024]{1,0:T(8,128)(2,1)S(1)} %get-tuple-element.67), channel_id=1, source_target_pairs={{0,8},{8,0},{16,24},{24,16},{1,9},{9,1},{17,25},{25,17},{2,10},{10... | collective-permute-start | bytes 786440 | tf_op jit(solution)/shard_map/ppermute | solution.py:110
  48.3 0.7 %collective-permute-start.18 = (bf16[128,1024]{1,0:T(8,128)(2,1)S(1)}, bf16[128,1024]{1,0:T(8,128)(2,1)S(1)}, u32[]{:S(2)}, u32[]{:S(2)}) collective-permute-start(bf16[128,1024]{1,0:T(8,128)(2,1)S(1)} %add_clips.1.refs_1_), channel_id=1, source_target_pairs={{0,2},{1,3},{2,0},{3,1},{4,6},{5,7},{6,4},{7,5},{8,10},{9,11},{10,... | collective-permute-start | bytes 786440 | tf_op jit(solution)/shard_map/ppermute | solution.py:110
  49.0 0.7 %collective-permute-start.15 = (f32[2,128]{1,0:T(2,128)S(1)}, f32[2,128]{1,0:T(2,128)S(1)}, u32[]{:S(2)}, u32[]{:S(2)}) collective-permute-start(f32[2,128]{1,0:T(2,128)S(1)} %get-tuple-element.64), channel_id=1, source_target_pairs={{0,8},{8,0},{16,24},{24,16},{1,9},{9,1},{17,25},{25,17},{2,10},{10... | collective-permute-start | bytes 3080 | tf_op jit(solution)/shard_map/ppermute | solution.py:110
  49.7 2.9 %collective-permute-done.21.refs_0_ = bf16[64,1024]{1,0:T(8,128)(2,1)S(1)} collective-permute-done((bf16[64,1024]{1,0:T(8,128)(2,1)S(1)}, bf16[64,1024]{1,0:T(8,128)(2,1)S(1)}, u32[]{:S(2)}, u32[]{:S(2)}) %collective-permute-start.21) | collective-permute-done | bytes 131104 | tf_op jit(solution)/shard_map/ppermute | solution.py:110
  52.6 2.5 %collective-permute-done.17.refs_0_ = bf16[128,1024]{1,0:T(8,128)(2,1)S(1)} collective-permute-done((bf16[128,1024]{1,0:T(8,128)(2,1)S(1)}, bf16[128,1024]{1,0:T(8,128)(2,1)S(1)}, u32[]{:S(2)}, u32[]{:S(2)}) %collective-permute-start.17) | collective-permute-done | bytes 262176 | tf_op jit(solution)/shard_map/ppermute | solution.py:110
  55.1 1.1 %finish_captions.1 = f32[128,1024]{1,0:T(8,128)} custom-call(f32[2,128]{1,0:T(2,128)S(1)} %consts.1.refs_1_, f32[128,1024]{1,0:T(8,128)S(1)} %get-tuple-element.70.hat_ref, f32[128,1]{1,0:T(8,128)S(1)} %get-tuple-element.71.inverse_ref, f32[128,1024]{1,0:T(8,128)S(1)} %get-tuple-element.52.refs_1_.refs_0_, bf16[128,1024]{1,0:T(8,128)(2,1)S(1)} %captions_y.1.refs_1_, ...), custom_call_target="tpu_custom_call" | custom-call | tf_op jit(solution)/shard_map/finish_captions/pallas_call | solution.py:28
  56.2 0.7 %collective-permute-done.18.refs_0_ = bf16[128,1024]{1,0:T(8,128)(2,1)S(1)} collective-permute-done((bf16[128,1024]{1,0:T(8,128)(2,1)S(1)}, bf16[128,1024]{1,0:T(8,128)(2,1)S(1)}, u32[]{:S(2)}, u32[]{:S(2)}) %collective-permute-start.18) | collective-permute-done | bytes 262176 | tf_op jit(solution)/shard_map/ppermute | solution.py:110
  56.9 1.8 %collective-permute-done.16.refs_2_ = f32[1,128]{1,0:T(1,128)S(1)} collective-permute-done((f32[1,128]{1,0:T(1,128)S(1)}, f32[1,128]{1,0:T(1,128)S(1)}, u32[]{:S(2)}, u32[]{:S(2)}) %collective-permute-start.16) | collective-permute-done | bytes 544 | tf_op jit(solution)/shard_map/ppermute | solution.py:110
  58.7 1.1 %finish_clips.1 = (f32[128,1024]{1,0:T(8,128)}, f32[1,128]{1,0:T(1,128)}) custom-call(f32[2,128]{1,0:T(2,128)S(1)} %consts.1.refs_1_, f32[128,1024]{1,0:T(8,128)S(1)} %get-tuple-element.39.hat_ref, f32[128,1]{1,0:T(8,128)S(1)} %get-tuple-element.40.inverse_ref, f32[1,128]{1,0:T(1,128)S(1)} %get-tuple-element.63.refs_0_, ...), custom_call_target="tpu_custom_call" | custom-call | tf_op jit(solution)/shard_map/finish_clips/pallas_call | solution.py:28
  (42 shorter events, 2.2 us)
Async XLA Ops:
  2.2 10.5 %collective-permute-start.2 = (bf16[64,1024]{1,0:T(8,128)(2,1)S(1)}, bf16[64,1024]{1,0:T(8,128)(2,1)S(1)}, u32[]{:S(2)}, u32[]{:S(2)}) collective-permute-start(bf16[64,1024]{1,0:T(8,128)(2,1)S(1)} %get-tuple-element.44), channel_id=1, source_target_pairs={{0,2},{1,3},{2,0},{3,1},{4,6},{5,7},{6,4},{7,5},{8,10},{9,11},{10,... | collective-permute-start | bytes 393224 | tf_op jit(solution)/shard_map/ppermute | solution.py:110
  5.3 14.3 %collective-permute-start.5 = (bf16[128,1024]{1,0:T(8,128)(2,1)S(1)}, bf16[128,1024]{1,0:T(8,128)(2,1)S(1)}, u32[]{:S(2)}, u32[]{:S(2)}) collective-permute-start(bf16[128,1024]{1,0:T(8,128)(2,1)S(1)} %get-tuple-element.42.refs_0_), channel_id=1, source_target_pairs={{0,4},{1,5},{2,6},{3,7},{4,0},{5,1},{6,2},{7,3},{8,12},{9,13},{10,... | collective-permute-start | bytes 786440 | tf_op jit(solution)/shard_map/ppermute | solution.py:110
  7.8 10.3 %collective-permute-start = (bf16[128,1024]{1,0:T(8,128)(2,1)S(1)}, bf16[128,1024]{1,0:T(8,128)(2,1)S(1)}, u32[]{:S(2)}, u32[]{:S(2)}) collective-permute-start(bf16[128,1024]{1,0:T(8,128)(2,1)S(1)} %get-tuple-element.42.refs_0_), channel_id=1, source_target_pairs={{0,16},{8,24},{16,0},{24,8},{1,17},{9,25},{17,1},{25,9},{2,18},{10... | collective-permute-start | bytes 786440 | tf_op jit(solution)/shard_map/ppermute | solution.py:110
  9.4 7.1 %collective-permute-start.3 = (bf16[64,1024]{1,0:T(8,128)(2,1)S(1)}, bf16[64,1024]{1,0:T(8,128)(2,1)S(1)}, u32[]{:S(2)}, u32[]{:S(2)}) collective-permute-start(bf16[64,1024]{1,0:T(8,128)(2,1)S(1)} %get-tuple-element.45), channel_id=1, source_target_pairs={{0,2},{1,3},{2,0},{3,1},{4,6},{5,7},{6,4},{7,5},{8,10},{9,11},{10,... | collective-permute-start | bytes 393224 | tf_op jit(solution)/shard_map/ppermute | solution.py:110
  9.8 8.3 %collective-permute-start.1 = (bf16[128,1024]{1,0:T(8,128)(2,1)S(1)}, bf16[128,1024]{1,0:T(8,128)(2,1)S(1)}, u32[]{:S(2)}, u32[]{:S(2)}) collective-permute-start(bf16[128,1024]{1,0:T(8,128)(2,1)S(1)} %get-tuple-element.43.refs_2_), channel_id=1, source_target_pairs={{0,8},{8,0},{16,24},{24,16},{1,9},{9,1},{17,25},{25,17},{2,10},{10... | collective-permute-start | bytes 786440 | tf_op jit(solution)/shard_map/ppermute | solution.py:110
  12.6 8.5 %collective-permute-start.7 = (bf16[64,1024]{1,0:T(8,128)(2,1)S(1)}, bf16[64,1024]{1,0:T(8,128)(2,1)S(1)}, u32[]{:S(2)}, u32[]{:S(2)}) collective-permute-start(bf16[64,1024]{1,0:T(8,128)(2,1)S(1)} %clips_z.2.refs_4_), channel_id=1, source_target_pairs={{0,8},{8,0},{16,24},{24,16},{1,9},{9,1},{17,25},{25,17},{2,10},{10... | collective-permute-start | bytes 393224 | tf_op jit(solution)/shard_map/ppermute | solution.py:110
  16.5 5.9 %collective-permute-start.8 = (bf16[64,1024]{1,0:T(8,128)(2,1)S(1)}, bf16[64,1024]{1,0:T(8,128)(2,1)S(1)}, u32[]{:S(2)}, u32[]{:S(2)}) collective-permute-start(bf16[64,1024]{1,0:T(8,128)(2,1)S(1)} %clips_z.3.refs_5_), channel_id=1, source_target_pairs={{0,8},{8,0},{16,24},{24,16},{1,9},{9,1},{17,25},{25,17},{2,10},{10... | collective-permute-start | bytes 393224 | tf_op jit(solution)/shard_map/ppermute | solution.py:110
  18.2 4.2 %collective-permute-start.4 = (bf16[640,1024]{1,0:T(8,128)(2,1)S(1)}, bf16[640,1024]{1,0:T(8,128)(2,1)S(1)}, u32[]{:S(2)}, u32[]{:S(2)}) collective-permute-start(bf16[640,1024]{1,0:T(8,128)(2,1)S(1)} %near_blocks.1.N), channel_id=1, source_target_pairs={{0,1},{1,0},{2,3},{3,2},{4,5},{5,4},{6,7},{7,6},{8,9},{9,8},{10,11... | collective-permute-start | bytes 3932168 | tf_op jit(solution)/shard_map/ppermute | solution.py:110
  19.6 7.6 %collective-permute-start.10 = (bf16[128,1024]{1,0:T(8,128)(2,1)S(1)}, bf16[128,1024]{1,0:T(8,128)(2,1)S(1)}, u32[]{:S(2)}, u32[]{:S(2)}) collective-permute-start(bf16[128,1024]{1,0:T(8,128)(2,1)S(1)} %captions_z.1.refs_0_), channel_id=1, source_target_pairs={{0,16},{8,24},{16,0},{24,8},{1,17},{9,25},{17,1},{25,9},{2,18},{10... | collective-permute-start | bytes 786440 | tf_op jit(solution)/shard_map/ppermute | solution.py:110
  21.1 1.5 %collective-permute-start.6 = (bf16[128,1024]{1,0:T(8,128)(2,1)S(1)}, bf16[128,1024]{1,0:T(8,128)(2,1)S(1)}, u32[]{:S(2)}, u32[]{:S(2)}) collective-permute-start(bf16[128,1024]{1,0:T(8,128)(2,1)S(1)} %captions_z.1.refs_0_), channel_id=1, source_target_pairs={{0,1},{1,0},{2,3},{3,2},{4,5},{5,4},{6,7},{7,6},{8,9},{9,8},{10,11... | collective-permute-start | bytes 786440 | tf_op jit(solution)/shard_map/ppermute | solution.py:110
  22.4 2.8 %collective-permute-start.9 = (bf16[128,1024]{1,0:T(8,128)(2,1)S(1)}, bf16[128,1024]{1,0:T(8,128)(2,1)S(1)}, u32[]{:S(2)}, u32[]{:S(2)}) collective-permute-start(bf16[128,1024]{1,0:T(8,128)(2,1)S(1)} %diagonal_clips.1.vd), channel_id=1, source_target_pairs={{0,1},{1,0},{2,3},{3,2},{4,5},{5,4},{6,7},{7,6},{8,9},{9,8},{10,11... | collective-permute-start | bytes 786440 | tf_op jit(solution)/shard_map/ppermute | solution.py:110
  27.2 4.8 %collective-permute-start.11 = (bf16[128,1024]{1,0:T(8,128)(2,1)S(1)}, bf16[128,1024]{1,0:T(8,128)(2,1)S(1)}, u32[]{:S(2)}, u32[]{:S(2)}) collective-permute-start(bf16[128,1024]{1,0:T(8,128)(2,1)S(1)} %captions_d.1.refs_0_), channel_id=1, source_target_pairs={{0,1},{1,0},{2,3},{3,2},{4,5},{5,4},{6,7},{7,6},{8,9},{9,8},{10,11... | collective-permute-start | bytes 786440 | tf_op jit(solution)/shard_map/ppermute | solution.py:110
  29.0 6.4 %collective-permute-start.12 = (bf16[64,1024]{1,0:T(8,128)(2,1)S(1)}, bf16[64,1024]{1,0:T(8,128)(2,1)S(1)}, u32[]{:S(2)}, u32[]{:S(2)}) collective-permute-start(bf16[64,1024]{1,0:T(8,128)(2,1)S(1)} %get-tuple-element.58), channel_id=1, source_target_pairs={{0,16},{8,24},{16,0},{24,8},{1,17},{9,25},{17,1},{25,9},{2,18},{10... | collective-permute-start | bytes 393224 | tf_op jit(solution)/shard_map/ppermute | solution.py:110
  29.9 22.7 %collective-permute-start.19 = (bf16[128,1024]{1,0:T(8,128)(2,1)S(1)}, bf16[128,1024]{1,0:T(8,128)(2,1)S(1)}, u32[]{:S(2)}, u32[]{:S(2)}) collective-permute-start(bf16[128,1024]{1,0:T(8,128)(2,1)S(1)} %get-tuple-element.72), channel_id=1, source_target_pairs={{0,16},{8,24},{16,0},{24,8},{1,17},{9,25},{17,1},{25,9},{2,18},{10... | collective-permute-start | bytes 786440 | tf_op jit(solution)/shard_map/ppermute | solution.py:110
  31.1 12.0 %collective-permute-start.20 = (bf16[64,1024]{1,0:T(8,128)(2,1)S(1)}, bf16[64,1024]{1,0:T(8,128)(2,1)S(1)}, u32[]{:S(2)}, u32[]{:S(2)}) collective-permute-start(bf16[64,1024]{1,0:T(8,128)(2,1)S(1)} %get-tuple-element.74), channel_id=1, source_target_pairs={{0,16},{8,24},{16,0},{24,8},{1,17},{9,25},{17,1},{25,9},{2,18},{10... | collective-permute-start | bytes 393224 | tf_op jit(solution)/shard_map/ppermute | solution.py:110
  33.1 15.1 %collective-permute-start.14 = (bf16[128,1024]{1,0:T(8,128)(2,1)S(1)}, bf16[128,1024]{1,0:T(8,128)(2,1)S(1)}, u32[]{:S(2)}, u32[]{:S(2)}) collective-permute-start(bf16[128,1024]{1,0:T(8,128)(2,1)S(1)} %get-tuple-element.59.refs_1_), channel_id=1, source_target_pairs={{0,8},{8,0},{16,24},{24,16},{1,9},{9,1},{17,25},{25,17},{2,10},{10... | collective-permute-start | bytes 786440 | tf_op jit(solution)/shard_map/ppermute | solution.py:110
  35.5 13.5 %collective-permute-start.13 = (bf16[64,1024]{1,0:T(8,128)(2,1)S(1)}, bf16[64,1024]{1,0:T(8,128)(2,1)S(1)}, u32[]{:S(2)}, u32[]{:S(2)}) collective-permute-start(bf16[64,1024]{1,0:T(8,128)(2,1)S(1)} %add_a.1.refs_1_), channel_id=1, source_target_pairs={{0,4},{1,5},{2,6},{3,7},{4,0},{5,1},{6,2},{7,3},{8,12},{9,13},{10,... | collective-permute-start | bytes 393224 | tf_op jit(solution)/shard_map/ppermute | solution.py:110
  43.2 9.5 %collective-permute-start.21 = (bf16[64,1024]{1,0:T(8,128)(2,1)S(1)}, bf16[64,1024]{1,0:T(8,128)(2,1)S(1)}, u32[]{:S(2)}, u32[]{:S(2)}) collective-permute-start(bf16[64,1024]{1,0:T(8,128)(2,1)S(1)} %add_b.1), channel_id=1, source_target_pairs={{0,4},{1,5},{2,6},{3,7},{4,0},{5,1},{6,2},{7,3},{8,12},{9,13},{10,... | collective-permute-start | bytes 393224 | tf_op jit(solution)/shard_map/ppermute | solution.py:110
  47.4 7.7 %collective-permute-start.17 = (bf16[128,1024]{1,0:T(8,128)(2,1)S(1)}, bf16[128,1024]{1,0:T(8,128)(2,1)S(1)}, u32[]{:S(2)}, u32[]{:S(2)}) collective-permute-start(bf16[128,1024]{1,0:T(8,128)(2,1)S(1)} %get-tuple-element.67), channel_id=1, source_target_pairs={{0,8},{8,0},{16,24},{24,16},{1,9},{9,1},{17,25},{25,17},{2,10},{10... | collective-permute-start | bytes 786440 | tf_op jit(solution)/shard_map/ppermute | solution.py:110
  48.3 8.6 %collective-permute-start.18 = (bf16[128,1024]{1,0:T(8,128)(2,1)S(1)}, bf16[128,1024]{1,0:T(8,128)(2,1)S(1)}, u32[]{:S(2)}, u32[]{:S(2)}) collective-permute-start(bf16[128,1024]{1,0:T(8,128)(2,1)S(1)} %add_clips.1.refs_1_), channel_id=1, source_target_pairs={{0,2},{1,3},{2,0},{3,1},{4,6},{5,7},{6,4},{7,5},{8,10},{9,11},{10,... | collective-permute-start | bytes 786440 | tf_op jit(solution)/shard_map/ppermute | solution.py:110
  49.0 6.1 %collective-permute-start.15 = (f32[2,128]{1,0:T(2,128)S(1)}, f32[2,128]{1,0:T(2,128)S(1)}, u32[]{:S(2)}, u32[]{:S(2)}) collective-permute-start(f32[2,128]{1,0:T(2,128)S(1)} %get-tuple-element.64), channel_id=1, source_target_pairs={{0,8},{8,0},{16,24},{24,16},{1,9},{9,1},{17,25},{25,17},{2,10},{10... | collective-permute-start | bytes 3080 | tf_op jit(solution)/shard_map/ppermute | solution.py:110
  55.1 3.5 %collective-permute-start.16 = (f32[1,128]{1,0:T(1,128)S(1)}, f32[1,128]{1,0:T(1,128)S(1)}, u32[]{:S(2)}, u32[]{:S(2)}) collective-permute-start(f32[1,128]{1,0:T(1,128)S(1)} %add_loss.1.refs_4_), channel_id=1, source_target_pairs={{0,2},{1,3},{2,0},{3,1},{4,6},{5,7},{6,4},{7,5},{8,10},{9,11},{10,... | collective-permute-start | bytes 1544 | tf_op jit(solution)/shard_map/ppermute | solution.py:110

commit v6 on v5

--- a/solution.py
+++ b/solution.py
@@ -188,8 +188,8 @@
 
         return call(name, join_kernel, [vm((sum(b.shape[0] for b in blocks), width))], blocks)[0]
 
-    v_z = [hand_on("clips_z", swap(b, "col", 2), flops=LONG) for b in (va, vb)]
-    c_z = [hand_on("captions_z", swap(c16, "col", 4 * s), consts, flops=1 * LONG) for s in range(1, Z)]
+    v_z = [hand_on("clips_z", swap(b, "col", 2), flops=n * LONG // 4) for b, n in ((va, 4), (vb, 24))]
+    c_z = [hand_on("captions_z", swap(c16, "col", 4 * s), consts, flops=4 * LONG // 4) for s in range(1, Z)]
     c_y = [swap(c16, "row", 2 * t) for t in range(1, Y)]
     v_x = swap(v16, "row", 1)
     v_d = [hand_on("clips_d", swap(b, "row", 1), flops=2 * LONG // 4) for b in v_z]
@@ -289,7 +289,28 @@
     )
     far_v = swap(dv_d, "row", 1)
 
-    def near_clips_kernel(S1, S2, G1, G2, dv0, dvx, dvz):
+    def add_kernel(*refs):
+        total = refs[0][...].astype(F32)
+        for ref in refs[1:-1]:
+            total += ref[...].astype(F32)
+        refs[-1][...] = total.astype(BF16)
+
+    def add(name, *terms):
+        return call(name, add_kernel, [vm(terms[0].shape)], terms)[0]
+
+    def captions_back(h, *after):
+        sums = []
+        for s in range(Z - 1):
+            far = [
+                hand_on("far_" + "ab"[h], swap(dcd[2 * (s * (Y - 1) + t - 1) + h], "row", 2 * t), *after, flops=(4, 0)[h] * LONG // 4)
+                for t in range(1, Y)
+            ]
+            sums.append(add("add_" + "ab"[h], dcz[2 * s + h], *far))
+        return sums, [swap(sums[s], "col", 4 * (s + 1)) for s in range(Z - 1)]
+
+    sums_a, got_a = captions_back(0, dv_d)
+    dcd = [hand_on("far_b", b, dv_d) if i % 2 else b for i, b in enumerate(dcd)]
+    def near_clips_kernel(S1, S2, G1, G2, after, dv0, dvx, dvz):
         for i in range(width // CHUNK):
             cols = pl.ds(i * CHUNK, CHUNK)
             part = dot_tn(G1[:, :n3], S1[:, cols]) + dot_tn(G2[:, :n3], S2[:, cols])
@@ -297,38 +318,19 @@
                 ref[:, cols] = part[j * rows : (j + 1) * rows].astype(ref.dtype)
 
     dv0, dvx, dvz = call(
-        "near_clips", near_clips_kernel, [vm(mat, F32), vm(mat), vm(mat, F32)], [S1, S2, G1, G2],
+        "near_clips", near_clips_kernel, [vm(mat, F32), vm(mat), vm(mat, F32)], [S1, S2, G1, G2, sums_a[0]],
         flops=2 * 24 * rows * rows * width, limit=limit,
     )
 
-    def add_kernel(*refs):
-        total = refs[0][...].astype(F32)
-        for ref in refs[1:-1]:
-            total += ref[...].astype(F32)
-        refs[-1][...] = total.astype(BF16)
-
-    def add(name, *terms):
-        return call(name, add_kernel, [vm(terms[0].shape)], terms)[0]
-
-    def captions_back(h, *after):
-        sums = []
-        for s in range(Z - 1):
-            far = [
-                hand_on("far_" + "ab"[h], swap(dcd[2 * (s * (Y - 1) + t - 1) + h], "row", 2 * t), *after, flops=LONG)
-                for t in range(1, Y)
-            ]
-            sums.append(add("add_" + "ab"[h], dcz[2 * s + h], *far))
-        return sums, [swap(sums[s], "col", 4 * (s + 1)) for s in range(Z - 1)]
-
-    sums_a, got_a = captions_back(0, dv_d)
-    sums_b, got_b = captions_back(1, sums_a[0])
+    sums_b, got_b = captions_back(1, dvz)
     sum_v = add("add_clips", dvz, far_v)
     got_z = hand_on("clips_back", swap(sum_v, "col", 2), flops=3 * LONG)
     got_h = [[hand_on("captions_back", b, sum_v, flops=3 * LONG) for b in got] for got in (got_a, got_b)]
+    dcy = [hand_on("near_y", b, *sums_b) for b in dcy]
     got_y = [hand_on("captions_y", swap(dcy[t - 1], "row", 2 * t), sum_v, flops=LONG) for t in range(1, Y)]
-    got_x = hand_on("clips_x", swap(dvx, "row", 1), sum_v, flops=LONG)
-
-    def losses_kernel(l_a, l_m, l_c, l_d, *refs):
+    got_x = hand_on("clips_x", swap(dvx, "row", 1), sum_v, flops=4 * LONG)
+
+    def losses_kernel(l_a, l_m, l_c, l_d, after, *refs):
         loss_0, loss_x, loss_z = refs[-3:]
         total = l_c[...] + l_d[...]
         own = total[:, :n3] + l_a[...]
@@ -337,15 +339,15 @@
         loss_x[1:2, :] = total[:, n3:] + l_m[...]
         loss_z[...] = own[:, 2 * n1 :]
 
-    def add_loss_kernel(loss_z, arrived, out):
+    def add_loss_kernel(loss_z, arrived, got, sum_v, out):
         out[...] = loss_z[...] + arrived[1:2, :]
 
     loss_0, loss_x, loss_z = call(
         "losses", losses_kernel, [vm((1, n1), F32), vm((2, n1), F32), vm((1, n1), F32)],
-        [loss_a, loss_m, loss_c, loss_d, got_a[0], sum_v],
-    )
-    far_loss = swap(loss_x, "row", 1)
-    (sum_loss,) = call("add_loss", add_loss_kernel, [vm((1, n1), F32)], [loss_z, far_loss])
+        [loss_a, loss_m, loss_c, loss_d, sums_a[0]],
+    )
+    far_loss = hand_on("losses_x", swap(loss_x, "row", 1), *sums_b)
+    (sum_loss,) = call("add_loss", add_loss_kernel, [vm((1, n1), F32)], [loss_z, far_loss, got_a[0], sum_v])
     got_loss = swap(sum_loss, "col", 2)
 
     def finish(name, losses, consts, hat, inverse, own, whole, halves, *after):

time: 59.9 us -> 58.1 us (0.970)
  waiting for transfers between devices: 19.7 us -> 16.2 us
  starting transfers between devices: 25.8 us -> 27.6 us
    ppermute x22, waiting for transfers between devices: 19.7 us -> 16.2 us  [swap(): return lax.ppermute(value, axis, [(i, i ^ bits) for i in range(size)])]
    ppermute x22, starting transfers between devices: 25.8 us -> 27.6 us  [swap(): return lax.ppermute(value, axis, [(i, i ^ bits) for i in range(size)])]
    pallas_call x30 -> x33, Pallas kernels: 12.1 us -> 12.1 us  [call(): pl.pallas_call(kernel, name=name, out_shape=out_shape, in_specs=[SPECS[sp...]
  transfers between devices with their start and end apart: 22 -> 22, of which waited for: 11 -> 12; matrix products, arithmetic and copies ran while one was open for 0% -> 0% of each run, Pallas kernels for 16% -> 16%
where the time goes in v6:
time: 58.1 us; the launch traced here: 58 us
  starting transfers between devices  27.6 us (48%)
  waiting for transfers between devices  16.2 us (28%)
  Pallas kernels  12.1 us (21%)
  between operations  2.12 us (4%)
    ppermute x22, starting transfers between devices, swap(): return lax.ppermute(value, axis, [(i, i ^ bits) for i in range(size)])  27.6 us
    ppermute x22, waiting for transfers between devices, swap(): return lax.ppermute(value, axis, [(i, i ^ bits) for i in range(size)])  16.2 us
    pallas_call x33, Pallas kernels, call(): pl.pallas_call(kernel, name=name, out_shape=out_shape, in_specs=[SPECS[sp...  12.1 us
  transfers between devices with their start and end apart: 22, of which 12 were waited for; matrix products, arithmetic and copies ran while one was open for 0% of the time, Pallas kernels for 16%

profile of v6, /device:TPU:0, one launch (start us, length us, event | category | flops | bytes accessed | tf_op | source)
XLA Modules:
  0.0 58.0 jit_solution(1917017031156476241)
XLA Ops:
  0.6 1.5 %normalize.1 = (bf16[128,1024]{1,0:T(8,128)(2,1)S(1)}, bf16[128,1024]{1,0:T(8,128)(2,1)S(1)}, bf16[64,1024]{1,0:T(8,128)(2,1)S(1)}, bf16[64,1024]{1,0:T(8,128)(2...) custom-call(f32[128,1024]{1,0:T(8,128)} %film.1, ...), custom_call_target="tpu_custom_call" | custom-call | tf_op jit(solution)/shard_map/normalize/pallas_call | solution.py:28
  2.2 3.1 %collective-permute-start.2 = (bf16[64,1024]{1,0:T(8,128)(2,1)S(1)}, bf16[64,1024]{1,0:T(8,128)(2,1)S(1)}, u32[]{:S(2)}, u32[]{:S(2)}) collective-permute-start(bf16[64,1024]{1,0:T(8,128)(2,1)S(1)} %get-tuple-element.44), channel_id=1, source_target_pairs={{0,2},{1,3},{2,0},{3,1},{4,6},{5,7},{6,4},{7,5},{8,10},{9,11},{10,... | collective-permute-start | bytes 393224 | tf_op jit(solution)/shard_map/ppermute | solution.py:110
  5.3 2.6 %collective-permute-start.5 = (bf16[128,1024]{1,0:T(8,128)(2,1)S(1)}, bf16[128,1024]{1,0:T(8,128)(2,1)S(1)}, u32[]{:S(2)}, u32[]{:S(2)}) collective-permute-start(bf16[128,1024]{1,0:T(8,128)(2,1)S(1)} %get-tuple-element.42.refs_0_), channel_id=1, source_target_pairs={{0,4},{1,5},{2,6},{3,7},{4,0},{5,1},{6,2},{7,3},{8,12},{9,13},{10,... | collective-permute-start | bytes 786440 | tf_op jit(solution)/shard_map/ppermute | solution.py:110
  7.8 1.5 %collective-permute-start = (bf16[128,1024]{1,0:T(8,128)(2,1)S(1)}, bf16[128,1024]{1,0:T(8,128)(2,1)S(1)}, u32[]{:S(2)}, u32[]{:S(2)}) collective-permute-start(bf16[128,1024]{1,0:T(8,128)(2,1)S(1)} %get-tuple-element.42.refs_0_), channel_id=1, source_target_pairs={{0,16},{8,24},{16,0},{24,8},{1,17},{9,25},{17,1},{25,9},{2,18},{10... | collective-permute-start | bytes 786440 | tf_op jit(solution)/shard_map/ppermute | solution.py:110
  9.8 1.5 %collective-permute-start.1 = (bf16[128,1024]{1,0:T(8,128)(2,1)S(1)}, bf16[128,1024]{1,0:T(8,128)(2,1)S(1)}, u32[]{:S(2)}, u32[]{:S(2)}) collective-permute-start(bf16[128,1024]{1,0:T(8,128)(2,1)S(1)} %get-tuple-element.43.refs_2_), channel_id=1, source_target_pairs={{0,8},{8,0},{16,24},{24,16},{1,9},{9,1},{17,25},{25,17},{2,10},{10... | collective-permute-start | bytes 786440 | tf_op jit(solution)/shard_map/ppermute | solution.py:110
  12.6 0.6 %collective-permute-start.7 = (bf16[64,1024]{1,0:T(8,128)(2,1)S(1)}, bf16[64,1024]{1,0:T(8,128)(2,1)S(1)}, u32[]{:S(2)}, u32[]{:S(2)}) collective-permute-start(bf16[64,1024]{1,0:T(8,128)(2,1)S(1)} %clips_z.2.refs_4_), channel_id=1, source_target_pairs={{0,8},{8,0},{16,24},{24,16},{1,9},{9,1},{17,25},{25,17},{2,10},{10... | collective-permute-start | bytes 393224 | tf_op jit(solution)/shard_map/ppermute | solution.py:110
  13.2 3.2 %collective-permute-done.3.refs_0_ = bf16[64,1024]{1,0:T(8,128)(2,1)S(1)} collective-permute-done((bf16[64,1024]{1,0:T(8,128)(2,1)S(1)}, bf16[64,1024]{1,0:T(8,128)(2,1)S(1)}, u32[]{:S(2)}, u32[]{:S(2)}) %collective-permute-start.3) | collective-permute-done | bytes 131104 | tf_op jit(solution)/shard_map/ppermute | solution.py:110
  16.5 1.5 %collective-permute-start.8 = (bf16[64,1024]{1,0:T(8,128)(2,1)S(1)}, bf16[64,1024]{1,0:T(8,128)(2,1)S(1)}, u32[]{:S(2)}, u32[]{:S(2)}) collective-permute-start(bf16[64,1024]{1,0:T(8,128)(2,1)S(1)} %clips_z.3.refs_5_), channel_id=1, source_target_pairs={{0,8},{8,0},{16,24},{24,16},{1,9},{9,1},{17,25},{25,17},{2,10},{10... | collective-permute-start | bytes 393224 | tf_op jit(solution)/shard_map/ppermute | solution.py:110
  18.3 1.3 %collective-permute-done.5.refs_0_ = bf16[128,1024]{1,0:T(8,128)(2,1)S(1)} collective-permute-done((bf16[128,1024]{1,0:T(8,128)(2,1)S(1)}, bf16[128,1024]{1,0:T(8,128)(2,1)S(1)}, u32[]{:S(2)}, u32[]{:S(2)}) %collective-permute-start.5) | collective-permute-done | bytes 262176 | tf_op jit(solution)/shard_map/ppermute | solution.py:110
  19.6 1.5 %collective-permute-start.10 = (bf16[128,1024]{1,0:T(8,128)(2,1)S(1)}, bf16[128,1024]{1,0:T(8,128)(2,1)S(1)}, u32[]{:S(2)}, u32[]{:S(2)}) collective-permute-start(bf16[128,1024]{1,0:T(8,128)(2,1)S(1)} %captions_z.1.refs_0_), channel_id=1, source_target_pairs={{0,16},{8,24},{16,0},{24,8},{1,17},{9,25},{17,1},{25,9},{2,18},{10... | collective-permute-start | bytes 786440 | tf_op jit(solution)/shard_map/ppermute | solution.py:110
  21.1 1.2 %collective-permute-done.8.refs_0_ = bf16[64,1024]{1,0:T(8,128)(2,1)S(1)} collective-permute-done((bf16[64,1024]{1,0:T(8,128)(2,1)S(1)}, bf16[64,1024]{1,0:T(8,128)(2,1)S(1)}, u32[]{:S(2)}, u32[]{:S(2)}) %collective-permute-start.8) | collective-permute-done | bytes 131104 | tf_op jit(solution)/shard_map/ppermute | solution.py:110
  22.6 2.5 %early_pairs.1 = (bf16[768,1024]{1,0:T(8,128)(2,1)S(1)}, bf16[384,768]{1,0:T(8,128)(2,1)S(1)}, bf16[384,384]{1,0:T(8,128)(2,1)S(1)}, f32[1,384]{1,0:T(1,128)S(1)}) custom-call(f32[2,128]{1,0:T(2,128)S(1)} %consts.1.refs_1_, s32[1,1024]{1,0:T(1,128)S(1)} %get-tuple-element.41.labels, bf16[640,1024]{1,0:T(8,128)(2,1)S(1)} %near_blocks.1.N, ...), custom_call_target="tpu_custom_call" | custom-call | flops 905969664 | tf_op jit(solution)/shard_map/early_pairs/pallas_call | solution.py:28
  25.2 2.0 %middle_sums.1 = (bf16[1024,1024]{1,0:T(8,128)(2,1)S(1)}, bf16[768,512]{1,0:T(8,128)(2,1)S(1)}, f32[1,128]{1,0:T(1,128)S(1)}, f32[128,1024]{1,0:T(8,128)S(1)}, b...) custom-call(f32[2,128]{1,0:T(2,128)S(1)} %consts.1.refs_1_, ...), custom_call_target="tpu_custom_call" | custom-call | flops 1107296256 | tf_op jit(solution)/shard_map/middle_sums/pallas_call | solution.py:28
  27.6 1.4 %far_captions.1 = (f32[1,512]{1,0:T(1,128)S(1)}, bf16[128,512]{1,0:T(8,128)(2,1)S(1)}, bf16[64,1024]{1,0:T(8,128)(2,1)S(1)}, bf16[64,1024]{1,0:T(8,128)(2,1)S(1)}) custom-call(f32[2,128]{1,0:T(2,128)S(1)} %consts.1.refs_1_, s32[1,1024]{1,0:T(1,128)S(1)} %get-tuple-element.41.labels, bf16[1024,1024]{1,0:T(8,128)(2,1)S(1)} %get-tuple-element.51.VV, ...), custom_call_target="tpu_custom_call" | custom-call | flops 536870912 | tf_op jit(solution)/shard_map/far_captions/pallas_call | solution.py:28
  29.0 0.9 %collective-permute-start.12 = (bf16[64,1024]{1,0:T(8,128)(2,1)S(1)}, bf16[64,1024]{1,0:T(8,128)(2,1)S(1)}, u32[]{:S(2)}, u32[]{:S(2)}) collective-permute-start(bf16[64,1024]{1,0:T(8,128)(2,1)S(1)} %get-tuple-element.58), channel_id=1, source_target_pairs={{0,16},{8,24},{16,0},{24,8},{1,17},{9,25},{17,1},{25,9},{2,18},{10... | collective-permute-start | bytes 393224 | tf_op jit(solution)/shard_map/ppermute | solution.py:110
  29.9 1.2 %far_clips.1 = (bf16[256,1024]{1,0:T(8,128)(2,1)S(1)}, bf16[256,512]{1,0:T(8,128)(2,1)S(1)}, f32[1,512]{1,0:T(1,128)S(1)}, bf16[128,1024]{1,0:T(8,128)(2,1)S(1)}) custom-call(f32[2,128]{1,0:T(2,128)S(1)} %consts.1.refs_1_, s32[1,1024]{1,0:T(1,128)S(1)} %get-tuple-element.41.labels, bf16[1024,1024]{1,0:T(8,128)(2,1)S(1)} %get-tuple-element.51.VV, ...), custom_call_target="tpu_custom_call" | custom-call | flops 402653184 | tf_op jit(solution)/shard_map/far_clips/pallas_call | solution.py:28
  31.1 1.4 %collective-permute-start.16 = (bf16[128,1024]{1,0:T(8,128)(2,1)S(1)}, bf16[128,1024]{1,0:T(8,128)(2,1)S(1)}, u32[]{:S(2)}, u32[]{:S(2)}) collective-permute-start(bf16[128,1024]{1,0:T(8,128)(2,1)S(1)} %get-tuple-element.59.refs_1_), channel_id=1, source_target_pairs={{0,8},{8,0},{16,24},{24,16},{1,9},{9,1},{17,25},{25,17},{2,10},{10... | collective-permute-start | bytes 786440 | tf_op jit(solution)/shard_map/ppermute | solution.py:110
  32.4 2.2 %collective-permute-done.12.refs_0_ = bf16[64,1024]{1,0:T(8,128)(2,1)S(1)} collective-permute-done((bf16[64,1024]{1,0:T(8,128)(2,1)S(1)}, bf16[64,1024]{1,0:T(8,128)(2,1)S(1)}, u32[]{:S(2)}, u32[]{:S(2)}) %collective-permute-start.12) | collective-permute-done | bytes 131104 | tf_op jit(solution)/shard_map/ppermute | solution.py:110
  34.7 1.0 %near_clips.1 = (f32[128,1024]{1,0:T(8,128)S(1)}, bf16[128,1024]{1,0:T(8,128)(2,1)S(1)}, f32[128,1024]{1,0:T(8,128)S(1)}) custom-call(bf16[768,1024]{1,0:T(8,128)(2,1)S(1)} %get-tuple-element.47.S1, bf16[256,1024]{1,0:T(8,128)(2,1)S(1)} %get-tuple-element.64.S2, bf16[768,512]{1,0:T(8,128)(2,1)S(1)} %get-tuple-element.54.G1, ...), custom_call_target="tpu_custom_call" | custom-call | flops 805306368 | tf_op jit(solution)/shard_map/near_clips/pallas_call | solution.py:28
  35.7 1.6 %collective-permute-start.18 = (bf16[128,1024]{1,0:T(8,128)(2,1)S(1)}, bf16[128,1024]{1,0:T(8,128)(2,1)S(1)}, u32[]{:S(2)}, u32[]{:S(2)}) collective-permute-start(bf16[128,1024]{1,0:T(8,128)(2,1)S(1)} %get-tuple-element.69), channel_id=1, source_target_pairs={{0,8},{8,0},{16,24},{24,16},{1,9},{9,1},{17,25},{25,17},{2,10},{10... | collective-permute-start | bytes 786440 | tf_op jit(solution)/shard_map/ppermute | solution.py:110
  37.3 0.8 %collective-permute-start.14 = (bf16[64,1024]{1,0:T(8,128)(2,1)S(1)}, bf16[64,1024]{1,0:T(8,128)(2,1)S(1)}, u32[]{:S(2)}, u32[]{:S(2)}) collective-permute-start(bf16[64,1024]{1,0:T(8,128)(2,1)S(1)} %far_b.2), channel_id=1, source_target_pairs={{0,16},{8,24},{16,0},{24,8},{1,17},{9,25},{17,1},{25,9},{2,18},{10... | collective-permute-start | bytes 393224 | tf_op jit(solution)/shard_map/ppermute | solution.py:110
  38.1 3.2 %collective-permute-start.15 = (bf16[64,1024]{1,0:T(8,128)(2,1)S(1)}, bf16[64,1024]{1,0:T(8,128)(2,1)S(1)}, u32[]{:S(2)}, u32[]{:S(2)}) collective-permute-start(bf16[64,1024]{1,0:T(8,128)(2,1)S(1)} %add_a.1.after), channel_id=1, source_target_pairs={{0,4},{1,5},{2,6},{3,7},{4,0},{5,1},{6,2},{7,3},{8,12},{9,13},{10,... | collective-permute-start | bytes 393224 | tf_op jit(solution)/shard_map/ppermute | solution.py:110
  41.3 1.2 %collective-permute-start.13 = (f32[2,128]{1,0:T(2,128)S(1)}, f32[2,128]{1,0:T(2,128)S(1)}, u32[]{:S(2)}, u32[]{:S(2)}) collective-permute-start(f32[2,128]{1,0:T(2,128)S(1)} %get-tuple-element.61), channel_id=1, source_target_pairs={{0,8},{8,0},{16,24},{24,16},{1,9},{9,1},{17,25},{25,17},{2,10},{10... | collective-permute-start | bytes 3080 | tf_op jit(solution)/shard_map/ppermute | solution.py:110
  42.5 2.3 %collective-permute-start.21 = (bf16[64,1024]{1,0:T(8,128)(2,1)S(1)}, bf16[64,1024]{1,0:T(8,128)(2,1)S(1)}, u32[]{:S(2)}, u32[]{:S(2)}) collective-permute-start(bf16[64,1024]{1,0:T(8,128)(2,1)S(1)} %add_b.1.refs_1_), channel_id=1, source_target_pairs={{0,4},{1,5},{2,6},{3,7},{4,0},{5,1},{6,2},{7,3},{8,12},{9,13},{10,... | collective-permute-start | bytes 393224 | tf_op jit(solution)/shard_map/ppermute | solution.py:110
  45.3 1.1 %collective-permute-start.20 = (bf16[128,1024]{1,0:T(8,128)(2,1)S(1)}, bf16[128,1024]{1,0:T(8,128)(2,1)S(1)}, u32[]{:S(2)}, u32[]{:S(2)}) collective-permute-start(bf16[128,1024]{1,0:T(8,128)(2,1)S(1)} %near_y.1), channel_id=1, source_target_pairs={{0,16},{8,24},{16,0},{24,8},{1,17},{9,25},{17,1},{25,9},{2,18},{10... | collective-permute-start | bytes 786440 | tf_op jit(solution)/shard_map/ppermute | solution.py:110
  46.4 2.0 %collective-permute-start.19 = (bf16[128,1024]{1,0:T(8,128)(2,1)S(1)}, bf16[128,1024]{1,0:T(8,128)(2,1)S(1)}, u32[]{:S(2)}, u32[]{:S(2)}) collective-permute-start(bf16[128,1024]{1,0:T(8,128)(2,1)S(1)} %add_clips.1.sum_v.refs_1_), channel_id=1, source_target_pairs={{0,2},{1,3},{2,0},{3,1},{4,6},{5,7},{6,4},{7,5},{8,10},{9,11},{10,... | collective-permute-start | bytes 786440 | tf_op jit(solution)/shard_map/ppermute | solution.py:110
  48.4 1.7 %collective-permute-done.15.got.refs_0_ = bf16[64,1024]{1,0:T(8,128)(2,1)S(1)} collective-permute-done((bf16[64,1024]{1,0:T(8,128)(2,1)S(1)}, bf16[64,1024]{1,0:T(8,128)(2,1)S(1)}, u32[]{:S(2)}, u32[]{:S(2)}) %collective-permute-start.15) | collective-permute-done | bytes 131104 | tf_op jit(solution)/shard_map/ppermute | solution.py:110
  50.2 2.0 %collective-permute-done.21.refs_0_ = bf16[64,1024]{1,0:T(8,128)(2,1)S(1)} collective-permute-done((bf16[64,1024]{1,0:T(8,128)(2,1)S(1)}, bf16[64,1024]{1,0:T(8,128)(2,1)S(1)}, u32[]{:S(2)}, u32[]{:S(2)}) %collective-permute-start.21) | collective-permute-done | bytes 131104 | tf_op jit(solution)/shard_map/ppermute | solution.py:110
  52.2 0.6 %collective-permute-done.20.refs_0_ = bf16[128,1024]{1,0:T(8,128)(2,1)S(1)} collective-permute-done((bf16[128,1024]{1,0:T(8,128)(2,1)S(1)}, bf16[128,1024]{1,0:T(8,128)(2,1)S(1)}, u32[]{:S(2)}, u32[]{:S(2)}) %collective-permute-start.20) | collective-permute-done | bytes 262176 | tf_op jit(solution)/shard_map/ppermute | solution.py:110
  52.8 1.1 %finish_captions.1 = f32[128,1024]{1,0:T(8,128)} custom-call(f32[2,128]{1,0:T(2,128)S(1)} %consts.1.refs_1_, f32[128,1024]{1,0:T(8,128)S(1)} %get-tuple-element.72.hat_ref, f32[128,1]{1,0:T(8,128)S(1)} %get-tuple-element.73.inverse_ref, f32[128,1024]{1,0:T(8,128)S(1)} %get-tuple-element.52.refs_1_.refs_0_, bf16[128,1024]{1,0:T(8,128)(2,1)S(1)} %captions_y.1.refs_1_, ...), custom_call_target="tpu_custom_call" | custom-call | tf_op jit(solution)/shard_map/finish_captions/pallas_call | solution.py:28
  53.9 2.9 %collective-permute-done.19.refs_0_ = bf16[128,1024]{1,0:T(8,128)(2,1)S(1)} collective-permute-done((bf16[128,1024]{1,0:T(8,128)(2,1)S(1)}, bf16[128,1024]{1,0:T(8,128)(2,1)S(1)}, u32[]{:S(2)}, u32[]{:S(2)}) %collective-permute-start.19) | collective-permute-done | bytes 262176 | tf_op jit(solution)/shard_map/ppermute | solution.py:110
  56.9 1.1 %finish_clips.1 = (f32[128,1024]{1,0:T(8,128)}, f32[1,128]{1,0:T(1,128)}) custom-call(f32[2,128]{1,0:T(2,128)S(1)} %consts.1.refs_1_, f32[128,1024]{1,0:T(8,128)S(1)} %get-tuple-element.39.hat_ref, f32[128,1]{1,0:T(8,128)S(1)} %get-tuple-element.40.inverse_ref, f32[1,128]{1,0:T(1,128)S(1)} %get-tuple-element.60.refs_0_, ...), custom_call_target="tpu_custom_call" | custom-call | tf_op jit(solution)/shard_map/finish_clips/pallas_call | solution.py:28
  (45 shorter events, 2.1 us)
Async XLA Ops:
  2.2 10.5 %collective-permute-start.2 = (bf16[64,1024]{1,0:T(8,128)(2,1)S(1)}, bf16[64,1024]{1,0:T(8,128)(2,1)S(1)}, u32[]{:S(2)}, u32[]{:S(2)}) collective-permute-start(bf16[64,1024]{1,0:T(8,128)(2,1)S(1)} %get-tuple-element.44), channel_id=1, source_target_pairs={{0,2},{1,3},{2,0},{3,1},{4,6},{5,7},{6,4},{7,5},{8,10},{9,11},{10,... | collective-permute-start | bytes 393224 | tf_op jit(solution)/shard_map/ppermute | solution.py:110
  5.3 14.3 %collective-permute-start.5 = (bf16[128,1024]{1,0:T(8,128)(2,1)S(1)}, bf16[128,1024]{1,0:T(8,128)(2,1)S(1)}, u32[]{:S(2)}, u32[]{:S(2)}) collective-permute-start(bf16[128,1024]{1,0:T(8,128)(2,1)S(1)} %get-tuple-element.42.refs_0_), channel_id=1, source_target_pairs={{0,4},{1,5},{2,6},{3,7},{4,0},{5,1},{6,2},{7,3},{8,12},{9,13},{10,... | collective-permute-start | bytes 786440 | tf_op jit(solution)/shard_map/ppermute | solution.py:110
  7.8 10.3 %collective-permute-start = (bf16[128,1024]{1,0:T(8,128)(2,1)S(1)}, bf16[128,1024]{1,0:T(8,128)(2,1)S(1)}, u32[]{:S(2)}, u32[]{:S(2)}) collective-permute-start(bf16[128,1024]{1,0:T(8,128)(2,1)S(1)} %get-tuple-element.42.refs_0_), channel_id=1, source_target_pairs={{0,16},{8,24},{16,0},{24,8},{1,17},{9,25},{17,1},{25,9},{2,18},{10... | collective-permute-start | bytes 786440 | tf_op jit(solution)/shard_map/ppermute | solution.py:110
  9.4 7.1 %collective-permute-start.3 = (bf16[64,1024]{1,0:T(8,128)(2,1)S(1)}, bf16[64,1024]{1,0:T(8,128)(2,1)S(1)}, u32[]{:S(2)}, u32[]{:S(2)}) collective-permute-start(bf16[64,1024]{1,0:T(8,128)(2,1)S(1)} %get-tuple-element.45), channel_id=1, source_target_pairs={{0,2},{1,3},{2,0},{3,1},{4,6},{5,7},{6,4},{7,5},{8,10},{9,11},{10,... | collective-permute-start | bytes 393224 | tf_op jit(solution)/shard_map/ppermute | solution.py:110
  9.8 8.3 %collective-permute-start.1 = (bf16[128,1024]{1,0:T(8,128)(2,1)S(1)}, bf16[128,1024]{1,0:T(8,128)(2,1)S(1)}, u32[]{:S(2)}, u32[]{:S(2)}) collective-permute-start(bf16[128,1024]{1,0:T(8,128)(2,1)S(1)} %get-tuple-element.43.refs_2_), channel_id=1, source_target_pairs={{0,8},{8,0},{16,24},{24,16},{1,9},{9,1},{17,25},{25,17},{2,10},{10... | collective-permute-start | bytes 786440 | tf_op jit(solution)/shard_map/ppermute | solution.py:110
  12.6 8.5 %collective-permute-start.7 = (bf16[64,1024]{1,0:T(8,128)(2,1)S(1)}, bf16[64,1024]{1,0:T(8,128)(2,1)S(1)}, u32[]{:S(2)}, u32[]{:S(2)}) collective-permute-start(bf16[64,1024]{1,0:T(8,128)(2,1)S(1)} %clips_z.2.refs_4_), channel_id=1, source_target_pairs={{0,8},{8,0},{16,24},{24,16},{1,9},{9,1},{17,25},{25,17},{2,10},{10... | collective-permute-start | bytes 393224 | tf_op jit(solution)/shard_map/ppermute | solution.py:110
  16.5 5.9 %collective-permute-start.8 = (bf16[64,1024]{1,0:T(8,128)(2,1)S(1)}, bf16[64,1024]{1,0:T(8,128)(2,1)S(1)}, u32[]{:S(2)}, u32[]{:S(2)}) collective-permute-start(bf16[64,1024]{1,0:T(8,128)(2,1)S(1)} %clips_z.3.refs_5_), channel_id=1, source_target_pairs={{0,8},{8,0},{16,24},{24,16},{1,9},{9,1},{17,25},{25,17},{2,10},{10... | collective-permute-start | bytes 393224 | tf_op jit(solution)/shard_map/ppermute | solution.py:110
  18.2 4.2 %collective-permute-start.4 = (bf16[640,1024]{1,0:T(8,128)(2,1)S(1)}, bf16[640,1024]{1,0:T(8,128)(2,1)S(1)}, u32[]{:S(2)}, u32[]{:S(2)}) collective-permute-start(bf16[640,1024]{1,0:T(8,128)(2,1)S(1)} %near_blocks.1.N), channel_id=1, source_target_pairs={{0,1},{1,0},{2,3},{3,2},{4,5},{5,4},{6,7},{7,6},{8,9},{9,8},{10,11... | collective-permute-start | bytes 3932168 | tf_op jit(solution)/shard_map/ppermute | solution.py:110
  19.6 7.6 %collective-permute-start.10 = (bf16[128,1024]{1,0:T(8,128)(2,1)S(1)}, bf16[128,1024]{1,0:T(8,128)(2,1)S(1)}, u32[]{:S(2)}, u32[]{:S(2)}) collective-permute-start(bf16[128,1024]{1,0:T(8,128)(2,1)S(1)} %captions_z.1.refs_0_), channel_id=1, source_target_pairs={{0,16},{8,24},{16,0},{24,8},{1,17},{9,25},{17,1},{25,9},{2,18},{10... | collective-permute-start | bytes 786440 | tf_op jit(solution)/shard_map/ppermute | solution.py:110
  21.1 1.5 %collective-permute-start.6 = (bf16[128,1024]{1,0:T(8,128)(2,1)S(1)}, bf16[128,1024]{1,0:T(8,128)(2,1)S(1)}, u32[]{:S(2)}, u32[]{:S(2)}) collective-permute-start(bf16[128,1024]{1,0:T(8,128)(2,1)S(1)} %captions_z.1.refs_0_), channel_id=1, source_target_pairs={{0,1},{1,0},{2,3},{3,2},{4,5},{5,4},{6,7},{7,6},{8,9},{9,8},{10,11... | collective-permute-start | bytes 786440 | tf_op jit(solution)/shard_map/ppermute | solution.py:110
  22.4 2.8 %collective-permute-start.9 = (bf16[128,1024]{1,0:T(8,128)(2,1)S(1)}, bf16[128,1024]{1,0:T(8,128)(2,1)S(1)}, u32[]{:S(2)}, u32[]{:S(2)}) collective-permute-start(bf16[128,1024]{1,0:T(8,128)(2,1)S(1)} %diagonal_clips.1.vd), channel_id=1, source_target_pairs={{0,1},{1,0},{2,3},{3,2},{4,5},{5,4},{6,7},{7,6},{8,9},{9,8},{10,11... | collective-permute-start | bytes 786440 | tf_op jit(solution)/shard_map/ppermute | solution.py:110
  27.2 2.7 %collective-permute-start.11 = (bf16[128,1024]{1,0:T(8,128)(2,1)S(1)}, bf16[128,1024]{1,0:T(8,128)(2,1)S(1)}, u32[]{:S(2)}, u32[]{:S(2)}) collective-permute-start(bf16[128,1024]{1,0:T(8,128)(2,1)S(1)} %captions_d.1.refs_0_), channel_id=1, source_target_pairs={{0,1},{1,0},{2,3},{3,2},{4,5},{5,4},{6,7},{7,6},{8,9},{9,8},{10,11... | collective-permute-start | bytes 786440 | tf_op jit(solution)/shard_map/ppermute | solution.py:110
  29.0 5.6 %collective-permute-start.12 = (bf16[64,1024]{1,0:T(8,128)(2,1)S(1)}, bf16[64,1024]{1,0:T(8,128)(2,1)S(1)}, u32[]{:S(2)}, u32[]{:S(2)}) collective-permute-start(bf16[64,1024]{1,0:T(8,128)(2,1)S(1)} %get-tuple-element.58), channel_id=1, source_target_pairs={{0,16},{8,24},{16,0},{24,8},{1,17},{9,25},{17,1},{25,9},{2,18},{10... | collective-permute-start | bytes 393224 | tf_op jit(solution)/shard_map/ppermute | solution.py:110
  31.1 15.2 %collective-permute-start.16 = (bf16[128,1024]{1,0:T(8,128)(2,1)S(1)}, bf16[128,1024]{1,0:T(8,128)(2,1)S(1)}, u32[]{:S(2)}, u32[]{:S(2)}) collective-permute-start(bf16[128,1024]{1,0:T(8,128)(2,1)S(1)} %get-tuple-element.59.refs_1_), channel_id=1, source_target_pairs={{0,8},{8,0},{16,24},{24,16},{1,9},{9,1},{17,25},{25,17},{2,10},{10... | collective-permute-start | bytes 786440 | tf_op jit(solution)/shard_map/ppermute | solution.py:110
  35.7 14.4 %collective-permute-start.18 = (bf16[128,1024]{1,0:T(8,128)(2,1)S(1)}, bf16[128,1024]{1,0:T(8,128)(2,1)S(1)}, u32[]{:S(2)}, u32[]{:S(2)}) collective-permute-start(bf16[128,1024]{1,0:T(8,128)(2,1)S(1)} %get-tuple-element.69), channel_id=1, source_target_pairs={{0,8},{8,0},{16,24},{24,16},{1,9},{9,1},{17,25},{25,17},{2,10},{10... | collective-permute-start | bytes 786440 | tf_op jit(solution)/shard_map/ppermute | solution.py:110
  37.3 5.2 %collective-permute-start.14 = (bf16[64,1024]{1,0:T(8,128)(2,1)S(1)}, bf16[64,1024]{1,0:T(8,128)(2,1)S(1)}, u32[]{:S(2)}, u32[]{:S(2)}) collective-permute-start(bf16[64,1024]{1,0:T(8,128)(2,1)S(1)} %far_b.2), channel_id=1, source_target_pairs={{0,16},{8,24},{16,0},{24,8},{1,17},{9,25},{17,1},{25,9},{2,18},{10... | collective-permute-start | bytes 393224 | tf_op jit(solution)/shard_map/ppermute | solution.py:110
  38.1 12.1 %collective-permute-start.15 = (bf16[64,1024]{1,0:T(8,128)(2,1)S(1)}, bf16[64,1024]{1,0:T(8,128)(2,1)S(1)}, u32[]{:S(2)}, u32[]{:S(2)}) collective-permute-start(bf16[64,1024]{1,0:T(8,128)(2,1)S(1)} %add_a.1.after), channel_id=1, source_target_pairs={{0,4},{1,5},{2,6},{3,7},{4,0},{5,1},{6,2},{7,3},{8,12},{9,13},{10,... | collective-permute-start | bytes 393224 | tf_op jit(solution)/shard_map/ppermute | solution.py:110
  41.3 4.0 %collective-permute-start.13 = (f32[2,128]{1,0:T(2,128)S(1)}, f32[2,128]{1,0:T(2,128)S(1)}, u32[]{:S(2)}, u32[]{:S(2)}) collective-permute-start(f32[2,128]{1,0:T(2,128)S(1)} %get-tuple-element.61), channel_id=1, source_target_pairs={{0,8},{8,0},{16,24},{24,16},{1,9},{9,1},{17,25},{25,17},{2,10},{10... | collective-permute-start | bytes 3080 | tf_op jit(solution)/shard_map/ppermute | solution.py:110
  42.5 9.7 %collective-permute-start.21 = (bf16[64,1024]{1,0:T(8,128)(2,1)S(1)}, bf16[64,1024]{1,0:T(8,128)(2,1)S(1)}, u32[]{:S(2)}, u32[]{:S(2)}) collective-permute-start(bf16[64,1024]{1,0:T(8,128)(2,1)S(1)} %add_b.1.refs_1_), channel_id=1, source_target_pairs={{0,4},{1,5},{2,6},{3,7},{4,0},{5,1},{6,2},{7,3},{8,12},{9,13},{10,... | collective-permute-start | bytes 393224 | tf_op jit(solution)/shard_map/ppermute | solution.py:110
  45.3 7.6 %collective-permute-start.20 = (bf16[128,1024]{1,0:T(8,128)(2,1)S(1)}, bf16[128,1024]{1,0:T(8,128)(2,1)S(1)}, u32[]{:S(2)}, u32[]{:S(2)}) collective-permute-start(bf16[128,1024]{1,0:T(8,128)(2,1)S(1)} %near_y.1), channel_id=1, source_target_pairs={{0,16},{8,24},{16,0},{24,8},{1,17},{9,25},{17,1},{25,9},{2,18},{10... | collective-permute-start | bytes 786440 | tf_op jit(solution)/shard_map/ppermute | solution.py:110
  46.4 10.4 %collective-permute-start.19 = (bf16[128,1024]{1,0:T(8,128)(2,1)S(1)}, bf16[128,1024]{1,0:T(8,128)(2,1)S(1)}, u32[]{:S(2)}, u32[]{:S(2)}) collective-permute-start(bf16[128,1024]{1,0:T(8,128)(2,1)S(1)} %add_clips.1.sum_v.refs_1_), channel_id=1, source_target_pairs={{0,2},{1,3},{2,0},{3,1},{4,6},{5,7},{6,4},{7,5},{8,10},{9,11},{10,... | collective-permute-start | bytes 786440 | tf_op jit(solution)/shard_map/ppermute | solution.py:110
  50.1 6.8 %collective-permute-start.17 = (f32[1,128]{1,0:T(1,128)S(1)}, f32[1,128]{1,0:T(1,128)S(1)}, u32[]{:S(2)}, u32[]{:S(2)}) collective-permute-start(f32[1,128]{1,0:T(1,128)S(1)} %add_loss.1.refs_4_), channel_id=1, source_target_pairs={{0,2},{1,3},{2,0},{3,1},{4,6},{5,7},{6,4},{7,5},{8,10},{9,11},{10,... | collective-permute-start | bytes 1544 | tf_op jit(solution)/shard_map/ppermute | solution.py:110

commit v7 on v6

--- a/solution.py
+++ b/solution.py
@@ -327,6 +327,7 @@
     got_z = hand_on("clips_back", swap(sum_v, "col", 2), flops=3 * LONG)
     got_h = [[hand_on("captions_back", b, sum_v, flops=3 * LONG) for b in got] for got in (got_a, got_b)]
     dcy = [hand_on("near_y", b, *sums_b) for b in dcy]
+    dvx = hand_on("near_x", dvx, *sums_b)
     got_y = [hand_on("captions_y", swap(dcy[t - 1], "row", 2 * t), sum_v, flops=LONG) for t in range(1, Y)]
     got_x = hand_on("clips_x", swap(dvx, "row", 1), sum_v, flops=4 * LONG)
 

time: 58.1 us -> 55.2 us (0.950)
  starting transfers between devices: 27.6 us -> 26.1 us
  waiting for transfers between devices: 16.2 us -> 14.8 us
    ppermute x22, starting transfers between devices: 27.6 us -> 26.1 us  [swap(): return lax.ppermute(value, axis, [(i, i ^ bits) for i in range(size)])]
    ppermute x22, waiting for transfers between devices: 16.2 us -> 14.8 us  [swap(): return lax.ppermute(value, axis, [(i, i ^ bits) for i in range(size)])]
    pallas_call x33 -> x34, Pallas kernels: 12.1 us -> 12.1 us  [call(): pl.pallas_call(kernel, name=name, out_shape=out_shape, in_specs=[SPECS[sp...]
  transfers between devices with their start and end apart: 22 -> 22, of which waited for: 12 -> 10; matrix products, arithmetic and copies ran while one was open for 0% -> 0% of each run, Pallas kernels for 16% -> 17%
where the time goes in v7:
time: 55.2 us; the launch traced here: 55.1 us
  starting transfers between devices  26.1 us (47%)
  waiting for transfers between devices  14.8 us (27%)
  Pallas kernels  12.1 us (22%)
  between operations  2.13 us (4%)
    ppermute x22, starting transfers between devices, swap(): return lax.ppermute(value, axis, [(i, i ^ bits) for i in range(size)])  26.1 us
    ppermute x22, waiting for transfers between devices, swap(): return lax.ppermute(value, axis, [(i, i ^ bits) for i in range(size)])  14.8 us
    pallas_call x34, Pallas kernels, call(): pl.pallas_call(kernel, name=name, out_shape=out_shape, in_specs=[SPECS[sp...  12.1 us
  transfers between devices with their start and end apart: 22, of which 10 were waited for; matrix products, arithmetic and copies ran while one was open for 0% of the time, Pallas kernels for 17%

profile of v7, /device:TPU:0, one launch (start us, length us, event | category | flops | bytes accessed | tf_op | source)
XLA Modules:
  0.0 55.1 jit_solution(16081839558270603357)
XLA Ops:
  0.6 1.5 %normalize.1 = (bf16[128,1024]{1,0:T(8,128)(2,1)S(1)}, bf16[128,1024]{1,0:T(8,128)(2,1)S(1)}, bf16[64,1024]{1,0:T(8,128)(2,1)S(1)}, bf16[64,1024]{1,0:T(8,128)(2...) custom-call(f32[128,1024]{1,0:T(8,128)} %film.1, ...), custom_call_target="tpu_custom_call" | custom-call | tf_op jit(solution)/shard_map/normalize/pallas_call | solution.py:28
  2.2 3.1 %collective-permute-start.2 = (bf16[64,1024]{1,0:T(8,128)(2,1)S(1)}, bf16[64,1024]{1,0:T(8,128)(2,1)S(1)}, u32[]{:S(2)}, u32[]{:S(2)}) collective-permute-start(bf16[64,1024]{1,0:T(8,128)(2,1)S(1)} %get-tuple-element.44), channel_id=1, source_target_pairs={{0,2},{1,3},{2,0},{3,1},{4,6},{5,7},{6,4},{7,5},{8,10},{9,11},{10,... | collective-permute-start | bytes 393224 | tf_op jit(solution)/shard_map/ppermute | solution.py:110
  5.3 2.6 %collective-permute-start.5 = (bf16[128,1024]{1,0:T(8,128)(2,1)S(1)}, bf16[128,1024]{1,0:T(8,128)(2,1)S(1)}, u32[]{:S(2)}, u32[]{:S(2)}) collective-permute-start(bf16[128,1024]{1,0:T(8,128)(2,1)S(1)} %get-tuple-element.42.refs_0_), channel_id=1, source_target_pairs={{0,4},{1,5},{2,6},{3,7},{4,0},{5,1},{6,2},{7,3},{8,12},{9,13},{10,... | collective-permute-start | bytes 786440 | tf_op jit(solution)/shard_map/ppermute | solution.py:110
  7.8 1.5 %collective-permute-start = (bf16[128,1024]{1,0:T(8,128)(2,1)S(1)}, bf16[128,1024]{1,0:T(8,128)(2,1)S(1)}, u32[]{:S(2)}, u32[]{:S(2)}) collective-permute-start(bf16[128,1024]{1,0:T(8,128)(2,1)S(1)} %get-tuple-element.42.refs_0_), channel_id=1, source_target_pairs={{0,16},{8,24},{16,0},{24,8},{1,17},{9,25},{17,1},{25,9},{2,18},{10... | collective-permute-start | bytes 786440 | tf_op jit(solution)/shard_map/ppermute | solution.py:110
  9.4 0.4 collective-permute-start.3
  9.8 1.5 %collective-permute-start.1 = (bf16[128,1024]{1,0:T(8,128)(2,1)S(1)}, bf16[128,1024]{1,0:T(8,128)(2,1)S(1)}, u32[]{:S(2)}, u32[]{:S(2)}) collective-permute-start(bf16[128,1024]{1,0:T(8,128)(2,1)S(1)} %get-tuple-element.43.refs_2_), channel_id=1, source_target_pairs={{0,8},{8,0},{16,24},{24,16},{1,9},{9,1},{17,25},{25,17},{2,10},{10... | collective-permute-start | bytes 786440 | tf_op jit(solution)/shard_map/ppermute | solution.py:110
  12.6 0.6 %collective-permute-start.7 = (bf16[64,1024]{1,0:T(8,128)(2,1)S(1)}, bf16[64,1024]{1,0:T(8,128)(2,1)S(1)}, u32[]{:S(2)}, u32[]{:S(2)}) collective-permute-start(bf16[64,1024]{1,0:T(8,128)(2,1)S(1)} %clips_z.2.refs_4_), channel_id=1, source_target_pairs={{0,8},{8,0},{16,24},{24,16},{1,9},{9,1},{17,25},{25,17},{2,10},{10... | collective-permute-start | bytes 393224 | tf_op jit(solution)/shard_map/ppermute | solution.py:110
  13.2 3.2 %collective-permute-done.3.refs_0_ = bf16[64,1024]{1,0:T(8,128)(2,1)S(1)} collective-permute-done((bf16[64,1024]{1,0:T(8,128)(2,1)S(1)}, bf16[64,1024]{1,0:T(8,128)(2,1)S(1)}, u32[]{:S(2)}, u32[]{:S(2)}) %collective-permute-start.3) | collective-permute-done | bytes 131104 | tf_op jit(solution)/shard_map/ppermute | solution.py:110
  16.5 1.5 %collective-permute-start.8 = (bf16[64,1024]{1,0:T(8,128)(2,1)S(1)}, bf16[64,1024]{1,0:T(8,128)(2,1)S(1)}, u32[]{:S(2)}, u32[]{:S(2)}) collective-permute-start(bf16[64,1024]{1,0:T(8,128)(2,1)S(1)} %clips_z.3.refs_5_), channel_id=1, source_target_pairs={{0,8},{8,0},{16,24},{24,16},{1,9},{9,1},{17,25},{25,17},{2,10},{10... | collective-permute-start | bytes 393224 | tf_op jit(solution)/shard_map/ppermute | solution.py:110
  18.3 1.3 %collective-permute-done.5.refs_0_ = bf16[128,1024]{1,0:T(8,128)(2,1)S(1)} collective-permute-done((bf16[128,1024]{1,0:T(8,128)(2,1)S(1)}, bf16[128,1024]{1,0:T(8,128)(2,1)S(1)}, u32[]{:S(2)}, u32[]{:S(2)}) %collective-permute-start.5) | collective-permute-done | bytes 262176 | tf_op jit(solution)/shard_map/ppermute | solution.py:110
  19.6 1.5 %collective-permute-start.10 = (bf16[128,1024]{1,0:T(8,128)(2,1)S(1)}, bf16[128,1024]{1,0:T(8,128)(2,1)S(1)}, u32[]{:S(2)}, u32[]{:S(2)}) collective-permute-start(bf16[128,1024]{1,0:T(8,128)(2,1)S(1)} %captions_z.1.refs_0_), channel_id=1, source_target_pairs={{0,16},{8,24},{16,0},{24,8},{1,17},{9,25},{17,1},{25,9},{2,18},{10... | collective-permute-start | bytes 786440 | tf_op jit(solution)/shard_map/ppermute | solution.py:110
  21.1 1.2 %collective-permute-done.8.refs_0_ = bf16[64,1024]{1,0:T(8,128)(2,1)S(1)} collective-permute-done((bf16[64,1024]{1,0:T(8,128)(2,1)S(1)}, bf16[64,1024]{1,0:T(8,128)(2,1)S(1)}, u32[]{:S(2)}, u32[]{:S(2)}) %collective-permute-start.8) | collective-permute-done | bytes 131104 | tf_op jit(solution)/shard_map/ppermute | solution.py:110
  22.6 2.5 %early_pairs.1 = (bf16[768,1024]{1,0:T(8,128)(2,1)S(1)}, bf16[384,768]{1,0:T(8,128)(2,1)S(1)}, bf16[384,384]{1,0:T(8,128)(2,1)S(1)}, f32[1,384]{1,0:T(1,128)S(1)}) custom-call(f32[2,128]{1,0:T(2,128)S(1)} %consts.1.refs_1_, s32[1,1024]{1,0:T(1,128)S(1)} %get-tuple-element.41.labels, bf16[640,1024]{1,0:T(8,128)(2,1)S(1)} %near_blocks.1.N, ...), custom_call_target="tpu_custom_call" | custom-call | flops 905969664 | tf_op jit(solution)/shard_map/early_pairs/pallas_call | solution.py:28
  25.2 2.0 %middle_sums.1 = (bf16[1024,1024]{1,0:T(8,128)(2,1)S(1)}, bf16[768,512]{1,0:T(8,128)(2,1)S(1)}, f32[1,128]{1,0:T(1,128)S(1)}, f32[128,1024]{1,0:T(8,128)S(1)}, b...) custom-call(f32[2,128]{1,0:T(2,128)S(1)} %consts.1.refs_1_, ...), custom_call_target="tpu_custom_call" | custom-call | flops 1107296256 | tf_op jit(solution)/shard_map/middle_sums/pallas_call | solution.py:28
  27.6 1.5 %far_captions.1 = (f32[1,512]{1,0:T(1,128)S(1)}, bf16[128,512]{1,0:T(8,128)(2,1)S(1)}, bf16[64,1024]{1,0:T(8,128)(2,1)S(1)}, bf16[64,1024]{1,0:T(8,128)(2,1)S(1)}) custom-call(f32[2,128]{1,0:T(2,128)S(1)} %consts.1.refs_1_, s32[1,1024]{1,0:T(1,128)S(1)} %get-tuple-element.41.labels, bf16[1024,1024]{1,0:T(8,128)(2,1)S(1)} %get-tuple-element.51.VV, ...), custom_call_target="tpu_custom_call" | custom-call | flops 536870912 | tf_op jit(solution)/shard_map/far_captions/pallas_call | solution.py:28
  29.1 0.9 %collective-permute-start.12 = (bf16[64,1024]{1,0:T(8,128)(2,1)S(1)}, bf16[64,1024]{1,0:T(8,128)(2,1)S(1)}, u32[]{:S(2)}, u32[]{:S(2)}) collective-permute-start(bf16[64,1024]{1,0:T(8,128)(2,1)S(1)} %get-tuple-element.58), channel_id=1, source_target_pairs={{0,16},{8,24},{16,0},{24,8},{1,17},{9,25},{17,1},{25,9},{2,18},{10... | collective-permute-start | bytes 393224 | tf_op jit(solution)/shard_map/ppermute | solution.py:110
  29.9 1.2 %far_clips.1 = (bf16[256,1024]{1,0:T(8,128)(2,1)S(1)}, bf16[256,512]{1,0:T(8,128)(2,1)S(1)}, f32[1,512]{1,0:T(1,128)S(1)}, bf16[128,1024]{1,0:T(8,128)(2,1)S(1)}) custom-call(f32[2,128]{1,0:T(2,128)S(1)} %consts.1.refs_1_, s32[1,1024]{1,0:T(1,128)S(1)} %get-tuple-element.41.labels, bf16[1024,1024]{1,0:T(8,128)(2,1)S(1)} %get-tuple-element.51.VV, ...), custom_call_target="tpu_custom_call" | custom-call | flops 402653184 | tf_op jit(solution)/shard_map/far_clips/pallas_call | solution.py:28
  31.1 1.4 %collective-permute-start.16 = (bf16[128,1024]{1,0:T(8,128)(2,1)S(1)}, bf16[128,1024]{1,0:T(8,128)(2,1)S(1)}, u32[]{:S(2)}, u32[]{:S(2)}) collective-permute-start(bf16[128,1024]{1,0:T(8,128)(2,1)S(1)} %get-tuple-element.59.refs_1_), channel_id=1, source_target_pairs={{0,8},{8,0},{16,24},{24,16},{1,9},{9,1},{17,25},{25,17},{2,10},{10... | collective-permute-start | bytes 786440 | tf_op jit(solution)/shard_map/ppermute | solution.py:110
  32.5 1.4 %collective-permute-start.14 = (bf16[64,1024]{1,0:T(8,128)(2,1)S(1)}, bf16[64,1024]{1,0:T(8,128)(2,1)S(1)}, u32[]{:S(2)}, u32[]{:S(2)}) collective-permute-start(bf16[64,1024]{1,0:T(8,128)(2,1)S(1)} %far_b.2), channel_id=1, source_target_pairs={{0,16},{8,24},{16,0},{24,8},{1,17},{9,25},{17,1},{25,9},{2,18},{10... | collective-permute-start | bytes 393224 | tf_op jit(solution)/shard_map/ppermute | solution.py:110
  33.9 0.8 %collective-permute-done.12.refs_0_ = bf16[64,1024]{1,0:T(8,128)(2,1)S(1)} collective-permute-done((bf16[64,1024]{1,0:T(8,128)(2,1)S(1)}, bf16[64,1024]{1,0:T(8,128)(2,1)S(1)}, u32[]{:S(2)}, u32[]{:S(2)}) %collective-permute-start.12) | collective-permute-done | bytes 131104 | tf_op jit(solution)/shard_map/ppermute | solution.py:110
  34.7 3.2 %collective-permute-start.15 = (bf16[64,1024]{1,0:T(8,128)(2,1)S(1)}, bf16[64,1024]{1,0:T(8,128)(2,1)S(1)}, u32[]{:S(2)}, u32[]{:S(2)}) collective-permute-start(bf16[64,1024]{1,0:T(8,128)(2,1)S(1)} %add_a.1.after), channel_id=1, source_target_pairs={{0,4},{1,5},{2,6},{3,7},{4,0},{5,1},{6,2},{7,3},{8,12},{9,13},{10,... | collective-permute-start | bytes 393224 | tf_op jit(solution)/shard_map/ppermute | solution.py:110
  37.9 0.8 %collective-permute-start.13 = (f32[2,128]{1,0:T(2,128)S(1)}, f32[2,128]{1,0:T(2,128)S(1)}, u32[]{:S(2)}, u32[]{:S(2)}) collective-permute-start(f32[2,128]{1,0:T(2,128)S(1)} %get-tuple-element.61), channel_id=1, source_target_pairs={{0,8},{8,0},{16,24},{24,16},{1,9},{9,1},{17,25},{25,17},{2,10},{10... | collective-permute-start | bytes 3080 | tf_op jit(solution)/shard_map/ppermute | solution.py:110
  38.7 1.0 %near_clips.1 = (f32[128,1024]{1,0:T(8,128)S(1)}, bf16[128,1024]{1,0:T(8,128)(2,1)S(1)}, f32[128,1024]{1,0:T(8,128)S(1)}) custom-call(bf16[768,1024]{1,0:T(8,128)(2,1)S(1)} %get-tuple-element.47.S1, bf16[256,1024]{1,0:T(8,128)(2,1)S(1)} %get-tuple-element.64.S2, bf16[768,512]{1,0:T(8,128)(2,1)S(1)} %get-tuple-element.54.G1, ...), custom_call_target="tpu_custom_call" | custom-call | flops 805306368 | tf_op jit(solution)/shard_map/near_clips/pallas_call | solution.py:28
  39.8 1.2 %collective-permute-start.21 = (bf16[64,1024]{1,0:T(8,128)(2,1)S(1)}, bf16[64,1024]{1,0:T(8,128)(2,1)S(1)}, u32[]{:S(2)}, u32[]{:S(2)}) collective-permute-start(bf16[64,1024]{1,0:T(8,128)(2,1)S(1)} %add_b.1.refs_1_), channel_id=1, source_target_pairs={{0,4},{1,5},{2,6},{3,7},{4,0},{5,1},{6,2},{7,3},{8,12},{9,13},{10,... | collective-permute-start | bytes 393224 | tf_op jit(solution)/shard_map/ppermute | solution.py:110
  41.0 1.1 %collective-permute-start.18 = (bf16[128,1024]{1,0:T(8,128)(2,1)S(1)}, bf16[128,1024]{1,0:T(8,128)(2,1)S(1)}, u32[]{:S(2)}, u32[]{:S(2)}) collective-permute-start(bf16[128,1024]{1,0:T(8,128)(2,1)S(1)} %near_x.1), channel_id=1, source_target_pairs={{0,8},{8,0},{16,24},{24,16},{1,9},{9,1},{17,25},{25,17},{2,10},{10... | collective-permute-start | bytes 786440 | tf_op jit(solution)/shard_map/ppermute | solution.py:110
  42.2 1.2 %collective-permute-start.20 = (bf16[128,1024]{1,0:T(8,128)(2,1)S(1)}, bf16[128,1024]{1,0:T(8,128)(2,1)S(1)}, u32[]{:S(2)}, u32[]{:S(2)}) collective-permute-start(bf16[128,1024]{1,0:T(8,128)(2,1)S(1)} %near_y.1), channel_id=1, source_target_pairs={{0,16},{8,24},{16,0},{24,8},{1,17},{9,25},{17,1},{25,9},{2,18},{10... | collective-permute-start | bytes 786440 | tf_op jit(solution)/shard_map/ppermute | solution.py:110
  43.4 1.6 %collective-permute-start.19 = (bf16[128,1024]{1,0:T(8,128)(2,1)S(1)}, bf16[128,1024]{1,0:T(8,128)(2,1)S(1)}, u32[]{:S(2)}, u32[]{:S(2)}) collective-permute-start(bf16[128,1024]{1,0:T(8,128)(2,1)S(1)} %add_clips.1.sum_v.refs_1_), channel_id=1, source_target_pairs={{0,2},{1,3},{2,0},{3,1},{4,6},{5,7},{6,4},{7,5},{8,10},{9,11},{10,... | collective-permute-start | bytes 786440 | tf_op jit(solution)/shard_map/ppermute | solution.py:110
  45.0 2.9 %collective-permute-done.15.got.refs_0_ = bf16[64,1024]{1,0:T(8,128)(2,1)S(1)} collective-permute-done((bf16[64,1024]{1,0:T(8,128)(2,1)S(1)}, bf16[64,1024]{1,0:T(8,128)(2,1)S(1)}, u32[]{:S(2)}, u32[]{:S(2)}) %collective-permute-start.15) | collective-permute-done | bytes 131104 | tf_op jit(solution)/shard_map/ppermute | solution.py:110
  48.0 1.8 %collective-permute-done.21.refs_0_ = bf16[64,1024]{1,0:T(8,128)(2,1)S(1)} collective-permute-done((bf16[64,1024]{1,0:T(8,128)(2,1)S(1)}, bf16[64,1024]{1,0:T(8,128)(2,1)S(1)}, u32[]{:S(2)}, u32[]{:S(2)}) %collective-permute-start.21) | collective-permute-done | bytes 131104 | tf_op jit(solution)/shard_map/ppermute | solution.py:110
  49.8 1.1 %finish_captions.1 = f32[128,1024]{1,0:T(8,128)} custom-call(f32[2,128]{1,0:T(2,128)S(1)} %consts.1.refs_1_, f32[128,1024]{1,0:T(8,128)S(1)} %get-tuple-element.72.hat_ref, f32[128,1]{1,0:T(8,128)S(1)} %get-tuple-element.73.inverse_ref, f32[128,1024]{1,0:T(8,128)S(1)} %get-tuple-element.52.refs_1_.refs_0_, bf16[128,1024]{1,0:T(8,128)(2,1)S(1)} %captions_y.1.refs_1_, ...), custom_call_target="tpu_custom_call" | custom-call | tf_op jit(solution)/shard_map/finish_captions/pallas_call | solution.py:28
  50.9 3.0 %collective-permute-done.19.refs_0_ = bf16[128,1024]{1,0:T(8,128)(2,1)S(1)} collective-permute-done((bf16[128,1024]{1,0:T(8,128)(2,1)S(1)}, bf16[128,1024]{1,0:T(8,128)(2,1)S(1)}, u32[]{:S(2)}, u32[]{:S(2)}) %collective-permute-start.19) | collective-permute-done | bytes 262176 | tf_op jit(solution)/shard_map/ppermute | solution.py:110
  54.0 1.1 %finish_clips.1 = (f32[128,1024]{1,0:T(8,128)}, f32[1,128]{1,0:T(1,128)}) custom-call(f32[2,128]{1,0:T(2,128)S(1)} %consts.1.refs_1_, f32[128,1024]{1,0:T(8,128)S(1)} %get-tuple-element.39.hat_ref, f32[128,1]{1,0:T(8,128)S(1)} %get-tuple-element.40.inverse_ref, f32[1,128]{1,0:T(1,128)S(1)} %get-tuple-element.60.refs_0_, ...), custom_call_target="tpu_custom_call" | custom-call | tf_op jit(solution)/shard_map/finish_clips/pallas_call | solution.py:28
  (46 shorter events, 1.2 us)
Async XLA Ops:
  2.2 10.5 %collective-permute-start.2 = (bf16[64,1024]{1,0:T(8,128)(2,1)S(1)}, bf16[64,1024]{1,0:T(8,128)(2,1)S(1)}, u32[]{:S(2)}, u32[]{:S(2)}) collective-permute-start(bf16[64,1024]{1,0:T(8,128)(2,1)S(1)} %get-tuple-element.44), channel_id=1, source_target_pairs={{0,2},{1,3},{2,0},{3,1},{4,6},{5,7},{6,4},{7,5},{8,10},{9,11},{10,... | collective-permute-start | bytes 393224 | tf_op jit(solution)/shard_map/ppermute | solution.py:110
  5.3 14.3 %collective-permute-start.5 = (bf16[128,1024]{1,0:T(8,128)(2,1)S(1)}, bf16[128,1024]{1,0:T(8,128)(2,1)S(1)}, u32[]{:S(2)}, u32[]{:S(2)}) collective-permute-start(bf16[128,1024]{1,0:T(8,128)(2,1)S(1)} %get-tuple-element.42.refs_0_), channel_id=1, source_target_pairs={{0,4},{1,5},{2,6},{3,7},{4,0},{5,1},{6,2},{7,3},{8,12},{9,13},{10,... | collective-permute-start | bytes 786440 | tf_op jit(solution)/shard_map/ppermute | solution.py:110
  7.8 10.3 %collective-permute-start = (bf16[128,1024]{1,0:T(8,128)(2,1)S(1)}, bf16[128,1024]{1,0:T(8,128)(2,1)S(1)}, u32[]{:S(2)}, u32[]{:S(2)}) collective-permute-start(bf16[128,1024]{1,0:T(8,128)(2,1)S(1)} %get-tuple-element.42.refs_0_), channel_id=1, source_target_pairs={{0,16},{8,24},{16,0},{24,8},{1,17},{9,25},{17,1},{25,9},{2,18},{10... | collective-permute-start | bytes 786440 | tf_op jit(solution)/shard_map/ppermute | solution.py:110
  9.4 7.1 %collective-permute-start.3 = (bf16[64,1024]{1,0:T(8,128)(2,1)S(1)}, bf16[64,1024]{1,0:T(8,128)(2,1)S(1)}, u32[]{:S(2)}, u32[]{:S(2)}) collective-permute-start(bf16[64,1024]{1,0:T(8,128)(2,1)S(1)} %get-tuple-element.45), channel_id=1, source_target_pairs={{0,2},{1,3},{2,0},{3,1},{4,6},{5,7},{6,4},{7,5},{8,10},{9,11},{10,... | collective-permute-start | bytes 393224 | tf_op jit(solution)/shard_map/ppermute | solution.py:110
  9.8 8.3 %collective-permute-start.1 = (bf16[128,1024]{1,0:T(8,128)(2,1)S(1)}, bf16[128,1024]{1,0:T(8,128)(2,1)S(1)}, u32[]{:S(2)}, u32[]{:S(2)}) collective-permute-start(bf16[128,1024]{1,0:T(8,128)(2,1)S(1)} %get-tuple-element.43.refs_2_), channel_id=1, source_target_pairs={{0,8},{8,0},{16,24},{24,16},{1,9},{9,1},{17,25},{25,17},{2,10},{10... | collective-permute-start | bytes 786440 | tf_op jit(solution)/shard_map/ppermute | solution.py:110
  12.6 8.5 %collective-permute-start.7 = (bf16[64,1024]{1,0:T(8,128)(2,1)S(1)}, bf16[64,1024]{1,0:T(8,128)(2,1)S(1)}, u32[]{:S(2)}, u32[]{:S(2)}) collective-permute-start(bf16[64,1024]{1,0:T(8,128)(2,1)S(1)} %clips_z.2.refs_4_), channel_id=1, source_target_pairs={{0,8},{8,0},{16,24},{24,16},{1,9},{9,1},{17,25},{25,17},{2,10},{10... | collective-permute-start | bytes 393224 | tf_op jit(solution)/shard_map/ppermute | solution.py:110
  16.5 5.9 %collective-permute-start.8 = (bf16[64,1024]{1,0:T(8,128)(2,1)S(1)}, bf16[64,1024]{1,0:T(8,128)(2,1)S(1)}, u32[]{:S(2)}, u32[]{:S(2)}) collective-permute-start(bf16[64,1024]{1,0:T(8,128)(2,1)S(1)} %clips_z.3.refs_5_), channel_id=1, source_target_pairs={{0,8},{8,0},{16,24},{24,16},{1,9},{9,1},{17,25},{25,17},{2,10},{10... | collective-permute-start | bytes 393224 | tf_op jit(solution)/shard_map/ppermute | solution.py:110
  18.2 4.2 %collective-permute-start.4 = (bf16[640,1024]{1,0:T(8,128)(2,1)S(1)}, bf16[640,1024]{1,0:T(8,128)(2,1)S(1)}, u32[]{:S(2)}, u32[]{:S(2)}) collective-permute-start(bf16[640,1024]{1,0:T(8,128)(2,1)S(1)} %near_blocks.1.N), channel_id=1, source_target_pairs={{0,1},{1,0},{2,3},{3,2},{4,5},{5,4},{6,7},{7,6},{8,9},{9,8},{10,11... | collective-permute-start | bytes 3932168 | tf_op jit(solution)/shard_map/ppermute | solution.py:110
  19.6 7.6 %collective-permute-start.10 = (bf16[128,1024]{1,0:T(8,128)(2,1)S(1)}, bf16[128,1024]{1,0:T(8,128)(2,1)S(1)}, u32[]{:S(2)}, u32[]{:S(2)}) collective-permute-start(bf16[128,1024]{1,0:T(8,128)(2,1)S(1)} %captions_z.1.refs_0_), channel_id=1, source_target_pairs={{0,16},{8,24},{16,0},{24,8},{1,17},{9,25},{17,1},{25,9},{2,18},{10... | collective-permute-start | bytes 786440 | tf_op jit(solution)/shard_map/ppermute | solution.py:110
  21.1 1.5 %collective-permute-start.6 = (bf16[128,1024]{1,0:T(8,128)(2,1)S(1)}, bf16[128,1024]{1,0:T(8,128)(2,1)S(1)}, u32[]{:S(2)}, u32[]{:S(2)}) collective-permute-start(bf16[128,1024]{1,0:T(8,128)(2,1)S(1)} %captions_z.1.refs_0_), channel_id=1, source_target_pairs={{0,1},{1,0},{2,3},{3,2},{4,5},{5,4},{6,7},{7,6},{8,9},{9,8},{10,11... | collective-permute-start | bytes 786440 | tf_op jit(solution)/shard_map/ppermute | solution.py:110
  22.4 2.8 %collective-permute-start.9 = (bf16[128,1024]{1,0:T(8,128)(2,1)S(1)}, bf16[128,1024]{1,0:T(8,128)(2,1)S(1)}, u32[]{:S(2)}, u32[]{:S(2)}) collective-permute-start(bf16[128,1024]{1,0:T(8,128)(2,1)S(1)} %diagonal_clips.1.vd), channel_id=1, source_target_pairs={{0,1},{1,0},{2,3},{3,2},{4,5},{5,4},{6,7},{7,6},{8,9},{9,8},{10,11... | collective-permute-start | bytes 786440 | tf_op jit(solution)/shard_map/ppermute | solution.py:110
  27.2 2.7 %collective-permute-start.11 = (bf16[128,1024]{1,0:T(8,128)(2,1)S(1)}, bf16[128,1024]{1,0:T(8,128)(2,1)S(1)}, u32[]{:S(2)}, u32[]{:S(2)}) collective-permute-start(bf16[128,1024]{1,0:T(8,128)(2,1)S(1)} %captions_d.1.refs_0_), channel_id=1, source_target_pairs={{0,1},{1,0},{2,3},{3,2},{4,5},{5,4},{6,7},{7,6},{8,9},{9,8},{10,11... | collective-permute-start | bytes 786440 | tf_op jit(solution)/shard_map/ppermute | solution.py:110
  29.1 5.6 %collective-permute-start.12 = (bf16[64,1024]{1,0:T(8,128)(2,1)S(1)}, bf16[64,1024]{1,0:T(8,128)(2,1)S(1)}, u32[]{:S(2)}, u32[]{:S(2)}) collective-permute-start(bf16[64,1024]{1,0:T(8,128)(2,1)S(1)} %get-tuple-element.58), channel_id=1, source_target_pairs={{0,16},{8,24},{16,0},{24,8},{1,17},{9,25},{17,1},{25,9},{2,18},{10... | collective-permute-start | bytes 393224 | tf_op jit(solution)/shard_map/ppermute | solution.py:110
  31.1 12.3 %collective-permute-start.16 = (bf16[128,1024]{1,0:T(8,128)(2,1)S(1)}, bf16[128,1024]{1,0:T(8,128)(2,1)S(1)}, u32[]{:S(2)}, u32[]{:S(2)}) collective-permute-start(bf16[128,1024]{1,0:T(8,128)(2,1)S(1)} %get-tuple-element.59.refs_1_), channel_id=1, source_target_pairs={{0,8},{8,0},{16,24},{24,16},{1,9},{9,1},{17,25},{25,17},{2,10},{10... | collective-permute-start | bytes 786440 | tf_op jit(solution)/shard_map/ppermute | solution.py:110
  32.5 7.3 %collective-permute-start.14 = (bf16[64,1024]{1,0:T(8,128)(2,1)S(1)}, bf16[64,1024]{1,0:T(8,128)(2,1)S(1)}, u32[]{:S(2)}, u32[]{:S(2)}) collective-permute-start(bf16[64,1024]{1,0:T(8,128)(2,1)S(1)} %far_b.2), channel_id=1, source_target_pairs={{0,16},{8,24},{16,0},{24,8},{1,17},{9,25},{17,1},{25,9},{2,18},{10... | collective-permute-start | bytes 393224 | tf_op jit(solution)/shard_map/ppermute | solution.py:110
  34.7 13.2 %collective-permute-start.15 = (bf16[64,1024]{1,0:T(8,128)(2,1)S(1)}, bf16[64,1024]{1,0:T(8,128)(2,1)S(1)}, u32[]{:S(2)}, u32[]{:S(2)}) collective-permute-start(bf16[64,1024]{1,0:T(8,128)(2,1)S(1)} %add_a.1.after), channel_id=1, source_target_pairs={{0,4},{1,5},{2,6},{3,7},{4,0},{5,1},{6,2},{7,3},{8,12},{9,13},{10,... | collective-permute-start | bytes 393224 | tf_op jit(solution)/shard_map/ppermute | solution.py:110
  37.9 4.3 %collective-permute-start.13 = (f32[2,128]{1,0:T(2,128)S(1)}, f32[2,128]{1,0:T(2,128)S(1)}, u32[]{:S(2)}, u32[]{:S(2)}) collective-permute-start(f32[2,128]{1,0:T(2,128)S(1)} %get-tuple-element.61), channel_id=1, source_target_pairs={{0,8},{8,0},{16,24},{24,16},{1,9},{9,1},{17,25},{25,17},{2,10},{10... | collective-permute-start | bytes 3080 | tf_op jit(solution)/shard_map/ppermute | solution.py:110
  39.8 10.0 %collective-permute-start.21 = (bf16[64,1024]{1,0:T(8,128)(2,1)S(1)}, bf16[64,1024]{1,0:T(8,128)(2,1)S(1)}, u32[]{:S(2)}, u32[]{:S(2)}) collective-permute-start(bf16[64,1024]{1,0:T(8,128)(2,1)S(1)} %add_b.1.refs_1_), channel_id=1, source_target_pairs={{0,4},{1,5},{2,6},{3,7},{4,0},{5,1},{6,2},{7,3},{8,12},{9,13},{10,... | collective-permute-start | bytes 393224 | tf_op jit(solution)/shard_map/ppermute | solution.py:110
  41.0 8.8 %collective-permute-start.18 = (bf16[128,1024]{1,0:T(8,128)(2,1)S(1)}, bf16[128,1024]{1,0:T(8,128)(2,1)S(1)}, u32[]{:S(2)}, u32[]{:S(2)}) collective-permute-start(bf16[128,1024]{1,0:T(8,128)(2,1)S(1)} %near_x.1), channel_id=1, source_target_pairs={{0,8},{8,0},{16,24},{24,16},{1,9},{9,1},{17,25},{25,17},{2,10},{10... | collective-permute-start | bytes 786440 | tf_op jit(solution)/shard_map/ppermute | solution.py:110
  42.2 7.7 %collective-permute-start.20 = (bf16[128,1024]{1,0:T(8,128)(2,1)S(1)}, bf16[128,1024]{1,0:T(8,128)(2,1)S(1)}, u32[]{:S(2)}, u32[]{:S(2)}) collective-permute-start(bf16[128,1024]{1,0:T(8,128)(2,1)S(1)} %near_y.1), channel_id=1, source_target_pairs={{0,16},{8,24},{16,0},{24,8},{1,17},{9,25},{17,1},{25,9},{2,18},{10... | collective-permute-start | bytes 786440 | tf_op jit(solution)/shard_map/ppermute | solution.py:110
  43.4 10.5 %collective-permute-start.19 = (bf16[128,1024]{1,0:T(8,128)(2,1)S(1)}, bf16[128,1024]{1,0:T(8,128)(2,1)S(1)}, u32[]{:S(2)}, u32[]{:S(2)}) collective-permute-start(bf16[128,1024]{1,0:T(8,128)(2,1)S(1)} %add_clips.1.sum_v.refs_1_), channel_id=1, source_target_pairs={{0,2},{1,3},{2,0},{3,1},{4,6},{5,7},{6,4},{7,5},{8,10},{9,11},{10,... | collective-permute-start | bytes 786440 | tf_op jit(solution)/shard_map/ppermute | solution.py:110
  48.0 6.0 %collective-permute-start.17 = (f32[1,128]{1,0:T(1,128)S(1)}, f32[1,128]{1,0:T(1,128)S(1)}, u32[]{:S(2)}, u32[]{:S(2)}) collective-permute-start(f32[1,128]{1,0:T(1,128)S(1)} %add_loss.1.refs_4_), channel_id=1, source_target_pairs={{0,2},{1,3},{2,0},{3,1},{4,6},{5,7},{6,4},{7,5},{8,10},{9,11},{10,... | collective-permute-start | bytes 1544 | tf_op jit(solution)/shard_map/ppermute | solution.py:110

commit v8 on v6

--- a/solution.py
+++ b/solution.py
@@ -219,8 +219,7 @@
         flops=2 * 27 * rows * rows * width, limit=limit,
     )
 
-    def middle_kernel(consts, labels, N, N_k, vd, vdk, S1, p, q, VV, G1, loss, dc0, *refs):
-        dcy, dcz, coef = refs[: Y - 1], refs[Y - 1 : -1], refs[-1]
+    def middle_kernel(consts, labels, N, N_k, vd, vdk, S1, p, q, VV, G1, coef, loss):
         stack(VV, [N.at[nn:], vd, N_k.at[nn:], vdk])
         coef[:, :n3] = p[:, :n3]
         coef[:, n4:n7] = p[:, n3:]
@@ -231,24 +230,14 @@
         ) + strip(consts, near + up, 1, S1[na:, :], vd[...], late, n1, put_in(G1, na, n3))
         strip(consts, near + up, 0, S1[:na, :], vdk[...], labels[:, n7:], 0, put_in(coef, left=n7))
         G1[:na, :] = coef[:, :n4]
-        for i in range(width // CHUNK):
-            cols = pl.ds(i * CHUNK, CHUNK)
-            part = dot_nn(coef[...], VV[:, cols])
-            for j, ref in enumerate((dc0, *dcy)):
-                ref[:, cols] = part[j * rows : (j + 1) * rows].astype(ref.dtype)
-            for j, ref in enumerate(dcz):
-                ref[:, cols] = part[nn + j * half : nn + (j + 1) * half]
-
-    VV, G1, loss_m, dc0, *dcs = call(
-        "middle_sums", middle_kernel,
-        [vm((8 * n1, width)), vm((2 * na, n4)), vm((1, n1), F32), vm(mat, F32)]
-        + [vm(mat)] * (Y - 1) + [vm(hmat, F32)] * (2 * (Z - 1)),
+
+    VV, G1, coef_a, loss_m = call(
+        "middle_pairs", middle_kernel,
+        [vm((8 * n1, width)), vm((2 * na, n4)), vm((na, 8 * n1)), vm((1, n1), F32)],
         [consts, labels, N, N_k, v_d, vd_k, S1, p, q],
-        flops=2 * 33 * rows * rows * width, limit=limit,
-        scratch=[pltpu.VMEM((na, 8 * n1), BF16)],
-    )
-    dcy, dcz = dcs[: Y - 1], dcs[Y - 1 :]
-    c_d = [hand_on("captions_d", b, dc0, flops=3 * LONG) for b in c_d]
+        flops=2 * 9 * rows * rows * width, limit=limit,
+    )
+    c_d = [hand_on("captions_d", b, loss_m, flops=3 * LONG) for b in c_d]
     D_k = [swap(b, "col", 1) for b in c_d]
 
     def far_captions_kernel(consts, labels, VV, *refs):
@@ -289,6 +278,24 @@
     )
     far_v = swap(dv_d, "row", 1)
 
+    def near_captions_kernel(coef, VV, after, dc0, *refs):
+        dcy, dcz = refs[: Y - 1], refs[Y - 1 :]
+        for i in range(width // CHUNK):
+            cols = pl.ds(i * CHUNK, CHUNK)
+            part = dot_nn(coef[...], VV[:, cols])
+            for j, ref in enumerate((dc0, *dcy)):
+                ref[:, cols] = part[j * rows : (j + 1) * rows].astype(ref.dtype)
+            for j, ref in enumerate(dcz):
+                ref[:, cols] = part[nn + j * half : nn + (j + 1) * half]
+
+    dc0, *dcs = call(
+        "near_captions", near_captions_kernel,
+        [vm(mat, F32)] + [vm(mat)] * (Y - 1) + [vm(hmat, F32)] * (2 * (Z - 1)),
+        [coef_a, VV, dv_d],
+        flops=2 * 24 * rows * rows * width, limit=limit,
+    )
+    dcy, dcz = dcs[: Y - 1], dcs[Y - 1 :]
+
     def add_kernel(*refs):
         total = refs[0][...].astype(F32)
         for ref in refs[1:-1]:
@@ -308,7 +315,7 @@
             sums.append(add("add_" + "ab"[h], dcz[2 * s + h], *far))
         return sums, [swap(sums[s], "col", 4 * (s + 1)) for s in range(Z - 1)]
 
-    sums_a, got_a = captions_back(0, dv_d)
+    sums_a, got_a = captions_back(0, dc0)
     dcd = [hand_on("far_b", b, dv_d) if i % 2 else b for i, b in enumerate(dcd)]
     def near_clips_kernel(S1, S2, G1, G2, after, dv0, dvx, dvz):
         for i in range(width // CHUNK):
@@ -327,6 +334,7 @@
     got_z = hand_on("clips_back", swap(sum_v, "col", 2), flops=3 * LONG)
     got_h = [[hand_on("captions_back", b, sum_v, flops=3 * LONG) for b in got] for got in (got_a, got_b)]
     dcy = [hand_on("near_y", b, *sums_b) for b in dcy]
+    dvx = hand_on("near_x", dvx, sum_v)
     got_y = [hand_on("captions_y", swap(dcy[t - 1], "row", 2 * t), sum_v, flops=LONG) for t in range(1, Y)]
     got_x = hand_on("clips_x", swap(dvx, "row", 1), sum_v, flops=4 * LONG)
 
@@ -347,7 +355,7 @@
         [loss_a, loss_m, loss_c, loss_d, sums_a[0]],
     )
     far_loss = hand_on("losses_x", swap(loss_x, "row", 1), *sums_b)
-    (sum_loss,) = call("add_loss", add_loss_kernel, [vm((1, n1), F32)], [loss_z, far_loss, got_a[0], sum_v])
+    (sum_loss,) = call("add_loss", add_loss_kernel, [vm((1, n1), F32)], [loss_z, far_loss, got_b[0], sum_v])
     got_loss = swap(sum_loss, "col", 2)
 
     def finish(name, losses, consts, hat, inverse, own, whole, halves, *after):

time: 58.1 us -> 55.5 us (0.955)
  starting transfers between devices: 27.6 us -> 25.9 us
  waiting for transfers between devices: 16.2 us -> 15 us
    ppermute x22, starting transfers between devices: 27.6 us -> 25.9 us  [swap(): return lax.ppermute(value, axis, [(i, i ^ bits) for i in range(size)])]
    ppermute x22, waiting for transfers between devices: 16.2 us -> 15 us  [swap(): return lax.ppermute(value, axis, [(i, i ^ bits) for i in range(size)])]
    pallas_call x33 -> x35, Pallas kernels: 12.1 us -> 12.4 us  [call(): pl.pallas_call(kernel, name=name, out_shape=out_shape, in_specs=[SPECS[sp...]
  transfers between devices with their start and end apart: 22 -> 22, of which waited for: 12 -> 11; matrix products, arithmetic and copies ran while one was open for 0% -> 0% of each run, Pallas kernels for 16% -> 18%
where the time goes in v8:
time: 55.5 us; the launch traced here: 55.4 us
  starting transfers between devices  25.9 us (47%)
  waiting for transfers between devices  15 us (27%)
  Pallas kernels  12.4 us (22%)
  between operations  2.13 us (4%)
    ppermute x22, starting transfers between devices, swap(): return lax.ppermute(value, axis, [(i, i ^ bits) for i in range(size)])  25.9 us
    ppermute x22, waiting for transfers between devices, swap(): return lax.ppermute(value, axis, [(i, i ^ bits) for i in range(size)])  15 us
    pallas_call x35, Pallas kernels, call(): pl.pallas_call(kernel, name=name, out_shape=out_shape, in_specs=[SPECS[sp...  12.4 us
  transfers between devices with their start and end apart: 22, of which 11 were waited for; matrix products, arithmetic and copies ran while one was open for 0% of the time, Pallas kernels for 18%

profile of v8, /device:TPU:0, one launch (start us, length us, event | category | flops | bytes accessed | tf_op | source)
XLA Modules:
  0.0 55.4 jit_solution(5885445182135895808)
XLA Ops:
  0.6 1.5 %normalize.1 = (bf16[128,1024]{1,0:T(8,128)(2,1)S(1)}, bf16[128,1024]{1,0:T(8,128)(2,1)S(1)}, bf16[64,1024]{1,0:T(8,128)(2,1)S(1)}, bf16[64,1024]{1,0:T(8,128)(2...) custom-call(f32[128,1024]{1,0:T(8,128)} %film.1, ...), custom_call_target="tpu_custom_call" | custom-call | tf_op jit(solution)/shard_map/normalize/pallas_call | solution.py:28
  2.2 3.1 %collective-permute-start.2 = (bf16[64,1024]{1,0:T(8,128)(2,1)S(1)}, bf16[64,1024]{1,0:T(8,128)(2,1)S(1)}, u32[]{:S(2)}, u32[]{:S(2)}) collective-permute-start(bf16[64,1024]{1,0:T(8,128)(2,1)S(1)} %get-tuple-element.45), channel_id=1, source_target_pairs={{0,2},{1,3},{2,0},{3,1},{4,6},{5,7},{6,4},{7,5},{8,10},{9,11},{10,... | collective-permute-start | bytes 393224 | tf_op jit(solution)/shard_map/ppermute | solution.py:110
  5.3 2.6 %collective-permute-start.5 = (bf16[128,1024]{1,0:T(8,128)(2,1)S(1)}, bf16[128,1024]{1,0:T(8,128)(2,1)S(1)}, u32[]{:S(2)}, u32[]{:S(2)}) collective-permute-start(bf16[128,1024]{1,0:T(8,128)(2,1)S(1)} %get-tuple-element.43.refs_0_), channel_id=1, source_target_pairs={{0,4},{1,5},{2,6},{3,7},{4,0},{5,1},{6,2},{7,3},{8,12},{9,13},{10,... | collective-permute-start | bytes 786440 | tf_op jit(solution)/shard_map/ppermute | solution.py:110
  7.8 1.5 %collective-permute-start = (bf16[128,1024]{1,0:T(8,128)(2,1)S(1)}, bf16[128,1024]{1,0:T(8,128)(2,1)S(1)}, u32[]{:S(2)}, u32[]{:S(2)}) collective-permute-start(bf16[128,1024]{1,0:T(8,128)(2,1)S(1)} %get-tuple-element.43.refs_0_), channel_id=1, source_target_pairs={{0,16},{8,24},{16,0},{24,8},{1,17},{9,25},{17,1},{25,9},{2,18},{10... | collective-permute-start | bytes 786440 | tf_op jit(solution)/shard_map/ppermute | solution.py:110
  9.8 1.5 %collective-permute-start.1 = (bf16[128,1024]{1,0:T(8,128)(2,1)S(1)}, bf16[128,1024]{1,0:T(8,128)(2,1)S(1)}, u32[]{:S(2)}, u32[]{:S(2)}) collective-permute-start(bf16[128,1024]{1,0:T(8,128)(2,1)S(1)} %get-tuple-element.44.refs_2_), channel_id=1, source_target_pairs={{0,8},{8,0},{16,24},{24,16},{1,9},{9,1},{17,25},{25,17},{2,10},{10... | collective-permute-start | bytes 786440 | tf_op jit(solution)/shard_map/ppermute | solution.py:110
  12.6 0.6 %collective-permute-start.7 = (bf16[64,1024]{1,0:T(8,128)(2,1)S(1)}, bf16[64,1024]{1,0:T(8,128)(2,1)S(1)}, u32[]{:S(2)}, u32[]{:S(2)}) collective-permute-start(bf16[64,1024]{1,0:T(8,128)(2,1)S(1)} %clips_z.2.refs_4_), channel_id=1, source_target_pairs={{0,8},{8,0},{16,24},{24,16},{1,9},{9,1},{17,25},{25,17},{2,10},{10... | collective-permute-start | bytes 393224 | tf_op jit(solution)/shard_map/ppermute | solution.py:110
  13.2 3.2 %collective-permute-done.3.refs_0_ = bf16[64,1024]{1,0:T(8,128)(2,1)S(1)} collective-permute-done((bf16[64,1024]{1,0:T(8,128)(2,1)S(1)}, bf16[64,1024]{1,0:T(8,128)(2,1)S(1)}, u32[]{:S(2)}, u32[]{:S(2)}) %collective-permute-start.3) | collective-permute-done | bytes 131104 | tf_op jit(solution)/shard_map/ppermute | solution.py:110
  16.5 1.5 %collective-permute-start.8 = (bf16[64,1024]{1,0:T(8,128)(2,1)S(1)}, bf16[64,1024]{1,0:T(8,128)(2,1)S(1)}, u32[]{:S(2)}, u32[]{:S(2)}) collective-permute-start(bf16[64,1024]{1,0:T(8,128)(2,1)S(1)} %clips_z.3.refs_5_), channel_id=1, source_target_pairs={{0,8},{8,0},{16,24},{24,16},{1,9},{9,1},{17,25},{25,17},{2,10},{10... | collective-permute-start | bytes 393224 | tf_op jit(solution)/shard_map/ppermute | solution.py:110
  18.3 1.3 %collective-permute-done.5.refs_0_ = bf16[128,1024]{1,0:T(8,128)(2,1)S(1)} collective-permute-done((bf16[128,1024]{1,0:T(8,128)(2,1)S(1)}, bf16[128,1024]{1,0:T(8,128)(2,1)S(1)}, u32[]{:S(2)}, u32[]{:S(2)}) %collective-permute-start.5) | collective-permute-done | bytes 262176 | tf_op jit(solution)/shard_map/ppermute | solution.py:110
  19.6 1.5 %collective-permute-start.10 = (bf16[128,1024]{1,0:T(8,128)(2,1)S(1)}, bf16[128,1024]{1,0:T(8,128)(2,1)S(1)}, u32[]{:S(2)}, u32[]{:S(2)}) collective-permute-start(bf16[128,1024]{1,0:T(8,128)(2,1)S(1)} %captions_z.1.refs_0_), channel_id=1, source_target_pairs={{0,16},{8,24},{16,0},{24,8},{1,17},{9,25},{17,1},{25,9},{2,18},{10... | collective-permute-start | bytes 786440 | tf_op jit(solution)/shard_map/ppermute | solution.py:110
  21.1 1.2 %collective-permute-done.8.refs_0_ = bf16[64,1024]{1,0:T(8,128)(2,1)S(1)} collective-permute-done((bf16[64,1024]{1,0:T(8,128)(2,1)S(1)}, bf16[64,1024]{1,0:T(8,128)(2,1)S(1)}, u32[]{:S(2)}, u32[]{:S(2)}) %collective-permute-start.8) | collective-permute-done | bytes 131104 | tf_op jit(solution)/shard_map/ppermute | solution.py:110
  22.6 2.5 %early_pairs.1 = (bf16[768,1024]{1,0:T(8,128)(2,1)S(1)}, bf16[384,768]{1,0:T(8,128)(2,1)S(1)}, bf16[384,384]{1,0:T(8,128)(2,1)S(1)}, f32[1,384]{1,0:T(1,128)S(1)}) custom-call(f32[2,128]{1,0:T(2,128)S(1)} %consts.1.refs_1_, s32[1,1024]{1,0:T(1,128)S(1)} %get-tuple-element.42.labels, bf16[640,1024]{1,0:T(8,128)(2,1)S(1)} %near_blocks.1.N, ...), custom_call_target="tpu_custom_call" | custom-call | flops 905969664 | tf_op jit(solution)/shard_map/early_pairs/pallas_call | solution.py:28
  25.2 1.3 %middle_pairs.1 = (bf16[1024,1024]{1,0:T(8,128)(2,1)S(1)}, bf16[768,512]{1,0:T(8,128)(2,1)S(1)}, bf16[384,1024]{1,0:T(8,128)(2,1)S(1)}, f32[1,128]{1,0:T(1,128)S(1)}) custom-call(f32[2,128]{1,0:T(2,128)S(1)} %consts.1.refs_1_, s32[1,1024]{1,0:T(1,128)S(1)} %get-tuple-element.42.labels, bf16[640,1024]{1,0:T(8,128)(2,1)S(1)} %near_blocks.1.N, ...), custom_call_target="tpu_custom_call" | custom-call | flops 301989888 | tf_op jit(solution)/shard_map/middle_pairs/pallas_call | solution.py:28
  26.5 0.6 %collective-permute-done.10.refs_0_ = bf16[128,1024]{1,0:T(8,128)(2,1)S(1)} collective-permute-done((bf16[128,1024]{1,0:T(8,128)(2,1)S(1)}, bf16[128,1024]{1,0:T(8,128)(2,1)S(1)}, u32[]{:S(2)}, u32[]{:S(2)}) %collective-permute-start.10) | collective-permute-done | bytes 262176 | tf_op jit(solution)/shard_map/ppermute | solution.py:110
  27.0 1.5 %far_captions.1 = (f32[1,512]{1,0:T(1,128)S(1)}, bf16[128,512]{1,0:T(8,128)(2,1)S(1)}, bf16[64,1024]{1,0:T(8,128)(2,1)S(1)}, bf16[64,1024]{1,0:T(8,128)(2,1)S(1)}) custom-call(f32[2,128]{1,0:T(2,128)S(1)} %consts.1.refs_1_, s32[1,1024]{1,0:T(1,128)S(1)} %get-tuple-element.42.labels, bf16[1024,1024]{1,0:T(8,128)(2,1)S(1)} %get-tuple-element.52.VV, ...), custom_call_target="tpu_custom_call" | custom-call | flops 536870912 | tf_op jit(solution)/shard_map/far_captions/pallas_call | solution.py:28
  28.5 1.4 %collective-permute-start.12 = (bf16[64,1024]{1,0:T(8,128)(2,1)S(1)}, bf16[64,1024]{1,0:T(8,128)(2,1)S(1)}, u32[]{:S(2)}, u32[]{:S(2)}) collective-permute-start(bf16[64,1024]{1,0:T(8,128)(2,1)S(1)} %get-tuple-element.60), channel_id=1, source_target_pairs={{0,16},{8,24},{16,0},{24,8},{1,17},{9,25},{17,1},{25,9},{2,18},{10... | collective-permute-start | bytes 393224 | tf_op jit(solution)/shard_map/ppermute | solution.py:110
  29.9 1.2 %far_clips.1 = (bf16[256,1024]{1,0:T(8,128)(2,1)S(1)}, bf16[256,512]{1,0:T(8,128)(2,1)S(1)}, f32[1,512]{1,0:T(1,128)S(1)}, bf16[128,1024]{1,0:T(8,128)(2,1)S(1)}) custom-call(f32[2,128]{1,0:T(2,128)S(1)} %consts.1.refs_1_, s32[1,1024]{1,0:T(1,128)S(1)} %get-tuple-element.42.labels, bf16[1024,1024]{1,0:T(8,128)(2,1)S(1)} %get-tuple-element.52.VV, ...), custom_call_target="tpu_custom_call" | custom-call | flops 402653184 | tf_op jit(solution)/shard_map/far_clips/pallas_call | solution.py:28
  31.1 1.2 %collective-permute-start.16 = (bf16[128,1024]{1,0:T(8,128)(2,1)S(1)}, bf16[128,1024]{1,0:T(8,128)(2,1)S(1)}, u32[]{:S(2)}, u32[]{:S(2)}) collective-permute-start(bf16[128,1024]{1,0:T(8,128)(2,1)S(1)} %get-tuple-element.58.after.refs_1_), channel_id=1, source_target_pairs={{0,8},{8,0},{16,24},{24,16},{1,9},{9,1},{17,25},{25,17},{2,10},{10... | collective-permute-start | bytes 786440 | tf_op jit(solution)/shard_map/ppermute | solution.py:110
  32.3 1.1 %collective-permute-start.14 = (bf16[64,1024]{1,0:T(8,128)(2,1)S(1)}, bf16[64,1024]{1,0:T(8,128)(2,1)S(1)}, u32[]{:S(2)}, u32[]{:S(2)}) collective-permute-start(bf16[64,1024]{1,0:T(8,128)(2,1)S(1)} %far_b.2), channel_id=1, source_target_pairs={{0,16},{8,24},{16,0},{24,8},{1,17},{9,25},{17,1},{25,9},{2,18},{10... | collective-permute-start | bytes 393224 | tf_op jit(solution)/shard_map/ppermute | solution.py:110
  33.3 1.0 %near_captions.1 = (f32[128,1024]{1,0:T(8,128)S(1)}, bf16[128,1024]{1,0:T(8,128)(2,1)S(1)}, f32[64,1024]{1,0:T(8,128)S(1)}, f32[64,1024]{1,0:T(8,128)S(1)}) custom-call(bf16[384,1024]{1,0:T(8,128)(2,1)S(1)} %get-tuple-element.57.coef, bf16[1024,1024]{1,0:T(8,128)(2,1)S(1)} %get-tuple-element.52.VV, bf16[128,1024]{1,0:T(8,128)(2,1)S(1)} %get-tuple-element.58.after.refs_1_), custom_call_target="tpu_custom_call" | custom-call | flops 805306368 | tf_op jit(solution)/shard_map/near_captions/pallas_call | solution.py:28
  34.5 3.4 %collective-permute-start.21 = (bf16[64,1024]{1,0:T(8,128)(2,1)S(1)}, bf16[64,1024]{1,0:T(8,128)(2,1)S(1)}, u32[]{:S(2)}, u32[]{:S(2)}) collective-permute-start(bf16[64,1024]{1,0:T(8,128)(2,1)S(1)} %add_a.1.after), channel_id=1, source_target_pairs={{0,4},{1,5},{2,6},{3,7},{4,0},{5,1},{6,2},{7,3},{8,12},{9,13},{10,... | collective-permute-start | bytes 393224 | tf_op jit(solution)/shard_map/ppermute | solution.py:110
  37.9 0.6 collective-permute-start.13
  38.5 1.0 %near_clips.1 = (f32[128,1024]{1,0:T(8,128)S(1)}, bf16[128,1024]{1,0:T(8,128)(2,1)S(1)}, f32[128,1024]{1,0:T(8,128)S(1)}) custom-call(bf16[768,1024]{1,0:T(8,128)(2,1)S(1)} %get-tuple-element.48.S1, bf16[256,1024]{1,0:T(8,128)(2,1)S(1)} %get-tuple-element.66.S2, bf16[768,512]{1,0:T(8,128)(2,1)S(1)} %get-tuple-element.54.G1, ...), custom_call_target="tpu_custom_call" | custom-call | flops 805306368 | tf_op jit(solution)/shard_map/near_clips/pallas_call | solution.py:28
  39.5 1.2 %collective-permute-start.15 = (bf16[64,1024]{1,0:T(8,128)(2,1)S(1)}, bf16[64,1024]{1,0:T(8,128)(2,1)S(1)}, u32[]{:S(2)}, u32[]{:S(2)}) collective-permute-start(bf16[64,1024]{1,0:T(8,128)(2,1)S(1)} %add_b.1.refs_1_), channel_id=1, source_target_pairs={{0,4},{1,5},{2,6},{3,7},{4,0},{5,1},{6,2},{7,3},{8,12},{9,13},{10,... | collective-permute-start | bytes 393224 | tf_op jit(solution)/shard_map/ppermute | solution.py:110
  40.7 1.5 %collective-permute-start.20 = (bf16[128,1024]{1,0:T(8,128)(2,1)S(1)}, bf16[128,1024]{1,0:T(8,128)(2,1)S(1)}, u32[]{:S(2)}, u32[]{:S(2)}) collective-permute-start(bf16[128,1024]{1,0:T(8,128)(2,1)S(1)} %near_y.1), channel_id=1, source_target_pairs={{0,16},{8,24},{16,0},{24,8},{1,17},{9,25},{17,1},{25,9},{2,18},{10... | collective-permute-start | bytes 786440 | tf_op jit(solution)/shard_map/ppermute | solution.py:110
  42.3 0.9 %collective-permute-start.19 = (bf16[128,1024]{1,0:T(8,128)(2,1)S(1)}, bf16[128,1024]{1,0:T(8,128)(2,1)S(1)}, u32[]{:S(2)}, u32[]{:S(2)}) collective-permute-start(bf16[128,1024]{1,0:T(8,128)(2,1)S(1)} %add_clips.1.sum_v.refs_1_), channel_id=1, source_target_pairs={{0,2},{1,3},{2,0},{3,1},{4,6},{5,7},{6,4},{7,5},{8,10},{9,11},{10,... | collective-permute-start | bytes 786440 | tf_op jit(solution)/shard_map/ppermute | solution.py:110
  43.2 1.8 %collective-permute-start.18 = (bf16[128,1024]{1,0:T(8,128)(2,1)S(1)}, bf16[128,1024]{1,0:T(8,128)(2,1)S(1)}, u32[]{:S(2)}, u32[]{:S(2)}) collective-permute-start(bf16[128,1024]{1,0:T(8,128)(2,1)S(1)} %near_x.1), channel_id=1, source_target_pairs={{0,8},{8,0},{16,24},{24,16},{1,9},{9,1},{17,25},{25,17},{2,10},{10... | collective-permute-start | bytes 786440 | tf_op jit(solution)/shard_map/ppermute | solution.py:110
  45.0 2.9 %collective-permute-done.21.refs_0_ = bf16[64,1024]{1,0:T(8,128)(2,1)S(1)} collective-permute-done((bf16[64,1024]{1,0:T(8,128)(2,1)S(1)}, bf16[64,1024]{1,0:T(8,128)(2,1)S(1)}, u32[]{:S(2)}, u32[]{:S(2)}) %collective-permute-start.21) | collective-permute-done | bytes 131104 | tf_op jit(solution)/shard_map/ppermute | solution.py:110
  48.0 1.9 %collective-permute-done.15.got.refs_0_ = bf16[64,1024]{1,0:T(8,128)(2,1)S(1)} collective-permute-done((bf16[64,1024]{1,0:T(8,128)(2,1)S(1)}, bf16[64,1024]{1,0:T(8,128)(2,1)S(1)}, u32[]{:S(2)}, u32[]{:S(2)}) %collective-permute-start.15) | collective-permute-done | bytes 131104 | tf_op jit(solution)/shard_map/ppermute | solution.py:110
  49.8 1.1 %finish_captions.1 = f32[128,1024]{1,0:T(8,128)} custom-call(f32[2,128]{1,0:T(2,128)S(1)} %consts.1.refs_1_, f32[128,1024]{1,0:T(8,128)S(1)} %get-tuple-element.74.hat_ref, f32[128,1]{1,0:T(8,128)S(1)} %get-tuple-element.75.inverse_ref, f32[128,1024]{1,0:T(8,128)S(1)} %get-tuple-element.61.refs_1_.refs_0_, bf16[128,1024]{1,0:T(8,128)(2,1)S(1)} %captions_y.1.refs_1_, ...), custom_call_target="tpu_custom_call" | custom-call | tf_op jit(solution)/shard_map/finish_captions/pallas_call | solution.py:28
  51.0 3.3 %collective-permute-done.19.refs_0_ = bf16[128,1024]{1,0:T(8,128)(2,1)S(1)} collective-permute-done((bf16[128,1024]{1,0:T(8,128)(2,1)S(1)}, bf16[128,1024]{1,0:T(8,128)(2,1)S(1)}, u32[]{:S(2)}, u32[]{:S(2)}) %collective-permute-start.19) | collective-permute-done | bytes 262176 | tf_op jit(solution)/shard_map/ppermute | solution.py:110
  54.3 1.1 %finish_clips.1 = (f32[128,1024]{1,0:T(8,128)}, f32[1,128]{1,0:T(1,128)}) custom-call(f32[2,128]{1,0:T(2,128)S(1)} %consts.1.refs_1_, f32[128,1024]{1,0:T(8,128)S(1)} %get-tuple-element.40.hat_ref, f32[128,1]{1,0:T(8,128)S(1)} %get-tuple-element.41.inverse_ref, f32[1,128]{1,0:T(1,128)S(1)} %get-tuple-element.62.refs_0_, ...), custom_call_target="tpu_custom_call" | custom-call | tf_op jit(solution)/shard_map/finish_clips/pallas_call | solution.py:28
  (47 shorter events, 1.4 us)
Async XLA Ops:
  2.2 10.5 %collective-permute-start.2 = (bf16[64,1024]{1,0:T(8,128)(2,1)S(1)}, bf16[64,1024]{1,0:T(8,128)(2,1)S(1)}, u32[]{:S(2)}, u32[]{:S(2)}) collective-permute-start(bf16[64,1024]{1,0:T(8,128)(2,1)S(1)} %get-tuple-element.45), channel_id=1, source_target_pairs={{0,2},{1,3},{2,0},{3,1},{4,6},{5,7},{6,4},{7,5},{8,10},{9,11},{10,... | collective-permute-start | bytes 393224 | tf_op jit(solution)/shard_map/ppermute | solution.py:110
  5.3 14.3 %collective-permute-start.5 = (bf16[128,1024]{1,0:T(8,128)(2,1)S(1)}, bf16[128,1024]{1,0:T(8,128)(2,1)S(1)}, u32[]{:S(2)}, u32[]{:S(2)}) collective-permute-start(bf16[128,1024]{1,0:T(8,128)(2,1)S(1)} %get-tuple-element.43.refs_0_), channel_id=1, source_target_pairs={{0,4},{1,5},{2,6},{3,7},{4,0},{5,1},{6,2},{7,3},{8,12},{9,13},{10,... | collective-permute-start | bytes 786440 | tf_op jit(solution)/shard_map/ppermute | solution.py:110
  7.8 10.3 %collective-permute-start = (bf16[128,1024]{1,0:T(8,128)(2,1)S(1)}, bf16[128,1024]{1,0:T(8,128)(2,1)S(1)}, u32[]{:S(2)}, u32[]{:S(2)}) collective-permute-start(bf16[128,1024]{1,0:T(8,128)(2,1)S(1)} %get-tuple-element.43.refs_0_), channel_id=1, source_target_pairs={{0,16},{8,24},{16,0},{24,8},{1,17},{9,25},{17,1},{25,9},{2,18},{10... | collective-permute-start | bytes 786440 | tf_op jit(solution)/shard_map/ppermute | solution.py:110
  9.4 7.1 %collective-permute-start.3 = (bf16[64,1024]{1,0:T(8,128)(2,1)S(1)}, bf16[64,1024]{1,0:T(8,128)(2,1)S(1)}, u32[]{:S(2)}, u32[]{:S(2)}) collective-permute-start(bf16[64,1024]{1,0:T(8,128)(2,1)S(1)} %get-tuple-element.46), channel_id=1, source_target_pairs={{0,2},{1,3},{2,0},{3,1},{4,6},{5,7},{6,4},{7,5},{8,10},{9,11},{10,... | collective-permute-start | bytes 393224 | tf_op jit(solution)/shard_map/ppermute | solution.py:110
  9.8 8.3 %collective-permute-start.1 = (bf16[128,1024]{1,0:T(8,128)(2,1)S(1)}, bf16[128,1024]{1,0:T(8,128)(2,1)S(1)}, u32[]{:S(2)}, u32[]{:S(2)}) collective-permute-start(bf16[128,1024]{1,0:T(8,128)(2,1)S(1)} %get-tuple-element.44.refs_2_), channel_id=1, source_target_pairs={{0,8},{8,0},{16,24},{24,16},{1,9},{9,1},{17,25},{25,17},{2,10},{10... | collective-permute-start | bytes 786440 | tf_op jit(solution)/shard_map/ppermute | solution.py:110
  12.6 8.5 %collective-permute-start.7 = (bf16[64,1024]{1,0:T(8,128)(2,1)S(1)}, bf16[64,1024]{1,0:T(8,128)(2,1)S(1)}, u32[]{:S(2)}, u32[]{:S(2)}) collective-permute-start(bf16[64,1024]{1,0:T(8,128)(2,1)S(1)} %clips_z.2.refs_4_), channel_id=1, source_target_pairs={{0,8},{8,0},{16,24},{24,16},{1,9},{9,1},{17,25},{25,17},{2,10},{10... | collective-permute-start | bytes 393224 | tf_op jit(solution)/shard_map/ppermute | solution.py:110
  16.5 5.9 %collective-permute-start.8 = (bf16[64,1024]{1,0:T(8,128)(2,1)S(1)}, bf16[64,1024]{1,0:T(8,128)(2,1)S(1)}, u32[]{:S(2)}, u32[]{:S(2)}) collective-permute-start(bf16[64,1024]{1,0:T(8,128)(2,1)S(1)} %clips_z.3.refs_5_), channel_id=1, source_target_pairs={{0,8},{8,0},{16,24},{24,16},{1,9},{9,1},{17,25},{25,17},{2,10},{10... | collective-permute-start | bytes 393224 | tf_op jit(solution)/shard_map/ppermute | solution.py:110
  18.2 4.2 %collective-permute-start.4 = (bf16[640,1024]{1,0:T(8,128)(2,1)S(1)}, bf16[640,1024]{1,0:T(8,128)(2,1)S(1)}, u32[]{:S(2)}, u32[]{:S(2)}) collective-permute-start(bf16[640,1024]{1,0:T(8,128)(2,1)S(1)} %near_blocks.1.N), channel_id=1, source_target_pairs={{0,1},{1,0},{2,3},{3,2},{4,5},{5,4},{6,7},{7,6},{8,9},{9,8},{10,11... | collective-permute-start | bytes 3932168 | tf_op jit(solution)/shard_map/ppermute | solution.py:110
  19.6 7.4 %collective-permute-start.10 = (bf16[128,1024]{1,0:T(8,128)(2,1)S(1)}, bf16[128,1024]{1,0:T(8,128)(2,1)S(1)}, u32[]{:S(2)}, u32[]{:S(2)}) collective-permute-start(bf16[128,1024]{1,0:T(8,128)(2,1)S(1)} %captions_z.1.refs_0_), channel_id=1, source_target_pairs={{0,16},{8,24},{16,0},{24,8},{1,17},{9,25},{17,1},{25,9},{2,18},{10... | collective-permute-start | bytes 786440 | tf_op jit(solution)/shard_map/ppermute | solution.py:110
  21.1 1.5 %collective-permute-start.6 = (bf16[128,1024]{1,0:T(8,128)(2,1)S(1)}, bf16[128,1024]{1,0:T(8,128)(2,1)S(1)}, u32[]{:S(2)}, u32[]{:S(2)}) collective-permute-start(bf16[128,1024]{1,0:T(8,128)(2,1)S(1)} %captions_z.1.refs_0_), channel_id=1, source_target_pairs={{0,1},{1,0},{2,3},{3,2},{4,5},{5,4},{6,7},{7,6},{8,9},{9,8},{10,11... | collective-permute-start | bytes 786440 | tf_op jit(solution)/shard_map/ppermute | solution.py:110
  22.4 2.8 %collective-permute-start.9 = (bf16[128,1024]{1,0:T(8,128)(2,1)S(1)}, bf16[128,1024]{1,0:T(8,128)(2,1)S(1)}, u32[]{:S(2)}, u32[]{:S(2)}) collective-permute-start(bf16[128,1024]{1,0:T(8,128)(2,1)S(1)} %diagonal_clips.1.vd), channel_id=1, source_target_pairs={{0,1},{1,0},{2,3},{3,2},{4,5},{5,4},{6,7},{7,6},{8,9},{9,8},{10,11... | collective-permute-start | bytes 786440 | tf_op jit(solution)/shard_map/ppermute | solution.py:110
  27.0 2.9 %collective-permute-start.11 = (bf16[128,1024]{1,0:T(8,128)(2,1)S(1)}, bf16[128,1024]{1,0:T(8,128)(2,1)S(1)}, u32[]{:S(2)}, u32[]{:S(2)}) collective-permute-start(bf16[128,1024]{1,0:T(8,128)(2,1)S(1)} %captions_d.1.refs_0_), channel_id=1, source_target_pairs={{0,1},{1,0},{2,3},{3,2},{4,5},{5,4},{6,7},{7,6},{8,9},{9,8},{10,11... | collective-permute-start | bytes 786440 | tf_op jit(solution)/shard_map/ppermute | solution.py:110
  28.5 6.0 %collective-permute-start.12 = (bf16[64,1024]{1,0:T(8,128)(2,1)S(1)}, bf16[64,1024]{1,0:T(8,128)(2,1)S(1)}, u32[]{:S(2)}, u32[]{:S(2)}) collective-permute-start(bf16[64,1024]{1,0:T(8,128)(2,1)S(1)} %get-tuple-element.60), channel_id=1, source_target_pairs={{0,16},{8,24},{16,0},{24,8},{1,17},{9,25},{17,1},{25,9},{2,18},{10... | collective-permute-start | bytes 393224 | tf_op jit(solution)/shard_map/ppermute | solution.py:110
  31.1 11.2 %collective-permute-start.16 = (bf16[128,1024]{1,0:T(8,128)(2,1)S(1)}, bf16[128,1024]{1,0:T(8,128)(2,1)S(1)}, u32[]{:S(2)}, u32[]{:S(2)}) collective-permute-start(bf16[128,1024]{1,0:T(8,128)(2,1)S(1)} %get-tuple-element.58.after.refs_1_), channel_id=1, source_target_pairs={{0,8},{8,0},{16,24},{24,16},{1,9},{9,1},{17,25},{25,17},{2,10},{10... | collective-permute-start | bytes 786440 | tf_op jit(solution)/shard_map/ppermute | solution.py:110
  32.3 7.2 %collective-permute-start.14 = (bf16[64,1024]{1,0:T(8,128)(2,1)S(1)}, bf16[64,1024]{1,0:T(8,128)(2,1)S(1)}, u32[]{:S(2)}, u32[]{:S(2)}) collective-permute-start(bf16[64,1024]{1,0:T(8,128)(2,1)S(1)} %far_b.2), channel_id=1, source_target_pairs={{0,16},{8,24},{16,0},{24,8},{1,17},{9,25},{17,1},{25,9},{2,18},{10... | collective-permute-start | bytes 393224 | tf_op jit(solution)/shard_map/ppermute | solution.py:110
  34.5 13.5 %collective-permute-start.21 = (bf16[64,1024]{1,0:T(8,128)(2,1)S(1)}, bf16[64,1024]{1,0:T(8,128)(2,1)S(1)}, u32[]{:S(2)}, u32[]{:S(2)}) collective-permute-start(bf16[64,1024]{1,0:T(8,128)(2,1)S(1)} %add_a.1.after), channel_id=1, source_target_pairs={{0,4},{1,5},{2,6},{3,7},{4,0},{5,1},{6,2},{7,3},{8,12},{9,13},{10,... | collective-permute-start | bytes 393224 | tf_op jit(solution)/shard_map/ppermute | solution.py:110
  37.9 4.3 %collective-permute-start.13 = (f32[2,128]{1,0:T(2,128)S(1)}, f32[2,128]{1,0:T(2,128)S(1)}, u32[]{:S(2)}, u32[]{:S(2)}) collective-permute-start(f32[2,128]{1,0:T(2,128)S(1)} %get-tuple-element.63), channel_id=1, source_target_pairs={{0,8},{8,0},{16,24},{24,16},{1,9},{9,1},{17,25},{25,17},{2,10},{10... | collective-permute-start | bytes 3080 | tf_op jit(solution)/shard_map/ppermute | solution.py:110
  39.5 10.3 %collective-permute-start.15 = (bf16[64,1024]{1,0:T(8,128)(2,1)S(1)}, bf16[64,1024]{1,0:T(8,128)(2,1)S(1)}, u32[]{:S(2)}, u32[]{:S(2)}) collective-permute-start(bf16[64,1024]{1,0:T(8,128)(2,1)S(1)} %add_b.1.refs_1_), channel_id=1, source_target_pairs={{0,4},{1,5},{2,6},{3,7},{4,0},{5,1},{6,2},{7,3},{8,12},{9,13},{10,... | collective-permute-start | bytes 393224 | tf_op jit(solution)/shard_map/ppermute | solution.py:110
  40.7 9.1 %collective-permute-start.20 = (bf16[128,1024]{1,0:T(8,128)(2,1)S(1)}, bf16[128,1024]{1,0:T(8,128)(2,1)S(1)}, u32[]{:S(2)}, u32[]{:S(2)}) collective-permute-start(bf16[128,1024]{1,0:T(8,128)(2,1)S(1)} %near_y.1), channel_id=1, source_target_pairs={{0,16},{8,24},{16,0},{24,8},{1,17},{9,25},{17,1},{25,9},{2,18},{10... | collective-permute-start | bytes 786440 | tf_op jit(solution)/shard_map/ppermute | solution.py:110
  42.3 11.9 %collective-permute-start.19 = (bf16[128,1024]{1,0:T(8,128)(2,1)S(1)}, bf16[128,1024]{1,0:T(8,128)(2,1)S(1)}, u32[]{:S(2)}, u32[]{:S(2)}) collective-permute-start(bf16[128,1024]{1,0:T(8,128)(2,1)S(1)} %add_clips.1.sum_v.refs_1_), channel_id=1, source_target_pairs={{0,2},{1,3},{2,0},{3,1},{4,6},{5,7},{6,4},{7,5},{8,10},{9,11},{10,... | collective-permute-start | bytes 786440 | tf_op jit(solution)/shard_map/ppermute | solution.py:110
  43.2 7.7 %collective-permute-start.18 = (bf16[128,1024]{1,0:T(8,128)(2,1)S(1)}, bf16[128,1024]{1,0:T(8,128)(2,1)S(1)}, u32[]{:S(2)}, u32[]{:S(2)}) collective-permute-start(bf16[128,1024]{1,0:T(8,128)(2,1)S(1)} %near_x.1), channel_id=1, source_target_pairs={{0,8},{8,0},{16,24},{24,16},{1,9},{9,1},{17,25},{25,17},{2,10},{10... | collective-permute-start | bytes 786440 | tf_op jit(solution)/shard_map/ppermute | solution.py:110
  49.8 4.5 %collective-permute-start.17 = (f32[1,128]{1,0:T(1,128)S(1)}, f32[1,128]{1,0:T(1,128)S(1)}, u32[]{:S(2)}, u32[]{:S(2)}) collective-permute-start(f32[1,128]{1,0:T(1,128)S(1)} %add_loss.1.refs_4_), channel_id=1, source_target_pairs={{0,2},{1,3},{2,0},{3,1},{4,6},{5,7},{6,4},{7,5},{8,10},{9,11},{10,... | collective-permute-start | bytes 1544 | tf_op jit(solution)/shard_map/ppermute | solution.py:110

commit v9 on v8

--- a/solution.py
+++ b/solution.py
@@ -30,7 +30,7 @@
         name=name,
         out_shape=out_shape,
         in_specs=[SPECS[spec]] * len(args),
-        out_specs=[SPECS[out_spec]] * len(out_shape),
+        out_specs=[SPECS[s] for s in (out_spec if len(out_spec) > 1 else out_spec * len(out_shape))],
         scratch_shapes=list(scratch),
         input_output_aliases=aliases,
         compiler_params=pltpu.CompilerParams(vmem_limit_bytes=limit * MIB),
@@ -331,9 +331,9 @@
 
     sums_b, got_b = captions_back(1, dvz)
     sum_v = add("add_clips", dvz, far_v)
-    got_z = hand_on("clips_back", swap(sum_v, "col", 2), flops=3 * LONG)
+    got_z = swap(sum_v, "col", 2)
     got_h = [[hand_on("captions_back", b, sum_v, flops=3 * LONG) for b in got] for got in (got_a, got_b)]
-    dcy = [hand_on("near_y", b, *sums_b) for b in dcy]
+    dcy = [hand_on("near_y", b, sum_v) for b in dcy]
     dvx = hand_on("near_x", dvx, sum_v)
     got_y = [hand_on("captions_y", swap(dcy[t - 1], "row", 2 * t), sum_v, flops=LONG) for t in range(1, Y)]
     got_x = hand_on("clips_x", swap(dvx, "row", 1), sum_v, flops=4 * LONG)
@@ -359,11 +359,13 @@
     got_loss = swap(sum_loss, "col", 2)
 
     def finish(name, losses, consts, hat, inverse, own, whole, halves, *after):
-        tail = 2 + 2 * bool(losses)
+        tail = 3 + bool(losses)
 
         def finish_kernel(consts, hat_ref, inverse_ref, *refs):
             adds, (grad, *loss, buf, sems) = refs[: -1 - tail - len(after)], refs[-1 - tail :]
             copies = []
+            if not losses:
+                loss[0][...] = jnp.zeros((8, 128), F32)
             if losses:
                 out, lbuf = loss
                 loss_0, far_loss, got_loss = adds[:3]
@@ -389,13 +391,15 @@
 
         return call(
             name, finish_kernel,
-            [jax.ShapeDtypeStruct(mat, F32)] + [jax.ShapeDtypeStruct((1, rows), F32)] * bool(losses),
-            [consts, hat, inverse, *losses, own, *whole, *halves[0], *halves[1], *after], out_spec="h",
+            [jax.ShapeDtypeStruct(mat, F32)]
+            + ([jax.ShapeDtypeStruct((1, rows), F32)] if losses else [vm((8, 128), F32)]),
+            [consts, hat, inverse, *losses, own, *whole, *halves[0], *halves[1], *after], out_spec="hh" if losses else "hv",
             scratch=[pltpu.VMEM((1, rows), F32)] * bool(losses)
             + [pltpu.VMEM(mat, F32), pltpu.SemaphoreType.DMA((3,))],
         )
 
-    (gc,) = finish("finish_captions", [], consts, chat, cinv, dc0, got_y, got_h, sum_loss)
+    gc, done = finish("finish_captions", [], consts, chat, cinv, dc0, got_y, got_h, sum_loss)
+    got_z = hand_on("clips_back", got_z, done, flops=3 * LONG)
     gv, clip_loss = finish(
         "finish_clips", [loss_0, far_loss, got_loss], consts, vhat, vinv, dv0, [got_x, got_z], ([], [])
     )

time: 55.5 us -> 54.6 us (0.984)
  starting transfers between devices: 25.9 us -> 25.2 us
    ppermute x22, starting transfers between devices: 25.9 us -> 25.2 us  [swap(): return lax.ppermute(value, axis, [(i, i ^ bits) for i in range(size)])]
  transfers between devices with their start and end apart: 22 -> 22, of which waited for: 11 -> 12; matrix products, arithmetic and copies ran while one was open for 0% -> 0% of each run, Pallas kernels for 18% -> 18%
where the time goes in v9:
time: 54.6 us; the launch traced here: 54.4 us
  starting transfers between devices  25.2 us (46%)
  waiting for transfers between devices  14.8 us (27%)
  Pallas kernels  12.4 us (23%)
  between operations  2.13 us (4%)
    ppermute x22, starting transfers between devices, swap(): return lax.ppermute(value, axis, [(i, i ^ bits) for i in range(size)])  25.2 us
    ppermute x22, waiting for transfers between devices, swap(): return lax.ppermute(value, axis, [(i, i ^ bits) for i in range(size)])  14.8 us
    pallas_call x35, Pallas kernels, call(): pl.pallas_call(kernel, name=name, out_shape=out_shape, in_specs=[SPECS[sp...  12.4 us
  transfers between devices with their start and end apart: 22, of which 12 were waited for; matrix products, arithmetic and copies ran while one was open for 0% of the time, Pallas kernels for 18%

profile of v9, /device:TPU:0, one launch (start us, length us, event | category | flops | bytes accessed | tf_op | source)
XLA Modules:
  0.0 54.4 jit_solution(16498327034674263867)
XLA Ops:
  0.6 1.5 %normalize.1 = (bf16[128,1024]{1,0:T(8,128)(2,1)S(1)}, bf16[128,1024]{1,0:T(8,128)(2,1)S(1)}, bf16[64,1024]{1,0:T(8,128)(2,1)S(1)}, bf16[64,1024]{1,0:T(8,128)(2...) custom-call(f32[128,1024]{1,0:T(8,128)} %film.1, ...), custom_call_target="tpu_custom_call" | custom-call | tf_op jit(solution)/shard_map/normalize/pallas_call | solution.py:28
  2.2 3.1 %collective-permute-start.2 = (bf16[64,1024]{1,0:T(8,128)(2,1)S(1)}, bf16[64,1024]{1,0:T(8,128)(2,1)S(1)}, u32[]{:S(2)}, u32[]{:S(2)}) collective-permute-start(bf16[64,1024]{1,0:T(8,128)(2,1)S(1)} %get-tuple-element.47), channel_id=1, source_target_pairs={{0,2},{1,3},{2,0},{3,1},{4,6},{5,7},{6,4},{7,5},{8,10},{9,11},{10,... | collective-permute-start | bytes 393224 | tf_op jit(solution)/shard_map/ppermute | solution.py:110
  5.3 2.6 %collective-permute-start.5 = (bf16[128,1024]{1,0:T(8,128)(2,1)S(1)}, bf16[128,1024]{1,0:T(8,128)(2,1)S(1)}, u32[]{:S(2)}, u32[]{:S(2)}) collective-permute-start(bf16[128,1024]{1,0:T(8,128)(2,1)S(1)} %get-tuple-element.45.refs_0_), channel_id=1, source_target_pairs={{0,4},{1,5},{2,6},{3,7},{4,0},{5,1},{6,2},{7,3},{8,12},{9,13},{10,... | collective-permute-start | bytes 786440 | tf_op jit(solution)/shard_map/ppermute | solution.py:110
  7.8 1.5 %collective-permute-start = (bf16[128,1024]{1,0:T(8,128)(2,1)S(1)}, bf16[128,1024]{1,0:T(8,128)(2,1)S(1)}, u32[]{:S(2)}, u32[]{:S(2)}) collective-permute-start(bf16[128,1024]{1,0:T(8,128)(2,1)S(1)} %get-tuple-element.45.refs_0_), channel_id=1, source_target_pairs={{0,16},{8,24},{16,0},{24,8},{1,17},{9,25},{17,1},{25,9},{2,18},{10... | collective-permute-start | bytes 786440 | tf_op jit(solution)/shard_map/ppermute | solution.py:110
  9.8 1.5 %collective-permute-start.1 = (bf16[128,1024]{1,0:T(8,128)(2,1)S(1)}, bf16[128,1024]{1,0:T(8,128)(2,1)S(1)}, u32[]{:S(2)}, u32[]{:S(2)}) collective-permute-start(bf16[128,1024]{1,0:T(8,128)(2,1)S(1)} %get-tuple-element.46.refs_2_), channel_id=1, source_target_pairs={{0,8},{8,0},{16,24},{24,16},{1,9},{9,1},{17,25},{25,17},{2,10},{10... | collective-permute-start | bytes 786440 | tf_op jit(solution)/shard_map/ppermute | solution.py:110
  12.6 0.6 %collective-permute-start.7 = (bf16[64,1024]{1,0:T(8,128)(2,1)S(1)}, bf16[64,1024]{1,0:T(8,128)(2,1)S(1)}, u32[]{:S(2)}, u32[]{:S(2)}) collective-permute-start(bf16[64,1024]{1,0:T(8,128)(2,1)S(1)} %clips_z.2.refs_4_), channel_id=1, source_target_pairs={{0,8},{8,0},{16,24},{24,16},{1,9},{9,1},{17,25},{25,17},{2,10},{10... | collective-permute-start | bytes 393224 | tf_op jit(solution)/shard_map/ppermute | solution.py:110
  13.2 3.2 %collective-permute-done.3.refs_0_ = bf16[64,1024]{1,0:T(8,128)(2,1)S(1)} collective-permute-done((bf16[64,1024]{1,0:T(8,128)(2,1)S(1)}, bf16[64,1024]{1,0:T(8,128)(2,1)S(1)}, u32[]{:S(2)}, u32[]{:S(2)}) %collective-permute-start.3) | collective-permute-done | bytes 131104 | tf_op jit(solution)/shard_map/ppermute | solution.py:110
  16.5 1.5 %collective-permute-start.8 = (bf16[64,1024]{1,0:T(8,128)(2,1)S(1)}, bf16[64,1024]{1,0:T(8,128)(2,1)S(1)}, u32[]{:S(2)}, u32[]{:S(2)}) collective-permute-start(bf16[64,1024]{1,0:T(8,128)(2,1)S(1)} %clips_z.3.refs_5_), channel_id=1, source_target_pairs={{0,8},{8,0},{16,24},{24,16},{1,9},{9,1},{17,25},{25,17},{2,10},{10... | collective-permute-start | bytes 393224 | tf_op jit(solution)/shard_map/ppermute | solution.py:110
  18.3 1.3 %collective-permute-done.5.refs_0_ = bf16[128,1024]{1,0:T(8,128)(2,1)S(1)} collective-permute-done((bf16[128,1024]{1,0:T(8,128)(2,1)S(1)}, bf16[128,1024]{1,0:T(8,128)(2,1)S(1)}, u32[]{:S(2)}, u32[]{:S(2)}) %collective-permute-start.5) | collective-permute-done | bytes 262176 | tf_op jit(solution)/shard_map/ppermute | solution.py:110
  19.6 1.5 %collective-permute-start.10 = (bf16[128,1024]{1,0:T(8,128)(2,1)S(1)}, bf16[128,1024]{1,0:T(8,128)(2,1)S(1)}, u32[]{:S(2)}, u32[]{:S(2)}) collective-permute-start(bf16[128,1024]{1,0:T(8,128)(2,1)S(1)} %captions_z.1.refs_0_), channel_id=1, source_target_pairs={{0,16},{8,24},{16,0},{24,8},{1,17},{9,25},{17,1},{25,9},{2,18},{10... | collective-permute-start | bytes 786440 | tf_op jit(solution)/shard_map/ppermute | solution.py:110
  21.1 1.2 %collective-permute-done.8.refs_0_ = bf16[64,1024]{1,0:T(8,128)(2,1)S(1)} collective-permute-done((bf16[64,1024]{1,0:T(8,128)(2,1)S(1)}, bf16[64,1024]{1,0:T(8,128)(2,1)S(1)}, u32[]{:S(2)}, u32[]{:S(2)}) %collective-permute-start.8) | collective-permute-done | bytes 131104 | tf_op jit(solution)/shard_map/ppermute | solution.py:110
  22.6 2.5 %early_pairs.1 = (bf16[768,1024]{1,0:T(8,128)(2,1)S(1)}, bf16[384,768]{1,0:T(8,128)(2,1)S(1)}, bf16[384,384]{1,0:T(8,128)(2,1)S(1)}, f32[1,384]{1,0:T(1,128)S(1)}) custom-call(f32[2,128]{1,0:T(2,128)S(1)} %consts.1.refs_1_, s32[1,1024]{1,0:T(1,128)S(1)} %get-tuple-element.44.labels, bf16[640,1024]{1,0:T(8,128)(2,1)S(1)} %near_blocks.1.N, ...), custom_call_target="tpu_custom_call" | custom-call | flops 905969664 | tf_op jit(solution)/shard_map/early_pairs/pallas_call | solution.py:28
  25.2 1.3 %middle_pairs.1 = (bf16[1024,1024]{1,0:T(8,128)(2,1)S(1)}, bf16[768,512]{1,0:T(8,128)(2,1)S(1)}, bf16[384,1024]{1,0:T(8,128)(2,1)S(1)}, f32[1,128]{1,0:T(1,128)S(1)}) custom-call(f32[2,128]{1,0:T(2,128)S(1)} %consts.1.refs_1_, s32[1,1024]{1,0:T(1,128)S(1)} %get-tuple-element.44.labels, bf16[640,1024]{1,0:T(8,128)(2,1)S(1)} %near_blocks.1.N, ...), custom_call_target="tpu_custom_call" | custom-call | flops 301989888 | tf_op jit(solution)/shard_map/middle_pairs/pallas_call | solution.py:28
  26.5 0.6 %collective-permute-done.10.refs_0_ = bf16[128,1024]{1,0:T(8,128)(2,1)S(1)} collective-permute-done((bf16[128,1024]{1,0:T(8,128)(2,1)S(1)}, bf16[128,1024]{1,0:T(8,128)(2,1)S(1)}, u32[]{:S(2)}, u32[]{:S(2)}) %collective-permute-start.10) | collective-permute-done | bytes 262176 | tf_op jit(solution)/shard_map/ppermute | solution.py:110
  27.0 1.5 %far_captions.1 = (f32[1,512]{1,0:T(1,128)S(1)}, bf16[128,512]{1,0:T(8,128)(2,1)S(1)}, bf16[64,1024]{1,0:T(8,128)(2,1)S(1)}, bf16[64,1024]{1,0:T(8,128)(2,1)S(1)}) custom-call(f32[2,128]{1,0:T(2,128)S(1)} %consts.1.refs_1_, s32[1,1024]{1,0:T(1,128)S(1)} %get-tuple-element.44.labels, bf16[1024,1024]{1,0:T(8,128)(2,1)S(1)} %get-tuple-element.54.VV, ...), custom_call_target="tpu_custom_call" | custom-call | flops 536870912 | tf_op jit(solution)/shard_map/far_captions/pallas_call | solution.py:28
  28.5 1.4 %collective-permute-start.12 = (bf16[64,1024]{1,0:T(8,128)(2,1)S(1)}, bf16[64,1024]{1,0:T(8,128)(2,1)S(1)}, u32[]{:S(2)}, u32[]{:S(2)}) collective-permute-start(bf16[64,1024]{1,0:T(8,128)(2,1)S(1)} %get-tuple-element.62), channel_id=1, source_target_pairs={{0,16},{8,24},{16,0},{24,8},{1,17},{9,25},{17,1},{25,9},{2,18},{10... | collective-permute-start | bytes 393224 | tf_op jit(solution)/shard_map/ppermute | solution.py:110
  29.9 1.2 %far_clips.1 = (bf16[256,1024]{1,0:T(8,128)(2,1)S(1)}, bf16[256,512]{1,0:T(8,128)(2,1)S(1)}, f32[1,512]{1,0:T(1,128)S(1)}, bf16[128,1024]{1,0:T(8,128)(2,1)S(1)}) custom-call(f32[2,128]{1,0:T(2,128)S(1)} %consts.1.refs_1_, s32[1,1024]{1,0:T(1,128)S(1)} %get-tuple-element.44.labels, bf16[1024,1024]{1,0:T(8,128)(2,1)S(1)} %get-tuple-element.54.VV, ...), custom_call_target="tpu_custom_call" | custom-call | flops 402653184 | tf_op jit(solution)/shard_map/far_clips/pallas_call | solution.py:28
  31.1 1.2 %collective-permute-start.16 = (bf16[128,1024]{1,0:T(8,128)(2,1)S(1)}, bf16[128,1024]{1,0:T(8,128)(2,1)S(1)}, u32[]{:S(2)}, u32[]{:S(2)}) collective-permute-start(bf16[128,1024]{1,0:T(8,128)(2,1)S(1)} %get-tuple-element.60.after.refs_1_), channel_id=1, source_target_pairs={{0,8},{8,0},{16,24},{24,16},{1,9},{9,1},{17,25},{25,17},{2,10},{10... | collective-permute-start | bytes 786440 | tf_op jit(solution)/shard_map/ppermute | solution.py:110
  32.3 1.1 %collective-permute-start.14 = (bf16[64,1024]{1,0:T(8,128)(2,1)S(1)}, bf16[64,1024]{1,0:T(8,128)(2,1)S(1)}, u32[]{:S(2)}, u32[]{:S(2)}) collective-permute-start(bf16[64,1024]{1,0:T(8,128)(2,1)S(1)} %far_b.2), channel_id=1, source_target_pairs={{0,16},{8,24},{16,0},{24,8},{1,17},{9,25},{17,1},{25,9},{2,18},{10... | collective-permute-start | bytes 393224 | tf_op jit(solution)/shard_map/ppermute | solution.py:110
  33.3 1.0 %near_captions.1 = (f32[128,1024]{1,0:T(8,128)S(1)}, bf16[128,1024]{1,0:T(8,128)(2,1)S(1)}, f32[64,1024]{1,0:T(8,128)S(1)}, f32[64,1024]{1,0:T(8,128)S(1)}) custom-call(bf16[384,1024]{1,0:T(8,128)(2,1)S(1)} %get-tuple-element.59.coef, bf16[1024,1024]{1,0:T(8,128)(2,1)S(1)} %get-tuple-element.54.VV, bf16[128,1024]{1,0:T(8,128)(2,1)S(1)} %get-tuple-element.60.after.refs_1_), custom_call_target="tpu_custom_call" | custom-call | flops 805306368 | tf_op jit(solution)/shard_map/near_captions/pallas_call | solution.py:28
  34.5 3.4 %collective-permute-start.21 = (bf16[64,1024]{1,0:T(8,128)(2,1)S(1)}, bf16[64,1024]{1,0:T(8,128)(2,1)S(1)}, u32[]{:S(2)}, u32[]{:S(2)}) collective-permute-start(bf16[64,1024]{1,0:T(8,128)(2,1)S(1)} %add_a.1.after), channel_id=1, source_target_pairs={{0,4},{1,5},{2,6},{3,7},{4,0},{5,1},{6,2},{7,3},{8,12},{9,13},{10,... | collective-permute-start | bytes 393224 | tf_op jit(solution)/shard_map/ppermute | solution.py:110
  38.5 1.0 %near_clips.1 = (f32[128,1024]{1,0:T(8,128)S(1)}, bf16[128,1024]{1,0:T(8,128)(2,1)S(1)}, f32[128,1024]{1,0:T(8,128)S(1)}) custom-call(bf16[768,1024]{1,0:T(8,128)(2,1)S(1)} %get-tuple-element.50.S1, bf16[256,1024]{1,0:T(8,128)(2,1)S(1)} %get-tuple-element.68.S2, bf16[768,512]{1,0:T(8,128)(2,1)S(1)} %get-tuple-element.56.G1, ...), custom_call_target="tpu_custom_call" | custom-call | flops 805306368 | tf_op jit(solution)/shard_map/near_clips/pallas_call | solution.py:28
  39.5 1.2 %collective-permute-start.15 = (bf16[64,1024]{1,0:T(8,128)(2,1)S(1)}, bf16[64,1024]{1,0:T(8,128)(2,1)S(1)}, u32[]{:S(2)}, u32[]{:S(2)}) collective-permute-start(bf16[64,1024]{1,0:T(8,128)(2,1)S(1)} %add_b.1.refs_1_), channel_id=1, source_target_pairs={{0,4},{1,5},{2,6},{3,7},{4,0},{5,1},{6,2},{7,3},{8,12},{9,13},{10,... | collective-permute-start | bytes 393224 | tf_op jit(solution)/shard_map/ppermute | solution.py:110
  40.7 0.8 %collective-permute-done.13.refs_0_ = f32[2,128]{1,0:T(2,128)S(1)} collective-permute-done((f32[2,128]{1,0:T(2,128)S(1)}, f32[2,128]{1,0:T(2,128)S(1)}, u32[]{:S(2)}, u32[]{:S(2)}) %collective-permute-start.13) | collective-permute-done | bytes 1056 | tf_op jit(solution)/shard_map/ppermute | solution.py:110
  41.5 0.7 %collective-permute-start.19 = (bf16[128,1024]{1,0:T(8,128)(2,1)S(1)}, bf16[128,1024]{1,0:T(8,128)(2,1)S(1)}, u32[]{:S(2)}, u32[]{:S(2)}) collective-permute-start(bf16[128,1024]{1,0:T(8,128)(2,1)S(1)} %add_clips.1.sum_v.refs_1_), channel_id=1, source_target_pairs={{0,2},{1,3},{2,0},{3,1},{4,6},{5,7},{6,4},{7,5},{8,10},{9,11},{10,... | collective-permute-start | bytes 786440 | tf_op jit(solution)/shard_map/ppermute | solution.py:110
  42.3 0.9 %collective-permute-start.18 = (bf16[128,1024]{1,0:T(8,128)(2,1)S(1)}, bf16[128,1024]{1,0:T(8,128)(2,1)S(1)}, u32[]{:S(2)}, u32[]{:S(2)}) collective-permute-start(bf16[128,1024]{1,0:T(8,128)(2,1)S(1)} %near_x.1), channel_id=1, source_target_pairs={{0,8},{8,0},{16,24},{24,16},{1,9},{9,1},{17,25},{25,17},{2,10},{10... | collective-permute-start | bytes 786440 | tf_op jit(solution)/shard_map/ppermute | solution.py:110
  43.1 1.9 %collective-permute-start.20 = (bf16[128,1024]{1,0:T(8,128)(2,1)S(1)}, bf16[128,1024]{1,0:T(8,128)(2,1)S(1)}, u32[]{:S(2)}, u32[]{:S(2)}) collective-permute-start(bf16[128,1024]{1,0:T(8,128)(2,1)S(1)} %near_y.1), channel_id=1, source_target_pairs={{0,16},{8,24},{16,0},{24,8},{1,17},{9,25},{17,1},{25,9},{2,18},{10... | collective-permute-start | bytes 786440 | tf_op jit(solution)/shard_map/ppermute | solution.py:110
  45.0 2.9 %collective-permute-done.21.refs_0_ = bf16[64,1024]{1,0:T(8,128)(2,1)S(1)} collective-permute-done((bf16[64,1024]{1,0:T(8,128)(2,1)S(1)}, bf16[64,1024]{1,0:T(8,128)(2,1)S(1)}, u32[]{:S(2)}, u32[]{:S(2)}) %collective-permute-start.21) | collective-permute-done | bytes 131104 | tf_op jit(solution)/shard_map/ppermute | solution.py:110
  48.0 1.9 %collective-permute-done.15.got.refs_0_ = bf16[64,1024]{1,0:T(8,128)(2,1)S(1)} collective-permute-done((bf16[64,1024]{1,0:T(8,128)(2,1)S(1)}, bf16[64,1024]{1,0:T(8,128)(2,1)S(1)}, u32[]{:S(2)}, u32[]{:S(2)}) %collective-permute-start.15) | collective-permute-done | bytes 131104 | tf_op jit(solution)/shard_map/ppermute | solution.py:110
  49.9 1.1 %finish_captions.1 = (f32[128,1024]{1,0:T(8,128)}, f32[8,128]{1,0:T(8,128)S(1)}) custom-call(f32[2,128]{1,0:T(2,128)S(1)} %consts.1.refs_1_, f32[128,1024]{1,0:T(8,128)S(1)} %get-tuple-element.74.hat_ref, f32[128,1]{1,0:T(8,128)S(1)} %get-tuple-element.75.inverse_ref, f32[128,1024]{1,0:T(8,128)S(1)} %get-tuple-element.63.refs_1_.refs_0_, ...), custom_call_target="tpu_custom_call" | custom-call | tf_op jit(solution)/shard_map/finish_captions/pallas_call | solution.py:28
  51.0 1.9 %collective-permute-done.19.refs_0_ = bf16[128,1024]{1,0:T(8,128)(2,1)S(1)} collective-permute-done((bf16[128,1024]{1,0:T(8,128)(2,1)S(1)}, bf16[128,1024]{1,0:T(8,128)(2,1)S(1)}, u32[]{:S(2)}, u32[]{:S(2)}) %collective-permute-start.19) | collective-permute-done | bytes 262176 | tf_op jit(solution)/shard_map/ppermute | solution.py:110
  53.4 1.1 %finish_clips.1 = (f32[128,1024]{1,0:T(8,128)}, f32[1,128]{1,0:T(1,128)}) custom-call(f32[2,128]{1,0:T(2,128)S(1)} %consts.1.refs_1_, f32[128,1024]{1,0:T(8,128)S(1)} %get-tuple-element.42.hat_ref, f32[128,1]{1,0:T(8,128)S(1)} %get-tuple-element.43.inverse_ref, f32[1,128]{1,0:T(1,128)S(1)} %get-tuple-element.64.refs_0_, ...), custom_call_target="tpu_custom_call" | custom-call | tf_op jit(solution)/shard_map/finish_clips/pallas_call | solution.py:28
  (47 shorter events, 2.4 us)
Async XLA Ops:
  2.2 10.5 %collective-permute-start.2 = (bf16[64,1024]{1,0:T(8,128)(2,1)S(1)}, bf16[64,1024]{1,0:T(8,128)(2,1)S(1)}, u32[]{:S(2)}, u32[]{:S(2)}) collective-permute-start(bf16[64,1024]{1,0:T(8,128)(2,1)S(1)} %get-tuple-element.47), channel_id=1, source_target_pairs={{0,2},{1,3},{2,0},{3,1},{4,6},{5,7},{6,4},{7,5},{8,10},{9,11},{10,... | collective-permute-start | bytes 393224 | tf_op jit(solution)/shard_map/ppermute | solution.py:110
  5.3 14.3 %collective-permute-start.5 = (bf16[128,1024]{1,0:T(8,128)(2,1)S(1)}, bf16[128,1024]{1,0:T(8,128)(2,1)S(1)}, u32[]{:S(2)}, u32[]{:S(2)}) collective-permute-start(bf16[128,1024]{1,0:T(8,128)(2,1)S(1)} %get-tuple-element.45.refs_0_), channel_id=1, source_target_pairs={{0,4},{1,5},{2,6},{3,7},{4,0},{5,1},{6,2},{7,3},{8,12},{9,13},{10,... | collective-permute-start | bytes 786440 | tf_op jit(solution)/shard_map/ppermute | solution.py:110
  7.8 10.3 %collective-permute-start = (bf16[128,1024]{1,0:T(8,128)(2,1)S(1)}, bf16[128,1024]{1,0:T(8,128)(2,1)S(1)}, u32[]{:S(2)}, u32[]{:S(2)}) collective-permute-start(bf16[128,1024]{1,0:T(8,128)(2,1)S(1)} %get-tuple-element.45.refs_0_), channel_id=1, source_target_pairs={{0,16},{8,24},{16,0},{24,8},{1,17},{9,25},{17,1},{25,9},{2,18},{10... | collective-permute-start | bytes 786440 | tf_op jit(solution)/shard_map/ppermute | solution.py:110
  9.4 7.1 %collective-permute-start.3 = (bf16[64,1024]{1,0:T(8,128)(2,1)S(1)}, bf16[64,1024]{1,0:T(8,128)(2,1)S(1)}, u32[]{:S(2)}, u32[]{:S(2)}) collective-permute-start(bf16[64,1024]{1,0:T(8,128)(2,1)S(1)} %get-tuple-element.48), channel_id=1, source_target_pairs={{0,2},{1,3},{2,0},{3,1},{4,6},{5,7},{6,4},{7,5},{8,10},{9,11},{10,... | collective-permute-start | bytes 393224 | tf_op jit(solution)/shard_map/ppermute | solution.py:110
  9.8 8.3 %collective-permute-start.1 = (bf16[128,1024]{1,0:T(8,128)(2,1)S(1)}, bf16[128,1024]{1,0:T(8,128)(2,1)S(1)}, u32[]{:S(2)}, u32[]{:S(2)}) collective-permute-start(bf16[128,1024]{1,0:T(8,128)(2,1)S(1)} %get-tuple-element.46.refs_2_), channel_id=1, source_target_pairs={{0,8},{8,0},{16,24},{24,16},{1,9},{9,1},{17,25},{25,17},{2,10},{10... | collective-permute-start | bytes 786440 | tf_op jit(solution)/shard_map/ppermute | solution.py:110
  12.6 8.5 %collective-permute-start.7 = (bf16[64,1024]{1,0:T(8,128)(2,1)S(1)}, bf16[64,1024]{1,0:T(8,128)(2,1)S(1)}, u32[]{:S(2)}, u32[]{:S(2)}) collective-permute-start(bf16[64,1024]{1,0:T(8,128)(2,1)S(1)} %clips_z.2.refs_4_), channel_id=1, source_target_pairs={{0,8},{8,0},{16,24},{24,16},{1,9},{9,1},{17,25},{25,17},{2,10},{10... | collective-permute-start | bytes 393224 | tf_op jit(solution)/shard_map/ppermute | solution.py:110
  16.5 5.9 %collective-permute-start.8 = (bf16[64,1024]{1,0:T(8,128)(2,1)S(1)}, bf16[64,1024]{1,0:T(8,128)(2,1)S(1)}, u32[]{:S(2)}, u32[]{:S(2)}) collective-permute-start(bf16[64,1024]{1,0:T(8,128)(2,1)S(1)} %clips_z.3.refs_5_), channel_id=1, source_target_pairs={{0,8},{8,0},{16,24},{24,16},{1,9},{9,1},{17,25},{25,17},{2,10},{10... | collective-permute-start | bytes 393224 | tf_op jit(solution)/shard_map/ppermute | solution.py:110
  18.2 4.2 %collective-permute-start.4 = (bf16[640,1024]{1,0:T(8,128)(2,1)S(1)}, bf16[640,1024]{1,0:T(8,128)(2,1)S(1)}, u32[]{:S(2)}, u32[]{:S(2)}) collective-permute-start(bf16[640,1024]{1,0:T(8,128)(2,1)S(1)} %near_blocks.1.N), channel_id=1, source_target_pairs={{0,1},{1,0},{2,3},{3,2},{4,5},{5,4},{6,7},{7,6},{8,9},{9,8},{10,11... | collective-permute-start | bytes 3932168 | tf_op jit(solution)/shard_map/ppermute | solution.py:110
  19.6 7.4 %collective-permute-start.10 = (bf16[128,1024]{1,0:T(8,128)(2,1)S(1)}, bf16[128,1024]{1,0:T(8,128)(2,1)S(1)}, u32[]{:S(2)}, u32[]{:S(2)}) collective-permute-start(bf16[128,1024]{1,0:T(8,128)(2,1)S(1)} %captions_z.1.refs_0_), channel_id=1, source_target_pairs={{0,16},{8,24},{16,0},{24,8},{1,17},{9,25},{17,1},{25,9},{2,18},{10... | collective-permute-start | bytes 786440 | tf_op jit(solution)/shard_map/ppermute | solution.py:110
  21.1 1.5 %collective-permute-start.6 = (bf16[128,1024]{1,0:T(8,128)(2,1)S(1)}, bf16[128,1024]{1,0:T(8,128)(2,1)S(1)}, u32[]{:S(2)}, u32[]{:S(2)}) collective-permute-start(bf16[128,1024]{1,0:T(8,128)(2,1)S(1)} %captions_z.1.refs_0_), channel_id=1, source_target_pairs={{0,1},{1,0},{2,3},{3,2},{4,5},{5,4},{6,7},{7,6},{8,9},{9,8},{10,11... | collective-permute-start | bytes 786440 | tf_op jit(solution)/shard_map/ppermute | solution.py:110
  22.4 2.8 %collective-permute-start.9 = (bf16[128,1024]{1,0:T(8,128)(2,1)S(1)}, bf16[128,1024]{1,0:T(8,128)(2,1)S(1)}, u32[]{:S(2)}, u32[]{:S(2)}) collective-permute-start(bf16[128,1024]{1,0:T(8,128)(2,1)S(1)} %diagonal_clips.1.vd), channel_id=1, source_target_pairs={{0,1},{1,0},{2,3},{3,2},{4,5},{5,4},{6,7},{7,6},{8,9},{9,8},{10,11... | collective-permute-start | bytes 786440 | tf_op jit(solution)/shard_map/ppermute | solution.py:110
  27.0 2.9 %collective-permute-start.11 = (bf16[128,1024]{1,0:T(8,128)(2,1)S(1)}, bf16[128,1024]{1,0:T(8,128)(2,1)S(1)}, u32[]{:S(2)}, u32[]{:S(2)}) collective-permute-start(bf16[128,1024]{1,0:T(8,128)(2,1)S(1)} %captions_d.1.refs_0_), channel_id=1, source_target_pairs={{0,1},{1,0},{2,3},{3,2},{4,5},{5,4},{6,7},{7,6},{8,9},{9,8},{10,11... | collective-permute-start | bytes 786440 | tf_op jit(solution)/shard_map/ppermute | solution.py:110
  28.5 6.0 %collective-permute-start.12 = (bf16[64,1024]{1,0:T(8,128)(2,1)S(1)}, bf16[64,1024]{1,0:T(8,128)(2,1)S(1)}, u32[]{:S(2)}, u32[]{:S(2)}) collective-permute-start(bf16[64,1024]{1,0:T(8,128)(2,1)S(1)} %get-tuple-element.62), channel_id=1, source_target_pairs={{0,16},{8,24},{16,0},{24,8},{1,17},{9,25},{17,1},{25,9},{2,18},{10... | collective-permute-start | bytes 393224 | tf_op jit(solution)/shard_map/ppermute | solution.py:110
  31.1 10.4 %collective-permute-start.16 = (bf16[128,1024]{1,0:T(8,128)(2,1)S(1)}, bf16[128,1024]{1,0:T(8,128)(2,1)S(1)}, u32[]{:S(2)}, u32[]{:S(2)}) collective-permute-start(bf16[128,1024]{1,0:T(8,128)(2,1)S(1)} %get-tuple-element.60.after.refs_1_), channel_id=1, source_target_pairs={{0,8},{8,0},{16,24},{24,16},{1,9},{9,1},{17,25},{25,17},{2,10},{10... | collective-permute-start | bytes 786440 | tf_op jit(solution)/shard_map/ppermute | solution.py:110
  32.3 7.2 %collective-permute-start.14 = (bf16[64,1024]{1,0:T(8,128)(2,1)S(1)}, bf16[64,1024]{1,0:T(8,128)(2,1)S(1)}, u32[]{:S(2)}, u32[]{:S(2)}) collective-permute-start(bf16[64,1024]{1,0:T(8,128)(2,1)S(1)} %far_b.2), channel_id=1, source_target_pairs={{0,16},{8,24},{16,0},{24,8},{1,17},{9,25},{17,1},{25,9},{2,18},{10... | collective-permute-start | bytes 393224 | tf_op jit(solution)/shard_map/ppermute | solution.py:110
  34.5 13.5 %collective-permute-start.21 = (bf16[64,1024]{1,0:T(8,128)(2,1)S(1)}, bf16[64,1024]{1,0:T(8,128)(2,1)S(1)}, u32[]{:S(2)}, u32[]{:S(2)}) collective-permute-start(bf16[64,1024]{1,0:T(8,128)(2,1)S(1)} %add_a.1.after), channel_id=1, source_target_pairs={{0,4},{1,5},{2,6},{3,7},{4,0},{5,1},{6,2},{7,3},{8,12},{9,13},{10,... | collective-permute-start | bytes 393224 | tf_op jit(solution)/shard_map/ppermute | solution.py:110
  37.9 3.6 %collective-permute-start.13 = (f32[2,128]{1,0:T(2,128)S(1)}, f32[2,128]{1,0:T(2,128)S(1)}, u32[]{:S(2)}, u32[]{:S(2)}) collective-permute-start(f32[2,128]{1,0:T(2,128)S(1)} %get-tuple-element.65), channel_id=1, source_target_pairs={{0,8},{8,0},{16,24},{24,16},{1,9},{9,1},{17,25},{25,17},{2,10},{10... | collective-permute-start | bytes 3080 | tf_op jit(solution)/shard_map/ppermute | solution.py:110
  39.5 10.3 %collective-permute-start.15 = (bf16[64,1024]{1,0:T(8,128)(2,1)S(1)}, bf16[64,1024]{1,0:T(8,128)(2,1)S(1)}, u32[]{:S(2)}, u32[]{:S(2)}) collective-permute-start(bf16[64,1024]{1,0:T(8,128)(2,1)S(1)} %add_b.1.refs_1_), channel_id=1, source_target_pairs={{0,4},{1,5},{2,6},{3,7},{4,0},{5,1},{6,2},{7,3},{8,12},{9,13},{10,... | collective-permute-start | bytes 393224 | tf_op jit(solution)/shard_map/ppermute | solution.py:110
  41.5 11.3 %collective-permute-start.19 = (bf16[128,1024]{1,0:T(8,128)(2,1)S(1)}, bf16[128,1024]{1,0:T(8,128)(2,1)S(1)}, u32[]{:S(2)}, u32[]{:S(2)}) collective-permute-start(bf16[128,1024]{1,0:T(8,128)(2,1)S(1)} %add_clips.1.sum_v.refs_1_), channel_id=1, source_target_pairs={{0,2},{1,3},{2,0},{3,1},{4,6},{5,7},{6,4},{7,5},{8,10},{9,11},{10,... | collective-permute-start | bytes 786440 | tf_op jit(solution)/shard_map/ppermute | solution.py:110
  42.3 7.5 %collective-permute-start.18 = (bf16[128,1024]{1,0:T(8,128)(2,1)S(1)}, bf16[128,1024]{1,0:T(8,128)(2,1)S(1)}, u32[]{:S(2)}, u32[]{:S(2)}) collective-permute-start(bf16[128,1024]{1,0:T(8,128)(2,1)S(1)} %near_x.1), channel_id=1, source_target_pairs={{0,8},{8,0},{16,24},{24,16},{1,9},{9,1},{17,25},{25,17},{2,10},{10... | collective-permute-start | bytes 786440 | tf_op jit(solution)/shard_map/ppermute | solution.py:110
  43.1 6.7 %collective-permute-start.20 = (bf16[128,1024]{1,0:T(8,128)(2,1)S(1)}, bf16[128,1024]{1,0:T(8,128)(2,1)S(1)}, u32[]{:S(2)}, u32[]{:S(2)}) collective-permute-start(bf16[128,1024]{1,0:T(8,128)(2,1)S(1)} %near_y.1), channel_id=1, source_target_pairs={{0,16},{8,24},{16,0},{24,8},{1,17},{9,25},{17,1},{25,9},{2,18},{10... | collective-permute-start | bytes 786440 | tf_op jit(solution)/shard_map/ppermute | solution.py:110
  49.8 3.5 %collective-permute-start.17 = (f32[1,128]{1,0:T(1,128)S(1)}, f32[1,128]{1,0:T(1,128)S(1)}, u32[]{:S(2)}, u32[]{:S(2)}) collective-permute-start(f32[1,128]{1,0:T(1,128)S(1)} %add_loss.1.refs_4_), channel_id=1, source_target_pairs={{0,2},{1,3},{2,0},{3,1},{4,6},{5,7},{6,4},{7,5},{8,10},{9,11},{10,... | collective-permute-start | bytes 1544 | tf_op jit(solution)/shard_map/ppermute | solution.py:110

commit v10 on v9

--- a/solution.py
+++ b/solution.py
@@ -192,35 +192,32 @@
     c_z = [hand_on("captions_z", swap(c16, "col", 4 * s), consts, flops=4 * LONG // 4) for s in range(1, Z)]
     c_y = [swap(c16, "row", 2 * t) for t in range(1, Y)]
     v_x = swap(v16, "row", 1)
-    v_d = [hand_on("clips_d", swap(b, "row", 1), flops=2 * LONG // 4) for b in v_z]
+    v_d = [hand_on("clips_d", swap(b, "row", 1), flops=LONG) for b in v_z]
     c_d = [swap(b, "row", 2 * t) for b in c_z for t in range(1, Y)]
-    N = join("near_blocks", c16, *c_y, v16, v_x, *v_z)
+    N = join("near_blocks", c16, *c_y, *c_z, v16, v_x, *v_z)
     N_k = hand_on("near_other", swap(N, "col", 1), flops=4 * LONG // 4)
-    cz_k = [swap(b, "col", 1) for b in c_z]
     v_d = join("diagonal_clips", *v_d)
     vd_k = swap(v_d, "col", 1)
 
-    def early_kernel(consts, labels, N, N_k, *refs):
-        n = len(up)
-        cz, czk, (S1, p, q, loss) = refs[:n], refs[n : 2 * n], refs[2 * n :]
-        stack(S1, [N.at[:nn], *cz, N_k.at[:nn], *czk])
-        own = N[nn:, :]
+    def early_kernel(consts, labels, N, N_k, S1, p, q, loss):
+        stack(S1, [N.at[:na], N_k.at[:na]])
+        own = N[na:, :]
         loss[...] = strip(
             consts, near + up, 0, S1[:na, :], own, labels[:, :n3], n3, put_in(p)
         ) + strip(consts, near + up, 1, S1[na:, :], own, labels[:, :n3], n3, put_in(q))
         strip(
-            consts, near + up, 0, S1[:na, :], N_k[nn:, :], labels[:, n4:n7], 0, put_in(p, left=n3)
+            consts, near + up, 0, S1[:na, :], N_k[na:, :], labels[:, n4:n7], 0, put_in(p, left=n3)
         )
 
     S1, p, q, loss_a = call(
         "early_pairs", early_kernel,
         [vm((2 * na, width)), vm((na, 2 * n3)), vm((na, n3)), vm((1, n3), F32)],
-        [consts, labels, N, N_k, *c_z, *cz_k],
+        [consts, labels, N, N_k],
         flops=2 * 27 * rows * rows * width, limit=limit,
     )
 
     def middle_kernel(consts, labels, N, N_k, vd, vdk, S1, p, q, VV, G1, coef, loss):
-        stack(VV, [N.at[nn:], vd, N_k.at[nn:], vdk])
+        stack(VV, [N.at[na:], vd, N_k.at[na:], vdk])
         coef[:, :n3] = p[:, :n3]
         coef[:, n4:n7] = p[:, n3:]
         G1[na:, :n3] = q[...]

time: 54.6 us -> 55.3 us (1.013)
  waiting for transfers between devices: 14.8 us -> 16.2 us
  starting transfers between devices: 25.2 us -> 24.4 us
    ppermute x22 -> x21, waiting for transfers between devices: 14.8 us -> 16.2 us  [swap(): return lax.ppermute(value, axis, [(i, i ^ bits) for i in range(size)])]
    ppermute x22 -> x21, starting transfers between devices: 25.2 us -> 24.4 us  [swap(): return lax.ppermute(value, axis, [(i, i ^ bits) for i in range(size)])]
  transfers between devices with their start and end apart: 22 -> 21, of which waited for: 12 -> 9; matrix products, arithmetic and copies ran while one was open for 0% -> 0% of each run, Pallas kernels for 18% -> 18%
where the time goes in v10:
time: 55.3 us; the launch traced here: 55.1 us
  starting transfers between devices  24.4 us (44%)
  waiting for transfers between devices  16.2 us (29%)
  Pallas kernels  12.4 us (22%)
  between operations  2.13 us (4%)
    ppermute x21, starting transfers between devices, swap(): return lax.ppermute(value, axis, [(i, i ^ bits) for i in range(size)])  24.4 us
    ppermute x21, waiting for transfers between devices, swap(): return lax.ppermute(value, axis, [(i, i ^ bits) for i in range(size)])  16.2 us
    pallas_call x35, Pallas kernels, call(): pl.pallas_call(kernel, name=name, out_shape=out_shape, in_specs=[SPECS[sp...  12.4 us
  transfers between devices with their start and end apart: 21, of which 9 were waited for; matrix products, arithmetic and copies ran while one was open for 0% of the time, Pallas kernels for 18%

profile of v10, /device:TPU:0, one launch (start us, length us, event | category | flops | bytes accessed | tf_op | source)
XLA Modules:
  0.0 55.1 jit_solution(16688889757453190843)
XLA Ops:
  0.6 1.5 %normalize.1 = (bf16[128,1024]{1,0:T(8,128)(2,1)S(1)}, bf16[128,1024]{1,0:T(8,128)(2,1)S(1)}, bf16[64,1024]{1,0:T(8,128)(2,1)S(1)}, bf16[64,1024]{1,0:T(8,128)(2...) custom-call(f32[128,1024]{1,0:T(8,128)} %film.1, ...), custom_call_target="tpu_custom_call" | custom-call | tf_op jit(solution)/shard_map/normalize/pallas_call | solution.py:28
  2.2 3.1 %collective-permute-start.3 = (bf16[64,1024]{1,0:T(8,128)(2,1)S(1)}, bf16[64,1024]{1,0:T(8,128)(2,1)S(1)}, u32[]{:S(2)}, u32[]{:S(2)}) collective-permute-start(bf16[64,1024]{1,0:T(8,128)(2,1)S(1)} %get-tuple-element.47), channel_id=1, source_target_pairs={{0,2},{1,3},{2,0},{3,1},{4,6},{5,7},{6,4},{7,5},{8,10},{9,11},{10,... | collective-permute-start | bytes 393224 | tf_op jit(solution)/shard_map/ppermute | solution.py:110
  5.3 2.6 %collective-permute-start.1 = (bf16[128,1024]{1,0:T(8,128)(2,1)S(1)}, bf16[128,1024]{1,0:T(8,128)(2,1)S(1)}, u32[]{:S(2)}, u32[]{:S(2)}) collective-permute-start(bf16[128,1024]{1,0:T(8,128)(2,1)S(1)} %get-tuple-element.45.refs_0_), channel_id=1, source_target_pairs={{0,4},{1,5},{2,6},{3,7},{4,0},{5,1},{6,2},{7,3},{8,12},{9,13},{10,... | collective-permute-start | bytes 786440 | tf_op jit(solution)/shard_map/ppermute | solution.py:110
  7.8 1.5 %collective-permute-start = (bf16[128,1024]{1,0:T(8,128)(2,1)S(1)}, bf16[128,1024]{1,0:T(8,128)(2,1)S(1)}, u32[]{:S(2)}, u32[]{:S(2)}) collective-permute-start(bf16[128,1024]{1,0:T(8,128)(2,1)S(1)} %get-tuple-element.45.refs_0_), channel_id=1, source_target_pairs={{0,16},{8,24},{16,0},{24,8},{1,17},{9,25},{17,1},{25,9},{2,18},{10... | collective-permute-start | bytes 786440 | tf_op jit(solution)/shard_map/ppermute | solution.py:110
  9.8 1.5 %collective-permute-start.2 = (bf16[128,1024]{1,0:T(8,128)(2,1)S(1)}, bf16[128,1024]{1,0:T(8,128)(2,1)S(1)}, u32[]{:S(2)}, u32[]{:S(2)}) collective-permute-start(bf16[128,1024]{1,0:T(8,128)(2,1)S(1)} %get-tuple-element.46.refs_3_), channel_id=1, source_target_pairs={{0,8},{8,0},{16,24},{24,16},{1,9},{9,1},{17,25},{25,17},{2,10},{10... | collective-permute-start | bytes 786440 | tf_op jit(solution)/shard_map/ppermute | solution.py:110
  12.6 0.6 %collective-permute-start.6 = (bf16[64,1024]{1,0:T(8,128)(2,1)S(1)}, bf16[64,1024]{1,0:T(8,128)(2,1)S(1)}, u32[]{:S(2)}, u32[]{:S(2)}) collective-permute-start(bf16[64,1024]{1,0:T(8,128)(2,1)S(1)} %clips_z.2.refs_5_), channel_id=1, source_target_pairs={{0,8},{8,0},{16,24},{24,16},{1,9},{9,1},{17,25},{25,17},{2,10},{10... | collective-permute-start | bytes 393224 | tf_op jit(solution)/shard_map/ppermute | solution.py:110
  13.2 3.2 %collective-permute-done.4.refs_0_ = bf16[64,1024]{1,0:T(8,128)(2,1)S(1)} collective-permute-done((bf16[64,1024]{1,0:T(8,128)(2,1)S(1)}, bf16[64,1024]{1,0:T(8,128)(2,1)S(1)}, u32[]{:S(2)}, u32[]{:S(2)}) %collective-permute-start.4) | collective-permute-done | bytes 131104 | tf_op jit(solution)/shard_map/ppermute | solution.py:110
  16.5 1.5 %collective-permute-start.7 = (bf16[64,1024]{1,0:T(8,128)(2,1)S(1)}, bf16[64,1024]{1,0:T(8,128)(2,1)S(1)}, u32[]{:S(2)}, u32[]{:S(2)}) collective-permute-start(bf16[64,1024]{1,0:T(8,128)(2,1)S(1)} %clips_z.3.refs_6_), channel_id=1, source_target_pairs={{0,8},{8,0},{16,24},{24,16},{1,9},{9,1},{17,25},{25,17},{2,10},{10... | collective-permute-start | bytes 393224 | tf_op jit(solution)/shard_map/ppermute | solution.py:110
  18.0 1.6 %collective-permute-done.1.refs_0_ = bf16[128,1024]{1,0:T(8,128)(2,1)S(1)} collective-permute-done((bf16[128,1024]{1,0:T(8,128)(2,1)S(1)}, bf16[128,1024]{1,0:T(8,128)(2,1)S(1)}, u32[]{:S(2)}, u32[]{:S(2)}) %collective-permute-start.1) | collective-permute-done | bytes 262176 | tf_op jit(solution)/shard_map/ppermute | solution.py:110
  19.6 1.5 %collective-permute-start.9 = (bf16[128,1024]{1,0:T(8,128)(2,1)S(1)}, bf16[128,1024]{1,0:T(8,128)(2,1)S(1)}, u32[]{:S(2)}, u32[]{:S(2)}) collective-permute-start(bf16[128,1024]{1,0:T(8,128)(2,1)S(1)} %captions_z.1.refs_2_), channel_id=1, source_target_pairs={{0,16},{8,24},{16,0},{24,8},{1,17},{9,25},{17,1},{25,9},{2,18},{10... | collective-permute-start | bytes 786440 | tf_op jit(solution)/shard_map/ppermute | solution.py:110
  21.3 1.0 %collective-permute-done.7.refs_0_ = bf16[64,1024]{1,0:T(8,128)(2,1)S(1)} collective-permute-done((bf16[64,1024]{1,0:T(8,128)(2,1)S(1)}, bf16[64,1024]{1,0:T(8,128)(2,1)S(1)}, u32[]{:S(2)}, u32[]{:S(2)}) %collective-permute-start.7) | collective-permute-done | bytes 131104 | tf_op jit(solution)/shard_map/ppermute | solution.py:110
  22.5 2.2 %collective-permute-done.5.refs_0_ = bf16[768,1024]{1,0:T(8,128)(2,1)S(1)} collective-permute-done((bf16[768,1024]{1,0:T(8,128)(2,1)S(1)}, bf16[768,1024]{1,0:T(8,128)(2,1)S(1)}, u32[]{:S(2)}, u32[]{:S(2)}) %collective-permute-start.5) | collective-permute-done | bytes 1572896 | tf_op jit(solution)/shard_map/ppermute | solution.py:110
  24.7 2.5 %early_pairs.1 = (bf16[768,1024]{1,0:T(8,128)(2,1)S(1)}, bf16[384,768]{1,0:T(8,128)(2,1)S(1)}, bf16[384,384]{1,0:T(8,128)(2,1)S(1)}, f32[1,384]{1,0:T(1,128)S(1)}) custom-call(f32[2,128]{1,0:T(2,128)S(1)} %consts.1.refs_1_, s32[1,1024]{1,0:T(1,128)S(1)} %get-tuple-element.44.labels, bf16[768,1024]{1,0:T(8,128)(2,1)S(1)} %near_blocks.1.N, ...), custom_call_target="tpu_custom_call" | custom-call | flops 905969664 | tf_op jit(solution)/shard_map/early_pairs/pallas_call | solution.py:28
  27.2 1.3 %middle_pairs.1 = (bf16[1024,1024]{1,0:T(8,128)(2,1)S(1)}, bf16[768,512]{1,0:T(8,128)(2,1)S(1)}, bf16[384,1024]{1,0:T(8,128)(2,1)S(1)}, f32[1,128]{1,0:T(1,128)S(1)}) custom-call(f32[2,128]{1,0:T(2,128)S(1)} %consts.1.refs_1_, s32[1,1024]{1,0:T(1,128)S(1)} %get-tuple-element.44.labels, bf16[768,1024]{1,0:T(8,128)(2,1)S(1)} %near_blocks.1.N, ...), custom_call_target="tpu_custom_call" | custom-call | flops 301989888 | tf_op jit(solution)/shard_map/middle_pairs/pallas_call | solution.py:28
  28.8 1.4 %far_captions.1 = (f32[1,512]{1,0:T(1,128)S(1)}, bf16[128,512]{1,0:T(8,128)(2,1)S(1)}, bf16[64,1024]{1,0:T(8,128)(2,1)S(1)}, bf16[64,1024]{1,0:T(8,128)(2,1)S(1)}) custom-call(f32[2,128]{1,0:T(2,128)S(1)} %consts.1.refs_1_, s32[1,1024]{1,0:T(1,128)S(1)} %get-tuple-element.44.labels, bf16[1024,1024]{1,0:T(8,128)(2,1)S(1)} %get-tuple-element.54.VV, ...), custom_call_target="tpu_custom_call" | custom-call | flops 536870912 | tf_op jit(solution)/shard_map/far_captions/pallas_call | solution.py:28
  30.2 0.6 %collective-permute-start.11 = (bf16[64,1024]{1,0:T(8,128)(2,1)S(1)}, bf16[64,1024]{1,0:T(8,128)(2,1)S(1)}, u32[]{:S(2)}, u32[]{:S(2)}) collective-permute-start(bf16[64,1024]{1,0:T(8,128)(2,1)S(1)} %get-tuple-element.62), channel_id=1, source_target_pairs={{0,16},{8,24},{16,0},{24,8},{1,17},{9,25},{17,1},{25,9},{2,18},{10... | collective-permute-start | bytes 393224 | tf_op jit(solution)/shard_map/ppermute | solution.py:110
  30.8 1.2 %far_clips.1 = (bf16[256,1024]{1,0:T(8,128)(2,1)S(1)}, bf16[256,512]{1,0:T(8,128)(2,1)S(1)}, f32[1,512]{1,0:T(1,128)S(1)}, bf16[128,1024]{1,0:T(8,128)(2,1)S(1)}) custom-call(f32[2,128]{1,0:T(2,128)S(1)} %consts.1.refs_1_, s32[1,1024]{1,0:T(1,128)S(1)} %get-tuple-element.44.labels, bf16[1024,1024]{1,0:T(8,128)(2,1)S(1)} %get-tuple-element.54.VV, ...), custom_call_target="tpu_custom_call" | custom-call | flops 402653184 | tf_op jit(solution)/shard_map/far_clips/pallas_call | solution.py:28
  32.0 1.6 %collective-permute-start.15 = (bf16[128,1024]{1,0:T(8,128)(2,1)S(1)}, bf16[128,1024]{1,0:T(8,128)(2,1)S(1)}, u32[]{:S(2)}, u32[]{:S(2)}) collective-permute-start(bf16[128,1024]{1,0:T(8,128)(2,1)S(1)} %get-tuple-element.60.after.refs_1_), channel_id=1, source_target_pairs={{0,8},{8,0},{16,24},{24,16},{1,9},{9,1},{17,25},{25,17},{2,10},{10... | collective-permute-start | bytes 786440 | tf_op jit(solution)/shard_map/ppermute | solution.py:110
  33.5 1.5 %collective-permute-start.13 = (bf16[64,1024]{1,0:T(8,128)(2,1)S(1)}, bf16[64,1024]{1,0:T(8,128)(2,1)S(1)}, u32[]{:S(2)}, u32[]{:S(2)}) collective-permute-start(bf16[64,1024]{1,0:T(8,128)(2,1)S(1)} %far_b.2), channel_id=1, source_target_pairs={{0,16},{8,24},{16,0},{24,8},{1,17},{9,25},{17,1},{25,9},{2,18},{10... | collective-permute-start | bytes 393224 | tf_op jit(solution)/shard_map/ppermute | solution.py:110
  35.1 1.0 %near_captions.1 = (f32[128,1024]{1,0:T(8,128)S(1)}, bf16[128,1024]{1,0:T(8,128)(2,1)S(1)}, f32[64,1024]{1,0:T(8,128)S(1)}, f32[64,1024]{1,0:T(8,128)S(1)}) custom-call(bf16[384,1024]{1,0:T(8,128)(2,1)S(1)} %get-tuple-element.59.coef, bf16[1024,1024]{1,0:T(8,128)(2,1)S(1)} %get-tuple-element.54.VV, bf16[128,1024]{1,0:T(8,128)(2,1)S(1)} %get-tuple-element.60.after.refs_1_), custom_call_target="tpu_custom_call" | custom-call | flops 805306368 | tf_op jit(solution)/shard_map/near_captions/pallas_call | solution.py:28
  36.1 2.5 %collective-permute-start.20 = (bf16[64,1024]{1,0:T(8,128)(2,1)S(1)}, bf16[64,1024]{1,0:T(8,128)(2,1)S(1)}, u32[]{:S(2)}, u32[]{:S(2)}) collective-permute-start(bf16[64,1024]{1,0:T(8,128)(2,1)S(1)} %add_a.1.after), channel_id=1, source_target_pairs={{0,4},{1,5},{2,6},{3,7},{4,0},{5,1},{6,2},{7,3},{8,12},{9,13},{10,... | collective-permute-start | bytes 393224 | tf_op jit(solution)/shard_map/ppermute | solution.py:110
  38.6 1.0 %near_clips.1 = (f32[128,1024]{1,0:T(8,128)S(1)}, bf16[128,1024]{1,0:T(8,128)(2,1)S(1)}, f32[128,1024]{1,0:T(8,128)S(1)}) custom-call(bf16[768,1024]{1,0:T(8,128)(2,1)S(1)} %get-tuple-element.50.S1, bf16[256,1024]{1,0:T(8,128)(2,1)S(1)} %get-tuple-element.68.S2, bf16[768,512]{1,0:T(8,128)(2,1)S(1)} %get-tuple-element.56.G1, ...), custom_call_target="tpu_custom_call" | custom-call | flops 805306368 | tf_op jit(solution)/shard_map/near_clips/pallas_call | solution.py:28
  39.7 2.6 %collective-permute-start.14 = (bf16[64,1024]{1,0:T(8,128)(2,1)S(1)}, bf16[64,1024]{1,0:T(8,128)(2,1)S(1)}, u32[]{:S(2)}, u32[]{:S(2)}) collective-permute-start(bf16[64,1024]{1,0:T(8,128)(2,1)S(1)} %add_b.1.refs_1_), channel_id=1, source_target_pairs={{0,4},{1,5},{2,6},{3,7},{4,0},{5,1},{6,2},{7,3},{8,12},{9,13},{10,... | collective-permute-start | bytes 393224 | tf_op jit(solution)/shard_map/ppermute | solution.py:110
  42.3 0.6 %collective-permute-start.18 = (bf16[128,1024]{1,0:T(8,128)(2,1)S(1)}, bf16[128,1024]{1,0:T(8,128)(2,1)S(1)}, u32[]{:S(2)}, u32[]{:S(2)}) collective-permute-start(bf16[128,1024]{1,0:T(8,128)(2,1)S(1)} %add_clips.1.sum_v.refs_1_), channel_id=1, source_target_pairs={{0,2},{1,3},{2,0},{3,1},{4,6},{5,7},{6,4},{7,5},{8,10},{9,11},{10,... | collective-permute-start | bytes 786440 | tf_op jit(solution)/shard_map/ppermute | solution.py:110
  42.9 2.0 %collective-permute-start.17 = (bf16[128,1024]{1,0:T(8,128)(2,1)S(1)}, bf16[128,1024]{1,0:T(8,128)(2,1)S(1)}, u32[]{:S(2)}, u32[]{:S(2)}) collective-permute-start(bf16[128,1024]{1,0:T(8,128)(2,1)S(1)} %near_x.1), channel_id=1, source_target_pairs={{0,8},{8,0},{16,24},{24,16},{1,9},{9,1},{17,25},{25,17},{2,10},{10... | collective-permute-start | bytes 786440 | tf_op jit(solution)/shard_map/ppermute | solution.py:110
  44.9 2.2 %collective-permute-done.20.refs_0_ = bf16[64,1024]{1,0:T(8,128)(2,1)S(1)} collective-permute-done((bf16[64,1024]{1,0:T(8,128)(2,1)S(1)}, bf16[64,1024]{1,0:T(8,128)(2,1)S(1)}, u32[]{:S(2)}, u32[]{:S(2)}) %collective-permute-start.20) | collective-permute-done | bytes 131104 | tf_op jit(solution)/shard_map/ppermute | solution.py:110
  47.1 3.4 %collective-permute-done.14.got.refs_0_ = bf16[64,1024]{1,0:T(8,128)(2,1)S(1)} collective-permute-done((bf16[64,1024]{1,0:T(8,128)(2,1)S(1)}, bf16[64,1024]{1,0:T(8,128)(2,1)S(1)}, u32[]{:S(2)}, u32[]{:S(2)}) %collective-permute-start.14) | collective-permute-done | bytes 131104 | tf_op jit(solution)/shard_map/ppermute | solution.py:110
  50.5 0.8 %collective-permute-done.19.refs_0_ = bf16[128,1024]{1,0:T(8,128)(2,1)S(1)} collective-permute-done((bf16[128,1024]{1,0:T(8,128)(2,1)S(1)}, bf16[128,1024]{1,0:T(8,128)(2,1)S(1)}, u32[]{:S(2)}, u32[]{:S(2)}) %collective-permute-start.19) | collective-permute-done | bytes 262176 | tf_op jit(solution)/shard_map/ppermute | solution.py:110
  51.3 1.1 %finish_captions.1 = (f32[128,1024]{1,0:T(8,128)}, f32[8,128]{1,0:T(8,128)S(1)}) custom-call(f32[2,128]{1,0:T(2,128)S(1)} %consts.1.refs_1_, f32[128,1024]{1,0:T(8,128)S(1)} %get-tuple-element.74.hat_ref, f32[128,1]{1,0:T(8,128)S(1)} %get-tuple-element.75.inverse_ref, f32[128,1024]{1,0:T(8,128)S(1)} %get-tuple-element.63.refs_1_.refs_0_, ...), custom_call_target="tpu_custom_call" | custom-call | tf_op jit(solution)/shard_map/finish_captions/pallas_call | solution.py:28
  52.4 0.9 %collective-permute-done.18.refs_0_ = bf16[128,1024]{1,0:T(8,128)(2,1)S(1)} collective-permute-done((bf16[128,1024]{1,0:T(8,128)(2,1)S(1)}, bf16[128,1024]{1,0:T(8,128)(2,1)S(1)}, u32[]{:S(2)}, u32[]{:S(2)}) %collective-permute-start.18) | collective-permute-done | bytes 262176 | tf_op jit(solution)/shard_map/ppermute | solution.py:110
  53.2 0.8 %collective-permute-done.16.refs_2_ = f32[1,128]{1,0:T(1,128)S(1)} collective-permute-done((f32[1,128]{1,0:T(1,128)S(1)}, f32[1,128]{1,0:T(1,128)S(1)}, u32[]{:S(2)}, u32[]{:S(2)}) %collective-permute-start.16) | collective-permute-done | bytes 544 | tf_op jit(solution)/shard_map/ppermute | solution.py:110
  54.1 1.1 %finish_clips.1 = (f32[128,1024]{1,0:T(8,128)}, f32[1,128]{1,0:T(1,128)}) custom-call(f32[2,128]{1,0:T(2,128)S(1)} %consts.1.refs_1_, f32[128,1024]{1,0:T(8,128)S(1)} %get-tuple-element.42.hat_ref, f32[128,1]{1,0:T(8,128)S(1)} %get-tuple-element.43.inverse_ref, f32[1,128]{1,0:T(1,128)S(1)} %get-tuple-element.64.refs_0_, ...), custom_call_target="tpu_custom_call" | custom-call | tf_op jit(solution)/shard_map/finish_clips/pallas_call | solution.py:28
  (45 shorter events, 1.2 us)
Async XLA Ops:
  2.2 10.5 %collective-permute-start.3 = (bf16[64,1024]{1,0:T(8,128)(2,1)S(1)}, bf16[64,1024]{1,0:T(8,128)(2,1)S(1)}, u32[]{:S(2)}, u32[]{:S(2)}) collective-permute-start(bf16[64,1024]{1,0:T(8,128)(2,1)S(1)} %get-tuple-element.47), channel_id=1, source_target_pairs={{0,2},{1,3},{2,0},{3,1},{4,6},{5,7},{6,4},{7,5},{8,10},{9,11},{10,... | collective-permute-start | bytes 393224 | tf_op jit(solution)/shard_map/ppermute | solution.py:110
  5.3 14.3 %collective-permute-start.1 = (bf16[128,1024]{1,0:T(8,128)(2,1)S(1)}, bf16[128,1024]{1,0:T(8,128)(2,1)S(1)}, u32[]{:S(2)}, u32[]{:S(2)}) collective-permute-start(bf16[128,1024]{1,0:T(8,128)(2,1)S(1)} %get-tuple-element.45.refs_0_), channel_id=1, source_target_pairs={{0,4},{1,5},{2,6},{3,7},{4,0},{5,1},{6,2},{7,3},{8,12},{9,13},{10,... | collective-permute-start | bytes 786440 | tf_op jit(solution)/shard_map/ppermute | solution.py:110
  7.8 13.3 %collective-permute-start = (bf16[128,1024]{1,0:T(8,128)(2,1)S(1)}, bf16[128,1024]{1,0:T(8,128)(2,1)S(1)}, u32[]{:S(2)}, u32[]{:S(2)}) collective-permute-start(bf16[128,1024]{1,0:T(8,128)(2,1)S(1)} %get-tuple-element.45.refs_0_), channel_id=1, source_target_pairs={{0,16},{8,24},{16,0},{24,8},{1,17},{9,25},{17,1},{25,9},{2,18},{10... | collective-permute-start | bytes 786440 | tf_op jit(solution)/shard_map/ppermute | solution.py:110
  9.4 7.1 %collective-permute-start.4 = (bf16[64,1024]{1,0:T(8,128)(2,1)S(1)}, bf16[64,1024]{1,0:T(8,128)(2,1)S(1)}, u32[]{:S(2)}, u32[]{:S(2)}) collective-permute-start(bf16[64,1024]{1,0:T(8,128)(2,1)S(1)} %get-tuple-element.48), channel_id=1, source_target_pairs={{0,2},{1,3},{2,0},{3,1},{4,6},{5,7},{6,4},{7,5},{8,10},{9,11},{10,... | collective-permute-start | bytes 393224 | tf_op jit(solution)/shard_map/ppermute | solution.py:110
  9.8 11.3 %collective-permute-start.2 = (bf16[128,1024]{1,0:T(8,128)(2,1)S(1)}, bf16[128,1024]{1,0:T(8,128)(2,1)S(1)}, u32[]{:S(2)}, u32[]{:S(2)}) collective-permute-start(bf16[128,1024]{1,0:T(8,128)(2,1)S(1)} %get-tuple-element.46.refs_3_), channel_id=1, source_target_pairs={{0,8},{8,0},{16,24},{24,16},{1,9},{9,1},{17,25},{25,17},{2,10},{10... | collective-permute-start | bytes 786440 | tf_op jit(solution)/shard_map/ppermute | solution.py:110
  12.6 8.7 %collective-permute-start.6 = (bf16[64,1024]{1,0:T(8,128)(2,1)S(1)}, bf16[64,1024]{1,0:T(8,128)(2,1)S(1)}, u32[]{:S(2)}, u32[]{:S(2)}) collective-permute-start(bf16[64,1024]{1,0:T(8,128)(2,1)S(1)} %clips_z.2.refs_5_), channel_id=1, source_target_pairs={{0,8},{8,0},{16,24},{24,16},{1,9},{9,1},{17,25},{25,17},{2,10},{10... | collective-permute-start | bytes 393224 | tf_op jit(solution)/shard_map/ppermute | solution.py:110
  16.5 5.9 %collective-permute-start.7 = (bf16[64,1024]{1,0:T(8,128)(2,1)S(1)}, bf16[64,1024]{1,0:T(8,128)(2,1)S(1)}, u32[]{:S(2)}, u32[]{:S(2)}) collective-permute-start(bf16[64,1024]{1,0:T(8,128)(2,1)S(1)} %clips_z.3.refs_6_), channel_id=1, source_target_pairs={{0,8},{8,0},{16,24},{24,16},{1,9},{9,1},{17,25},{25,17},{2,10},{10... | collective-permute-start | bytes 393224 | tf_op jit(solution)/shard_map/ppermute | solution.py:110
  19.6 8.9 %collective-permute-start.9 = (bf16[128,1024]{1,0:T(8,128)(2,1)S(1)}, bf16[128,1024]{1,0:T(8,128)(2,1)S(1)}, u32[]{:S(2)}, u32[]{:S(2)}) collective-permute-start(bf16[128,1024]{1,0:T(8,128)(2,1)S(1)} %captions_z.1.refs_2_), channel_id=1, source_target_pairs={{0,16},{8,24},{16,0},{24,8},{1,17},{9,25},{17,1},{25,9},{2,18},{10... | collective-permute-start | bytes 786440 | tf_op jit(solution)/shard_map/ppermute | solution.py:110
  21.2 3.5 %collective-permute-start.5 = (bf16[768,1024]{1,0:T(8,128)(2,1)S(1)}, bf16[768,1024]{1,0:T(8,128)(2,1)S(1)}, u32[]{:S(2)}, u32[]{:S(2)}) collective-permute-start(bf16[768,1024]{1,0:T(8,128)(2,1)S(1)} %near_blocks.1.N), channel_id=1, source_target_pairs={{0,1},{1,0},{2,3},{3,2},{4,5},{5,4},{6,7},{7,6},{8,9},{9,8},{10,11... | collective-permute-start | bytes 4718600 | tf_op jit(solution)/shard_map/ppermute | solution.py:110
  22.4 4.8 %collective-permute-start.8 = (bf16[128,1024]{1,0:T(8,128)(2,1)S(1)}, bf16[128,1024]{1,0:T(8,128)(2,1)S(1)}, u32[]{:S(2)}, u32[]{:S(2)}) collective-permute-start(bf16[128,1024]{1,0:T(8,128)(2,1)S(1)} %diagonal_clips.1.vd), channel_id=1, source_target_pairs={{0,1},{1,0},{2,3},{3,2},{4,5},{5,4},{6,7},{7,6},{8,9},{9,8},{10,11... | collective-permute-start | bytes 786440 | tf_op jit(solution)/shard_map/ppermute | solution.py:110
  28.5 2.2 %collective-permute-start.10 = (bf16[128,1024]{1,0:T(8,128)(2,1)S(1)}, bf16[128,1024]{1,0:T(8,128)(2,1)S(1)}, u32[]{:S(2)}, u32[]{:S(2)}) collective-permute-start(bf16[128,1024]{1,0:T(8,128)(2,1)S(1)} %captions_d.1.refs_0_), channel_id=1, source_target_pairs={{0,1},{1,0},{2,3},{3,2},{4,5},{5,4},{6,7},{7,6},{8,9},{9,8},{10,11... | collective-permute-start | bytes 786440 | tf_op jit(solution)/shard_map/ppermute | solution.py:110
  30.2 5.9 %collective-permute-start.11 = (bf16[64,1024]{1,0:T(8,128)(2,1)S(1)}, bf16[64,1024]{1,0:T(8,128)(2,1)S(1)}, u32[]{:S(2)}, u32[]{:S(2)}) collective-permute-start(bf16[64,1024]{1,0:T(8,128)(2,1)S(1)} %get-tuple-element.62), channel_id=1, source_target_pairs={{0,16},{8,24},{16,0},{24,8},{1,17},{9,25},{17,1},{25,9},{2,18},{10... | collective-permute-start | bytes 393224 | tf_op jit(solution)/shard_map/ppermute | solution.py:110
  32.0 10.3 %collective-permute-start.15 = (bf16[128,1024]{1,0:T(8,128)(2,1)S(1)}, bf16[128,1024]{1,0:T(8,128)(2,1)S(1)}, u32[]{:S(2)}, u32[]{:S(2)}) collective-permute-start(bf16[128,1024]{1,0:T(8,128)(2,1)S(1)} %get-tuple-element.60.after.refs_1_), channel_id=1, source_target_pairs={{0,8},{8,0},{16,24},{24,16},{1,9},{9,1},{17,25},{25,17},{2,10},{10... | collective-permute-start | bytes 786440 | tf_op jit(solution)/shard_map/ppermute | solution.py:110
  33.5 6.1 %collective-permute-start.13 = (bf16[64,1024]{1,0:T(8,128)(2,1)S(1)}, bf16[64,1024]{1,0:T(8,128)(2,1)S(1)}, u32[]{:S(2)}, u32[]{:S(2)}) collective-permute-start(bf16[64,1024]{1,0:T(8,128)(2,1)S(1)} %far_b.2), channel_id=1, source_target_pairs={{0,16},{8,24},{16,0},{24,8},{1,17},{9,25},{17,1},{25,9},{2,18},{10... | collective-permute-start | bytes 393224 | tf_op jit(solution)/shard_map/ppermute | solution.py:110
  36.1 11.0 %collective-permute-start.20 = (bf16[64,1024]{1,0:T(8,128)(2,1)S(1)}, bf16[64,1024]{1,0:T(8,128)(2,1)S(1)}, u32[]{:S(2)}, u32[]{:S(2)}) collective-permute-start(bf16[64,1024]{1,0:T(8,128)(2,1)S(1)} %add_a.1.after), channel_id=1, source_target_pairs={{0,4},{1,5},{2,6},{3,7},{4,0},{5,1},{6,2},{7,3},{8,12},{9,13},{10,... | collective-permute-start | bytes 393224 | tf_op jit(solution)/shard_map/ppermute | solution.py:110
  38.6 3.7 %collective-permute-start.12 = (f32[2,128]{1,0:T(2,128)S(1)}, f32[2,128]{1,0:T(2,128)S(1)}, u32[]{:S(2)}, u32[]{:S(2)}) collective-permute-start(f32[2,128]{1,0:T(2,128)S(1)} %get-tuple-element.65), channel_id=1, source_target_pairs={{0,8},{8,0},{16,24},{24,16},{1,9},{9,1},{17,25},{25,17},{2,10},{10... | collective-permute-start | bytes 3080 | tf_op jit(solution)/shard_map/ppermute | solution.py:110
  39.7 10.8 %collective-permute-start.14 = (bf16[64,1024]{1,0:T(8,128)(2,1)S(1)}, bf16[64,1024]{1,0:T(8,128)(2,1)S(1)}, u32[]{:S(2)}, u32[]{:S(2)}) collective-permute-start(bf16[64,1024]{1,0:T(8,128)(2,1)S(1)} %add_b.1.refs_1_), channel_id=1, source_target_pairs={{0,4},{1,5},{2,6},{3,7},{4,0},{5,1},{6,2},{7,3},{8,12},{9,13},{10,... | collective-permute-start | bytes 393224 | tf_op jit(solution)/shard_map/ppermute | solution.py:110
  42.3 10.9 %collective-permute-start.18 = (bf16[128,1024]{1,0:T(8,128)(2,1)S(1)}, bf16[128,1024]{1,0:T(8,128)(2,1)S(1)}, u32[]{:S(2)}, u32[]{:S(2)}) collective-permute-start(bf16[128,1024]{1,0:T(8,128)(2,1)S(1)} %add_clips.1.sum_v.refs_1_), channel_id=1, source_target_pairs={{0,2},{1,3},{2,0},{3,1},{4,6},{5,7},{6,4},{7,5},{8,10},{9,11},{10,... | collective-permute-start | bytes 786440 | tf_op jit(solution)/shard_map/ppermute | solution.py:110
  42.9 7.6 %collective-permute-start.17 = (bf16[128,1024]{1,0:T(8,128)(2,1)S(1)}, bf16[128,1024]{1,0:T(8,128)(2,1)S(1)}, u32[]{:S(2)}, u32[]{:S(2)}) collective-permute-start(bf16[128,1024]{1,0:T(8,128)(2,1)S(1)} %near_x.1), channel_id=1, source_target_pairs={{0,8},{8,0},{16,24},{24,16},{1,9},{9,1},{17,25},{25,17},{2,10},{10... | collective-permute-start | bytes 786440 | tf_op jit(solution)/shard_map/ppermute | solution.py:110
  44.9 6.4 %collective-permute-start.19 = (bf16[128,1024]{1,0:T(8,128)(2,1)S(1)}, bf16[128,1024]{1,0:T(8,128)(2,1)S(1)}, u32[]{:S(2)}, u32[]{:S(2)}) collective-permute-start(bf16[128,1024]{1,0:T(8,128)(2,1)S(1)} %near_y.1), channel_id=1, source_target_pairs={{0,16},{8,24},{16,0},{24,8},{1,17},{9,25},{17,1},{25,9},{2,18},{10... | collective-permute-start | bytes 786440 | tf_op jit(solution)/shard_map/ppermute | solution.py:110
  50.5 3.5 %collective-permute-start.16 = (f32[1,128]{1,0:T(1,128)S(1)}, f32[1,128]{1,0:T(1,128)S(1)}, u32[]{:S(2)}, u32[]{:S(2)}) collective-permute-start(f32[1,128]{1,0:T(1,128)S(1)} %add_loss.1.refs_4_), channel_id=1, source_target_pairs={{0,2},{1,3},{2,0},{3,1},{4,6},{5,7},{6,4},{7,5},{8,10},{9,11},{10,... | collective-permute-start | bytes 1544 | tf_op jit(solution)/shard_map/ppermute | solution.py:110

commit v11 on v9

--- a/solution.py
+++ b/solution.py
@@ -126,18 +126,25 @@
 
     def strip(consts, blocks, k, captions, clips, labels, counted, put):
         scale, shift = consts[0:1, 0:1], consts[1:2, 0:1]
-        dots = dot_nt(captions, clips)
-        total = 0.0
-        for i, (s, t) in enumerate(blocks):
-            block = dots[i * rows : (i + 1) * rows]
-            coef, add = pairs(block, scale, shift, first_caption(s, t, k), labels, counted)
-            put(i * rows, coef)
-            total = total + add if counted else None
-        return total
+        losses = []
+        for left in range(0, clips.shape[0], CHUNK):
+            right = min(left + CHUNK, clips.shape[0])
+            dots = dot_nt(captions, clips[left:right])
+            count = max(0, min(counted - left, right - left))
+            total = 0.0
+            for i, (s, t) in enumerate(blocks):
+                block = dots[i * rows : (i + 1) * rows]
+                base = first_caption(s, t, k)
+                coef, add = pairs(block, scale, shift, base, labels[:, left:right], count)
+                put(i * rows, left, coef)
+                total = total + add if count else None
+            if count:
+                losses.append(total)
+        return jnp.concatenate(losses, axis=1) if losses else None
 
     def put_in(target, first=0, left=0):
-        def put(at, coef):
-            target[pl.ds(first + at, coef.shape[0]), pl.ds(left, coef.shape[1])] = coef
+        def put(at, column, coef):
+            target[pl.ds(first + at, coef.shape[0]), pl.ds(left + column, coef.shape[1])] = coef
         return put
 
     def normalize_kernel(film, text, matched, v16, c16, va, vb, vhat, chat, vinv, cinv, labels, fbuf, tbuf, mbuf, sems):

time: 54.6 us -> 54.6 us (level)
  no operation moved by 1% of the time
where the time goes in v11:
time: 54.6 us; the launch traced here: 54.4 us
  starting transfers between devices  25.2 us (46%)
  waiting for transfers between devices  14.8 us (27%)
  Pallas kernels  12.4 us (23%)
  between operations  2.13 us (4%)
    ppermute x22, starting transfers between devices, swap(): return lax.ppermute(value, axis, [(i, i ^ bits) for i in range(size)])  25.2 us
    ppermute x22, waiting for transfers between devices, swap(): return lax.ppermute(value, axis, [(i, i ^ bits) for i in range(size)])  14.8 us
    pallas_call x35, Pallas kernels, call(): pl.pallas_call(kernel, name=name, out_shape=out_shape, in_specs=[SPECS[sp...  12.4 us
  transfers between devices with their start and end apart: 22, of which 12 were waited for; matrix products, arithmetic and copies ran while one was open for 0% of the time, Pallas kernels for 18%

profile of v11, /device:TPU:0, one launch (start us, length us, event | category | flops | bytes accessed | tf_op | source)
XLA Modules:
  0.0 54.4 jit_solution(8824443788652757493)
XLA Ops:
  0.6 1.5 %normalize.1 = (bf16[128,1024]{1,0:T(8,128)(2,1)S(1)}, bf16[128,1024]{1,0:T(8,128)(2,1)S(1)}, bf16[64,1024]{1,0:T(8,128)(2,1)S(1)}, bf16[64,1024]{1,0:T(8,128)(2...) custom-call(f32[128,1024]{1,0:T(8,128)} %film.1, ...), custom_call_target="tpu_custom_call" | custom-call | tf_op jit(solution)/shard_map/normalize/pallas_call | solution.py:28
  2.2 3.1 %collective-permute-start.2 = (bf16[64,1024]{1,0:T(8,128)(2,1)S(1)}, bf16[64,1024]{1,0:T(8,128)(2,1)S(1)}, u32[]{:S(2)}, u32[]{:S(2)}) collective-permute-start(bf16[64,1024]{1,0:T(8,128)(2,1)S(1)} %get-tuple-element.47), channel_id=1, source_target_pairs={{0,2},{1,3},{2,0},{3,1},{4,6},{5,7},{6,4},{7,5},{8,10},{9,11},{10,... | collective-permute-start | bytes 393224 | tf_op jit(solution)/shard_map/ppermute | solution.py:110
  5.3 2.6 %collective-permute-start.5 = (bf16[128,1024]{1,0:T(8,128)(2,1)S(1)}, bf16[128,1024]{1,0:T(8,128)(2,1)S(1)}, u32[]{:S(2)}, u32[]{:S(2)}) collective-permute-start(bf16[128,1024]{1,0:T(8,128)(2,1)S(1)} %get-tuple-element.45.refs_0_), channel_id=1, source_target_pairs={{0,4},{1,5},{2,6},{3,7},{4,0},{5,1},{6,2},{7,3},{8,12},{9,13},{10,... | collective-permute-start | bytes 786440 | tf_op jit(solution)/shard_map/ppermute | solution.py:110
  7.8 1.5 %collective-permute-start = (bf16[128,1024]{1,0:T(8,128)(2,1)S(1)}, bf16[128,1024]{1,0:T(8,128)(2,1)S(1)}, u32[]{:S(2)}, u32[]{:S(2)}) collective-permute-start(bf16[128,1024]{1,0:T(8,128)(2,1)S(1)} %get-tuple-element.45.refs_0_), channel_id=1, source_target_pairs={{0,16},{8,24},{16,0},{24,8},{1,17},{9,25},{17,1},{25,9},{2,18},{10... | collective-permute-start | bytes 786440 | tf_op jit(solution)/shard_map/ppermute | solution.py:110
  9.8 1.5 %collective-permute-start.1 = (bf16[128,1024]{1,0:T(8,128)(2,1)S(1)}, bf16[128,1024]{1,0:T(8,128)(2,1)S(1)}, u32[]{:S(2)}, u32[]{:S(2)}) collective-permute-start(bf16[128,1024]{1,0:T(8,128)(2,1)S(1)} %get-tuple-element.46.refs_2_), channel_id=1, source_target_pairs={{0,8},{8,0},{16,24},{24,16},{1,9},{9,1},{17,25},{25,17},{2,10},{10... | collective-permute-start | bytes 786440 | tf_op jit(solution)/shard_map/ppermute | solution.py:110
  12.6 0.6 %collective-permute-start.7 = (bf16[64,1024]{1,0:T(8,128)(2,1)S(1)}, bf16[64,1024]{1,0:T(8,128)(2,1)S(1)}, u32[]{:S(2)}, u32[]{:S(2)}) collective-permute-start(bf16[64,1024]{1,0:T(8,128)(2,1)S(1)} %clips_z.2.refs_4_), channel_id=1, source_target_pairs={{0,8},{8,0},{16,24},{24,16},{1,9},{9,1},{17,25},{25,17},{2,10},{10... | collective-permute-start | bytes 393224 | tf_op jit(solution)/shard_map/ppermute | solution.py:110
  13.2 3.2 %collective-permute-done.3.refs_0_ = bf16[64,1024]{1,0:T(8,128)(2,1)S(1)} collective-permute-done((bf16[64,1024]{1,0:T(8,128)(2,1)S(1)}, bf16[64,1024]{1,0:T(8,128)(2,1)S(1)}, u32[]{:S(2)}, u32[]{:S(2)}) %collective-permute-start.3) | collective-permute-done | bytes 131104 | tf_op jit(solution)/shard_map/ppermute | solution.py:110
  16.5 1.5 %collective-permute-start.8 = (bf16[64,1024]{1,0:T(8,128)(2,1)S(1)}, bf16[64,1024]{1,0:T(8,128)(2,1)S(1)}, u32[]{:S(2)}, u32[]{:S(2)}) collective-permute-start(bf16[64,1024]{1,0:T(8,128)(2,1)S(1)} %clips_z.3.refs_5_), channel_id=1, source_target_pairs={{0,8},{8,0},{16,24},{24,16},{1,9},{9,1},{17,25},{25,17},{2,10},{10... | collective-permute-start | bytes 393224 | tf_op jit(solution)/shard_map/ppermute | solution.py:110
  18.3 1.3 %collective-permute-done.5.refs_0_ = bf16[128,1024]{1,0:T(8,128)(2,1)S(1)} collective-permute-done((bf16[128,1024]{1,0:T(8,128)(2,1)S(1)}, bf16[128,1024]{1,0:T(8,128)(2,1)S(1)}, u32[]{:S(2)}, u32[]{:S(2)}) %collective-permute-start.5) | collective-permute-done | bytes 262176 | tf_op jit(solution)/shard_map/ppermute | solution.py:110
  19.6 1.5 %collective-permute-start.10 = (bf16[128,1024]{1,0:T(8,128)(2,1)S(1)}, bf16[128,1024]{1,0:T(8,128)(2,1)S(1)}, u32[]{:S(2)}, u32[]{:S(2)}) collective-permute-start(bf16[128,1024]{1,0:T(8,128)(2,1)S(1)} %captions_z.1.refs_0_), channel_id=1, source_target_pairs={{0,16},{8,24},{16,0},{24,8},{1,17},{9,25},{17,1},{25,9},{2,18},{10... | collective-permute-start | bytes 786440 | tf_op jit(solution)/shard_map/ppermute | solution.py:110
  21.1 1.2 %collective-permute-done.8.refs_0_ = bf16[64,1024]{1,0:T(8,128)(2,1)S(1)} collective-permute-done((bf16[64,1024]{1,0:T(8,128)(2,1)S(1)}, bf16[64,1024]{1,0:T(8,128)(2,1)S(1)}, u32[]{:S(2)}, u32[]{:S(2)}) %collective-permute-start.8) | collective-permute-done | bytes 131104 | tf_op jit(solution)/shard_map/ppermute | solution.py:110
  22.6 2.5 %early_pairs.1 = (bf16[768,1024]{1,0:T(8,128)(2,1)S(1)}, bf16[384,768]{1,0:T(8,128)(2,1)S(1)}, bf16[384,384]{1,0:T(8,128)(2,1)S(1)}, f32[1,384]{1,0:T(1,128)S(1)}) custom-call(f32[2,128]{1,0:T(2,128)S(1)} %consts.1.refs_1_, s32[1,1024]{1,0:T(1,128)S(1)} %get-tuple-element.44.labels, bf16[640,1024]{1,0:T(8,128)(2,1)S(1)} %near_blocks.1.N, ...), custom_call_target="tpu_custom_call" | custom-call | flops 905969664 | tf_op jit(solution)/shard_map/early_pairs/pallas_call | solution.py:28
  25.1 1.3 %middle_pairs.1 = (bf16[1024,1024]{1,0:T(8,128)(2,1)S(1)}, bf16[768,512]{1,0:T(8,128)(2,1)S(1)}, bf16[384,1024]{1,0:T(8,128)(2,1)S(1)}, f32[1,128]{1,0:T(1,128)S(1)}) custom-call(f32[2,128]{1,0:T(2,128)S(1)} %consts.1.refs_1_, s32[1,1024]{1,0:T(1,128)S(1)} %get-tuple-element.44.labels, bf16[640,1024]{1,0:T(8,128)(2,1)S(1)} %near_blocks.1.N, ...), custom_call_target="tpu_custom_call" | custom-call | flops 301989888 | tf_op jit(solution)/shard_map/middle_pairs/pallas_call | solution.py:28
  26.5 0.6 %collective-permute-done.10.refs_0_ = bf16[128,1024]{1,0:T(8,128)(2,1)S(1)} collective-permute-done((bf16[128,1024]{1,0:T(8,128)(2,1)S(1)}, bf16[128,1024]{1,0:T(8,128)(2,1)S(1)}, u32[]{:S(2)}, u32[]{:S(2)}) %collective-permute-start.10) | collective-permute-done | bytes 262176 | tf_op jit(solution)/shard_map/ppermute | solution.py:110
  27.0 1.4 %far_captions.1 = (f32[1,512]{1,0:T(1,128)S(1)}, bf16[128,512]{1,0:T(8,128)(2,1)S(1)}, bf16[64,1024]{1,0:T(8,128)(2,1)S(1)}, bf16[64,1024]{1,0:T(8,128)(2,1)S(1)}) custom-call(f32[2,128]{1,0:T(2,128)S(1)} %consts.1.refs_1_, s32[1,1024]{1,0:T(1,128)S(1)} %get-tuple-element.44.labels, bf16[1024,1024]{1,0:T(8,128)(2,1)S(1)} %get-tuple-element.54.VV, ...), custom_call_target="tpu_custom_call" | custom-call | flops 536870912 | tf_op jit(solution)/shard_map/far_captions/pallas_call | solution.py:28
  28.5 1.4 %collective-permute-start.12 = (bf16[64,1024]{1,0:T(8,128)(2,1)S(1)}, bf16[64,1024]{1,0:T(8,128)(2,1)S(1)}, u32[]{:S(2)}, u32[]{:S(2)}) collective-permute-start(bf16[64,1024]{1,0:T(8,128)(2,1)S(1)} %get-tuple-element.62), channel_id=1, source_target_pairs={{0,16},{8,24},{16,0},{24,8},{1,17},{9,25},{17,1},{25,9},{2,18},{10... | collective-permute-start | bytes 393224 | tf_op jit(solution)/shard_map/ppermute | solution.py:110
  29.9 1.2 %far_clips.1 = (bf16[256,1024]{1,0:T(8,128)(2,1)S(1)}, bf16[256,512]{1,0:T(8,128)(2,1)S(1)}, f32[1,512]{1,0:T(1,128)S(1)}, bf16[128,1024]{1,0:T(8,128)(2,1)S(1)}) custom-call(f32[2,128]{1,0:T(2,128)S(1)} %consts.1.refs_1_, s32[1,1024]{1,0:T(1,128)S(1)} %get-tuple-element.44.labels, bf16[1024,1024]{1,0:T(8,128)(2,1)S(1)} %get-tuple-element.54.VV, ...), custom_call_target="tpu_custom_call" | custom-call | flops 402653184 | tf_op jit(solution)/shard_map/far_clips/pallas_call | solution.py:28
  31.1 1.2 %collective-permute-start.16 = (bf16[128,1024]{1,0:T(8,128)(2,1)S(1)}, bf16[128,1024]{1,0:T(8,128)(2,1)S(1)}, u32[]{:S(2)}, u32[]{:S(2)}) collective-permute-start(bf16[128,1024]{1,0:T(8,128)(2,1)S(1)} %get-tuple-element.60.after.refs_1_), channel_id=1, source_target_pairs={{0,8},{8,0},{16,24},{24,16},{1,9},{9,1},{17,25},{25,17},{2,10},{10... | collective-permute-start | bytes 786440 | tf_op jit(solution)/shard_map/ppermute | solution.py:110
  32.3 1.1 %collective-permute-start.14 = (bf16[64,1024]{1,0:T(8,128)(2,1)S(1)}, bf16[64,1024]{1,0:T(8,128)(2,1)S(1)}, u32[]{:S(2)}, u32[]{:S(2)}) collective-permute-start(bf16[64,1024]{1,0:T(8,128)(2,1)S(1)} %far_b.2), channel_id=1, source_target_pairs={{0,16},{8,24},{16,0},{24,8},{1,17},{9,25},{17,1},{25,9},{2,18},{10... | collective-permute-start | bytes 393224 | tf_op jit(solution)/shard_map/ppermute | solution.py:110
  33.3 1.0 %near_captions.1 = (f32[128,1024]{1,0:T(8,128)S(1)}, bf16[128,1024]{1,0:T(8,128)(2,1)S(1)}, f32[64,1024]{1,0:T(8,128)S(1)}, f32[64,1024]{1,0:T(8,128)S(1)}) custom-call(bf16[384,1024]{1,0:T(8,128)(2,1)S(1)} %get-tuple-element.59.coef, bf16[1024,1024]{1,0:T(8,128)(2,1)S(1)} %get-tuple-element.54.VV, bf16[128,1024]{1,0:T(8,128)(2,1)S(1)} %get-tuple-element.60.after.refs_1_), custom_call_target="tpu_custom_call" | custom-call | flops 805306368 | tf_op jit(solution)/shard_map/near_captions/pallas_call | solution.py:28
  34.5 3.4 %collective-permute-start.21 = (bf16[64,1024]{1,0:T(8,128)(2,1)S(1)}, bf16[64,1024]{1,0:T(8,128)(2,1)S(1)}, u32[]{:S(2)}, u32[]{:S(2)}) collective-permute-start(bf16[64,1024]{1,0:T(8,128)(2,1)S(1)} %add_a.1.after), channel_id=1, source_target_pairs={{0,4},{1,5},{2,6},{3,7},{4,0},{5,1},{6,2},{7,3},{8,12},{9,13},{10,... | collective-permute-start | bytes 393224 | tf_op jit(solution)/shard_map/ppermute | solution.py:110
  38.4 1.0 %near_clips.1 = (f32[128,1024]{1,0:T(8,128)S(1)}, bf16[128,1024]{1,0:T(8,128)(2,1)S(1)}, f32[128,1024]{1,0:T(8,128)S(1)}) custom-call(bf16[768,1024]{1,0:T(8,128)(2,1)S(1)} %get-tuple-element.50.S1, bf16[256,1024]{1,0:T(8,128)(2,1)S(1)} %get-tuple-element.68.S2, bf16[768,512]{1,0:T(8,128)(2,1)S(1)} %get-tuple-element.56.G1, ...), custom_call_target="tpu_custom_call" | custom-call | flops 805306368 | tf_op jit(solution)/shard_map/near_clips/pallas_call | solution.py:28
  39.5 1.2 %collective-permute-start.15 = (bf16[64,1024]{1,0:T(8,128)(2,1)S(1)}, bf16[64,1024]{1,0:T(8,128)(2,1)S(1)}, u32[]{:S(2)}, u32[]{:S(2)}) collective-permute-start(bf16[64,1024]{1,0:T(8,128)(2,1)S(1)} %add_b.1.refs_1_), channel_id=1, source_target_pairs={{0,4},{1,5},{2,6},{3,7},{4,0},{5,1},{6,2},{7,3},{8,12},{9,13},{10,... | collective-permute-start | bytes 393224 | tf_op jit(solution)/shard_map/ppermute | solution.py:110
  40.7 0.8 %collective-permute-done.13.refs_0_ = f32[2,128]{1,0:T(2,128)S(1)} collective-permute-done((f32[2,128]{1,0:T(2,128)S(1)}, f32[2,128]{1,0:T(2,128)S(1)}, u32[]{:S(2)}, u32[]{:S(2)}) %collective-permute-start.13) | collective-permute-done | bytes 1056 | tf_op jit(solution)/shard_map/ppermute | solution.py:110
  41.5 0.7 %collective-permute-start.19 = (bf16[128,1024]{1,0:T(8,128)(2,1)S(1)}, bf16[128,1024]{1,0:T(8,128)(2,1)S(1)}, u32[]{:S(2)}, u32[]{:S(2)}) collective-permute-start(bf16[128,1024]{1,0:T(8,128)(2,1)S(1)} %add_clips.1.sum_v.refs_1_), channel_id=1, source_target_pairs={{0,2},{1,3},{2,0},{3,1},{4,6},{5,7},{6,4},{7,5},{8,10},{9,11},{10,... | collective-permute-start | bytes 786440 | tf_op jit(solution)/shard_map/ppermute | solution.py:110
  42.3 0.8 %collective-permute-start.18 = (bf16[128,1024]{1,0:T(8,128)(2,1)S(1)}, bf16[128,1024]{1,0:T(8,128)(2,1)S(1)}, u32[]{:S(2)}, u32[]{:S(2)}) collective-permute-start(bf16[128,1024]{1,0:T(8,128)(2,1)S(1)} %near_x.1), channel_id=1, source_target_pairs={{0,8},{8,0},{16,24},{24,16},{1,9},{9,1},{17,25},{25,17},{2,10},{10... | collective-permute-start | bytes 786440 | tf_op jit(solution)/shard_map/ppermute | solution.py:110
  43.1 1.9 %collective-permute-start.20 = (bf16[128,1024]{1,0:T(8,128)(2,1)S(1)}, bf16[128,1024]{1,0:T(8,128)(2,1)S(1)}, u32[]{:S(2)}, u32[]{:S(2)}) collective-permute-start(bf16[128,1024]{1,0:T(8,128)(2,1)S(1)} %near_y.1), channel_id=1, source_target_pairs={{0,16},{8,24},{16,0},{24,8},{1,17},{9,25},{17,1},{25,9},{2,18},{10... | collective-permute-start | bytes 786440 | tf_op jit(solution)/shard_map/ppermute | solution.py:110
  45.0 2.9 %collective-permute-done.21.refs_0_ = bf16[64,1024]{1,0:T(8,128)(2,1)S(1)} collective-permute-done((bf16[64,1024]{1,0:T(8,128)(2,1)S(1)}, bf16[64,1024]{1,0:T(8,128)(2,1)S(1)}, u32[]{:S(2)}, u32[]{:S(2)}) %collective-permute-start.21) | collective-permute-done | bytes 131104 | tf_op jit(solution)/shard_map/ppermute | solution.py:110
  48.0 1.9 %collective-permute-done.15.got.refs_0_ = bf16[64,1024]{1,0:T(8,128)(2,1)S(1)} collective-permute-done((bf16[64,1024]{1,0:T(8,128)(2,1)S(1)}, bf16[64,1024]{1,0:T(8,128)(2,1)S(1)}, u32[]{:S(2)}, u32[]{:S(2)}) %collective-permute-start.15) | collective-permute-done | bytes 131104 | tf_op jit(solution)/shard_map/ppermute | solution.py:110
  49.9 1.1 %finish_captions.1 = (f32[128,1024]{1,0:T(8,128)}, f32[8,128]{1,0:T(8,128)S(1)}) custom-call(f32[2,128]{1,0:T(2,128)S(1)} %consts.1.refs_1_, f32[128,1024]{1,0:T(8,128)S(1)} %get-tuple-element.74.hat_ref, f32[128,1]{1,0:T(8,128)S(1)} %get-tuple-element.75.inverse_ref, f32[128,1024]{1,0:T(8,128)S(1)} %get-tuple-element.63.refs_1_.refs_0_, ...), custom_call_target="tpu_custom_call" | custom-call | tf_op jit(solution)/shard_map/finish_captions/pallas_call | solution.py:28
  51.0 1.9 %collective-permute-done.19.refs_0_ = bf16[128,1024]{1,0:T(8,128)(2,1)S(1)} collective-permute-done((bf16[128,1024]{1,0:T(8,128)(2,1)S(1)}, bf16[128,1024]{1,0:T(8,128)(2,1)S(1)}, u32[]{:S(2)}, u32[]{:S(2)}) %collective-permute-start.19) | collective-permute-done | bytes 262176 | tf_op jit(solution)/shard_map/ppermute | solution.py:110
  53.4 1.1 %finish_clips.1 = (f32[128,1024]{1,0:T(8,128)}, f32[1,128]{1,0:T(1,128)}) custom-call(f32[2,128]{1,0:T(2,128)S(1)} %consts.1.refs_1_, f32[128,1024]{1,0:T(8,128)S(1)} %get-tuple-element.42.hat_ref, f32[128,1]{1,0:T(8,128)S(1)} %get-tuple-element.43.inverse_ref, f32[1,128]{1,0:T(1,128)S(1)} %get-tuple-element.64.refs_0_, ...), custom_call_target="tpu_custom_call" | custom-call | tf_op jit(solution)/shard_map/finish_clips/pallas_call | solution.py:28
  (47 shorter events, 2.4 us)
Async XLA Ops:
  2.2 10.5 %collective-permute-start.2 = (bf16[64,1024]{1,0:T(8,128)(2,1)S(1)}, bf16[64,1024]{1,0:T(8,128)(2,1)S(1)}, u32[]{:S(2)}, u32[]{:S(2)}) collective-permute-start(bf16[64,1024]{1,0:T(8,128)(2,1)S(1)} %get-tuple-element.47), channel_id=1, source_target_pairs={{0,2},{1,3},{2,0},{3,1},{4,6},{5,7},{6,4},{7,5},{8,10},{9,11},{10,... | collective-permute-start | bytes 393224 | tf_op jit(solution)/shard_map/ppermute | solution.py:110
  5.3 14.3 %collective-permute-start.5 = (bf16[128,1024]{1,0:T(8,128)(2,1)S(1)}, bf16[128,1024]{1,0:T(8,128)(2,1)S(1)}, u32[]{:S(2)}, u32[]{:S(2)}) collective-permute-start(bf16[128,1024]{1,0:T(8,128)(2,1)S(1)} %get-tuple-element.45.refs_0_), channel_id=1, source_target_pairs={{0,4},{1,5},{2,6},{3,7},{4,0},{5,1},{6,2},{7,3},{8,12},{9,13},{10,... | collective-permute-start | bytes 786440 | tf_op jit(solution)/shard_map/ppermute | solution.py:110
  7.8 10.3 %collective-permute-start = (bf16[128,1024]{1,0:T(8,128)(2,1)S(1)}, bf16[128,1024]{1,0:T(8,128)(2,1)S(1)}, u32[]{:S(2)}, u32[]{:S(2)}) collective-permute-start(bf16[128,1024]{1,0:T(8,128)(2,1)S(1)} %get-tuple-element.45.refs_0_), channel_id=1, source_target_pairs={{0,16},{8,24},{16,0},{24,8},{1,17},{9,25},{17,1},{25,9},{2,18},{10... | collective-permute-start | bytes 786440 | tf_op jit(solution)/shard_map/ppermute | solution.py:110
  9.4 7.1 %collective-permute-start.3 = (bf16[64,1024]{1,0:T(8,128)(2,1)S(1)}, bf16[64,1024]{1,0:T(8,128)(2,1)S(1)}, u32[]{:S(2)}, u32[]{:S(2)}) collective-permute-start(bf16[64,1024]{1,0:T(8,128)(2,1)S(1)} %get-tuple-element.48), channel_id=1, source_target_pairs={{0,2},{1,3},{2,0},{3,1},{4,6},{5,7},{6,4},{7,5},{8,10},{9,11},{10,... | collective-permute-start | bytes 393224 | tf_op jit(solution)/shard_map/ppermute | solution.py:110
  9.8 8.3 %collective-permute-start.1 = (bf16[128,1024]{1,0:T(8,128)(2,1)S(1)}, bf16[128,1024]{1,0:T(8,128)(2,1)S(1)}, u32[]{:S(2)}, u32[]{:S(2)}) collective-permute-start(bf16[128,1024]{1,0:T(8,128)(2,1)S(1)} %get-tuple-element.46.refs_2_), channel_id=1, source_target_pairs={{0,8},{8,0},{16,24},{24,16},{1,9},{9,1},{17,25},{25,17},{2,10},{10... | collective-permute-start | bytes 786440 | tf_op jit(solution)/shard_map/ppermute | solution.py:110
  12.6 8.5 %collective-permute-start.7 = (bf16[64,1024]{1,0:T(8,128)(2,1)S(1)}, bf16[64,1024]{1,0:T(8,128)(2,1)S(1)}, u32[]{:S(2)}, u32[]{:S(2)}) collective-permute-start(bf16[64,1024]{1,0:T(8,128)(2,1)S(1)} %clips_z.2.refs_4_), channel_id=1, source_target_pairs={{0,8},{8,0},{16,24},{24,16},{1,9},{9,1},{17,25},{25,17},{2,10},{10... | collective-permute-start | bytes 393224 | tf_op jit(solution)/shard_map/ppermute | solution.py:110
  16.5 5.9 %collective-permute-start.8 = (bf16[64,1024]{1,0:T(8,128)(2,1)S(1)}, bf16[64,1024]{1,0:T(8,128)(2,1)S(1)}, u32[]{:S(2)}, u32[]{:S(2)}) collective-permute-start(bf16[64,1024]{1,0:T(8,128)(2,1)S(1)} %clips_z.3.refs_5_), channel_id=1, source_target_pairs={{0,8},{8,0},{16,24},{24,16},{1,9},{9,1},{17,25},{25,17},{2,10},{10... | collective-permute-start | bytes 393224 | tf_op jit(solution)/shard_map/ppermute | solution.py:110
  18.2 4.2 %collective-permute-start.4 = (bf16[640,1024]{1,0:T(8,128)(2,1)S(1)}, bf16[640,1024]{1,0:T(8,128)(2,1)S(1)}, u32[]{:S(2)}, u32[]{:S(2)}) collective-permute-start(bf16[640,1024]{1,0:T(8,128)(2,1)S(1)} %near_blocks.1.N), channel_id=1, source_target_pairs={{0,1},{1,0},{2,3},{3,2},{4,5},{5,4},{6,7},{7,6},{8,9},{9,8},{10,11... | collective-permute-start | bytes 3932168 | tf_op jit(solution)/shard_map/ppermute | solution.py:110
  19.6 7.4 %collective-permute-start.10 = (bf16[128,1024]{1,0:T(8,128)(2,1)S(1)}, bf16[128,1024]{1,0:T(8,128)(2,1)S(1)}, u32[]{:S(2)}, u32[]{:S(2)}) collective-permute-start(bf16[128,1024]{1,0:T(8,128)(2,1)S(1)} %captions_z.1.refs_0_), channel_id=1, source_target_pairs={{0,16},{8,24},{16,0},{24,8},{1,17},{9,25},{17,1},{25,9},{2,18},{10... | collective-permute-start | bytes 786440 | tf_op jit(solution)/shard_map/ppermute | solution.py:110
  21.1 1.5 %collective-permute-start.6 = (bf16[128,1024]{1,0:T(8,128)(2,1)S(1)}, bf16[128,1024]{1,0:T(8,128)(2,1)S(1)}, u32[]{:S(2)}, u32[]{:S(2)}) collective-permute-start(bf16[128,1024]{1,0:T(8,128)(2,1)S(1)} %captions_z.1.refs_0_), channel_id=1, source_target_pairs={{0,1},{1,0},{2,3},{3,2},{4,5},{5,4},{6,7},{7,6},{8,9},{9,8},{10,11... | collective-permute-start | bytes 786440 | tf_op jit(solution)/shard_map/ppermute | solution.py:110
  22.4 2.8 %collective-permute-start.9 = (bf16[128,1024]{1,0:T(8,128)(2,1)S(1)}, bf16[128,1024]{1,0:T(8,128)(2,1)S(1)}, u32[]{:S(2)}, u32[]{:S(2)}) collective-permute-start(bf16[128,1024]{1,0:T(8,128)(2,1)S(1)} %diagonal_clips.1.vd), channel_id=1, source_target_pairs={{0,1},{1,0},{2,3},{3,2},{4,5},{5,4},{6,7},{7,6},{8,9},{9,8},{10,11... | collective-permute-start | bytes 786440 | tf_op jit(solution)/shard_map/ppermute | solution.py:110
  27.0 2.9 %collective-permute-start.11 = (bf16[128,1024]{1,0:T(8,128)(2,1)S(1)}, bf16[128,1024]{1,0:T(8,128)(2,1)S(1)}, u32[]{:S(2)}, u32[]{:S(2)}) collective-permute-start(bf16[128,1024]{1,0:T(8,128)(2,1)S(1)} %captions_d.1.refs_0_), channel_id=1, source_target_pairs={{0,1},{1,0},{2,3},{3,2},{4,5},{5,4},{6,7},{7,6},{8,9},{9,8},{10,11... | collective-permute-start | bytes 786440 | tf_op jit(solution)/shard_map/ppermute | solution.py:110
  28.5 6.0 %collective-permute-start.12 = (bf16[64,1024]{1,0:T(8,128)(2,1)S(1)}, bf16[64,1024]{1,0:T(8,128)(2,1)S(1)}, u32[]{:S(2)}, u32[]{:S(2)}) collective-permute-start(bf16[64,1024]{1,0:T(8,128)(2,1)S(1)} %get-tuple-element.62), channel_id=1, source_target_pairs={{0,16},{8,24},{16,0},{24,8},{1,17},{9,25},{17,1},{25,9},{2,18},{10... | collective-permute-start | bytes 393224 | tf_op jit(solution)/shard_map/ppermute | solution.py:110
  31.1 10.4 %collective-permute-start.16 = (bf16[128,1024]{1,0:T(8,128)(2,1)S(1)}, bf16[128,1024]{1,0:T(8,128)(2,1)S(1)}, u32[]{:S(2)}, u32[]{:S(2)}) collective-permute-start(bf16[128,1024]{1,0:T(8,128)(2,1)S(1)} %get-tuple-element.60.after.refs_1_), channel_id=1, source_target_pairs={{0,8},{8,0},{16,24},{24,16},{1,9},{9,1},{17,25},{25,17},{2,10},{10... | collective-permute-start | bytes 786440 | tf_op jit(solution)/shard_map/ppermute | solution.py:110
  32.3 7.2 %collective-permute-start.14 = (bf16[64,1024]{1,0:T(8,128)(2,1)S(1)}, bf16[64,1024]{1,0:T(8,128)(2,1)S(1)}, u32[]{:S(2)}, u32[]{:S(2)}) collective-permute-start(bf16[64,1024]{1,0:T(8,128)(2,1)S(1)} %far_b.2), channel_id=1, source_target_pairs={{0,16},{8,24},{16,0},{24,8},{1,17},{9,25},{17,1},{25,9},{2,18},{10... | collective-permute-start | bytes 393224 | tf_op jit(solution)/shard_map/ppermute | solution.py:110
  34.5 13.5 %collective-permute-start.21 = (bf16[64,1024]{1,0:T(8,128)(2,1)S(1)}, bf16[64,1024]{1,0:T(8,128)(2,1)S(1)}, u32[]{:S(2)}, u32[]{:S(2)}) collective-permute-start(bf16[64,1024]{1,0:T(8,128)(2,1)S(1)} %add_a.1.after), channel_id=1, source_target_pairs={{0,4},{1,5},{2,6},{3,7},{4,0},{5,1},{6,2},{7,3},{8,12},{9,13},{10,... | collective-permute-start | bytes 393224 | tf_op jit(solution)/shard_map/ppermute | solution.py:110
  37.9 3.6 %collective-permute-start.13 = (f32[2,128]{1,0:T(2,128)S(1)}, f32[2,128]{1,0:T(2,128)S(1)}, u32[]{:S(2)}, u32[]{:S(2)}) collective-permute-start(f32[2,128]{1,0:T(2,128)S(1)} %get-tuple-element.65), channel_id=1, source_target_pairs={{0,8},{8,0},{16,24},{24,16},{1,9},{9,1},{17,25},{25,17},{2,10},{10... | collective-permute-start | bytes 3080 | tf_op jit(solution)/shard_map/ppermute | solution.py:110
  39.5 10.3 %collective-permute-start.15 = (bf16[64,1024]{1,0:T(8,128)(2,1)S(1)}, bf16[64,1024]{1,0:T(8,128)(2,1)S(1)}, u32[]{:S(2)}, u32[]{:S(2)}) collective-permute-start(bf16[64,1024]{1,0:T(8,128)(2,1)S(1)} %add_b.1.refs_1_), channel_id=1, source_target_pairs={{0,4},{1,5},{2,6},{3,7},{4,0},{5,1},{6,2},{7,3},{8,12},{9,13},{10,... | collective-permute-start | bytes 393224 | tf_op jit(solution)/shard_map/ppermute | solution.py:110
  41.5 11.3 %collective-permute-start.19 = (bf16[128,1024]{1,0:T(8,128)(2,1)S(1)}, bf16[128,1024]{1,0:T(8,128)(2,1)S(1)}, u32[]{:S(2)}, u32[]{:S(2)}) collective-permute-start(bf16[128,1024]{1,0:T(8,128)(2,1)S(1)} %add_clips.1.sum_v.refs_1_), channel_id=1, source_target_pairs={{0,2},{1,3},{2,0},{3,1},{4,6},{5,7},{6,4},{7,5},{8,10},{9,11},{10,... | collective-permute-start | bytes 786440 | tf_op jit(solution)/shard_map/ppermute | solution.py:110
  42.3 7.5 %collective-permute-start.18 = (bf16[128,1024]{1,0:T(8,128)(2,1)S(1)}, bf16[128,1024]{1,0:T(8,128)(2,1)S(1)}, u32[]{:S(2)}, u32[]{:S(2)}) collective-permute-start(bf16[128,1024]{1,0:T(8,128)(2,1)S(1)} %near_x.1), channel_id=1, source_target_pairs={{0,8},{8,0},{16,24},{24,16},{1,9},{9,1},{17,25},{25,17},{2,10},{10... | collective-permute-start | bytes 786440 | tf_op jit(solution)/shard_map/ppermute | solution.py:110
  43.1 6.7 %collective-permute-start.20 = (bf16[128,1024]{1,0:T(8,128)(2,1)S(1)}, bf16[128,1024]{1,0:T(8,128)(2,1)S(1)}, u32[]{:S(2)}, u32[]{:S(2)}) collective-permute-start(bf16[128,1024]{1,0:T(8,128)(2,1)S(1)} %near_y.1), channel_id=1, source_target_pairs={{0,16},{8,24},{16,0},{24,8},{1,17},{9,25},{17,1},{25,9},{2,18},{10... | collective-permute-start | bytes 786440 | tf_op jit(solution)/shard_map/ppermute | solution.py:110
  49.8 3.5 %collective-permute-start.17 = (f32[1,128]{1,0:T(1,128)S(1)}, f32[1,128]{1,0:T(1,128)S(1)}, u32[]{:S(2)}, u32[]{:S(2)}) collective-permute-start(f32[1,128]{1,0:T(1,128)S(1)} %add_loss.1.refs_4_), channel_id=1, source_target_pairs={{0,2},{1,3},{2,0},{3,1},{4,6},{5,7},{6,4},{7,5},{8,10},{9,11},{10,... | collective-permute-start | bytes 1544 | tf_op jit(solution)/shard_map/ppermute | solution.py:110

commit v12 on v11

--- a/solution.py
+++ b/solution.py
@@ -199,8 +199,9 @@
     c_z = [hand_on("captions_z", swap(c16, "col", 4 * s), consts, flops=4 * LONG // 4) for s in range(1, Z)]
     c_y = [swap(c16, "row", 2 * t) for t in range(1, Y)]
     v_x = swap(v16, "row", 1)
-    v_d = [hand_on("clips_d", swap(b, "row", 1), flops=2 * LONG // 4) for b in v_z]
+    v_d = [hand_on("clips_d", swap(b, "row", 1), flops=LONG) for b in v_z]
     c_d = [swap(b, "row", 2 * t) for b in c_z for t in range(1, Y)]
+    c_y = [hand_on("captions_y", b, c_z[0]) for b in c_y]
     N = join("near_blocks", c16, *c_y, v16, v_x, *v_z)
     N_k = hand_on("near_other", swap(N, "col", 1), flops=4 * LONG // 4)
     cz_k = [swap(b, "col", 1) for b in c_z]

time: 54.6 us -> 55.1 us (level)
  waiting for transfers between devices: 14.8 us -> 15.4 us
    ppermute x22, waiting for transfers between devices: 14.8 us -> 15.4 us  [swap(): return lax.ppermute(value, axis, [(i, i ^ bits) for i in range(size)])]
    pallas_call x35 -> x36, Pallas kernels: 12.4 us -> 12.4 us  [call(): pl.pallas_call(kernel, name=name, out_shape=out_shape, in_specs=[SPECS[sp...]
  transfers between devices with their start and end apart: 22 -> 22, of which waited for: 12 -> 9; matrix products, arithmetic and copies ran while one was open for 0% -> 0% of each run, Pallas kernels for 18% -> 18%
where the time goes in v12:
time: 55.1 us; the launch traced here: 54.9 us
  starting transfers between devices  25.1 us (46%)
  waiting for transfers between devices  15.4 us (28%)
  Pallas kernels  12.4 us (23%)
  between operations  2.13 us (4%)
    ppermute x22, starting transfers between devices, swap(): return lax.ppermute(value, axis, [(i, i ^ bits) for i in range(size)])  25.1 us
    ppermute x22, waiting for transfers between devices, swap(): return lax.ppermute(value, axis, [(i, i ^ bits) for i in range(size)])  15.4 us
    pallas_call x36, Pallas kernels, call(): pl.pallas_call(kernel, name=name, out_shape=out_shape, in_specs=[SPECS[sp...  12.4 us
  transfers between devices with their start and end apart: 22, of which 9 were waited for; matrix products, arithmetic and copies ran while one was open for 0% of the time, Pallas kernels for 18%

profile of v12, /device:TPU:0, one launch (start us, length us, event | category | flops | bytes accessed | tf_op | source)
XLA Modules:
  0.0 54.9 jit_solution(7565273058339456763)
XLA Ops:
  0.6 1.5 %normalize.1 = (bf16[128,1024]{1,0:T(8,128)(2,1)S(1)}, bf16[128,1024]{1,0:T(8,128)(2,1)S(1)}, bf16[64,1024]{1,0:T(8,128)(2,1)S(1)}, bf16[64,1024]{1,0:T(8,128)(2...) custom-call(f32[128,1024]{1,0:T(8,128)} %film.1, ...), custom_call_target="tpu_custom_call" | custom-call | tf_op jit(solution)/shard_map/normalize/pallas_call | solution.py:28
  2.2 3.1 %collective-permute-start.3 = (bf16[64,1024]{1,0:T(8,128)(2,1)S(1)}, bf16[64,1024]{1,0:T(8,128)(2,1)S(1)}, u32[]{:S(2)}, u32[]{:S(2)}) collective-permute-start(bf16[64,1024]{1,0:T(8,128)(2,1)S(1)} %get-tuple-element.47), channel_id=1, source_target_pairs={{0,2},{1,3},{2,0},{3,1},{4,6},{5,7},{6,4},{7,5},{8,10},{9,11},{10,... | collective-permute-start | bytes 393224 | tf_op jit(solution)/shard_map/ppermute | solution.py:110
  5.3 2.6 %collective-permute-start.1 = (bf16[128,1024]{1,0:T(8,128)(2,1)S(1)}, bf16[128,1024]{1,0:T(8,128)(2,1)S(1)}, u32[]{:S(2)}, u32[]{:S(2)}) collective-permute-start(bf16[128,1024]{1,0:T(8,128)(2,1)S(1)} %get-tuple-element.45.refs_0_), channel_id=1, source_target_pairs={{0,4},{1,5},{2,6},{3,7},{4,0},{5,1},{6,2},{7,3},{8,12},{9,13},{10,... | collective-permute-start | bytes 786440 | tf_op jit(solution)/shard_map/ppermute | solution.py:110
  7.8 1.5 %collective-permute-start = (bf16[128,1024]{1,0:T(8,128)(2,1)S(1)}, bf16[128,1024]{1,0:T(8,128)(2,1)S(1)}, u32[]{:S(2)}, u32[]{:S(2)}) collective-permute-start(bf16[128,1024]{1,0:T(8,128)(2,1)S(1)} %get-tuple-element.45.refs_0_), channel_id=1, source_target_pairs={{0,16},{8,24},{16,0},{24,8},{1,17},{9,25},{17,1},{25,9},{2,18},{10... | collective-permute-start | bytes 786440 | tf_op jit(solution)/shard_map/ppermute | solution.py:110
  9.8 1.5 %collective-permute-start.2 = (bf16[128,1024]{1,0:T(8,128)(2,1)S(1)}, bf16[128,1024]{1,0:T(8,128)(2,1)S(1)}, u32[]{:S(2)}, u32[]{:S(2)}) collective-permute-start(bf16[128,1024]{1,0:T(8,128)(2,1)S(1)} %get-tuple-element.46.refs_2_), channel_id=1, source_target_pairs={{0,8},{8,0},{16,24},{24,16},{1,9},{9,1},{17,25},{25,17},{2,10},{10... | collective-permute-start | bytes 786440 | tf_op jit(solution)/shard_map/ppermute | solution.py:110
  12.6 0.6 %collective-permute-start.7 = (bf16[64,1024]{1,0:T(8,128)(2,1)S(1)}, bf16[64,1024]{1,0:T(8,128)(2,1)S(1)}, u32[]{:S(2)}, u32[]{:S(2)}) collective-permute-start(bf16[64,1024]{1,0:T(8,128)(2,1)S(1)} %clips_z.2.refs_4_), channel_id=1, source_target_pairs={{0,8},{8,0},{16,24},{24,16},{1,9},{9,1},{17,25},{25,17},{2,10},{10... | collective-permute-start | bytes 393224 | tf_op jit(solution)/shard_map/ppermute | solution.py:110
  13.2 3.2 %collective-permute-done.4.refs_0_ = bf16[64,1024]{1,0:T(8,128)(2,1)S(1)} collective-permute-done((bf16[64,1024]{1,0:T(8,128)(2,1)S(1)}, bf16[64,1024]{1,0:T(8,128)(2,1)S(1)}, u32[]{:S(2)}, u32[]{:S(2)}) %collective-permute-start.4) | collective-permute-done | bytes 131104 | tf_op jit(solution)/shard_map/ppermute | solution.py:110
  16.5 1.5 %collective-permute-start.8 = (bf16[64,1024]{1,0:T(8,128)(2,1)S(1)}, bf16[64,1024]{1,0:T(8,128)(2,1)S(1)}, u32[]{:S(2)}, u32[]{:S(2)}) collective-permute-start(bf16[64,1024]{1,0:T(8,128)(2,1)S(1)} %clips_z.3.refs_5_), channel_id=1, source_target_pairs={{0,8},{8,0},{16,24},{24,16},{1,9},{9,1},{17,25},{25,17},{2,10},{10... | collective-permute-start | bytes 393224 | tf_op jit(solution)/shard_map/ppermute | solution.py:110
  18.0 1.6 %collective-permute-done.1.refs_0_ = bf16[128,1024]{1,0:T(8,128)(2,1)S(1)} collective-permute-done((bf16[128,1024]{1,0:T(8,128)(2,1)S(1)}, bf16[128,1024]{1,0:T(8,128)(2,1)S(1)}, u32[]{:S(2)}, u32[]{:S(2)}) %collective-permute-start.1) | collective-permute-done | bytes 262176 | tf_op jit(solution)/shard_map/ppermute | solution.py:110
  19.6 1.5 %collective-permute-start.10 = (bf16[128,1024]{1,0:T(8,128)(2,1)S(1)}, bf16[128,1024]{1,0:T(8,128)(2,1)S(1)}, u32[]{:S(2)}, u32[]{:S(2)}) collective-permute-start(bf16[128,1024]{1,0:T(8,128)(2,1)S(1)} %captions_z.1.refs_1_.refs_0_), channel_id=1, source_target_pairs={{0,16},{8,24},{16,0},{24,8},{1,17},{9,25},{17,1},{25,9},{2,18},{10... | collective-permute-start | bytes 786440 | tf_op jit(solution)/shard_map/ppermute | solution.py:110
  21.2 0.6 %collective-permute-start.5 = (bf16[640,1024]{1,0:T(8,128)(2,1)S(1)}, bf16[640,1024]{1,0:T(8,128)(2,1)S(1)}, u32[]{:S(2)}, u32[]{:S(2)}) collective-permute-start(bf16[640,1024]{1,0:T(8,128)(2,1)S(1)} %near_blocks.1.N), channel_id=1, source_target_pairs={{0,1},{1,0},{2,3},{3,2},{4,5},{5,4},{6,7},{7,6},{8,9},{9,8},{10,11... | collective-permute-start | bytes 3932168 | tf_op jit(solution)/shard_map/ppermute | solution.py:110
  21.8 0.6 %collective-permute-done.8.refs_0_ = bf16[64,1024]{1,0:T(8,128)(2,1)S(1)} collective-permute-done((bf16[64,1024]{1,0:T(8,128)(2,1)S(1)}, bf16[64,1024]{1,0:T(8,128)(2,1)S(1)}, u32[]{:S(2)}, u32[]{:S(2)}) %collective-permute-start.8) | collective-permute-done | bytes 131104 | tf_op jit(solution)/shard_map/ppermute | solution.py:110
  22.5 2.1 %collective-permute-done.5.refs_0_ = bf16[640,1024]{1,0:T(8,128)(2,1)S(1)} collective-permute-done((bf16[640,1024]{1,0:T(8,128)(2,1)S(1)}, bf16[640,1024]{1,0:T(8,128)(2,1)S(1)}, u32[]{:S(2)}, u32[]{:S(2)}) %collective-permute-start.5) | collective-permute-done | bytes 1310752 | tf_op jit(solution)/shard_map/ppermute | solution.py:110
  24.5 2.5 %early_pairs.1 = (bf16[768,1024]{1,0:T(8,128)(2,1)S(1)}, bf16[384,768]{1,0:T(8,128)(2,1)S(1)}, bf16[384,384]{1,0:T(8,128)(2,1)S(1)}, f32[1,384]{1,0:T(1,128)S(1)}) custom-call(f32[2,128]{1,0:T(2,128)S(1)} %consts.1.refs_1_, s32[1,1024]{1,0:T(1,128)S(1)} %get-tuple-element.44.labels, bf16[640,1024]{1,0:T(8,128)(2,1)S(1)} %near_blocks.1.N, ...), custom_call_target="tpu_custom_call" | custom-call | flops 905969664 | tf_op jit(solution)/shard_map/early_pairs/pallas_call | solution.py:28
  27.0 1.3 %middle_pairs.1 = (bf16[1024,1024]{1,0:T(8,128)(2,1)S(1)}, bf16[768,512]{1,0:T(8,128)(2,1)S(1)}, bf16[384,1024]{1,0:T(8,128)(2,1)S(1)}, f32[1,128]{1,0:T(1,128)S(1)}) custom-call(f32[2,128]{1,0:T(2,128)S(1)} %consts.1.refs_1_, s32[1,1024]{1,0:T(1,128)S(1)} %get-tuple-element.44.labels, bf16[640,1024]{1,0:T(8,128)(2,1)S(1)} %near_blocks.1.N, ...), custom_call_target="tpu_custom_call" | custom-call | flops 301989888 | tf_op jit(solution)/shard_map/middle_pairs/pallas_call | solution.py:28
  28.7 1.4 %far_captions.1 = (f32[1,512]{1,0:T(1,128)S(1)}, bf16[128,512]{1,0:T(8,128)(2,1)S(1)}, bf16[64,1024]{1,0:T(8,128)(2,1)S(1)}, bf16[64,1024]{1,0:T(8,128)(2,1)S(1)}) custom-call(f32[2,128]{1,0:T(2,128)S(1)} %consts.1.refs_1_, s32[1,1024]{1,0:T(1,128)S(1)} %get-tuple-element.44.labels, bf16[1024,1024]{1,0:T(8,128)(2,1)S(1)} %get-tuple-element.54.VV, ...), custom_call_target="tpu_custom_call" | custom-call | flops 536870912 | tf_op jit(solution)/shard_map/far_captions/pallas_call | solution.py:28
  30.2 0.6 %collective-permute-start.12 = (bf16[64,1024]{1,0:T(8,128)(2,1)S(1)}, bf16[64,1024]{1,0:T(8,128)(2,1)S(1)}, u32[]{:S(2)}, u32[]{:S(2)}) collective-permute-start(bf16[64,1024]{1,0:T(8,128)(2,1)S(1)} %get-tuple-element.62), channel_id=1, source_target_pairs={{0,16},{8,24},{16,0},{24,8},{1,17},{9,25},{17,1},{25,9},{2,18},{10... | collective-permute-start | bytes 393224 | tf_op jit(solution)/shard_map/ppermute | solution.py:110
  30.7 1.2 %far_clips.1 = (bf16[256,1024]{1,0:T(8,128)(2,1)S(1)}, bf16[256,512]{1,0:T(8,128)(2,1)S(1)}, f32[1,512]{1,0:T(1,128)S(1)}, bf16[128,1024]{1,0:T(8,128)(2,1)S(1)}) custom-call(f32[2,128]{1,0:T(2,128)S(1)} %consts.1.refs_1_, s32[1,1024]{1,0:T(1,128)S(1)} %get-tuple-element.44.labels, bf16[1024,1024]{1,0:T(8,128)(2,1)S(1)} %get-tuple-element.54.VV, ...), custom_call_target="tpu_custom_call" | custom-call | flops 402653184 | tf_op jit(solution)/shard_map/far_clips/pallas_call | solution.py:28
  31.9 1.6 %collective-permute-start.16 = (bf16[128,1024]{1,0:T(8,128)(2,1)S(1)}, bf16[128,1024]{1,0:T(8,128)(2,1)S(1)}, u32[]{:S(2)}, u32[]{:S(2)}) collective-permute-start(bf16[128,1024]{1,0:T(8,128)(2,1)S(1)} %get-tuple-element.60.after.refs_1_), channel_id=1, source_target_pairs={{0,8},{8,0},{16,24},{24,16},{1,9},{9,1},{17,25},{25,17},{2,10},{10... | collective-permute-start | bytes 786440 | tf_op jit(solution)/shard_map/ppermute | solution.py:110
  33.5 1.5 %collective-permute-start.14 = (bf16[64,1024]{1,0:T(8,128)(2,1)S(1)}, bf16[64,1024]{1,0:T(8,128)(2,1)S(1)}, u32[]{:S(2)}, u32[]{:S(2)}) collective-permute-start(bf16[64,1024]{1,0:T(8,128)(2,1)S(1)} %far_b.2), channel_id=1, source_target_pairs={{0,16},{8,24},{16,0},{24,8},{1,17},{9,25},{17,1},{25,9},{2,18},{10... | collective-permute-start | bytes 393224 | tf_op jit(solution)/shard_map/ppermute | solution.py:110
  35.0 1.0 %near_captions.1 = (f32[128,1024]{1,0:T(8,128)S(1)}, bf16[128,1024]{1,0:T(8,128)(2,1)S(1)}, f32[64,1024]{1,0:T(8,128)S(1)}, f32[64,1024]{1,0:T(8,128)S(1)}) custom-call(bf16[384,1024]{1,0:T(8,128)(2,1)S(1)} %get-tuple-element.59.coef, bf16[1024,1024]{1,0:T(8,128)(2,1)S(1)} %get-tuple-element.54.VV, bf16[128,1024]{1,0:T(8,128)(2,1)S(1)} %get-tuple-element.60.after.refs_1_), custom_call_target="tpu_custom_call" | custom-call | flops 805306368 | tf_op jit(solution)/shard_map/near_captions/pallas_call | solution.py:28
  36.1 2.2 %collective-permute-start.21 = (bf16[64,1024]{1,0:T(8,128)(2,1)S(1)}, bf16[64,1024]{1,0:T(8,128)(2,1)S(1)}, u32[]{:S(2)}, u32[]{:S(2)}) collective-permute-start(bf16[64,1024]{1,0:T(8,128)(2,1)S(1)} %add_a.1.after), channel_id=1, source_target_pairs={{0,4},{1,5},{2,6},{3,7},{4,0},{5,1},{6,2},{7,3},{8,12},{9,13},{10,... | collective-permute-start | bytes 393224 | tf_op jit(solution)/shard_map/ppermute | solution.py:110
  38.6 1.0 %near_clips.1 = (f32[128,1024]{1,0:T(8,128)S(1)}, bf16[128,1024]{1,0:T(8,128)(2,1)S(1)}, f32[128,1024]{1,0:T(8,128)S(1)}) custom-call(bf16[768,1024]{1,0:T(8,128)(2,1)S(1)} %get-tuple-element.50.S1, bf16[256,1024]{1,0:T(8,128)(2,1)S(1)} %get-tuple-element.68.S2, bf16[768,512]{1,0:T(8,128)(2,1)S(1)} %get-tuple-element.56.G1, ...), custom_call_target="tpu_custom_call" | custom-call | flops 805306368 | tf_op jit(solution)/shard_map/near_clips/pallas_call | solution.py:28
  39.6 2.6 %collective-permute-start.15 = (bf16[64,1024]{1,0:T(8,128)(2,1)S(1)}, bf16[64,1024]{1,0:T(8,128)(2,1)S(1)}, u32[]{:S(2)}, u32[]{:S(2)}) collective-permute-start(bf16[64,1024]{1,0:T(8,128)(2,1)S(1)} %add_b.1.refs_1_), channel_id=1, source_target_pairs={{0,4},{1,5},{2,6},{3,7},{4,0},{5,1},{6,2},{7,3},{8,12},{9,13},{10,... | collective-permute-start | bytes 393224 | tf_op jit(solution)/shard_map/ppermute | solution.py:110
  42.9 2.0 %collective-permute-start.18 = (bf16[128,1024]{1,0:T(8,128)(2,1)S(1)}, bf16[128,1024]{1,0:T(8,128)(2,1)S(1)}, u32[]{:S(2)}, u32[]{:S(2)}) collective-permute-start(bf16[128,1024]{1,0:T(8,128)(2,1)S(1)} %near_x.1), channel_id=1, source_target_pairs={{0,8},{8,0},{16,24},{24,16},{1,9},{9,1},{17,25},{25,17},{2,10},{10... | collective-permute-start | bytes 786440 | tf_op jit(solution)/shard_map/ppermute | solution.py:110
  44.9 1.4 %collective-permute-done.21.refs_0_ = bf16[64,1024]{1,0:T(8,128)(2,1)S(1)} collective-permute-done((bf16[64,1024]{1,0:T(8,128)(2,1)S(1)}, bf16[64,1024]{1,0:T(8,128)(2,1)S(1)}, u32[]{:S(2)}, u32[]{:S(2)}) %collective-permute-start.21) | collective-permute-done | bytes 131104 | tf_op jit(solution)/shard_map/ppermute | solution.py:110
  46.4 4.0 %collective-permute-done.15.got.refs_0_ = bf16[64,1024]{1,0:T(8,128)(2,1)S(1)} collective-permute-done((bf16[64,1024]{1,0:T(8,128)(2,1)S(1)}, bf16[64,1024]{1,0:T(8,128)(2,1)S(1)}, u32[]{:S(2)}, u32[]{:S(2)}) %collective-permute-start.15) | collective-permute-done | bytes 131104 | tf_op jit(solution)/shard_map/ppermute | solution.py:110
  50.3 0.9 %collective-permute-done.20.refs_0_ = bf16[128,1024]{1,0:T(8,128)(2,1)S(1)} collective-permute-done((bf16[128,1024]{1,0:T(8,128)(2,1)S(1)}, bf16[128,1024]{1,0:T(8,128)(2,1)S(1)}, u32[]{:S(2)}, u32[]{:S(2)}) %collective-permute-start.20) | collective-permute-done | bytes 262176 | tf_op jit(solution)/shard_map/ppermute | solution.py:110
  51.3 1.1 %finish_captions.1 = (f32[128,1024]{1,0:T(8,128)}, f32[8,128]{1,0:T(8,128)S(1)}) custom-call(f32[2,128]{1,0:T(2,128)S(1)} %consts.1.refs_1_, f32[128,1024]{1,0:T(8,128)S(1)} %get-tuple-element.74.hat_ref, f32[128,1]{1,0:T(8,128)S(1)} %get-tuple-element.75.inverse_ref, f32[128,1024]{1,0:T(8,128)S(1)} %get-tuple-element.63.refs_1_.refs_0_, ...), custom_call_target="tpu_custom_call" | custom-call | tf_op jit(solution)/shard_map/finish_captions/pallas_call | solution.py:28
  52.4 0.7 %collective-permute-done.19.refs_0_ = bf16[128,1024]{1,0:T(8,128)(2,1)S(1)} collective-permute-done((bf16[128,1024]{1,0:T(8,128)(2,1)S(1)}, bf16[128,1024]{1,0:T(8,128)(2,1)S(1)}, u32[]{:S(2)}, u32[]{:S(2)}) %collective-permute-start.19) | collective-permute-done | bytes 262176 | tf_op jit(solution)/shard_map/ppermute | solution.py:110
  53.0 0.8 %collective-permute-done.17.refs_2_ = f32[1,128]{1,0:T(1,128)S(1)} collective-permute-done((f32[1,128]{1,0:T(1,128)S(1)}, f32[1,128]{1,0:T(1,128)S(1)}, u32[]{:S(2)}, u32[]{:S(2)}) %collective-permute-start.17) | collective-permute-done | bytes 544 | tf_op jit(solution)/shard_map/ppermute | solution.py:110
  53.9 1.1 %finish_clips.1 = (f32[128,1024]{1,0:T(8,128)}, f32[1,128]{1,0:T(1,128)}) custom-call(f32[2,128]{1,0:T(2,128)S(1)} %consts.1.refs_1_, f32[128,1024]{1,0:T(8,128)S(1)} %get-tuple-element.42.hat_ref, f32[128,1]{1,0:T(8,128)S(1)} %get-tuple-element.43.inverse_ref, f32[1,128]{1,0:T(1,128)S(1)} %get-tuple-element.64.refs_0_, ...), custom_call_target="tpu_custom_call" | custom-call | tf_op jit(solution)/shard_map/finish_clips/pallas_call | solution.py:28
  (48 shorter events, 2.1 us)
Async XLA Ops:
  2.2 10.5 %collective-permute-start.3 = (bf16[64,1024]{1,0:T(8,128)(2,1)S(1)}, bf16[64,1024]{1,0:T(8,128)(2,1)S(1)}, u32[]{:S(2)}, u32[]{:S(2)}) collective-permute-start(bf16[64,1024]{1,0:T(8,128)(2,1)S(1)} %get-tuple-element.47), channel_id=1, source_target_pairs={{0,2},{1,3},{2,0},{3,1},{4,6},{5,7},{6,4},{7,5},{8,10},{9,11},{10,... | collective-permute-start | bytes 393224 | tf_op jit(solution)/shard_map/ppermute | solution.py:110
  5.3 14.3 %collective-permute-start.1 = (bf16[128,1024]{1,0:T(8,128)(2,1)S(1)}, bf16[128,1024]{1,0:T(8,128)(2,1)S(1)}, u32[]{:S(2)}, u32[]{:S(2)}) collective-permute-start(bf16[128,1024]{1,0:T(8,128)(2,1)S(1)} %get-tuple-element.45.refs_0_), channel_id=1, source_target_pairs={{0,4},{1,5},{2,6},{3,7},{4,0},{5,1},{6,2},{7,3},{8,12},{9,13},{10,... | collective-permute-start | bytes 786440 | tf_op jit(solution)/shard_map/ppermute | solution.py:110
  7.8 13.3 %collective-permute-start = (bf16[128,1024]{1,0:T(8,128)(2,1)S(1)}, bf16[128,1024]{1,0:T(8,128)(2,1)S(1)}, u32[]{:S(2)}, u32[]{:S(2)}) collective-permute-start(bf16[128,1024]{1,0:T(8,128)(2,1)S(1)} %get-tuple-element.45.refs_0_), channel_id=1, source_target_pairs={{0,16},{8,24},{16,0},{24,8},{1,17},{9,25},{17,1},{25,9},{2,18},{10... | collective-permute-start | bytes 786440 | tf_op jit(solution)/shard_map/ppermute | solution.py:110
  9.4 7.1 %collective-permute-start.4 = (bf16[64,1024]{1,0:T(8,128)(2,1)S(1)}, bf16[64,1024]{1,0:T(8,128)(2,1)S(1)}, u32[]{:S(2)}, u32[]{:S(2)}) collective-permute-start(bf16[64,1024]{1,0:T(8,128)(2,1)S(1)} %get-tuple-element.48), channel_id=1, source_target_pairs={{0,2},{1,3},{2,0},{3,1},{4,6},{5,7},{6,4},{7,5},{8,10},{9,11},{10,... | collective-permute-start | bytes 393224 | tf_op jit(solution)/shard_map/ppermute | solution.py:110
  9.8 11.3 %collective-permute-start.2 = (bf16[128,1024]{1,0:T(8,128)(2,1)S(1)}, bf16[128,1024]{1,0:T(8,128)(2,1)S(1)}, u32[]{:S(2)}, u32[]{:S(2)}) collective-permute-start(bf16[128,1024]{1,0:T(8,128)(2,1)S(1)} %get-tuple-element.46.refs_2_), channel_id=1, source_target_pairs={{0,8},{8,0},{16,24},{24,16},{1,9},{9,1},{17,25},{25,17},{2,10},{10... | collective-permute-start | bytes 786440 | tf_op jit(solution)/shard_map/ppermute | solution.py:110
  12.6 9.1 %collective-permute-start.7 = (bf16[64,1024]{1,0:T(8,128)(2,1)S(1)}, bf16[64,1024]{1,0:T(8,128)(2,1)S(1)}, u32[]{:S(2)}, u32[]{:S(2)}) collective-permute-start(bf16[64,1024]{1,0:T(8,128)(2,1)S(1)} %clips_z.2.refs_4_), channel_id=1, source_target_pairs={{0,8},{8,0},{16,24},{24,16},{1,9},{9,1},{17,25},{25,17},{2,10},{10... | collective-permute-start | bytes 393224 | tf_op jit(solution)/shard_map/ppermute | solution.py:110
  16.5 5.9 %collective-permute-start.8 = (bf16[64,1024]{1,0:T(8,128)(2,1)S(1)}, bf16[64,1024]{1,0:T(8,128)(2,1)S(1)}, u32[]{:S(2)}, u32[]{:S(2)}) collective-permute-start(bf16[64,1024]{1,0:T(8,128)(2,1)S(1)} %clips_z.3.refs_5_), channel_id=1, source_target_pairs={{0,8},{8,0},{16,24},{24,16},{1,9},{9,1},{17,25},{25,17},{2,10},{10... | collective-permute-start | bytes 393224 | tf_op jit(solution)/shard_map/ppermute | solution.py:110
  19.6 8.8 %collective-permute-start.10 = (bf16[128,1024]{1,0:T(8,128)(2,1)S(1)}, bf16[128,1024]{1,0:T(8,128)(2,1)S(1)}, u32[]{:S(2)}, u32[]{:S(2)}) collective-permute-start(bf16[128,1024]{1,0:T(8,128)(2,1)S(1)} %captions_z.1.refs_1_.refs_0_), channel_id=1, source_target_pairs={{0,16},{8,24},{16,0},{24,8},{1,17},{9,25},{17,1},{25,9},{2,18},{10... | collective-permute-start | bytes 786440 | tf_op jit(solution)/shard_map/ppermute | solution.py:110
  21.1 3.4 %collective-permute-start.6 = (bf16[128,1024]{1,0:T(8,128)(2,1)S(1)}, bf16[128,1024]{1,0:T(8,128)(2,1)S(1)}, u32[]{:S(2)}, u32[]{:S(2)}) collective-permute-start(bf16[128,1024]{1,0:T(8,128)(2,1)S(1)} %captions_z.1.refs_1_.refs_0_), channel_id=1, source_target_pairs={{0,1},{1,0},{2,3},{3,2},{4,5},{5,4},{6,7},{7,6},{8,9},{9,8},{10,11... | collective-permute-start | bytes 786440 | tf_op jit(solution)/shard_map/ppermute | solution.py:110
  21.2 3.3 %collective-permute-start.5 = (bf16[640,1024]{1,0:T(8,128)(2,1)S(1)}, bf16[640,1024]{1,0:T(8,128)(2,1)S(1)}, u32[]{:S(2)}, u32[]{:S(2)}) collective-permute-start(bf16[640,1024]{1,0:T(8,128)(2,1)S(1)} %near_blocks.1.N), channel_id=1, source_target_pairs={{0,1},{1,0},{2,3},{3,2},{4,5},{5,4},{6,7},{7,6},{8,9},{9,8},{10,11... | collective-permute-start | bytes 3932168 | tf_op jit(solution)/shard_map/ppermute | solution.py:110
  22.4 4.6 %collective-permute-start.9 = (bf16[128,1024]{1,0:T(8,128)(2,1)S(1)}, bf16[128,1024]{1,0:T(8,128)(2,1)S(1)}, u32[]{:S(2)}, u32[]{:S(2)}) collective-permute-start(bf16[128,1024]{1,0:T(8,128)(2,1)S(1)} %diagonal_clips.1.vd), channel_id=1, source_target_pairs={{0,1},{1,0},{2,3},{3,2},{4,5},{5,4},{6,7},{7,6},{8,9},{9,8},{10,11... | collective-permute-start | bytes 786440 | tf_op jit(solution)/shard_map/ppermute | solution.py:110
  28.4 2.4 %collective-permute-start.11 = (bf16[128,1024]{1,0:T(8,128)(2,1)S(1)}, bf16[128,1024]{1,0:T(8,128)(2,1)S(1)}, u32[]{:S(2)}, u32[]{:S(2)}) collective-permute-start(bf16[128,1024]{1,0:T(8,128)(2,1)S(1)} %captions_d.1.refs_0_), channel_id=1, source_target_pairs={{0,1},{1,0},{2,3},{3,2},{4,5},{5,4},{6,7},{7,6},{8,9},{9,8},{10,11... | collective-permute-start | bytes 786440 | tf_op jit(solution)/shard_map/ppermute | solution.py:110
  30.2 5.8 %collective-permute-start.12 = (bf16[64,1024]{1,0:T(8,128)(2,1)S(1)}, bf16[64,1024]{1,0:T(8,128)(2,1)S(1)}, u32[]{:S(2)}, u32[]{:S(2)}) collective-permute-start(bf16[64,1024]{1,0:T(8,128)(2,1)S(1)} %get-tuple-element.62), channel_id=1, source_target_pairs={{0,16},{8,24},{16,0},{24,8},{1,17},{9,25},{17,1},{25,9},{2,18},{10... | collective-permute-start | bytes 393224 | tf_op jit(solution)/shard_map/ppermute | solution.py:110
  31.9 10.3 %collective-permute-start.16 = (bf16[128,1024]{1,0:T(8,128)(2,1)S(1)}, bf16[128,1024]{1,0:T(8,128)(2,1)S(1)}, u32[]{:S(2)}, u32[]{:S(2)}) collective-permute-start(bf16[128,1024]{1,0:T(8,128)(2,1)S(1)} %get-tuple-element.60.after.refs_1_), channel_id=1, source_target_pairs={{0,8},{8,0},{16,24},{24,16},{1,9},{9,1},{17,25},{25,17},{2,10},{10... | collective-permute-start | bytes 786440 | tf_op jit(solution)/shard_map/ppermute | solution.py:110
  33.5 6.1 %collective-permute-start.14 = (bf16[64,1024]{1,0:T(8,128)(2,1)S(1)}, bf16[64,1024]{1,0:T(8,128)(2,1)S(1)}, u32[]{:S(2)}, u32[]{:S(2)}) collective-permute-start(bf16[64,1024]{1,0:T(8,128)(2,1)S(1)} %far_b.2), channel_id=1, source_target_pairs={{0,16},{8,24},{16,0},{24,8},{1,17},{9,25},{17,1},{25,9},{2,18},{10... | collective-permute-start | bytes 393224 | tf_op jit(solution)/shard_map/ppermute | solution.py:110
  36.1 10.3 %collective-permute-start.21 = (bf16[64,1024]{1,0:T(8,128)(2,1)S(1)}, bf16[64,1024]{1,0:T(8,128)(2,1)S(1)}, u32[]{:S(2)}, u32[]{:S(2)}) collective-permute-start(bf16[64,1024]{1,0:T(8,128)(2,1)S(1)} %add_a.1.after), channel_id=1, source_target_pairs={{0,4},{1,5},{2,6},{3,7},{4,0},{5,1},{6,2},{7,3},{8,12},{9,13},{10,... | collective-permute-start | bytes 393224 | tf_op jit(solution)/shard_map/ppermute | solution.py:110
  38.2 4.0 %collective-permute-start.13 = (f32[2,128]{1,0:T(2,128)S(1)}, f32[2,128]{1,0:T(2,128)S(1)}, u32[]{:S(2)}, u32[]{:S(2)}) collective-permute-start(f32[2,128]{1,0:T(2,128)S(1)} %get-tuple-element.65), channel_id=1, source_target_pairs={{0,8},{8,0},{16,24},{24,16},{1,9},{9,1},{17,25},{25,17},{2,10},{10... | collective-permute-start | bytes 3080 | tf_op jit(solution)/shard_map/ppermute | solution.py:110
  39.6 10.7 %collective-permute-start.15 = (bf16[64,1024]{1,0:T(8,128)(2,1)S(1)}, bf16[64,1024]{1,0:T(8,128)(2,1)S(1)}, u32[]{:S(2)}, u32[]{:S(2)}) collective-permute-start(bf16[64,1024]{1,0:T(8,128)(2,1)S(1)} %add_b.1.refs_1_), channel_id=1, source_target_pairs={{0,4},{1,5},{2,6},{3,7},{4,0},{5,1},{6,2},{7,3},{8,12},{9,13},{10,... | collective-permute-start | bytes 393224 | tf_op jit(solution)/shard_map/ppermute | solution.py:110
  42.3 10.7 %collective-permute-start.19 = (bf16[128,1024]{1,0:T(8,128)(2,1)S(1)}, bf16[128,1024]{1,0:T(8,128)(2,1)S(1)}, u32[]{:S(2)}, u32[]{:S(2)}) collective-permute-start(bf16[128,1024]{1,0:T(8,128)(2,1)S(1)} %add_clips.1.sum_v.refs_1_), channel_id=1, source_target_pairs={{0,2},{1,3},{2,0},{3,1},{4,6},{5,7},{6,4},{7,5},{8,10},{9,11},{10,... | collective-permute-start | bytes 786440 | tf_op jit(solution)/shard_map/ppermute | solution.py:110
  42.9 7.4 %collective-permute-start.18 = (bf16[128,1024]{1,0:T(8,128)(2,1)S(1)}, bf16[128,1024]{1,0:T(8,128)(2,1)S(1)}, u32[]{:S(2)}, u32[]{:S(2)}) collective-permute-start(bf16[128,1024]{1,0:T(8,128)(2,1)S(1)} %near_x.1), channel_id=1, source_target_pairs={{0,8},{8,0},{16,24},{24,16},{1,9},{9,1},{17,25},{25,17},{2,10},{10... | collective-permute-start | bytes 786440 | tf_op jit(solution)/shard_map/ppermute | solution.py:110
  44.9 6.4 %collective-permute-start.20 = (bf16[128,1024]{1,0:T(8,128)(2,1)S(1)}, bf16[128,1024]{1,0:T(8,128)(2,1)S(1)}, u32[]{:S(2)}, u32[]{:S(2)}) collective-permute-start(bf16[128,1024]{1,0:T(8,128)(2,1)S(1)} %near_y.1), channel_id=1, source_target_pairs={{0,16},{8,24},{16,0},{24,8},{1,17},{9,25},{17,1},{25,9},{2,18},{10... | collective-permute-start | bytes 786440 | tf_op jit(solution)/shard_map/ppermute | solution.py:110
  50.3 3.5 %collective-permute-start.17 = (f32[1,128]{1,0:T(1,128)S(1)}, f32[1,128]{1,0:T(1,128)S(1)}, u32[]{:S(2)}, u32[]{:S(2)}) collective-permute-start(f32[1,128]{1,0:T(1,128)S(1)} %add_loss.1.refs_4_), channel_id=1, source_target_pairs={{0,2},{1,3},{2,0},{3,1},{4,6},{5,7},{6,4},{7,5},{8,10},{9,11},{10,... | collective-permute-start | bytes 1544 | tf_op jit(solution)/shard_map/ppermute | solution.py:110

commit v13 on v11

--- a/solution.py
+++ b/solution.py
@@ -8,7 +8,7 @@
 F32, BF16 = jnp.float32, jnp.bfloat16
 MIB = 1024 * 1024
 CHUNK = 256
-PARTS = 4
+PARTS = 8
 LONG = 10**10
 SPECS = {
     "s": pl.BlockSpec(memory_space=pltpu.SMEM),

time: 54.6 us -> 54.7 us (level)
  no operation moved by 1% of the time
where the time goes in v13:
time: 54.7 us; the launch traced here: 54.5 us
  starting transfers between devices  25.2 us (46%)
  waiting for transfers between devices  14.8 us (27%)
  Pallas kernels  12.4 us (23%)
  between operations  2.13 us (4%)
    ppermute x22, starting transfers between devices, swap(): return lax.ppermute(value, axis, [(i, i ^ bits) for i in range(size)])  25.2 us
    ppermute x22, waiting for transfers between devices, swap(): return lax.ppermute(value, axis, [(i, i ^ bits) for i in range(size)])  14.8 us
    pallas_call x35, Pallas kernels, call(): pl.pallas_call(kernel, name=name, out_shape=out_shape, in_specs=[SPECS[sp...  12.4 us
  transfers between devices with their start and end apart: 22, of which 12 were waited for; matrix products, arithmetic and copies ran while one was open for 0% of the time, Pallas kernels for 18%

profile of v13, /device:TPU:0, one launch (start us, length us, event | category | flops | bytes accessed | tf_op | source)
XLA Modules:
  0.0 54.5 jit_solution(10741185568467352883)
XLA Ops:
  0.6 1.6 %normalize.1 = (bf16[128,1024]{1,0:T(8,128)(2,1)S(1)}, bf16[128,1024]{1,0:T(8,128)(2,1)S(1)}, bf16[64,1024]{1,0:T(8,128)(2,1)S(1)}, bf16[64,1024]{1,0:T(8,128)(2...) custom-call(f32[128,1024]{1,0:T(8,128)} %film.1, ...), custom_call_target="tpu_custom_call" | custom-call | tf_op jit(solution)/shard_map/normalize/pallas_call | solution.py:28
  2.2 3.1 %collective-permute-start.2 = (bf16[64,1024]{1,0:T(8,128)(2,1)S(1)}, bf16[64,1024]{1,0:T(8,128)(2,1)S(1)}, u32[]{:S(2)}, u32[]{:S(2)}) collective-permute-start(bf16[64,1024]{1,0:T(8,128)(2,1)S(1)} %get-tuple-element.47), channel_id=1, source_target_pairs={{0,2},{1,3},{2,0},{3,1},{4,6},{5,7},{6,4},{7,5},{8,10},{9,11},{10,... | collective-permute-start | bytes 393224 | tf_op jit(solution)/shard_map/ppermute | solution.py:110
  5.3 2.6 %collective-permute-start.5 = (bf16[128,1024]{1,0:T(8,128)(2,1)S(1)}, bf16[128,1024]{1,0:T(8,128)(2,1)S(1)}, u32[]{:S(2)}, u32[]{:S(2)}) collective-permute-start(bf16[128,1024]{1,0:T(8,128)(2,1)S(1)} %get-tuple-element.45.refs_0_), channel_id=1, source_target_pairs={{0,4},{1,5},{2,6},{3,7},{4,0},{5,1},{6,2},{7,3},{8,12},{9,13},{10,... | collective-permute-start | bytes 786440 | tf_op jit(solution)/shard_map/ppermute | solution.py:110
  7.9 1.5 %collective-permute-start = (bf16[128,1024]{1,0:T(8,128)(2,1)S(1)}, bf16[128,1024]{1,0:T(8,128)(2,1)S(1)}, u32[]{:S(2)}, u32[]{:S(2)}) collective-permute-start(bf16[128,1024]{1,0:T(8,128)(2,1)S(1)} %get-tuple-element.45.refs_0_), channel_id=1, source_target_pairs={{0,16},{8,24},{16,0},{24,8},{1,17},{9,25},{17,1},{25,9},{2,18},{10... | collective-permute-start | bytes 786440 | tf_op jit(solution)/shard_map/ppermute | solution.py:110
  9.8 1.5 %collective-permute-start.1 = (bf16[128,1024]{1,0:T(8,128)(2,1)S(1)}, bf16[128,1024]{1,0:T(8,128)(2,1)S(1)}, u32[]{:S(2)}, u32[]{:S(2)}) collective-permute-start(bf16[128,1024]{1,0:T(8,128)(2,1)S(1)} %get-tuple-element.46.refs_2_), channel_id=1, source_target_pairs={{0,8},{8,0},{16,24},{24,16},{1,9},{9,1},{17,25},{25,17},{2,10},{10... | collective-permute-start | bytes 786440 | tf_op jit(solution)/shard_map/ppermute | solution.py:110
  12.7 0.6 %collective-permute-start.7 = (bf16[64,1024]{1,0:T(8,128)(2,1)S(1)}, bf16[64,1024]{1,0:T(8,128)(2,1)S(1)}, u32[]{:S(2)}, u32[]{:S(2)}) collective-permute-start(bf16[64,1024]{1,0:T(8,128)(2,1)S(1)} %clips_z.2.refs_4_), channel_id=1, source_target_pairs={{0,8},{8,0},{16,24},{24,16},{1,9},{9,1},{17,25},{25,17},{2,10},{10... | collective-permute-start | bytes 393224 | tf_op jit(solution)/shard_map/ppermute | solution.py:110
  13.3 3.2 %collective-permute-done.3.refs_0_ = bf16[64,1024]{1,0:T(8,128)(2,1)S(1)} collective-permute-done((bf16[64,1024]{1,0:T(8,128)(2,1)S(1)}, bf16[64,1024]{1,0:T(8,128)(2,1)S(1)}, u32[]{:S(2)}, u32[]{:S(2)}) %collective-permute-start.3) | collective-permute-done | bytes 131104 | tf_op jit(solution)/shard_map/ppermute | solution.py:110
  16.5 1.5 %collective-permute-start.8 = (bf16[64,1024]{1,0:T(8,128)(2,1)S(1)}, bf16[64,1024]{1,0:T(8,128)(2,1)S(1)}, u32[]{:S(2)}, u32[]{:S(2)}) collective-permute-start(bf16[64,1024]{1,0:T(8,128)(2,1)S(1)} %clips_z.3.refs_5_), channel_id=1, source_target_pairs={{0,8},{8,0},{16,24},{24,16},{1,9},{9,1},{17,25},{25,17},{2,10},{10... | collective-permute-start | bytes 393224 | tf_op jit(solution)/shard_map/ppermute | solution.py:110
  18.3 1.3 %collective-permute-done.5.refs_0_ = bf16[128,1024]{1,0:T(8,128)(2,1)S(1)} collective-permute-done((bf16[128,1024]{1,0:T(8,128)(2,1)S(1)}, bf16[128,1024]{1,0:T(8,128)(2,1)S(1)}, u32[]{:S(2)}, u32[]{:S(2)}) %collective-permute-start.5) | collective-permute-done | bytes 262176 | tf_op jit(solution)/shard_map/ppermute | solution.py:110
  19.6 1.5 %collective-permute-start.10 = (bf16[128,1024]{1,0:T(8,128)(2,1)S(1)}, bf16[128,1024]{1,0:T(8,128)(2,1)S(1)}, u32[]{:S(2)}, u32[]{:S(2)}) collective-permute-start(bf16[128,1024]{1,0:T(8,128)(2,1)S(1)} %captions_z.1.refs_0_), channel_id=1, source_target_pairs={{0,16},{8,24},{16,0},{24,8},{1,17},{9,25},{17,1},{25,9},{2,18},{10... | collective-permute-start | bytes 786440 | tf_op jit(solution)/shard_map/ppermute | solution.py:110
  21.1 1.2 %collective-permute-done.8.refs_0_ = bf16[64,1024]{1,0:T(8,128)(2,1)S(1)} collective-permute-done((bf16[64,1024]{1,0:T(8,128)(2,1)S(1)}, bf16[64,1024]{1,0:T(8,128)(2,1)S(1)}, u32[]{:S(2)}, u32[]{:S(2)}) %collective-permute-start.8) | collective-permute-done | bytes 131104 | tf_op jit(solution)/shard_map/ppermute | solution.py:110
  22.7 2.5 %early_pairs.1 = (bf16[768,1024]{1,0:T(8,128)(2,1)S(1)}, bf16[384,768]{1,0:T(8,128)(2,1)S(1)}, bf16[384,384]{1,0:T(8,128)(2,1)S(1)}, f32[1,384]{1,0:T(1,128)S(1)}) custom-call(f32[2,128]{1,0:T(2,128)S(1)} %consts.1.refs_1_, s32[1,1024]{1,0:T(1,128)S(1)} %get-tuple-element.44.labels, bf16[640,1024]{1,0:T(8,128)(2,1)S(1)} %near_blocks.1.N, ...), custom_call_target="tpu_custom_call" | custom-call | flops 905969664 | tf_op jit(solution)/shard_map/early_pairs/pallas_call | solution.py:28
  25.2 1.3 %middle_pairs.1 = (bf16[1024,1024]{1,0:T(8,128)(2,1)S(1)}, bf16[768,512]{1,0:T(8,128)(2,1)S(1)}, bf16[384,1024]{1,0:T(8,128)(2,1)S(1)}, f32[1,128]{1,0:T(1,128)S(1)}) custom-call(f32[2,128]{1,0:T(2,128)S(1)} %consts.1.refs_1_, s32[1,1024]{1,0:T(1,128)S(1)} %get-tuple-element.44.labels, bf16[640,1024]{1,0:T(8,128)(2,1)S(1)} %near_blocks.1.N, ...), custom_call_target="tpu_custom_call" | custom-call | flops 301989888 | tf_op jit(solution)/shard_map/middle_pairs/pallas_call | solution.py:28
  26.5 0.6 %collective-permute-done.10.refs_0_ = bf16[128,1024]{1,0:T(8,128)(2,1)S(1)} collective-permute-done((bf16[128,1024]{1,0:T(8,128)(2,1)S(1)}, bf16[128,1024]{1,0:T(8,128)(2,1)S(1)}, u32[]{:S(2)}, u32[]{:S(2)}) %collective-permute-start.10) | collective-permute-done | bytes 262176 | tf_op jit(solution)/shard_map/ppermute | solution.py:110
  27.1 1.4 %far_captions.1 = (f32[1,512]{1,0:T(1,128)S(1)}, bf16[128,512]{1,0:T(8,128)(2,1)S(1)}, bf16[64,1024]{1,0:T(8,128)(2,1)S(1)}, bf16[64,1024]{1,0:T(8,128)(2,1)S(1)}) custom-call(f32[2,128]{1,0:T(2,128)S(1)} %consts.1.refs_1_, s32[1,1024]{1,0:T(1,128)S(1)} %get-tuple-element.44.labels, bf16[1024,1024]{1,0:T(8,128)(2,1)S(1)} %get-tuple-element.54.VV, ...), custom_call_target="tpu_custom_call" | custom-call | flops 536870912 | tf_op jit(solution)/shard_map/far_captions/pallas_call | solution.py:28
  28.5 1.4 %collective-permute-start.12 = (bf16[64,1024]{1,0:T(8,128)(2,1)S(1)}, bf16[64,1024]{1,0:T(8,128)(2,1)S(1)}, u32[]{:S(2)}, u32[]{:S(2)}) collective-permute-start(bf16[64,1024]{1,0:T(8,128)(2,1)S(1)} %get-tuple-element.62), channel_id=1, source_target_pairs={{0,16},{8,24},{16,0},{24,8},{1,17},{9,25},{17,1},{25,9},{2,18},{10... | collective-permute-start | bytes 393224 | tf_op jit(solution)/shard_map/ppermute | solution.py:110
  29.9 1.2 %far_clips.1 = (bf16[256,1024]{1,0:T(8,128)(2,1)S(1)}, bf16[256,512]{1,0:T(8,128)(2,1)S(1)}, f32[1,512]{1,0:T(1,128)S(1)}, bf16[128,1024]{1,0:T(8,128)(2,1)S(1)}) custom-call(f32[2,128]{1,0:T(2,128)S(1)} %consts.1.refs_1_, s32[1,1024]{1,0:T(1,128)S(1)} %get-tuple-element.44.labels, bf16[1024,1024]{1,0:T(8,128)(2,1)S(1)} %get-tuple-element.54.VV, ...), custom_call_target="tpu_custom_call" | custom-call | flops 402653184 | tf_op jit(solution)/shard_map/far_clips/pallas_call | solution.py:28
  31.1 1.2 %collective-permute-start.16 = (bf16[128,1024]{1,0:T(8,128)(2,1)S(1)}, bf16[128,1024]{1,0:T(8,128)(2,1)S(1)}, u32[]{:S(2)}, u32[]{:S(2)}) collective-permute-start(bf16[128,1024]{1,0:T(8,128)(2,1)S(1)} %get-tuple-element.60.after.refs_1_), channel_id=1, source_target_pairs={{0,8},{8,0},{16,24},{24,16},{1,9},{9,1},{17,25},{25,17},{2,10},{10... | collective-permute-start | bytes 786440 | tf_op jit(solution)/shard_map/ppermute | solution.py:110
  32.3 1.1 %collective-permute-start.14 = (bf16[64,1024]{1,0:T(8,128)(2,1)S(1)}, bf16[64,1024]{1,0:T(8,128)(2,1)S(1)}, u32[]{:S(2)}, u32[]{:S(2)}) collective-permute-start(bf16[64,1024]{1,0:T(8,128)(2,1)S(1)} %far_b.2), channel_id=1, source_target_pairs={{0,16},{8,24},{16,0},{24,8},{1,17},{9,25},{17,1},{25,9},{2,18},{10... | collective-permute-start | bytes 393224 | tf_op jit(solution)/shard_map/ppermute | solution.py:110
  33.4 1.0 %near_captions.1 = (f32[128,1024]{1,0:T(8,128)S(1)}, bf16[128,1024]{1,0:T(8,128)(2,1)S(1)}, f32[64,1024]{1,0:T(8,128)S(1)}, f32[64,1024]{1,0:T(8,128)S(1)}) custom-call(bf16[384,1024]{1,0:T(8,128)(2,1)S(1)} %get-tuple-element.59.coef, bf16[1024,1024]{1,0:T(8,128)(2,1)S(1)} %get-tuple-element.54.VV, bf16[128,1024]{1,0:T(8,128)(2,1)S(1)} %get-tuple-element.60.after.refs_1_), custom_call_target="tpu_custom_call" | custom-call | flops 805306368 | tf_op jit(solution)/shard_map/near_captions/pallas_call | solution.py:28
  34.5 3.4 %collective-permute-start.21 = (bf16[64,1024]{1,0:T(8,128)(2,1)S(1)}, bf16[64,1024]{1,0:T(8,128)(2,1)S(1)}, u32[]{:S(2)}, u32[]{:S(2)}) collective-permute-start(bf16[64,1024]{1,0:T(8,128)(2,1)S(1)} %add_a.1.after), channel_id=1, source_target_pairs={{0,4},{1,5},{2,6},{3,7},{4,0},{5,1},{6,2},{7,3},{8,12},{9,13},{10,... | collective-permute-start | bytes 393224 | tf_op jit(solution)/shard_map/ppermute | solution.py:110
  38.5 1.0 %near_clips.1 = (f32[128,1024]{1,0:T(8,128)S(1)}, bf16[128,1024]{1,0:T(8,128)(2,1)S(1)}, f32[128,1024]{1,0:T(8,128)S(1)}) custom-call(bf16[768,1024]{1,0:T(8,128)(2,1)S(1)} %get-tuple-element.50.S1, bf16[256,1024]{1,0:T(8,128)(2,1)S(1)} %get-tuple-element.68.S2, bf16[768,512]{1,0:T(8,128)(2,1)S(1)} %get-tuple-element.56.G1, ...), custom_call_target="tpu_custom_call" | custom-call | flops 805306368 | tf_op jit(solution)/shard_map/near_clips/pallas_call | solution.py:28
  39.6 1.2 %collective-permute-start.15 = (bf16[64,1024]{1,0:T(8,128)(2,1)S(1)}, bf16[64,1024]{1,0:T(8,128)(2,1)S(1)}, u32[]{:S(2)}, u32[]{:S(2)}) collective-permute-start(bf16[64,1024]{1,0:T(8,128)(2,1)S(1)} %add_b.1.refs_1_), channel_id=1, source_target_pairs={{0,4},{1,5},{2,6},{3,7},{4,0},{5,1},{6,2},{7,3},{8,12},{9,13},{10,... | collective-permute-start | bytes 393224 | tf_op jit(solution)/shard_map/ppermute | solution.py:110
  40.7 0.8 %collective-permute-done.13.refs_0_ = f32[2,128]{1,0:T(2,128)S(1)} collective-permute-done((f32[2,128]{1,0:T(2,128)S(1)}, f32[2,128]{1,0:T(2,128)S(1)}, u32[]{:S(2)}, u32[]{:S(2)}) %collective-permute-start.13) | collective-permute-done | bytes 1056 | tf_op jit(solution)/shard_map/ppermute | solution.py:110
  41.6 0.7 %collective-permute-start.19 = (bf16[128,1024]{1,0:T(8,128)(2,1)S(1)}, bf16[128,1024]{1,0:T(8,128)(2,1)S(1)}, u32[]{:S(2)}, u32[]{:S(2)}) collective-permute-start(bf16[128,1024]{1,0:T(8,128)(2,1)S(1)} %add_clips.1.sum_v.refs_1_), channel_id=1, source_target_pairs={{0,2},{1,3},{2,0},{3,1},{4,6},{5,7},{6,4},{7,5},{8,10},{9,11},{10,... | collective-permute-start | bytes 786440 | tf_op jit(solution)/shard_map/ppermute | solution.py:110
  42.3 0.8 %collective-permute-start.18 = (bf16[128,1024]{1,0:T(8,128)(2,1)S(1)}, bf16[128,1024]{1,0:T(8,128)(2,1)S(1)}, u32[]{:S(2)}, u32[]{:S(2)}) collective-permute-start(bf16[128,1024]{1,0:T(8,128)(2,1)S(1)} %near_x.1), channel_id=1, source_target_pairs={{0,8},{8,0},{16,24},{24,16},{1,9},{9,1},{17,25},{25,17},{2,10},{10... | collective-permute-start | bytes 786440 | tf_op jit(solution)/shard_map/ppermute | solution.py:110
  43.2 1.9 %collective-permute-start.20 = (bf16[128,1024]{1,0:T(8,128)(2,1)S(1)}, bf16[128,1024]{1,0:T(8,128)(2,1)S(1)}, u32[]{:S(2)}, u32[]{:S(2)}) collective-permute-start(bf16[128,1024]{1,0:T(8,128)(2,1)S(1)} %near_y.1), channel_id=1, source_target_pairs={{0,16},{8,24},{16,0},{24,8},{1,17},{9,25},{17,1},{25,9},{2,18},{10... | collective-permute-start | bytes 786440 | tf_op jit(solution)/shard_map/ppermute | solution.py:110
  45.1 2.9 %collective-permute-done.21.refs_0_ = bf16[64,1024]{1,0:T(8,128)(2,1)S(1)} collective-permute-done((bf16[64,1024]{1,0:T(8,128)(2,1)S(1)}, bf16[64,1024]{1,0:T(8,128)(2,1)S(1)}, u32[]{:S(2)}, u32[]{:S(2)}) %collective-permute-start.21) | collective-permute-done | bytes 131104 | tf_op jit(solution)/shard_map/ppermute | solution.py:110
  48.0 1.9 %collective-permute-done.15.got.refs_0_ = bf16[64,1024]{1,0:T(8,128)(2,1)S(1)} collective-permute-done((bf16[64,1024]{1,0:T(8,128)(2,1)S(1)}, bf16[64,1024]{1,0:T(8,128)(2,1)S(1)}, u32[]{:S(2)}, u32[]{:S(2)}) %collective-permute-start.15) | collective-permute-done | bytes 131104 | tf_op jit(solution)/shard_map/ppermute | solution.py:110
  49.9 1.1 %finish_captions.1 = (f32[128,1024]{1,0:T(8,128)}, f32[8,128]{1,0:T(8,128)S(1)}) custom-call(f32[2,128]{1,0:T(2,128)S(1)} %consts.1.refs_1_, f32[128,1024]{1,0:T(8,128)S(1)} %get-tuple-element.74.hat_ref, f32[128,1]{1,0:T(8,128)S(1)} %get-tuple-element.75.inverse_ref, f32[128,1024]{1,0:T(8,128)S(1)} %get-tuple-element.63.refs_1_.refs_0_, ...), custom_call_target="tpu_custom_call" | custom-call | tf_op jit(solution)/shard_map/finish_captions/pallas_call | solution.py:28
  51.0 1.9 %collective-permute-done.19.refs_0_ = bf16[128,1024]{1,0:T(8,128)(2,1)S(1)} collective-permute-done((bf16[128,1024]{1,0:T(8,128)(2,1)S(1)}, bf16[128,1024]{1,0:T(8,128)(2,1)S(1)}, u32[]{:S(2)}, u32[]{:S(2)}) %collective-permute-start.19) | collective-permute-done | bytes 262176 | tf_op jit(solution)/shard_map/ppermute | solution.py:110
  53.4 1.1 %finish_clips.1 = (f32[128,1024]{1,0:T(8,128)}, f32[1,128]{1,0:T(1,128)}) custom-call(f32[2,128]{1,0:T(2,128)S(1)} %consts.1.refs_1_, f32[128,1024]{1,0:T(8,128)S(1)} %get-tuple-element.42.hat_ref, f32[128,1]{1,0:T(8,128)S(1)} %get-tuple-element.43.inverse_ref, f32[1,128]{1,0:T(1,128)S(1)} %get-tuple-element.64.refs_0_, ...), custom_call_target="tpu_custom_call" | custom-call | tf_op jit(solution)/shard_map/finish_clips/pallas_call | solution.py:28
  (47 shorter events, 2.4 us)
Async XLA Ops:
  2.2 10.5 %collective-permute-start.2 = (bf16[64,1024]{1,0:T(8,128)(2,1)S(1)}, bf16[64,1024]{1,0:T(8,128)(2,1)S(1)}, u32[]{:S(2)}, u32[]{:S(2)}) collective-permute-start(bf16[64,1024]{1,0:T(8,128)(2,1)S(1)} %get-tuple-element.47), channel_id=1, source_target_pairs={{0,2},{1,3},{2,0},{3,1},{4,6},{5,7},{6,4},{7,5},{8,10},{9,11},{10,... | collective-permute-start | bytes 393224 | tf_op jit(solution)/shard_map/ppermute | solution.py:110
  5.3 14.3 %collective-permute-start.5 = (bf16[128,1024]{1,0:T(8,128)(2,1)S(1)}, bf16[128,1024]{1,0:T(8,128)(2,1)S(1)}, u32[]{:S(2)}, u32[]{:S(2)}) collective-permute-start(bf16[128,1024]{1,0:T(8,128)(2,1)S(1)} %get-tuple-element.45.refs_0_), channel_id=1, source_target_pairs={{0,4},{1,5},{2,6},{3,7},{4,0},{5,1},{6,2},{7,3},{8,12},{9,13},{10,... | collective-permute-start | bytes 786440 | tf_op jit(solution)/shard_map/ppermute | solution.py:110
  7.9 10.3 %collective-permute-start = (bf16[128,1024]{1,0:T(8,128)(2,1)S(1)}, bf16[128,1024]{1,0:T(8,128)(2,1)S(1)}, u32[]{:S(2)}, u32[]{:S(2)}) collective-permute-start(bf16[128,1024]{1,0:T(8,128)(2,1)S(1)} %get-tuple-element.45.refs_0_), channel_id=1, source_target_pairs={{0,16},{8,24},{16,0},{24,8},{1,17},{9,25},{17,1},{25,9},{2,18},{10... | collective-permute-start | bytes 786440 | tf_op jit(solution)/shard_map/ppermute | solution.py:110
  9.4 7.1 %collective-permute-start.3 = (bf16[64,1024]{1,0:T(8,128)(2,1)S(1)}, bf16[64,1024]{1,0:T(8,128)(2,1)S(1)}, u32[]{:S(2)}, u32[]{:S(2)}) collective-permute-start(bf16[64,1024]{1,0:T(8,128)(2,1)S(1)} %get-tuple-element.48), channel_id=1, source_target_pairs={{0,2},{1,3},{2,0},{3,1},{4,6},{5,7},{6,4},{7,5},{8,10},{9,11},{10,... | collective-permute-start | bytes 393224 | tf_op jit(solution)/shard_map/ppermute | solution.py:110
  9.8 8.3 %collective-permute-start.1 = (bf16[128,1024]{1,0:T(8,128)(2,1)S(1)}, bf16[128,1024]{1,0:T(8,128)(2,1)S(1)}, u32[]{:S(2)}, u32[]{:S(2)}) collective-permute-start(bf16[128,1024]{1,0:T(8,128)(2,1)S(1)} %get-tuple-element.46.refs_2_), channel_id=1, source_target_pairs={{0,8},{8,0},{16,24},{24,16},{1,9},{9,1},{17,25},{25,17},{2,10},{10... | collective-permute-start | bytes 786440 | tf_op jit(solution)/shard_map/ppermute | solution.py:110
  12.7 8.5 %collective-permute-start.7 = (bf16[64,1024]{1,0:T(8,128)(2,1)S(1)}, bf16[64,1024]{1,0:T(8,128)(2,1)S(1)}, u32[]{:S(2)}, u32[]{:S(2)}) collective-permute-start(bf16[64,1024]{1,0:T(8,128)(2,1)S(1)} %clips_z.2.refs_4_), channel_id=1, source_target_pairs={{0,8},{8,0},{16,24},{24,16},{1,9},{9,1},{17,25},{25,17},{2,10},{10... | collective-permute-start | bytes 393224 | tf_op jit(solution)/shard_map/ppermute | solution.py:110
  16.5 5.9 %collective-permute-start.8 = (bf16[64,1024]{1,0:T(8,128)(2,1)S(1)}, bf16[64,1024]{1,0:T(8,128)(2,1)S(1)}, u32[]{:S(2)}, u32[]{:S(2)}) collective-permute-start(bf16[64,1024]{1,0:T(8,128)(2,1)S(1)} %clips_z.3.refs_5_), channel_id=1, source_target_pairs={{0,8},{8,0},{16,24},{24,16},{1,9},{9,1},{17,25},{25,17},{2,10},{10... | collective-permute-start | bytes 393224 | tf_op jit(solution)/shard_map/ppermute | solution.py:110
  18.3 4.2 %collective-permute-start.4 = (bf16[640,1024]{1,0:T(8,128)(2,1)S(1)}, bf16[640,1024]{1,0:T(8,128)(2,1)S(1)}, u32[]{:S(2)}, u32[]{:S(2)}) collective-permute-start(bf16[640,1024]{1,0:T(8,128)(2,1)S(1)} %near_blocks.1.N), channel_id=1, source_target_pairs={{0,1},{1,0},{2,3},{3,2},{4,5},{5,4},{6,7},{7,6},{8,9},{9,8},{10,11... | collective-permute-start | bytes 3932168 | tf_op jit(solution)/shard_map/ppermute | solution.py:110
  19.6 7.4 %collective-permute-start.10 = (bf16[128,1024]{1,0:T(8,128)(2,1)S(1)}, bf16[128,1024]{1,0:T(8,128)(2,1)S(1)}, u32[]{:S(2)}, u32[]{:S(2)}) collective-permute-start(bf16[128,1024]{1,0:T(8,128)(2,1)S(1)} %captions_z.1.refs_0_), channel_id=1, source_target_pairs={{0,16},{8,24},{16,0},{24,8},{1,17},{9,25},{17,1},{25,9},{2,18},{10... | collective-permute-start | bytes 786440 | tf_op jit(solution)/shard_map/ppermute | solution.py:110
  21.1 1.5 %collective-permute-start.6 = (bf16[128,1024]{1,0:T(8,128)(2,1)S(1)}, bf16[128,1024]{1,0:T(8,128)(2,1)S(1)}, u32[]{:S(2)}, u32[]{:S(2)}) collective-permute-start(bf16[128,1024]{1,0:T(8,128)(2,1)S(1)} %captions_z.1.refs_0_), channel_id=1, source_target_pairs={{0,1},{1,0},{2,3},{3,2},{4,5},{5,4},{6,7},{7,6},{8,9},{9,8},{10,11... | collective-permute-start | bytes 786440 | tf_op jit(solution)/shard_map/ppermute | solution.py:110
  22.4 2.8 %collective-permute-start.9 = (bf16[128,1024]{1,0:T(8,128)(2,1)S(1)}, bf16[128,1024]{1,0:T(8,128)(2,1)S(1)}, u32[]{:S(2)}, u32[]{:S(2)}) collective-permute-start(bf16[128,1024]{1,0:T(8,128)(2,1)S(1)} %diagonal_clips.1.vd), channel_id=1, source_target_pairs={{0,1},{1,0},{2,3},{3,2},{4,5},{5,4},{6,7},{7,6},{8,9},{9,8},{10,11... | collective-permute-start | bytes 786440 | tf_op jit(solution)/shard_map/ppermute | solution.py:110
  27.1 2.9 %collective-permute-start.11 = (bf16[128,1024]{1,0:T(8,128)(2,1)S(1)}, bf16[128,1024]{1,0:T(8,128)(2,1)S(1)}, u32[]{:S(2)}, u32[]{:S(2)}) collective-permute-start(bf16[128,1024]{1,0:T(8,128)(2,1)S(1)} %captions_d.1.refs_0_), channel_id=1, source_target_pairs={{0,1},{1,0},{2,3},{3,2},{4,5},{5,4},{6,7},{7,6},{8,9},{9,8},{10,11... | collective-permute-start | bytes 786440 | tf_op jit(solution)/shard_map/ppermute | solution.py:110
  28.5 6.0 %collective-permute-start.12 = (bf16[64,1024]{1,0:T(8,128)(2,1)S(1)}, bf16[64,1024]{1,0:T(8,128)(2,1)S(1)}, u32[]{:S(2)}, u32[]{:S(2)}) collective-permute-start(bf16[64,1024]{1,0:T(8,128)(2,1)S(1)} %get-tuple-element.62), channel_id=1, source_target_pairs={{0,16},{8,24},{16,0},{24,8},{1,17},{9,25},{17,1},{25,9},{2,18},{10... | collective-permute-start | bytes 393224 | tf_op jit(solution)/shard_map/ppermute | solution.py:110
  31.1 10.4 %collective-permute-start.16 = (bf16[128,1024]{1,0:T(8,128)(2,1)S(1)}, bf16[128,1024]{1,0:T(8,128)(2,1)S(1)}, u32[]{:S(2)}, u32[]{:S(2)}) collective-permute-start(bf16[128,1024]{1,0:T(8,128)(2,1)S(1)} %get-tuple-element.60.after.refs_1_), channel_id=1, source_target_pairs={{0,8},{8,0},{16,24},{24,16},{1,9},{9,1},{17,25},{25,17},{2,10},{10... | collective-permute-start | bytes 786440 | tf_op jit(solution)/shard_map/ppermute | solution.py:110
  32.3 7.2 %collective-permute-start.14 = (bf16[64,1024]{1,0:T(8,128)(2,1)S(1)}, bf16[64,1024]{1,0:T(8,128)(2,1)S(1)}, u32[]{:S(2)}, u32[]{:S(2)}) collective-permute-start(bf16[64,1024]{1,0:T(8,128)(2,1)S(1)} %far_b.2), channel_id=1, source_target_pairs={{0,16},{8,24},{16,0},{24,8},{1,17},{9,25},{17,1},{25,9},{2,18},{10... | collective-permute-start | bytes 393224 | tf_op jit(solution)/shard_map/ppermute | solution.py:110
  34.5 13.5 %collective-permute-start.21 = (bf16[64,1024]{1,0:T(8,128)(2,1)S(1)}, bf16[64,1024]{1,0:T(8,128)(2,1)S(1)}, u32[]{:S(2)}, u32[]{:S(2)}) collective-permute-start(bf16[64,1024]{1,0:T(8,128)(2,1)S(1)} %add_a.1.after), channel_id=1, source_target_pairs={{0,4},{1,5},{2,6},{3,7},{4,0},{5,1},{6,2},{7,3},{8,12},{9,13},{10,... | collective-permute-start | bytes 393224 | tf_op jit(solution)/shard_map/ppermute | solution.py:110
  37.9 3.6 %collective-permute-start.13 = (f32[2,128]{1,0:T(2,128)S(1)}, f32[2,128]{1,0:T(2,128)S(1)}, u32[]{:S(2)}, u32[]{:S(2)}) collective-permute-start(f32[2,128]{1,0:T(2,128)S(1)} %get-tuple-element.65), channel_id=1, source_target_pairs={{0,8},{8,0},{16,24},{24,16},{1,9},{9,1},{17,25},{25,17},{2,10},{10... | collective-permute-start | bytes 3080 | tf_op jit(solution)/shard_map/ppermute | solution.py:110
  39.6 10.3 %collective-permute-start.15 = (bf16[64,1024]{1,0:T(8,128)(2,1)S(1)}, bf16[64,1024]{1,0:T(8,128)(2,1)S(1)}, u32[]{:S(2)}, u32[]{:S(2)}) collective-permute-start(bf16[64,1024]{1,0:T(8,128)(2,1)S(1)} %add_b.1.refs_1_), channel_id=1, source_target_pairs={{0,4},{1,5},{2,6},{3,7},{4,0},{5,1},{6,2},{7,3},{8,12},{9,13},{10,... | collective-permute-start | bytes 393224 | tf_op jit(solution)/shard_map/ppermute | solution.py:110
  41.6 11.4 %collective-permute-start.19 = (bf16[128,1024]{1,0:T(8,128)(2,1)S(1)}, bf16[128,1024]{1,0:T(8,128)(2,1)S(1)}, u32[]{:S(2)}, u32[]{:S(2)}) collective-permute-start(bf16[128,1024]{1,0:T(8,128)(2,1)S(1)} %add_clips.1.sum_v.refs_1_), channel_id=1, source_target_pairs={{0,2},{1,3},{2,0},{3,1},{4,6},{5,7},{6,4},{7,5},{8,10},{9,11},{10,... | collective-permute-start | bytes 786440 | tf_op jit(solution)/shard_map/ppermute | solution.py:110
  42.3 7.6 %collective-permute-start.18 = (bf16[128,1024]{1,0:T(8,128)(2,1)S(1)}, bf16[128,1024]{1,0:T(8,128)(2,1)S(1)}, u32[]{:S(2)}, u32[]{:S(2)}) collective-permute-start(bf16[128,1024]{1,0:T(8,128)(2,1)S(1)} %near_x.1), channel_id=1, source_target_pairs={{0,8},{8,0},{16,24},{24,16},{1,9},{9,1},{17,25},{25,17},{2,10},{10... | collective-permute-start | bytes 786440 | tf_op jit(solution)/shard_map/ppermute | solution.py:110
  43.2 6.7 %collective-permute-start.20 = (bf16[128,1024]{1,0:T(8,128)(2,1)S(1)}, bf16[128,1024]{1,0:T(8,128)(2,1)S(1)}, u32[]{:S(2)}, u32[]{:S(2)}) collective-permute-start(bf16[128,1024]{1,0:T(8,128)(2,1)S(1)} %near_y.1), channel_id=1, source_target_pairs={{0,16},{8,24},{16,0},{24,8},{1,17},{9,25},{17,1},{25,9},{2,18},{10... | collective-permute-start | bytes 786440 | tf_op jit(solution)/shard_map/ppermute | solution.py:110
  49.9 3.5 %collective-permute-start.17 = (f32[1,128]{1,0:T(1,128)S(1)}, f32[1,128]{1,0:T(1,128)S(1)}, u32[]{:S(2)}, u32[]{:S(2)}) collective-permute-start(f32[1,128]{1,0:T(1,128)S(1)} %add_loss.1.refs_4_), channel_id=1, source_target_pairs={{0,2},{1,3},{2,0},{3,1},{4,6},{5,7},{6,4},{7,5},{8,10},{9,11},{10,... | collective-permute-start | bytes 1544 | tf_op jit(solution)/shard_map/ppermute | solution.py:110
